TPU v7x, 32 devices: a whole 2x2x4 slice. The times are simulated.
32 devices in a mesh: lon: 8 (over y, x, core), lat: 4 (over z).
Axes of the slice: x: 2, y: 2, z: 4, core: 2. Of those that a mesh axis runs over, the one named last changes fastest.
Arguments:
- noise: bfloat16 [4, 4, 256, 1024], P(None, None, 'lon', 'lat'), may hold values from -6 to 6
- velocity_u: float32 [4, 2, 256, 1024], P(None, None, 'lon', 'lat'), may hold values from -3 to 3
- velocity_v: float32 [4, 2, 256, 1024], P(None, None, 'lon', 'lat'), may hold values from -3 to 3
- thickness: float32 [4, 2, 256, 1024], P(None, None, 'lon', 'lat'), may hold values from 0.5 to 1.5
- land_sea: int32 [256, 1024], P('lon', 'lat'), may hold values 0 or 1
- conv_first: bfloat16 [32, 10, 3, 3], replicated, may hold values from -0.625 to 0.625
- bias_first: float32 [32], replicated, may hold values from -4 to 4
- conv_second: bfloat16 [32, 32, 3, 3], replicated, may hold values from -0.375 to 0.375
- bias_second: float32 [32], replicated, may hold values from -4 to 4
- conv_third: bfloat16 [32, 32, 3, 3], replicated, may hold values from -0.375 to 0.375
- bias_third: float32 [32], replicated, may hold values from -4 to 4
- conv_last: bfloat16 [4, 32, 3, 3], replicated, may hold values from -0.375 to 0.375
- bias_last: float32 [4], replicated, may hold values from -4 to 4
Outputs:
- new_u: float32 [4, 2, 256, 1024], P(None, None, 'lon', 'lat')
- new_v: float32 [4, 2, 256, 1024], P(None, None, 'lon', 'lat')
- new_h: float32 [4, 2, 256, 1024], P(None, None, 'lon', 'lat')
All inputs are finite; a program needn't handle non-finite values. No bound on the sum of `land_sea` on one device may be relied on, other than what follows from the above.
Results may differ from a plain program's by a relative error of at most 0.0014.
Values may be sent and summed in bfloat16 or wider, within the bound.
No kernel may reach another device: no remote copies, remote signals or barrier semaphores. Data moves between devices by JAX's collectives and lax.ppermute only.
A program may use at most 128 MiB of HBM per device.

v0:
```python
import functools

import jax
import jax.numpy as jnp
from jax import lax
from jax.experimental import pallas as pl
from jax.experimental.pallas import tpu as pltpu
from jax.sharding import PartitionSpec as P

REDUCED = 0.5
TIME_STEP = 0.2
VISCOSITY = 0.05
CORIOLIS = 0.4

RIM = 4
GAP = 32
NORTH, STRIP, GHOST, SOUTH = 0, 12, 16, 28
SUB = 16
LANES = 128
GROUP = 8
LAND = 2.0**100

f32 = jnp.float32
bf16 = jnp.bfloat16


def iota(shape, dim):
    return lax.broadcasted_iota(jnp.int32, shape, dim)


def dot(a, b):
    return jnp.dot(a, b, preferred_element_type=f32)


def exact_dot(a, b):
    return jnp.dot(a, b, preferred_element_type=f32, precision=lax.Precision.HIGHEST)


def pack_lon_kernel(sizes, n_lo, u_lo, v_lo, h_lo, s_lo, n_hi, u_hi, v_hi, h_hi, s_hi, head, tail):
    members, noises, levels = sizes
    fields = noises + 3 * levels
    lats = head.shape[1]
    upper = iota((GROUP, lats), 0) < RIM

    def field(m, c, refs):
        noise, u, v, h = refs
        if c < noises:
            full = noise[m, c].astype(f32)
            return full[:GROUP] if noise is n_lo else full[-GROUP:]
        c -= noises
        return (u, v, h)[c // levels][m, c % levels]

    lo = (n_lo, u_lo, v_lo, h_lo)
    hi = (n_hi, u_hi, v_hi, h_hi)
    for m in range(members):
        for c in range(0, fields, 2):
            rows = pl.ds((m * fields + c) * RIM, GROUP)
            head[rows] = jnp.where(upper, field(m, c, lo), pltpu.roll(field(m, c + 1, lo), RIM, 0))
            tail[rows] = jnp.where(upper, pltpu.roll(field(m, c, hi), RIM, 0), field(m, c + 1, hi))
    rows = pl.ds(members * fields * RIM, GROUP)
    head[rows] = s_lo[...].astype(f32)
    tail[rows] = pltpu.roll(s_hi[...].astype(f32), RIM, 0)


def group_tile(sizes, m, c, g, refs, groups):
    noise, u, v, h, sea, left, right = refs
    members, noises, levels = sizes
    fields = noises + 3 * levels
    if c == fields + 1:
        if g == groups - 1:
            return None
        c, g = fields, g + 1
    if g == 0 or g == groups - 1:
        src = left if g == 0 else right
        row = (m * fields + c) * RIM if c < fields else members * fields * RIM
        odd = (row // RIM) % 2
        tile = src[pl.ds(row // GROUP * GROUP, GROUP)]
        if odd == (1 if g == 0 else 0):
            return tile
        return pltpu.roll(tile, RIM, 0)
    rows = slice((g - 1) * GROUP, g * GROUP)
    if c < noises:
        return noise[m, c].astype(f32)[rows]
    if c == fields:
        return sea[rows].astype(f32)
    c -= noises
    return (u, v, h)[c // levels][m, c % levels, rows]


def pack_lat_kernel(
    sizes, n_lo, u_lo, v_lo, h_lo, s_lo, n_hi, u_hi, v_hi, h_hi, s_hi, left, right, head, tail
):
    members, noises, levels = sizes
    channels = noises + 3 * levels + 2
    groups = s_lo.shape[0] // GROUP + 2
    lane = iota((GROUP, LANES), 1)
    for out, refs, lanes in (
        (head, (n_lo, u_lo, v_lo, h_lo, s_lo), slice(0, LANES)),
        (tail, (n_hi, u_hi, v_hi, h_hi, s_hi), slice(left.shape[1] - LANES, left.shape[1])),
    ):
        refs = refs + (left.at[:, lanes], right.at[:, lanes])
        first = 0 if out is head else LANES - RIM
        for c in range(channels):
            total = jnp.zeros((GROUP, LANES), f32)
            for g in range(groups):
                for m in range(members):
                    tile = group_tile(sizes, m, c, g, refs, groups)
                    if tile is None:
                        continue
                    place = (g * members + m) * RIM
                    moved = pltpu.roll(tile, (place - first) % LANES, 1)
                    total = jnp.where((lane >= place) & (lane < place + RIM), moved, total)
            out[pl.ds(c * GROUP, GROUP)] = total


def weights_kernel(w1, w2, w3, w4, biases, t1, t2, t3, t4):
    hidden = w2.shape[2]
    per = LANES // hidden
    lane = iota((hidden, LANES), 1)
    fields = w1.shape[1] // GROUP
    rows = fields * GROUP
    out_lon = iota((rows, LANES), 1) // hidden
    in_lon = iota((rows, LANES), 0) % GROUP
    bias_row = iota((GROUP, LANES), 0)

    def bias_rows(layer, tile):
        part = 0.5 * biases[pl.ds(layer, 1), :]
        b1 = part.astype(bf16).astype(f32)
        b2 = (part - b1).astype(bf16).astype(f32)
        b3 = part - b1 - b2
        zero = jnp.zeros((GROUP, LANES), f32)
        return jnp.where(
            bias_row == 0,
            b1,
            jnp.where(bias_row == 1, b2, jnp.where(bias_row == 2, b3, zero)),
        )

    def sea_rows(shift, tile):
        lon = iota((2 * GROUP, LANES), 0)
        out = iota((2 * GROUP, LANES), 1) // hidden + per * tile
        return jnp.where(lon == out + shift, LAND, 0.0)

    pad = jnp.zeros((LANES - rows - 3 * GROUP, LANES), f32)
    empty = jnp.zeros((3 * GROUP, LANES), f32)
    for dj in range(3):
        for half in range(2):
            for tile in range(2):
                total = jnp.zeros((rows, LANES), f32)
                for di in range(3):
                    hit = in_lon + GROUP * half == out_lon + per * tile + di + RIM
                    total = jnp.where(hit, 0.5 * w1[dj * 3 + di].astype(f32), total)
                extra = empty
                if dj == 1 and half == 0:
                    extra = jnp.concatenate([sea_rows(5, tile), bias_rows(0, tile)], axis=0)
                block = jnp.concatenate([total, extra, pad], axis=0)
                t1[pl.ds((dj * 2 + half) * LANES, LANES), pl.ds(tile * LANES, LANES)] = block.astype(bf16)

    for layer, (w, t) in enumerate(((w2, t2), (w3, t3))):
        for dj in range(3):
            taps = []
            for di in range(3):
                cell = 0.5 * w[di, dj].astype(f32)
                wide = jnp.concatenate([cell, jnp.zeros((hidden, LANES - hidden), f32)], axis=1)
                square = jnp.concatenate([wide] * per, axis=0)
                taps.append(jnp.transpose(square)[:hidden])
            for lon in range(GROUP + 2):
                for tile in range(2):
                    total = jnp.zeros((hidden, LANES), f32)
                    for di in range(3):
                        total = jnp.where(lane // hidden + per * tile == lon - di, taps[di], total)
                    if lon < GROUP:
                        row = dj * GROUP * hidden + lon * hidden
                    else:
                        row = 3 * GROUP * hidden + dj * 2 * hidden + (lon - GROUP) * hidden
                    t[pl.ds(row, hidden), pl.ds(tile * LANES, LANES)] = total.astype(bf16)
        for tile in range(2):
            block = jnp.concatenate(
                [
                    jnp.zeros((2 * GROUP, LANES), f32),
                    sea_rows(6 + layer, tile),
                    bias_rows(1 + layer, tile),
                    jnp.zeros((3 * GROUP, LANES), f32),
                ],
                axis=0,
            )
            row = 3 * GROUP * hidden + 6 * hidden
            t[pl.ds(row, 2 * hidden), pl.ds(tile * LANES, LANES)] = block.astype(bf16)

    outs = w4.shape[2]
    lons = LANES // outs
    depth = t4.shape[0] // 3
    for dj in range(3):
        taps = []
        for di in range(3):
            cell = w4[di, dj].astype(f32)
            wide = jnp.concatenate([cell, jnp.zeros((outs, LANES - hidden), f32)], axis=1)
            square = jnp.concatenate(
                [jnp.broadcast_to(wide[c : c + 1], (lons, LANES)) for c in range(outs)], axis=0
            )
            taps.append(jnp.transpose(square)[:hidden])
        for lon in range(depth // hidden):
            total = jnp.zeros((hidden, LANES), f32)
            for di in range(3):
                total = jnp.where(lane % lons == lon - di, taps[di], total)
            t4[pl.ds(dj * depth + lon * hidden, hidden), :] = total.astype(bf16)


def main_kernel(
    sizes,
    place,
    bias_last,
    noise,
    u,
    v,
    h,
    sea,
    coriolis,
    left,
    right,
    south,
    north,
    strip,
    own_tail,
    t1,
    t2,
    t3,
    t4,
    new_u,
    new_v,
    new_h,
    cells,
    first,
    odd,
    even,
    force,
    turned,
):
    members, noises, levels = sizes
    fields = noises + 3 * levels
    lons, lats = sea.shape
    groups = lons // GROUP + 2
    chunks = SUB // members
    blocks = (lats + GAP) // chunks
    rows = blocks * SUB
    gap_k = lats - (chunks - 1) * blocks
    top = place[0] == 1
    refs = (noise, u, v, h, sea, left, right)

    wide = fields * GROUP + 2 * GROUP
    lane = iota((wide, LANES), 1)
    row_to = iota((wide, wide), 0)
    row_from = iota((wide, wide), 1)
    channel = row_to // GROUP
    same = channel == row_from // GROUP
    mirrored = same & (row_from % GROUP == GROUP - 1 - row_to % GROUP)
    odd_parity = (channel >= noises) & (channel < noises + 2 * levels)
    flip_rows = jnp.where(mirrored, jnp.where(odd_parity, -1.0, 1.0), 0.0)
    lane_from = iota((LANES, LANES), 0)
    lane_to = iota((LANES, LANES), 1)
    span = members * RIM
    source = (groups - 1 - lane_to // span) * span + lane_to % span + RIM - 1
    flip_lanes = jnp.where((lane_to % RIM == 0) & (lane_to < groups * span) & (lane_from == source), 1.0, 0.0)
    pair = exact_dot(flip_rows, jnp.concatenate([strip[...], own_tail[...]], axis=1))
    folded = exact_dot(pair[:, :LANES], flip_lanes)
    ghost = exact_dot(pair[:, LANES:], flip_lanes)
    north_rim = jnp.where((lane % RIM == 0) & top, folded, north[...])

    ones = jnp.ones((GROUP, LANES), f32)
    blank = jnp.zeros((LANES - wide - GROUP, LANES), f32)
    for g in range(groups):
        for m in range(members):
            cells[g, pl.ds(gap_k * SUB + m * chunks + chunks - 1, GAP, stride=SUB), :] = jnp.zeros(
                (GAP, LANES), f32
            )
    for n, (message, offset) in enumerate(
        ((south[...], SOUTH), (north_rim, NORTH), (strip[...], STRIP), (ghost, GHOST))
    ):
        body_rows = fields * GROUP
        tall = jnp.concatenate([message[:body_rows], message[body_rows:] - 1.0, ones, blank], axis=0)
        turned[n] = jnp.transpose(tall)
        for g in range(groups):
            for m in range(members):
                gap = (m - 1) % members if offset == SOUTH else m
                start = (gap_k + offset) * SUB + gap * chunks + chunks - 1
                cells[g, pl.ds(start, RIM, stride=SUB), :] = turned[n, pl.ds((g * members + m) * RIM, RIM), :]

    for t in range(lats // LANES):
        lanes = slice(t * LANES, (t + 1) * LANES)
        views = (
            noise.at[:, :, :, lanes],
            u.at[:, :, :, lanes],
            v.at[:, :, :, lanes],
            h.at[:, :, :, lanes],
            sea.at[:, lanes],
            left.at[:, lanes],
            right.at[:, lanes],
        )
        for g in range(groups):
            for m in range(members):
                tiles = [group_tile(sizes, m, c, g, views, groups) for c in range(fields)]
                own = group_tile(sizes, m, fields, g, views, groups) - 1.0
                following = group_tile(sizes, m, fields + 1, g, views, groups)
                following = jnp.zeros_like(own) if following is None else following - 1.0
                block = jnp.transpose(jnp.concatenate(tiles + [own, following, ones, blank], axis=0))
                for q in range(chunks):
                    lo = max(q * blocks, t * LANES)
                    hi = min((q + 1) * blocks, (t + 1) * LANES, lats)
                    if lo < hi:
                        start = (lo - q * blocks) * SUB + m * chunks + q
                        cells[g, pl.ds(start, hi - lo, stride=SUB), :] = block[lo - t * LANES : hi - t * LANES]

    for g in range(groups):
        first[g, pl.ds(SUB, rows), :] = cells[g].astype(bf16)
        first[g, pl.ds(0, SUB), :] = pltpu.roll(cells[g, pl.ds(rows - SUB, SUB), :], 1, 0).astype(bf16)
        first[g, pl.ds(SUB + rows, SUB), :] = pltpu.roll(cells[g, pl.ds(0, SUB), :], SUB - 1, 0).astype(bf16)

    hidden = LANES // 4
    per = LANES // hidden
    tiles = odd.shape[0]
    step = rows // 3
    lower = iota((step, LANES), 1) < 2 * hidden

    def activate(pre):
        return (pre * jnp.tanh(pre) + pre).astype(bf16)

    def finish(x, valid):
        @pl.when(top)
        def _():
            strip_top = SUB * (1 + gap_k + STRIP + RIM - 1)
            own_top = SUB * gap_k
            strip_ghost = SUB * (1 + gap_k + GHOST)
            own_ghost = SUB * (1 + gap_k + NORTH)
            last_chunk = iota((SUB, LANES), 0) % chunks == chunks - 1
            spot = iota((SUB, LANES), 1) // hidden
            used = (valid + per - 1) // per
            for src, dst in ((strip_top, own_ghost), (own_top, strip_ghost)):
                found = [x[t, pl.ds(src, SUB), :].astype(f32) for t in range(used)]
                for t in range(used):
                    total = x[t, pl.ds(dst, SUB), :].astype(f32)
                    for i in range(per):
                        lon = valid - 1 - (per * t + i)
                        if lon < 0:
                            continue
                        moved = pltpu.roll(found[lon // per], (hidden * (i - lon % per)) % LANES, 1)
                        total = jnp.where(last_chunk & (spot == i), moved, total)
                    x[t, pl.ds(dst, SUB), :] = total.astype(bf16)

        for t in range(tiles):
            end = x[t, pl.ds(rows, SUB), :].astype(f32)
            x[t, pl.ds(0, SUB), :] = pltpu.roll(end, 1, 0).astype(bf16)
            begin = x[t, pl.ds(SUB, SUB), :].astype(f32)
            x[t, pl.ds(SUB + rows, SUB), :] = pltpu.roll(begin, SUB - 1, 0).astype(bf16)

    for x in (odd, even):
        x[tiles - 1] = jnp.zeros(x.shape[1:], bf16)

    spread = groups - 1

    def layer_first(b, carry):
        for n in range(rows // step):
            r = n * step
            parts = [first[b + e, pl.ds(r + SUB * d, step), :] for d in range(3) for e in range(2)]
            out = activate(dot(jnp.concatenate(parts, axis=1), t1[...]))
            odd[2 * b, pl.ds(SUB + r, step), :] = out[:, :LANES]
            odd[2 * b + 1, pl.ds(SUB + r, step), :] = out[:, LANES:]
        return carry

    lax.fori_loop(0, spread, layer_first, 0)
    finish(odd, lons + 6)

    def layer(x, y, t, b, carry):
        for n in range(rows // step):
            r = n * step
            parts = [x[2 * b + e, pl.ds(r + SUB * d, step), :] for d in range(3) for e in range(2)]
            rest = [x[2 * b + 2, pl.ds(r + SUB * d, step), :] for d in range(3)]
            parts.append(jnp.where(lower, rest[0], pltpu.roll(rest[1], 2 * hidden, 1)))
            parts.append(jnp.where(lower, rest[2], first[b, pl.ds(r + SUB, step), :]))
            out = activate(dot(jnp.concatenate(parts, axis=1), t[...]))
            y[2 * b, pl.ds(SUB + r, step), :] = out[:, :LANES]
            y[2 * b + 1, pl.ds(SUB + r, step), :] = out[:, LANES:]
        return carry

    lax.fori_loop(0, spread, functools.partial(layer, odd, even, t2), 0)
    finish(even, lons + 4)
    lax.fori_loop(0, spread, functools.partial(layer, even, odd, t3), 0)
    finish(odd, lons + 2)

    depth = t4.shape[0] // 3 // LANES
    for n in range(rows // step):
        r = n * step
        parts = [odd[t, pl.ds(r + SUB * d, step), :] for d in range(3) for t in range(depth)]
        force[pl.ds(r, step), :] = dot(jnp.concatenate(parts, axis=1), t4[...])

    ocean = sea[...].astype(f32)
    turn = coriolis[...]
    at_first = iota((lons, lats), 0) == 0
    at_last = iota((lons, lats), 0) == lons - 1
    at_south = iota((lons, lats), 1) == 0
    at_north = iota((lons, lats), 1) == lats - 1
    for m in range(members):
        pieces = []
        for q in range(chunks):
            size = min(blocks, lats - q * blocks)
            pieces.append(force[pl.ds(m * chunks + q, size, stride=SUB), :])
        forcing = jnp.transpose(jnp.concatenate(pieces, axis=0))

        def rims(c):
            row = (m * fields + c) * RIM
            west = left[pl.ds(row + RIM - 1, 1)]
            east = right[pl.ds(row, 1)]
            low, high = [], []
            for g in range(1, groups - 1):
                spot = (g * members + m) * RIM
                low.append(south[c * GROUP : (c + 1) * GROUP, spot + RIM - 1 : spot + RIM])
                high.append(north_rim[c * GROUP : (c + 1) * GROUP, spot : spot + 1])
            return west, east, jnp.concatenate(low, axis=0), jnp.concatenate(high, axis=0)

        def around(x, rim):
            west, east, low, high = rim
            return (
                jnp.where(at_first, west, pltpu.roll(x, 1, 0)),
                jnp.where(at_last, east, pltpu.roll(x, lons - 1, 0)),
                jnp.where(at_south, low, pltpu.roll(x, 1, 1)),
                jnp.where(at_north, high, pltpu.roll(x, lats - 1, 1)),
            )

        sets = []
        for level in range(levels):
            sets.append(
                [
                    (x[m, level], around(x[m, level], rims(noises + n * levels + level)))
                    for n, x in enumerate((u, v, h))
                ]
            )
        for level in range(levels):
            (cu, au), (cv, av), (ch, ah) = sets[level]
            upper, lower_h = sets[0][2][1], sets[1][2][1]
            pressure = [upper[i] + lower_h[i] for i in range(4)]
            if level == 1:
                pressure = [pressure[i] + REDUCED * lower_h[i] for i in range(4)]
            push_u = (forcing[level * lons : (level + 1) * lons] + bias_last[level]) * ocean
            wide_v = levels + level
            push_v = (forcing[wide_v * lons : (wide_v + 1) * lons] + bias_last[wide_v]) * ocean
            lap_u = au[1] + au[0] + au[3] + au[2] - 4.0 * cu
            lap_v = av[1] + av[0] + av[3] + av[2] - 4.0 * cv
            dx = 0.5 * (pressure[1] - pressure[0])
            dy = 0.5 * (pressure[3] - pressure[2])
            new_u[m, level] = ocean * (cu + TIME_STEP * (turn * cv - dx + push_u + VISCOSITY * lap_u))
            new_v[m, level] = ocean * (cv + TIME_STEP * (-turn * cu - dy + push_v + VISCOSITY * lap_v))
            flow = 0.5 * (ah[1] * au[1] - ah[0] * au[0]) + 0.5 * (ah[3] * av[3] - ah[2] * av[2])
            new_h[m, level] = ch - TIME_STEP * flow


def body(
    noise,
    velocity_u,
    velocity_v,
    thickness,
    land_sea,
    conv_first,
    bias_first,
    conv_second,
    bias_second,
    conv_third,
    bias_third,
    conv_last,
    bias_last,
):
    members, noises, lons, lats = noise.shape
    levels = velocity_u.shape[1]
    fields = noises + 3 * levels
    sizes = (members, noises, levels)
    hidden = conv_first.shape[0]
    outs = conv_last.shape[0]
    groups = lons // GROUP + 2
    rows = members * (lats + GAP)
    assert hidden * 4 == LANES and outs * lons == LANES and members * RIM * groups <= LANES
    assert lats % LANES == 0 and SUB % members == 0 and (lats + GAP) % (SUB // members) == 0
    lon_count, lat_count = lax.axis_size("lon"), lax.axis_size("lat")
    lat_index = lax.axis_index("lat")
    state = (noise, velocity_u, velocity_v, thickness, land_sea)
    whole = pl.BlockSpec(memory_space=pltpu.VMEM)

    def edge(index, dim, size):
        specs = []
        for x in state:
            shape, at = list(x.shape), [0] * x.ndim
            if not (dim == -2 and x.dtype == bf16):
                at[dim] = (shape[dim] // size - 1) * index
                shape[dim] = size
            specs.append(pl.BlockSpec(tuple(shape), functools.partial(lambda at, *_: tuple(at), at)))
        return specs

    tall = members * fields * RIM + GROUP
    head, tail = pl.pallas_call(
        functools.partial(pack_lon_kernel, sizes),
        grid=(1,),
        out_shape=[jax.ShapeDtypeStruct((tall, lats), f32)] * 2,
        in_specs=edge(0, -2, GROUP) + edge(1, -2, GROUP),
        out_specs=[pl.BlockSpec((tall, lats), lambda i: (0, 0))] * 2,
        name="pack_lon",
    )(*state, *state)
    ring = [(i, (i + 1) % lon_count) for i in range(lon_count)]
    left = lax.ppermute(tail, "lon", ring)
    right = lax.ppermute(head, "lon", [(b, a) for a, b in ring])

    wide = (fields + 2) * GROUP
    south_edge, north_edge = pl.pallas_call(
        functools.partial(pack_lat_kernel, sizes),
        grid=(1,),
        out_shape=[jax.ShapeDtypeStruct((wide, LANES), f32)] * 2,
        in_specs=edge(0, -1, LANES) + edge(1, -1, LANES) + [pl.BlockSpec((tall, lats), lambda i: (0, 0))] * 2,
        out_specs=[pl.BlockSpec((wide, LANES), lambda i: (0, 0))] * 2,
        name="pack_lat",
    )(*state, *state, left, right)
    south = lax.ppermute(north_edge, "lat", [(i, i + 1) for i in range(lat_count - 1)])
    north = lax.ppermute(south_edge, "lat", [(i + 1, i) for i in range(lat_count - 1)])
    last = lat_count - 1
    strip = lax.ppermute(
        north_edge,
        ("lon", "lat"),
        [(i * lat_count + last, (lon_count - 1 - i) * lat_count + last) for i in range(lon_count)],
    )

    taps = conv_first.transpose(3, 2, 1, 0)[:, :, :, None, None, :]
    taps = jnp.broadcast_to(taps, (3, 3, fields, GROUP, LANES // hidden, hidden)).reshape(9, -1, LANES)
    biases = jnp.tile(jnp.stack([bias_first, bias_second, bias_third]), (1, LANES // hidden))
    deep = -(-(lons + 2) * hidden // LANES) * LANES
    t1, t2, t3, t4 = pl.pallas_call(
        weights_kernel,
        out_shape=[
            jax.ShapeDtypeStruct((6 * LANES, 2 * LANES), bf16),
            jax.ShapeDtypeStruct((8 * LANES, 2 * LANES), bf16),
            jax.ShapeDtypeStruct((8 * LANES, 2 * LANES), bf16),
            jax.ShapeDtypeStruct((3 * deep, LANES), bf16),
        ],
        cost_estimate=pl.CostEstimate(flops=10**7, bytes_accessed=3 * 10**6, transcendentals=0),
        name="banded_matrices",
    )(
        taps,
        conv_second.transpose(2, 3, 0, 1),
        conv_third.transpose(2, 3, 0, 1),
        conv_last.transpose(2, 3, 0, 1),
        biases,
    )

    lat_rows = (lat_index * lats + jnp.arange(lats)).astype(f32)
    coriolis = CORIOLIS * (2.0 * (lat_rows + 0.5) / (lats * lat_count) - 1.0)
    place = (lat_index == last).astype(jnp.int32)[None]
    smem = pl.BlockSpec(memory_space=pltpu.SMEM)
    padded = rows + 2 * SUB
    tiles = 2 * (groups - 1) + 1
    out = jax.ShapeDtypeStruct(velocity_u.shape, f32)
    return pl.pallas_call(
        functools.partial(main_kernel, sizes),
        out_shape=[out] * 3,
        in_specs=[smem, smem] + [whole] * 16,
        out_specs=[whole] * 3,
        scratch_shapes=[
            pltpu.VMEM((groups, rows, LANES), f32),
            pltpu.VMEM((groups, padded, LANES), bf16),
            pltpu.VMEM((tiles, padded, LANES), bf16),
            pltpu.VMEM((tiles, padded, LANES), bf16),
            pltpu.VMEM((rows, LANES), f32),
            pltpu.VMEM((4, LANES, LANES), f32),
        ],
        compiler_params=pltpu.CompilerParams(vmem_limit_bytes=48 * 2**20),
        cost_estimate=pl.CostEstimate(flops=2 * 10**10, bytes_accessed=10**7, transcendentals=4 * 10**6),
        name="network_and_step",
    )(
        place,
        bias_last,
        *state,
        coriolis[None],
        left,
        right,
        south,
        north,
        strip,
        north_edge,
        t1,
        t2,
        t3,
        t4,
    )


def solution(mesh):
    tiles = P(None, None, "lon", "lat")
    return jax.shard_map(
        body,
        mesh=mesh,
        in_specs=(tiles,) * 4 + (P("lon", "lat"),) + (P(),) * 8,
        out_specs=(tiles,) * 3,
        check_vma=False,
    )
```

profile of v0, /device:TPU:27, one launch (start us, length us, event | category | flops | bytes accessed | tf_op | source)
XLA Modules:
  0.0 50.0 jit_solution(6452520532259612414)
XLA Ops:
  0.6 1.9 %pack_lon.1 = (f32[168,256]{1,0:T(8,128)}, f32[168,256]{1,0:T(8,128)}) custom-call(bf16[4,4,32,256]{3,2,1,0:T(8,128)(2,1)} %noise.1, f32[4,2,32,256]{3,2,1,0:T(8,128)} %u.1, f32[4,2,32,256]{3,2,1,0:T(8,128)} %v.1, f32[4,2,32,256]{3,2,1,0:T(8,128)} %h.1, s32[32,256]{1,0:T(8,128)} %sea.1, bf16[4,4,32,256]{3,2,1,0:T(8,128)(2,1)} %noise.1, f32[4,2,32,256]{3,2,1,0:T(8,128)} %u.1, ...), custom_call_target="tpu_custom_call" | custom-call | tf_op jit(solution)/shard_map/pack_lon/pallas_call | solution.py:495
  2.6 1.8 %collective-permute-start = (f32[168,256]{1,0:T(8,128)}, f32[168,256]{1,0:T(8,128)S(1)}, u32[]{:S(2)}, u32[]{:S(2)}) collective-permute-start(f32[168,256]{1,0:T(8,128)} %get-tuple-element.11), channel_id=1, source_target_pairs={{0,4},{4,8},{8,12},{12,16},{16,20},{20,24},{24,28},{28,0},{1,5},{5... | collective-permute-start | bytes 516104 | tf_op jit(solution)/shard_map/ppermute | solution.py:504
  4.3 0.0 collective-permute-start.1
  4.3 0.6 %copy-done.16 = f32[32]{0:T(128)S(1)} copy-done((f32[32]{0:T(128)S(1)}, f32[32]{0:T(128)}, u32[]{:S(2)}) %copy-start.16) | copy-done | bytes 152
  5.0 0.0 copy-done.17
  5.0 0.0 copy-done.18
  5.0 3.0 %collective-permute-done.left = f32[168,256]{1,0:T(8,128)S(1)} collective-permute-done((f32[168,256]{1,0:T(8,128)}, f32[168,256]{1,0:T(8,128)S(1)}, u32[]{:S(2)}, u32[]{:S(2)}) %collective-permute-start) | collective-permute-done | bytes 172064 | tf_op jit(solution)/shard_map/ppermute | solution.py:504
  8.0 2.3 %collective-permute-done.1.right = f32[168,256]{1,0:T(8,128)S(1)} collective-permute-done((f32[168,256]{1,0:T(8,128)}, f32[168,256]{1,0:T(8,128)S(1)}, u32[]{:S(2)}, u32[]{:S(2)}) %collective-permute-start.1) | collective-permute-done | bytes 172064 | tf_op jit(solution)/shard_map/ppermute | solution.py:505
  10.4 0.7 %copy-done.7 = f32[168,256]{1,0:T(8,128)} copy-done((f32[168,256]{1,0:T(8,128)}, f32[168,256]{1,0:T(8,128)S(1)}, u32[]{:S(2)}) %copy-start.7) | copy-done | bytes 172056
  11.1 2.6 %pack_lat.1 = (f32[96,128]{1,0:T(8,128)}, f32[96,128]{1,0:T(8,128)}) custom-call(bf16[4,4,32,256]{3,2,1,0:T(8,128)(2,1)} %noise.1, f32[4,2,32,256]{3,2,1,0:T(8,128)} %u.1, f32[4,2,32,256]{3,2,1,0:T(8,128)} %v.1, f32[4,2,32,256]{3,2,1,0:T(8,128)} %h.1, s32[32,256]{1,0:T(8,128)} %sea.1, bf16[4,4,32,256]{3,2,1,0:T(8,128)(2,1)} %noise.1, f32[4,2,32,256]{3,2,1,0:T(8,128)} %u.1, ...), custom_call_target="tpu_custom_call" | custom-call | tf_op jit(solution)/shard_map/pack_lat/pallas_call | solution.py:508
  13.7 3.5 %collective-permute-start.4 = (f32[96,128]{1,0:T(8,128)}, f32[96,128]{1,0:T(8,128)S(1)}, u32[]{:S(2)}, u32[]{:S(2)}) collective-permute-start(f32[96,128]{1,0:T(8,128)} %get-tuple-element.13.own_tail), channel_id=1, source_target_pairs={{3,31},{7,27},{11,23},{15,19},{19,15},{23,11},{27,7},{31,3}} | collective-permute-start | bytes 147464 | tf_op jit(solution)/shard_map/ppermute | solution.py:519
  17.2 1.3 %collective-permute-start.2 = (f32[96,128]{1,0:T(8,128)}, f32[96,128]{1,0:T(8,128)S(1)}, u32[]{:S(2)}, u32[]{:S(2)}) collective-permute-start(f32[96,128]{1,0:T(8,128)} %get-tuple-element.13.own_tail), channel_id=1, source_target_pairs={{0,1},{1,2},{2,3},{4,5},{5,6},{6,7},{8,9},{9,10},{10,11},{12,13},{... | collective-permute-start | bytes 147464 | tf_op jit(solution)/shard_map/ppermute | solution.py:516
  18.5 4.0 %collective-permute-start.3 = (f32[96,128]{1,0:T(8,128)}, f32[96,128]{1,0:T(8,128)S(1)}, u32[]{:S(2)}, u32[]{:S(2)}) collective-permute-start(f32[96,128]{1,0:T(8,128)} %get-tuple-element.14), channel_id=1, source_target_pairs={{1,0},{2,1},{3,2},{5,4},{6,5},{7,6},{9,8},{10,9},{11,10},{13,12},{... | collective-permute-start | bytes 147464 | tf_op jit(solution)/shard_map/ppermute | solution.py:517
  22.5 0.7 %tile.10.biases = f32[3,128]{1,0:T(4,128)} reshape(f32[3,4,32]{2,1,0:T(4,128)S(1)} %tile.4) | data formatting | bytes 3072 | tf_op jit(solution)/shard_map/tile | solution.py:527
  23.2 0.0 copy-start.8
  23.2 0.2 broadcast_in_dim.14
  23.4 0.0 copy-start.1
  23.5 0.0 copy-start.2
  23.5 0.0 copy-start.3
  23.5 0.0 copy-start.6
  23.5 1.1 %reshape.36.w1 = bf16[9,80,128]{2,1,0:T(8,128)(2,1)} reshape(bf16[3,3,10,8,4,32]{5,4,3,2,1,0:T(4,128)(2,1)S(1)} %broadcast_in_dim.14) | data formatting | bytes 368640 | tf_op jit(solution)/shard_map/reshape | solution.py:526
  24.6 3.3 %banded_matrices.1 = (bf16[768,256]{1,0:T(8,128)(2,1)}, bf16[1024,256]{1,0:T(8,128)(2,1)}, bf16[1024,256]{1,0:T(8,128)(2,1)}, bf16[3456,128]{1,0:T(8,128)(2,1)}) custom-call(bf16[9,80,128]{2,1,0:T(8,128)(2,1)} %reshape.36.w1, bf16[3,3,32,32]{3,2,1,0:T(8,128)(2,1)} %bitcast.8, bf16[3,3,32,32]{3,2,1,0:T(8,128)(2,1)} %bitcast.9, ...), custom_call_target="tpu_custom_call" | custom-call | flops 10000000 | bytes 3000000 | tf_op jit(solution)/shard_map/banded_matrices/pallas_call | solution.py:529
  27.8 0.0 collective-permute-done.3.north
  27.8 0.0 collective-permute-done.4.strip
  27.8 0.0 collective-permute-done.2.south
  27.8 0.0 copy-start.14
  27.9 0.6 %copy-done.14 = f32[4]{0:T(128)S(1)} copy-done((f32[4]{0:T(128)S(1)}, f32[4]{0:T(128)}, u32[]{:S(2)}) %copy-start.14) | copy-done | bytes 40
  28.5 1.2 %copy-done.9 = bf16[3456,128]{1,0:T(8,128)(2,1)S(1)} copy-done((bf16[3456,128]{1,0:T(8,128)(2,1)S(1)}, bf16[3456,128]{1,0:T(8,128)(2,1)}, u32[]{:S(2)}) %copy-start.9) | copy-done | bytes 884760
  29.7 1.0 %copy-done.10 = bf16[1024,256]{1,0:T(8,128)(2,1)S(1)} copy-done((bf16[1024,256]{1,0:T(8,128)(2,1)S(1)}, bf16[1024,256]{1,0:T(8,128)(2,1)}, u32[]{:S(2)}) %copy-start.10) | copy-done | bytes 524312
  30.7 1.0 %copy-done.11 = bf16[1024,256]{1,0:T(8,128)(2,1)S(1)} copy-done((bf16[1024,256]{1,0:T(8,128)(2,1)S(1)}, bf16[1024,256]{1,0:T(8,128)(2,1)}, u32[]{:S(2)}) %copy-start.11) | copy-done | bytes 524312
  31.7 1.0 %copy-done.12 = bf16[768,256]{1,0:T(8,128)(2,1)S(1)} copy-done((bf16[768,256]{1,0:T(8,128)(2,1)S(1)}, bf16[768,256]{1,0:T(8,128)(2,1)}, u32[]{:S(2)}) %copy-start.12) | copy-done | bytes 393240
  32.7 17.3 %network_and_step.1 = (f32[4,2,32,256]{3,2,1,0:T(8,128)}, f32[4,2,32,256]{3,2,1,0:T(8,128)}, f32[4,2,32,256]{3,2,1,0:T(8,128)}) custom-call(s32[1]{0:T(128)} %bitcast.place, f32[4]{0:T(128)S(1)} %copy-done.14, bf16[4,4,32,256]{3,2,1,0:T(8,128)(2,1)S(1)} %copy-done, f32[4,2,32,256]{3,2,1,0:T(8,128)S(1)} %copy-done.1, f32[4,2,32,256]{3,2,1,0:T(8,128)S(1)} %copy-done.2, ...), custom_call_target="tpu_custom_call" | custom-call | flops 20000000000 | bytes 10000000 | tf_op jit(solution)/shard_map/network_and_step/pallas_call | solution.py:554
  (27 shorter events, 0.1 us)
Async XLA Ops:
  2.6 5.5 %collective-permute-start = (f32[168,256]{1,0:T(8,128)}, f32[168,256]{1,0:T(8,128)S(1)}, u32[]{:S(2)}, u32[]{:S(2)}) collective-permute-start(f32[168,256]{1,0:T(8,128)} %get-tuple-element.11), channel_id=1, source_target_pairs={{0,4},{4,8},{8,12},{12,16},{16,20},{20,24},{24,28},{28,0},{1,5},{5... | collective-permute-start | bytes 516104 | tf_op jit(solution)/shard_map/ppermute | solution.py:504
  4.3 6.1 %collective-permute-start.1 = (f32[168,256]{1,0:T(8,128)}, f32[168,256]{1,0:T(8,128)S(1)}, u32[]{:S(2)}, u32[]{:S(2)}) collective-permute-start(f32[168,256]{1,0:T(8,128)} %get-tuple-element.12), channel_id=1, source_target_pairs={{4,0},{8,4},{12,8},{16,12},{20,16},{24,20},{28,24},{0,28},{5,1},{9... | collective-permute-start | bytes 516104 | tf_op jit(solution)/shard_map/ppermute | solution.py:505
  4.3 0.7 %copy-start.16 = (f32[32]{0:T(128)S(1)}, f32[32]{0:T(128)}, u32[]{:S(2)}) copy-start(f32[32]{0:T(128)} %param.23) | copy-start | bytes 388
  4.3 0.7 %copy-start.17 = (f32[32]{0:T(128)S(1)}, f32[32]{0:T(128)}, u32[]{:S(2)}) copy-start(f32[32]{0:T(128)} %param.21) | copy-start | bytes 388
  4.3 0.7 %copy-start.18 = (f32[32]{0:T(128)S(1)}, f32[32]{0:T(128)}, u32[]{:S(2)}) copy-start(f32[32]{0:T(128)} %param.19) | copy-start | bytes 388
  8.0 2.4 %copy-start.5 = (f32[168,256]{1,0:T(8,128)}, f32[168,256]{1,0:T(8,128)S(1)}, u32[]{:S(2)}) copy-start(f32[168,256]{1,0:T(8,128)S(1)} %collective-permute-done.left) | copy-start | bytes 516100
  10.4 0.7 %copy-start.7 = (f32[168,256]{1,0:T(8,128)}, f32[168,256]{1,0:T(8,128)S(1)}, u32[]{:S(2)}) copy-start(f32[168,256]{1,0:T(8,128)S(1)} %collective-permute-done.1.right) | copy-start | bytes 516100
  11.1 12.1 %copy-start.15 = (bf16[32,10,3,3]{0,3,2,1:T(4,128)(2,1)S(1)}, bf16[32,10,3,3]{0,3,2,1:T(4,128)(2,1)}, u32[]{:S(2)}) copy-start(bf16[32,10,3,3]{0,3,2,1:T(4,128)(2,1)} %param.18) | copy-start | bytes 17284
  13.7 14.1 %collective-permute-start.4 = (f32[96,128]{1,0:T(8,128)}, f32[96,128]{1,0:T(8,128)S(1)}, u32[]{:S(2)}, u32[]{:S(2)}) collective-permute-start(f32[96,128]{1,0:T(8,128)} %get-tuple-element.13.own_tail), channel_id=1, source_target_pairs={{3,31},{7,27},{11,23},{15,19},{19,15},{23,11},{27,7},{31,3}} | collective-permute-start | bytes 147464 | tf_op jit(solution)/shard_map/ppermute | solution.py:519
  17.2 10.6 %collective-permute-start.2 = (f32[96,128]{1,0:T(8,128)}, f32[96,128]{1,0:T(8,128)S(1)}, u32[]{:S(2)}, u32[]{:S(2)}) collective-permute-start(f32[96,128]{1,0:T(8,128)} %get-tuple-element.13.own_tail), channel_id=1, source_target_pairs={{0,1},{1,2},{2,3},{4,5},{5,6},{6,7},{8,9},{9,10},{10,11},{12,13},{... | collective-permute-start | bytes 147464 | tf_op jit(solution)/shard_map/ppermute | solution.py:516
  18.5 9.3 %collective-permute-start.3 = (f32[96,128]{1,0:T(8,128)}, f32[96,128]{1,0:T(8,128)S(1)}, u32[]{:S(2)}, u32[]{:S(2)}) collective-permute-start(f32[96,128]{1,0:T(8,128)} %get-tuple-element.14), channel_id=1, source_target_pairs={{1,0},{2,1},{3,2},{5,4},{6,5},{7,6},{9,8},{10,9},{11,10},{13,12},{... | collective-permute-start | bytes 147464 | tf_op jit(solution)/shard_map/ppermute | solution.py:517
  23.2 4.6 %copy-start.8 = (f32[168,256]{1,0:T(8,128)S(1)}, f32[168,256]{1,0:T(8,128)}, u32[]{:S(2)}) copy-start(f32[168,256]{1,0:T(8,128)} %copy-done.7) | copy-start | bytes 516100
  23.2 4.6 %copy-start.13 = (f32[96,128]{1,0:T(8,128)S(1)}, f32[96,128]{1,0:T(8,128)}, u32[]{:S(2)}) copy-start(f32[96,128]{1,0:T(8,128)} %get-tuple-element.13.own_tail) | copy-start | bytes 147460
  23.4 4.4 %copy-start.1 = (f32[4,2,32,256]{3,2,1,0:T(8,128)S(1)}, f32[4,2,32,256]{3,2,1,0:T(8,128)}, u32[]{:S(2)}) copy-start(f32[4,2,32,256]{3,2,1,0:T(8,128)} %u.1) | copy-start | bytes 786436
  23.5 4.4 %copy-start.2 = (f32[4,2,32,256]{3,2,1,0:T(8,128)S(1)}, f32[4,2,32,256]{3,2,1,0:T(8,128)}, u32[]{:S(2)}) copy-start(f32[4,2,32,256]{3,2,1,0:T(8,128)} %v.1) | copy-start | bytes 786436
  23.5 4.4 %copy-start.3 = (f32[4,2,32,256]{3,2,1,0:T(8,128)S(1)}, f32[4,2,32,256]{3,2,1,0:T(8,128)}, u32[]{:S(2)}) copy-start(f32[4,2,32,256]{3,2,1,0:T(8,128)} %h.1) | copy-start | bytes 786436
  23.5 4.4 %copy-start.6 = (f32[168,256]{1,0:T(8,128)S(1)}, f32[168,256]{1,0:T(8,128)}, u32[]{:S(2)}) copy-start(f32[168,256]{1,0:T(8,128)} %copy-done.5) | copy-start | bytes 516100
  24.5 3.4 %copy-start = (bf16[4,4,32,256]{3,2,1,0:T(8,128)(2,1)S(1)}, bf16[4,4,32,256]{3,2,1,0:T(8,128)(2,1)}, u32[]{:S(2)}) copy-start(bf16[4,4,32,256]{3,2,1,0:T(8,128)(2,1)} %noise.1) | copy-start | bytes 786436
  24.5 3.4 %copy-start.4 = (s32[32,256]{1,0:T(8,128)S(1)}, s32[32,256]{1,0:T(8,128)}, u32[]{:S(2)}) copy-start(s32[32,256]{1,0:T(8,128)} %sea.1) | copy-start | bytes 98308
  27.8 0.7 %copy-start.14 = (f32[4]{0:T(128)S(1)}, f32[4]{0:T(128)}, u32[]{:S(2)}) copy-start(f32[4]{0:T(128)} %bias_last.1) | copy-start | bytes 52
  28.5 1.2 %copy-start.9 = (bf16[3456,128]{1,0:T(8,128)(2,1)S(1)}, bf16[3456,128]{1,0:T(8,128)(2,1)}, u32[]{:S(2)}) copy-start(bf16[3456,128]{1,0:T(8,128)(2,1)} %get-tuple-element.18.t4) | copy-start | bytes 2654212
  29.7 1.0 %copy-start.10 = (bf16[1024,256]{1,0:T(8,128)(2,1)S(1)}, bf16[1024,256]{1,0:T(8,128)(2,1)}, u32[]{:S(2)}) copy-start(bf16[1024,256]{1,0:T(8,128)(2,1)} %get-tuple-element.16.t2) | copy-start | bytes 1572868
  30.7 1.0 %copy-start.11 = (bf16[1024,256]{1,0:T(8,128)(2,1)S(1)}, bf16[1024,256]{1,0:T(8,128)(2,1)}, u32[]{:S(2)}) copy-start(bf16[1024,256]{1,0:T(8,128)(2,1)} %get-tuple-element.17.t3) | copy-start | bytes 1572868
  31.7 1.0 %copy-start.12 = (bf16[768,256]{1,0:T(8,128)(2,1)S(1)}, bf16[768,256]{1,0:T(8,128)(2,1)}, u32[]{:S(2)}) copy-start(bf16[768,256]{1,0:T(8,128)(2,1)} %get-tuple-element.15.t1) | copy-start | bytes 1179652
where the time goes:
time: 50.5 us; the launch traced here: 50 us
  Pallas kernels  25.1 us (50%)
  starting transfers between devices  10.5 us (21%)
  local copies, waits for them, and re-layouts  8.15 us (16%)
  waiting for transfers between devices  5.36 us (11%)
  between operations  0.84 us (2%)
    pallas_call x1, Pallas kernels, body(): pl.pallas_call(functools.partial(main_kernel, sizes), out_shape=[out] * 3...  17.3 us
    unnamed x38, local copies, waits for them, and re-layouts  6.21 us
    ppermute x1, starting transfers between devices, body(): lax.ppermute(south_edge, 'lat', [(i + 1, i) for i in range(lat_count - 1)])  3.99 us
    ppermute x1, starting transfers between devices, body(): lax.ppermute(north_edge, ('lon', 'lat'), [(i * lat_count + last, (lon_cou...  3.48 us
    pallas_call x1, Pallas kernels, body(): pl.pallas_call(weights_kernel, out_shape=[jax.ShapeDtypeStruct((6 * LANES...  3.26 us
    ppermute x1, waiting for transfers between devices, body(): left = lax.ppermute(tail, 'lon', ring)  3 us
    pallas_call x1, Pallas kernels, body(): pl.pallas_call(functools.partial(pack_lat_kernel, sizes), grid=(1,), out_...  2.64 us
    ppermute x1, waiting for transfers between devices, body(): right = lax.ppermute(head, 'lon', [(b, a) for a, b in ring])  2.35 us
  transfers between devices with their start and end apart: 5, of which 2 were waited for; matrix products, arithmetic and copies ran while one was open for 4% of the time, Pallas kernels for 7%

commit v1 on v0

--- a/solution.py
+++ b/solution.py
@@ -36,30 +36,39 @@
     return jnp.dot(a, b, preferred_element_type=f32, precision=lax.Precision.HIGHEST)
 
 
-def pack_lon_kernel(sizes, n_lo, u_lo, v_lo, h_lo, s_lo, n_hi, u_hi, v_hi, h_hi, s_hi, head, tail):
+def pack_lon_kernel(sizes, noise, u, v, h, sea, head, tail, noises_in, states, seas, done):
     members, noises, levels = sizes
     fields = noises + 3 * levels
-    lats = head.shape[1]
+    lons, lats = sea.shape
+    copies = [pltpu.make_async_copy(noise, noises_in, done.at[0])]
+    for side in range(2):
+        at = pl.ds(side * (lons - GROUP), GROUP)
+        copies.append(pltpu.make_async_copy(sea.at[at], seas.at[side], done.at[1 + 4 * side]))
+        for n, x in enumerate((u, v, h)):
+            copies.append(
+                pltpu.make_async_copy(x.at[:, :, at], states.at[side, n], done.at[2 + 4 * side + n])
+            )
+    for copy in copies:
+        copy.start()
+    for copy in copies:
+        copy.wait()
     upper = iota((GROUP, lats), 0) < RIM
 
-    def field(m, c, refs):
-        noise, u, v, h = refs
+    def field(m, c, side):
         if c < noises:
-            full = noise[m, c].astype(f32)
-            return full[:GROUP] if noise is n_lo else full[-GROUP:]
+            full = noises_in[m, c].astype(f32)
+            return full[-GROUP:] if side else full[:GROUP]
         c -= noises
-        return (u, v, h)[c // levels][m, c % levels]
-
-    lo = (n_lo, u_lo, v_lo, h_lo)
-    hi = (n_hi, u_hi, v_hi, h_hi)
+        return states[side, c // levels, m, c % levels]
+
     for m in range(members):
         for c in range(0, fields, 2):
             rows = pl.ds((m * fields + c) * RIM, GROUP)
-            head[rows] = jnp.where(upper, field(m, c, lo), pltpu.roll(field(m, c + 1, lo), RIM, 0))
-            tail[rows] = jnp.where(upper, pltpu.roll(field(m, c, hi), RIM, 0), field(m, c + 1, hi))
+            head[rows] = jnp.where(upper, field(m, c, 0), pltpu.roll(field(m, c + 1, 0), RIM, 0))
+            tail[rows] = jnp.where(upper, pltpu.roll(field(m, c, 1), RIM, 0), field(m, c + 1, 1))
     rows = pl.ds(members * fields * RIM, GROUP)
-    head[rows] = s_lo[...].astype(f32)
-    tail[rows] = pltpu.roll(s_hi[...].astype(f32), RIM, 0)
+    head[rows] = seas[0].astype(f32)
+    tail[rows] = pltpu.roll(seas[1].astype(f32), RIM, 0)
 
 
 def group_tile(sizes, m, c, g, refs, groups):
@@ -72,6 +81,8 @@
         c, g = fields, g + 1
     if g == 0 or g == groups - 1:
         src = left if g == 0 else right
+        if src is None:
+            return None
         row = (m * fields + c) * RIM if c < fields else members * fields * RIM
         odd = (row // RIM) % 2
         tile = src[pl.ds(row // GROUP * GROUP, GROUP)]
@@ -79,38 +90,91 @@
             return tile
         return pltpu.roll(tile, RIM, 0)
     rows = slice((g - 1) * GROUP, g * GROUP)
+    if c == fields:
+        return None if sea is None else sea[rows].astype(f32)
+    if noise is None:
+        return None
     if c < noises:
         return noise[m, c].astype(f32)[rows]
-    if c == fields:
-        return sea[rows].astype(f32)
     c -= noises
     return (u, v, h)[c // levels][m, c % levels, rows]
 
 
-def pack_lat_kernel(
-    sizes, n_lo, u_lo, v_lo, h_lo, s_lo, n_hi, u_hi, v_hi, h_hi, s_hi, left, right, head, tail
-):
+def edge_message(sizes, refs, groups, first, part):
     members, noises, levels = sizes
-    channels = noises + 3 * levels + 2
-    groups = s_lo.shape[0] // GROUP + 2
     lane = iota((GROUP, LANES), 1)
-    for out, refs, lanes in (
-        (head, (n_lo, u_lo, v_lo, h_lo, s_lo), slice(0, LANES)),
-        (tail, (n_hi, u_hi, v_hi, h_hi, s_hi), slice(left.shape[1] - LANES, left.shape[1])),
-    ):
-        refs = refs + (left.at[:, lanes], right.at[:, lanes])
-        first = 0 if out is head else LANES - RIM
-        for c in range(channels):
-            total = jnp.zeros((GROUP, LANES), f32)
-            for g in range(groups):
-                for m in range(members):
-                    tile = group_tile(sizes, m, c, g, refs, groups)
-                    if tile is None:
-                        continue
-                    place = (g * members + m) * RIM
-                    moved = pltpu.roll(tile, (place - first) % LANES, 1)
-                    total = jnp.where((lane >= place) & (lane < place + RIM), moved, total)
-            out[pl.ds(c * GROUP, GROUP)] = total
+    rows = []
+    for c in range(noises + 3 * levels + 2):
+        total = jnp.zeros((GROUP, LANES), f32) if part is None else part[pl.ds(c * GROUP, GROUP)]
+        for g in range(groups):
+            for m in range(members):
+                tile = group_tile(sizes, m, c, g, refs, groups)
+                if tile is None:
+                    continue
+                place = (g * members + m) * RIM
+                moved = pltpu.roll(tile, (place - first) % LANES, 1)
+                total = jnp.where((lane >= place) & (lane < place + RIM), moved, total)
+        rows.append(total)
+    return rows
+
+
+def store_lats(block, t, dst, lats, chunks, m):
+    tile, m = m
+    blocks = (lats + GAP) // chunks
+    for q in range(chunks):
+        lo = max(q * blocks, t * LANES)
+        hi = min((q + 1) * blocks, (t + 1) * LANES, lats)
+        if lo < hi:
+            start = (lo - q * blocks) * SUB + m * chunks + q
+            dst[tile, pl.ds(start, hi - lo, stride=SUB), :] = block[lo - t * LANES : hi - t * LANES]
+
+
+def own_kernel(sizes, noise, u, v, h, sea, own, head, tail, cells):
+    members, noises, levels = sizes
+    fields = noises + 3 * levels
+    lons, lats = sea.shape
+    groups = lons // GROUP + 2
+    chunks = SUB // members
+    gap_k = lats - (chunks - 1) * ((lats + GAP) // chunks)
+    for g in range(groups - 2):
+        for m in range(members):
+            empty = pl.ds(gap_k * SUB + (m + 1) * chunks - 1, GAP, stride=SUB)
+            cells[g, empty, :] = jnp.zeros((GAP, LANES), f32)
+    for t in range(lats // LANES):
+        lanes = slice(t * LANES, (t + 1) * LANES)
+        refs = tuple(x.at[:, :, :, lanes] for x in (noise, u, v, h)) + (sea.at[:, lanes], None, None)
+        if t == 0:
+            for c, row in enumerate(edge_message(sizes, refs, groups, 0, None)):
+                head[pl.ds(c * GROUP, GROUP)] = row
+        if t == lats // LANES - 1:
+            for c, row in enumerate(edge_message(sizes, refs, groups, LANES - RIM, None)):
+                tail[pl.ds(c * GROUP, GROUP)] = row
+        ones = jnp.ones((GROUP, LANES), f32)
+        blank = jnp.zeros((LANES - (fields + 3) * GROUP, LANES), f32)
+        for g in range(1, groups - 1):
+            for m in range(members):
+                tiles = [group_tile(sizes, m, c, g, refs, groups) for c in range(fields)]
+                mask = group_tile(sizes, m, fields, g, refs, groups) - 1.0
+                following = group_tile(sizes, m, fields + 1, g, refs, groups)
+                following = jnp.zeros_like(mask) if following is None else following - 1.0
+                block = jnp.transpose(jnp.concatenate(tiles + [mask, following, ones, blank], axis=0))
+                store_lats(block, t, cells, lats, chunks, (g - 1, m))
+    for g in range(groups - 2):
+        own[g] = cells[g].astype(bf16)
+
+
+def join_kernel(sizes, place, sea, left, right, head, tail, even, odd):
+    groups = sea.shape[0] // GROUP + 2
+    lats = left.shape[1]
+    blank = (None,) * 5
+    low = edge_message(sizes, blank + (left.at[:, :LANES], right.at[:, :LANES]), groups, 0, head)
+    high = edge_message(
+        sizes, blank + (left.at[:, lats - LANES :], right.at[:, lats - LANES :]), groups, LANES - RIM, tail
+    )
+    to_south = place[1] == 1
+    for c, (a, b) in enumerate(zip(low, high)):
+        even[pl.ds(c * GROUP, GROUP)] = jnp.where(to_south, a, b)
+        odd[pl.ds(c * GROUP, GROUP)] = jnp.where(to_south, b, a)
 
 
 def weights_kernel(w1, w2, w3, w4, biases, t1, t2, t3, t4):
@@ -209,7 +273,7 @@
     sizes,
     place,
     bias_last,
-    noise,
+    own,
     u,
     v,
     h,
@@ -217,9 +281,8 @@
     coriolis,
     left,
     right,
-    south,
-    north,
-    strip,
+    even_rim,
+    odd_rim,
     own_tail,
     t1,
     t2,
@@ -234,6 +297,7 @@
     even,
     force,
     turned,
+    gaps,
 ):
     members, noises, levels = sizes
     fields = noises + 3 * levels
@@ -244,7 +308,10 @@
     rows = blocks * SUB
     gap_k = lats - (chunks - 1) * blocks
     top = place[0] == 1
-    refs = (noise, u, v, h, sea, left, right)
+    is_odd = place[1] == 1
+    bottom = place[2] == 1
+    strip = odd_rim[...]
+    south = jnp.where(is_odd, even_rim[...], jnp.where(bottom, 0.0, strip))
 
     wide = fields * GROUP + 2 * GROUP
     lane = iota((wide, LANES), 1)
@@ -260,59 +327,61 @@
     span = members * RIM
     source = (groups - 1 - lane_to // span) * span + lane_to % span + RIM - 1
     flip_lanes = jnp.where((lane_to % RIM == 0) & (lane_to < groups * span) & (lane_from == source), 1.0, 0.0)
-    pair = exact_dot(flip_rows, jnp.concatenate([strip[...], own_tail[...]], axis=1))
+    pair = exact_dot(flip_rows, jnp.concatenate([strip, own_tail[...]], axis=1))
     folded = exact_dot(pair[:, :LANES], flip_lanes)
     ghost = exact_dot(pair[:, LANES:], flip_lanes)
-    north_rim = jnp.where((lane % RIM == 0) & top, folded, north[...])
+    north = jnp.where(is_odd, strip, even_rim[...])
+    north_rim = jnp.where((lane % RIM == 0) & top, folded, north)
 
     ones = jnp.ones((GROUP, LANES), f32)
     blank = jnp.zeros((LANES - wide - GROUP, LANES), f32)
-    for g in range(groups):
-        for m in range(members):
-            cells[g, pl.ds(gap_k * SUB + m * chunks + chunks - 1, GAP, stride=SUB), :] = jnp.zeros(
-                (GAP, LANES), f32
-            )
-    for n, (message, offset) in enumerate(
-        ((south[...], SOUTH), (north_rim, NORTH), (strip[...], STRIP), (ghost, GHOST))
-    ):
-        body_rows = fields * GROUP
+    body_rows = fields * GROUP
+    offsets = (NORTH, STRIP, GHOST, SOUTH)
+    for n, message in enumerate((north_rim, strip, ghost, south)):
         tall = jnp.concatenate([message[:body_rows], message[body_rows:] - 1.0, ones, blank], axis=0)
         turned[n] = jnp.transpose(tall)
         for g in range(groups):
             for m in range(members):
-                gap = (m - 1) % members if offset == SOUTH else m
-                start = (gap_k + offset) * SUB + gap * chunks + chunks - 1
-                cells[g, pl.ds(start, RIM, stride=SUB), :] = turned[n, pl.ds((g * members + m) * RIM, RIM), :]
-
+                gap = (m - 1) % members if offsets[n] == SOUTH else m
+                start = n * RIM * SUB + gap * chunks + chunks - 1
+                gaps[g, pl.ds(start, RIM, stride=SUB), :] = turned[n, pl.ds((g * members + m) * RIM, RIM), :]
+
+    for side in range(2):
+        for m in range(members):
+            empty = pl.ds(gap_k * SUB + (m + 1) * chunks - 1, GAP, stride=SUB)
+            cells[side, empty, :] = jnp.zeros((GAP, LANES), f32)
     for t in range(lats // LANES):
         lanes = slice(t * LANES, (t + 1) * LANES)
-        views = (
-            noise.at[:, :, :, lanes],
-            u.at[:, :, :, lanes],
-            v.at[:, :, :, lanes],
-            h.at[:, :, :, lanes],
-            sea.at[:, lanes],
-            left.at[:, lanes],
-            right.at[:, lanes],
-        )
-        for g in range(groups):
+        refs = (None,) * 4 + (sea.at[:, lanes], left.at[:, lanes], right.at[:, lanes])
+        for side, g in enumerate((0, groups - 1)):
             for m in range(members):
-                tiles = [group_tile(sizes, m, c, g, views, groups) for c in range(fields)]
-                own = group_tile(sizes, m, fields, g, views, groups) - 1.0
-                following = group_tile(sizes, m, fields + 1, g, views, groups)
-                following = jnp.zeros_like(own) if following is None else following - 1.0
-                block = jnp.transpose(jnp.concatenate(tiles + [own, following, ones, blank], axis=0))
-                for q in range(chunks):
-                    lo = max(q * blocks, t * LANES)
-                    hi = min((q + 1) * blocks, (t + 1) * LANES, lats)
-                    if lo < hi:
-                        start = (lo - q * blocks) * SUB + m * chunks + q
-                        cells[g, pl.ds(start, hi - lo, stride=SUB), :] = block[lo - t * LANES : hi - t * LANES]
-
+                tiles = [group_tile(sizes, m, c, g, refs, groups) for c in range(fields)]
+                mask = group_tile(sizes, m, fields, g, refs, groups) - 1.0
+                following = group_tile(sizes, m, fields + 1, g, refs, groups)
+                following = jnp.zeros_like(mask) if following is None else following - 1.0
+                block = jnp.transpose(jnp.concatenate(tiles + [mask, following, ones, blank], axis=0))
+                store_lats(block, t, cells, lats, chunks, (side, m))
+
+    in_gap = iota((RIM * SUB, LANES), 0) % chunks == chunks - 1
+    next_mask = iota((rows, LANES), 1) // GROUP == fields + 1
     for g in range(groups):
-        first[g, pl.ds(SUB, rows), :] = cells[g].astype(bf16)
-        first[g, pl.ds(0, SUB), :] = pltpu.roll(cells[g, pl.ds(rows - SUB, SUB), :], 1, 0).astype(bf16)
-        first[g, pl.ds(SUB + rows, SUB), :] = pltpu.roll(cells[g, pl.ds(0, SUB), :], SUB - 1, 0).astype(bf16)
+        if g == 0:
+            first[g, pl.ds(SUB, rows), :] = cells[0].astype(bf16)
+        elif g == groups - 1:
+            first[g, pl.ds(SUB, rows), :] = cells[1].astype(bf16)
+        elif g == groups - 2:
+            moved = pltpu.roll(cells[1], GROUP, 1)
+            first[g, pl.ds(SUB, rows), :] = jnp.where(next_mask, moved, own[g - 1].astype(f32)).astype(bf16)
+        else:
+            first[g, pl.ds(SUB, rows), :] = own[g - 1]
+        for n, offset in enumerate(offsets):
+            spot = pl.ds((1 + gap_k + offset) * SUB, RIM * SUB)
+            kept = first[g, spot, :].astype(f32)
+            first[g, spot, :] = jnp.where(in_gap, gaps[g, pl.ds(n * RIM * SUB, RIM * SUB), :], kept).astype(bf16)
+        end = first[g, pl.ds(rows, SUB), :].astype(f32)
+        first[g, pl.ds(0, SUB), :] = pltpu.roll(end, 1, 0).astype(bf16)
+        begin = first[g, pl.ds(SUB, SUB), :].astype(f32)
+        first[g, pl.ds(SUB + rows, SUB), :] = pltpu.roll(begin, SUB - 1, 0).astype(bf16)
 
     hidden = LANES // 4
     per = LANES // hidden
@@ -477,50 +546,57 @@
     assert hidden * 4 == LANES and outs * lons == LANES and members * RIM * groups <= LANES
     assert lats % LANES == 0 and SUB % members == 0 and (lats + GAP) % (SUB // members) == 0
     lon_count, lat_count = lax.axis_size("lon"), lax.axis_size("lat")
+    assert lon_count % 2 == 0 and lat_count % 2 == 0
     lat_index = lax.axis_index("lat")
     state = (noise, velocity_u, velocity_v, thickness, land_sea)
     whole = pl.BlockSpec(memory_space=pltpu.VMEM)
 
-    def edge(index, dim, size):
-        specs = []
-        for x in state:
-            shape, at = list(x.shape), [0] * x.ndim
-            if not (dim == -2 and x.dtype == bf16):
-                at[dim] = (shape[dim] // size - 1) * index
-                shape[dim] = size
-            specs.append(pl.BlockSpec(tuple(shape), functools.partial(lambda at, *_: tuple(at), at)))
-        return specs
-
     tall = members * fields * RIM + GROUP
     head, tail = pl.pallas_call(
         functools.partial(pack_lon_kernel, sizes),
-        grid=(1,),
-        out_shape=[jax.ShapeDtypeStruct((tall, lats), f32)] * 2,
-        in_specs=edge(0, -2, GROUP) + edge(1, -2, GROUP),
-        out_specs=[pl.BlockSpec((tall, lats), lambda i: (0, 0))] * 2,
+        out_shape=[pltpu.VMEM((tall, lats), f32)] * 2,
+        in_specs=[pl.BlockSpec(memory_space=pltpu.HBM)] * 5,
+        out_specs=[whole] * 2,
+        scratch_shapes=[
+            pltpu.VMEM(noise.shape, noise.dtype),
+            pltpu.VMEM((2, 3, members, levels, GROUP, lats), f32),
+            pltpu.VMEM((2, GROUP, lats), land_sea.dtype),
+            pltpu.SemaphoreType.DMA((9,)),
+        ],
         name="pack_lon",
-    )(*state, *state)
+    )(*state)
     ring = [(i, (i + 1) % lon_count) for i in range(lon_count)]
     left = lax.ppermute(tail, "lon", ring)
     right = lax.ppermute(head, "lon", [(b, a) for a, b in ring])
 
     wide = (fields + 2) * GROUP
-    south_edge, north_edge = pl.pallas_call(
-        functools.partial(pack_lat_kernel, sizes),
-        grid=(1,),
-        out_shape=[jax.ShapeDtypeStruct((wide, LANES), f32)] * 2,
-        in_specs=edge(0, -1, LANES) + edge(1, -1, LANES) + [pl.BlockSpec((tall, lats), lambda i: (0, 0))] * 2,
-        out_specs=[pl.BlockSpec((wide, LANES), lambda i: (0, 0))] * 2,
-        name="pack_lat",
-    )(*state, *state, left, right)
-    south = lax.ppermute(north_edge, "lat", [(i, i + 1) for i in range(lat_count - 1)])
-    north = lax.ppermute(south_edge, "lat", [(i + 1, i) for i in range(lat_count - 1)])
+    message = pltpu.VMEM((wide, LANES), f32)
+    own, own_head, own_tail = pl.pallas_call(
+        functools.partial(own_kernel, sizes),
+        out_shape=[pltpu.VMEM((groups - 2, rows, LANES), bf16), message, message],
+        in_specs=[whole] * 5,
+        out_specs=[whole] * 3,
+        scratch_shapes=[pltpu.VMEM((groups - 2, rows, LANES), f32)],
+        cost_estimate=pl.CostEstimate(flops=10**7, bytes_accessed=10**7, transcendentals=0),
+        name="own_cells",
+    )(*state)
     last = lat_count - 1
-    strip = lax.ppermute(
-        north_edge,
-        ("lon", "lat"),
-        [(i * lat_count + last, (lon_count - 1 - i) * lat_count + last) for i in range(lon_count)],
-    )
+    place = jnp.stack([lat_index == last, lat_index % 2 == 1, lat_index == 0]).astype(jnp.int32)
+    smem = pl.BlockSpec(memory_space=pltpu.SMEM)
+    to_even, to_odd = pl.pallas_call(
+        functools.partial(join_kernel, sizes),
+        out_shape=[message] * 2,
+        in_specs=[smem] + [whole] * 5,
+        out_specs=[whole] * 2,
+        name="join_rims",
+    )(place, land_sea, left, right, own_head, own_tail)
+    even_rim = lax.ppermute(to_even, "lat", [(i, i ^ 1) for i in range(lat_count)])
+    pairs = []
+    for t in range(lon_count):
+        at = t * lat_count
+        pairs += [(at + k, at + k - 1 + 2 * (k % 2)) for k in range(1, last)]
+        pairs += [(at, (t ^ 1) * lat_count), (at + last, (lon_count - 1 - t) * lat_count + last)]
+    odd_rim = lax.ppermute(to_odd, ("lon", "lat"), pairs)
 
     taps = conv_first.transpose(3, 2, 1, 0)[:, :, :, None, None, :]
     taps = jnp.broadcast_to(taps, (3, 3, fields, GROUP, LANES // hidden, hidden)).reshape(9, -1, LANES)
@@ -529,11 +605,13 @@
     t1, t2, t3, t4 = pl.pallas_call(
         weights_kernel,
         out_shape=[
-            jax.ShapeDtypeStruct((6 * LANES, 2 * LANES), bf16),
-            jax.ShapeDtypeStruct((8 * LANES, 2 * LANES), bf16),
-            jax.ShapeDtypeStruct((8 * LANES, 2 * LANES), bf16),
-            jax.ShapeDtypeStruct((3 * deep, LANES), bf16),
+            pltpu.VMEM((6 * LANES, 2 * LANES), bf16),
+            pltpu.VMEM((8 * LANES, 2 * LANES), bf16),
+            pltpu.VMEM((8 * LANES, 2 * LANES), bf16),
+            pltpu.VMEM((3 * deep, LANES), bf16),
         ],
+        in_specs=[whole] * 5,
+        out_specs=[whole] * 4,
         cost_estimate=pl.CostEstimate(flops=10**7, bytes_accessed=3 * 10**6, transcendentals=0),
         name="banded_matrices",
     )(
@@ -546,38 +624,37 @@
 
     lat_rows = (lat_index * lats + jnp.arange(lats)).astype(f32)
     coriolis = CORIOLIS * (2.0 * (lat_rows + 0.5) / (lats * lat_count) - 1.0)
-    place = (lat_index == last).astype(jnp.int32)[None]
-    smem = pl.BlockSpec(memory_space=pltpu.SMEM)
     padded = rows + 2 * SUB
     tiles = 2 * (groups - 1) + 1
     out = jax.ShapeDtypeStruct(velocity_u.shape, f32)
     return pl.pallas_call(
         functools.partial(main_kernel, sizes),
         out_shape=[out] * 3,
-        in_specs=[smem, smem] + [whole] * 16,
+        in_specs=[smem, smem] + [whole] * 15,
         out_specs=[whole] * 3,
         scratch_shapes=[
-            pltpu.VMEM((groups, rows, LANES), f32),
+            pltpu.VMEM((2, rows, LANES), f32),
             pltpu.VMEM((groups, padded, LANES), bf16),
             pltpu.VMEM((tiles, padded, LANES), bf16),
             pltpu.VMEM((tiles, padded, LANES), bf16),
             pltpu.VMEM((rows, LANES), f32),
             pltpu.VMEM((4, LANES, LANES), f32),
+            pltpu.VMEM((groups, 4 * RIM * SUB, LANES), f32),
         ],
-        compiler_params=pltpu.CompilerParams(vmem_limit_bytes=48 * 2**20),
+        compiler_params=pltpu.CompilerParams(vmem_limit_bytes=32 * 2**20),
         cost_estimate=pl.CostEstimate(flops=2 * 10**10, bytes_accessed=10**7, transcendentals=4 * 10**6),
         name="network_and_step",
     )(
         place,
         bias_last,
-        *state,
+        own,
+        *state[1:],
         coriolis[None],
         left,
         right,
-        south,
-        north,
-        strip,
-        north_edge,
+        even_rim,
+        odd_rim,
+        to_odd,
         t1,
         t2,
         t3,

time: 50.5 us -> 38.3 us (0.76)
  the two profiles are of different devices: /device:TPU:27 before, /device:TPU:12 now
where the time goes in v1:
time: 38.3 us; the launch traced here: 38 us
  Pallas kernels  24.3 us (63%)
  local copies, waits for them, and re-layouts  6.21 us (16%)
  starting transfers between devices  5.91 us (15%)
  between operations  0.89 us (2%)
  other arithmetic  0.63 us (2%)
    pallas_call x1, Pallas kernels, body(): pl.pallas_call(functools.partial(main_kernel, sizes), out_shape=[out] * 3...  16.6 us
    unnamed x36, local copies, waits for them, and re-layouts  4.29 us
    ppermute x1, starting transfers between devices, body(): odd_rim = lax.ppermute(to_odd, ('lon', 'lat'), pairs)  2.7 us
    ppermute x1, starting transfers between devices, body(): right = lax.ppermute(head, 'lon', [(b, a) for a, b in ring])  2.63 us
    pallas_call x1, Pallas kernels, body(): pl.pallas_call(functools.partial(own_kernel, sizes), out_shape=[pltpu.VME...  2.51 us
    pallas_call x1, Pallas kernels, body(): pl.pallas_call(weights_kernel, out_shape=[pltpu.VMEM((6 * LANES, 2 * LANE...  2.05 us
    pallas_call x1, Pallas kernels, body(): pl.pallas_call(functools.partial(join_kernel, sizes), out_shape=[message]...  1.92 us
    pallas_call x1, Pallas kernels, body(): pl.pallas_call(functools.partial(pack_lon_kernel, sizes), out_shape=[pltp...  1.23 us
  transfers between devices with their start and end apart: 4, of which 0 were waited for; matrix products, arithmetic and copies ran while one was open for 7% of the time, Pallas kernels for 12%

profile of v1, /device:TPU:12, one launch (start us, length us, event | category | flops | bytes accessed | tf_op | source)
XLA Modules:
  0.0 38.0 jit_solution(4884479339388349874)
XLA Ops:
  0.7 1.2 %pack_lon.1 = (f32[168,256]{1,0:T(8,128)S(1)}, f32[168,256]{1,0:T(8,128)S(1)}) custom-call(bf16[4,4,32,256]{3,2,1,0:T(8,128)(2,1)} %noise.3, f32[4,2,32,256]{3,2,1,0:T(8,128)} %u.5, f32[4,2,32,256]{3,2,1,0:T(8,128)} %v.5, f32[4,2,32,256]{3,2,1,0:T(8,128)} %h.5, s32[32,256]{1,0:T(8,128)} %sea.7), custom_call_target="tpu_custom_call" | custom-call | tf_op jit(solution)/shard_map/pack_lon/pallas_call | solution.py:555
  1.9 0.1 collective-permute-start
  2.0 2.6 %collective-permute-start.1 = (f32[168,256]{1,0:T(8,128)S(1)}, f32[168,256]{1,0:T(8,128)S(1)}, u32[]{:S(2)}, u32[]{:S(2)}) collective-permute-start(f32[168,256]{1,0:T(8,128)S(1)} %get-tuple-element.16), channel_id=1, source_target_pairs={{4,0},{8,4},{12,8},{16,12},{20,16},{24,20},{28,24},{0,28},{5,1},{9... | collective-permute-start | bytes 516104 | tf_op jit(solution)/shard_map/ppermute | solution.py:570
  4.6 2.5 %own_cells.1 = (bf16[4,1152,128]{2,1,0:T(8,128)(2,1)S(1)}, f32[96,128]{1,0:T(8,128)S(1)}, f32[96,128]{1,0:T(8,128)S(1)}) custom-call(bf16[4,4,32,256]{3,2,1,0:T(8,128)(2,1)} %noise.3, f32[4,2,32,256]{3,2,1,0:T(8,128)} %u.5, f32[4,2,32,256]{3,2,1,0:T(8,128)} %v.5, f32[4,2,32,256]{3,2,1,0:T(8,128)} %h.5, s32[32,256]{1,0:T(8,128)} %sea.7), custom_call_target="tpu_custom_call" | custom-call | flops 10000000 | bytes 10000000 | tf_op jit(solution)/shard_map/own_cells/pallas_call | solution.py:574
  7.1 0.0 copy-start.8
  7.1 0.6 %copy-done.8 = f32[96,128]{1,0:T(8,128)} copy-done((f32[96,128]{1,0:T(8,128)}, f32[96,128]{1,0:T(8,128)S(1)}, u32[]{:S(2)}) %copy-start.8) | copy-done | bytes 49176
  7.8 0.6 %copy-done.9 = f32[96,128]{1,0:T(8,128)} copy-done((f32[96,128]{1,0:T(8,128)}, f32[96,128]{1,0:T(8,128)S(1)}, u32[]{:S(2)}) %copy-start.9) | copy-done | bytes 49176
  8.4 1.0 %copy-done.11 = bf16[4,1152,128]{2,1,0:T(8,128)(2,1)} copy-done((bf16[4,1152,128]{2,1,0:T(8,128)(2,1)}, bf16[4,1152,128]{2,1,0:T(8,128)(2,1)S(1)}, u32[]{:S(2)}) %copy-start.11) | copy-done | bytes 1179672
  9.4 0.6 %add_convert_fusion.place = s32[3]{0:T(128)} fusion(pred[1]{0:T(512)(128)(4,1)} %bitcast.2, pred[1]{0:T(512)(128)(4,1)} %bitcast.1, pred[1]{0:T(512)(128)(4,1)} %bitcast), kind=kLoop, calls=%fused_computation.1 | loop fusion | flops 9 | bytes 15 | tf_op jit(solution)/shard_map/convert_element_type | solution.py:584
  10.0 0.0 copy-done.15
  10.0 0.0 copy-done.17
  10.0 0.0 collective-permute-done.left
  10.0 0.0 copy-start.4
  10.1 0.0 collective-permute-done.1.right
  10.1 0.0 copy-start.6
  10.1 0.6 %copy-done.4 = f32[168,256]{1,0:T(8,128)} copy-done((f32[168,256]{1,0:T(8,128)}, f32[168,256]{1,0:T(8,128)S(1)}, u32[]{:S(2)}) %copy-start.4) | copy-done | bytes 172056
  10.7 0.1 copy-done.6
  10.8 1.9 %join_rims.1 = (f32[96,128]{1,0:T(8,128)}, f32[96,128]{1,0:T(8,128)S(1)}) custom-call(s32[3]{0:T(128)} %add_convert_fusion.place, s32[32,256]{1,0:T(8,128)} %sea.7, f32[168,256]{1,0:T(8,128)} %copy-done.4, f32[168,256]{1,0:T(8,128)} %copy-done.6, f32[96,128]{1,0:T(8,128)} %copy-done.8, f32[96,128]{1,0:T(8,128)} %copy-done.9), custom_call_target="tpu_custom_call" | custom-call | tf_op jit(solution)/shard_map/join_rims/pallas_call | solution.py:586
  12.7 0.0 copy-start.3
  12.7 0.0 copy-start.5
  12.7 0.0 copy-start.7
  12.7 0.0 copy-start.13
  12.8 0.5 %collective-permute-start.2 = (f32[96,128]{1,0:T(8,128)}, f32[96,128]{1,0:T(8,128)}, u32[]{:S(2)}, u32[]{:S(2)}) collective-permute-start(f32[96,128]{1,0:T(8,128)} %get-tuple-element.19), channel_id=1, source_target_pairs={{0,1},{1,0},{2,3},{3,2},{4,5},{5,4},{6,7},{7,6},{8,9},{9,8},{10,11... | collective-permute-start | bytes 147464 | tf_op jit(solution)/shard_map/ppermute | solution.py:593
  13.3 2.7 %collective-permute-start.3 = (f32[96,128]{1,0:T(8,128)S(1)}, f32[96,128]{1,0:T(8,128)}, u32[]{:S(2)}, u32[]{:S(2)}) collective-permute-start(f32[96,128]{1,0:T(8,128)S(1)} %get-tuple-element.20.own_tail), channel_id=1, source_target_pairs={{1,2},{2,1},{0,4},{3,31},{5,6},{6,5},{4,0},{7,27},{9,10},{10,9},{8... | collective-permute-start | bytes 147464 | tf_op jit(solution)/shard_map/ppermute | solution.py:599
  16.0 0.7 %tile.10.biases = f32[3,128]{1,0:T(4,128)} reshape(f32[3,4,32]{2,1,0:T(4,128)S(1)} %tile.4) | data formatting | bytes 3072 | tf_op jit(solution)/shard_map/tile | solution.py:603
  16.7 0.2 broadcast_in_dim.2
  16.9 1.1 %reshape.36.w1 = bf16[9,80,128]{2,1,0:T(8,128)(2,1)} reshape(bf16[3,3,10,8,4,32]{5,4,3,2,1,0:T(4,128)(2,1)S(1)} %broadcast_in_dim.2) | data formatting | bytes 368640 | tf_op jit(solution)/shard_map/reshape | solution.py:602
  17.9 2.1 %banded_matrices.1 = (bf16[768,256]{1,0:T(8,128)(2,1)S(1)}, bf16[1024,256]{1,0:T(8,128)(2,1)S(1)}, bf16[1024,256]{1,0:T(8,128)(2,1)S(1)}, bf16[3456,128]{1,0:T(8,128)(2,1)S(1)}) custom-call(bf16[9,80,128]{2,1,0:T(8,128)(2,1)} %reshape.36.w1, bf16[3,3,32,32]{3,2,1,0:T(8,128)(2,1)} %bitcast.10, bf16[3,3,32,32]{3,2,1,0:T(8,128)(2,1)} %bitcast.11, ...), custom_call_target="tpu_custom_call" | custom-call | flops 10000000 | bytes 3000000 | tf_op jit(solution)/shard_map/banded_matrices/pallas_call | solution.py:605
  20.0 0.0 collective-permute-done.2.even_rim
  20.0 0.0 collective-permute-done.3.odd_rim
  20.1 1.3 %copy-done.12 = bf16[4,1152,128]{2,1,0:T(8,128)(2,1)S(1)} copy-done((bf16[4,1152,128]{2,1,0:T(8,128)(2,1)S(1)}, bf16[4,1152,128]{2,1,0:T(8,128)(2,1)}, u32[]{:S(2)}) %copy-start.12) | copy-done | bytes 1179672
  21.4 16.6 %network_and_step.1 = (f32[4,2,32,256]{3,2,1,0:T(8,128)}, f32[4,2,32,256]{3,2,1,0:T(8,128)}, f32[4,2,32,256]{3,2,1,0:T(8,128)}) custom-call(s32[3]{0:T(128)S(1)} %copy-done.10, f32[4]{0:T(128)S(1)} %copy-done.13, bf16[4,1152,128]{2,1,0:T(8,128)(2,1)S(1)} %copy-done.12, f32[4,2,32,256]{3,2,1,0:T(8,128)S(1)} %copy-done, f32[4,2,32,256]{3,2,1,0:T(8,128)S(1)} %copy-done.1, ...), custom_call_target="tpu_custom_call" | custom-call | flops 20000000000 | bytes 10000000 | tf_op jit(solution)/shard_map/network_and_step/pallas_call | solution.py:630
  (25 shorter events, 0.1 us)
Async XLA Ops:
  0.6 9.4 %copy-start.15 = (f32[32]{0:T(128)S(1)}, f32[32]{0:T(128)}, u32[]{:S(2)}) copy-start(f32[32]{0:T(128)} %param.23) | copy-start | bytes 388
  0.6 9.4 %copy-start.16 = (f32[32]{0:T(128)S(1)}, f32[32]{0:T(128)}, u32[]{:S(2)}) copy-start(f32[32]{0:T(128)} %param.21) | copy-start | bytes 388
  0.7 9.4 %copy-start.17 = (f32[32]{0:T(128)S(1)}, f32[32]{0:T(128)}, u32[]{:S(2)}) copy-start(f32[32]{0:T(128)} %param.19) | copy-start | bytes 388
  0.7 16.0 %copy-start.14 = (bf16[32,10,3,3]{0,3,2,1:T(4,128)(2,1)S(1)}, bf16[32,10,3,3]{0,3,2,1:T(4,128)(2,1)}, u32[]{:S(2)}) copy-start(bf16[32,10,3,3]{0,3,2,1:T(4,128)(2,1)} %param.18) | copy-start | bytes 17284
  1.9 8.1 %collective-permute-start = (f32[168,256]{1,0:T(8,128)S(1)}, f32[168,256]{1,0:T(8,128)S(1)}, u32[]{:S(2)}, u32[]{:S(2)}) collective-permute-start(f32[168,256]{1,0:T(8,128)S(1)} %get-tuple-element.15), channel_id=1, source_target_pairs={{0,4},{4,8},{8,12},{12,16},{16,20},{20,24},{24,28},{28,0},{1,5},{5... | collective-permute-start | bytes 516104 | tf_op jit(solution)/shard_map/ppermute | solution.py:569
  2.0 8.1 %collective-permute-start.1 = (f32[168,256]{1,0:T(8,128)S(1)}, f32[168,256]{1,0:T(8,128)S(1)}, u32[]{:S(2)}, u32[]{:S(2)}) collective-permute-start(f32[168,256]{1,0:T(8,128)S(1)} %get-tuple-element.16), channel_id=1, source_target_pairs={{4,0},{8,4},{12,8},{16,12},{20,16},{24,20},{28,24},{0,28},{5,1},{9... | collective-permute-start | bytes 516104 | tf_op jit(solution)/shard_map/ppermute | solution.py:570
  7.1 0.6 %copy-start.8 = (f32[96,128]{1,0:T(8,128)}, f32[96,128]{1,0:T(8,128)S(1)}, u32[]{:S(2)}) copy-start(f32[96,128]{1,0:T(8,128)S(1)} %get-tuple-element.17.head) | copy-start | bytes 147460
  7.7 0.6 %copy-start.9 = (f32[96,128]{1,0:T(8,128)}, f32[96,128]{1,0:T(8,128)S(1)}, u32[]{:S(2)}) copy-start(f32[96,128]{1,0:T(8,128)S(1)} %get-tuple-element.18.tail) | copy-start | bytes 147460
  8.4 1.0 %copy-start.11 = (bf16[4,1152,128]{2,1,0:T(8,128)(2,1)}, bf16[4,1152,128]{2,1,0:T(8,128)(2,1)S(1)}, u32[]{:S(2)}) copy-start(bf16[4,1152,128]{2,1,0:T(8,128)(2,1)S(1)} %get-tuple-element.14.own) | copy-start | bytes 3538948
  10.0 0.7 %copy-start.4 = (f32[168,256]{1,0:T(8,128)}, f32[168,256]{1,0:T(8,128)S(1)}, u32[]{:S(2)}) copy-start(f32[168,256]{1,0:T(8,128)S(1)} %collective-permute-done.left) | copy-start | bytes 516100
  10.1 0.7 %copy-start.6 = (f32[168,256]{1,0:T(8,128)}, f32[168,256]{1,0:T(8,128)S(1)}, u32[]{:S(2)}) copy-start(f32[168,256]{1,0:T(8,128)S(1)} %collective-permute-done.1.right) | copy-start | bytes 516100
  12.7 7.3 %copy-start = (f32[4,2,32,256]{3,2,1,0:T(8,128)S(1)}, f32[4,2,32,256]{3,2,1,0:T(8,128)}, u32[]{:S(2)}) copy-start(f32[4,2,32,256]{3,2,1,0:T(8,128)} %u.5) | copy-start | bytes 786436
  12.7 7.3 %copy-start.1 = (f32[4,2,32,256]{3,2,1,0:T(8,128)S(1)}, f32[4,2,32,256]{3,2,1,0:T(8,128)}, u32[]{:S(2)}) copy-start(f32[4,2,32,256]{3,2,1,0:T(8,128)} %v.5) | copy-start | bytes 786436
  12.7 7.3 %copy-start.2 = (f32[4,2,32,256]{3,2,1,0:T(8,128)S(1)}, f32[4,2,32,256]{3,2,1,0:T(8,128)}, u32[]{:S(2)}) copy-start(f32[4,2,32,256]{3,2,1,0:T(8,128)} %h.5) | copy-start | bytes 786436
  12.7 7.3 %copy-start.3 = (s32[32,256]{1,0:T(8,128)S(1)}, s32[32,256]{1,0:T(8,128)}, u32[]{:S(2)}) copy-start(s32[32,256]{1,0:T(8,128)} %sea.7) | copy-start | bytes 98308
  12.7 7.3 %copy-start.5 = (f32[168,256]{1,0:T(8,128)S(1)}, f32[168,256]{1,0:T(8,128)}, u32[]{:S(2)}) copy-start(f32[168,256]{1,0:T(8,128)} %copy-done.4) | copy-start | bytes 516100
  12.7 7.3 %copy-start.7 = (f32[168,256]{1,0:T(8,128)S(1)}, f32[168,256]{1,0:T(8,128)}, u32[]{:S(2)}) copy-start(f32[168,256]{1,0:T(8,128)} %copy-done.6) | copy-start | bytes 516100
  12.7 7.3 %copy-start.10 = (s32[3]{0:T(128)S(1)}, s32[3]{0:T(128)}, u32[]{:S(2)}) copy-start(s32[3]{0:T(128)} %add_convert_fusion.place) | copy-start | bytes 40
  12.7 7.3 %copy-start.13 = (f32[4]{0:T(128)S(1)}, f32[4]{0:T(128)}, u32[]{:S(2)}) copy-start(f32[4]{0:T(128)} %bias_last.1) | copy-start | bytes 52
  12.8 7.2 %collective-permute-start.2 = (f32[96,128]{1,0:T(8,128)}, f32[96,128]{1,0:T(8,128)}, u32[]{:S(2)}, u32[]{:S(2)}) collective-permute-start(f32[96,128]{1,0:T(8,128)} %get-tuple-element.19), channel_id=1, source_target_pairs={{0,1},{1,0},{2,3},{3,2},{4,5},{5,4},{6,7},{7,6},{8,9},{9,8},{10,11... | collective-permute-start | bytes 147464 | tf_op jit(solution)/shard_map/ppermute | solution.py:593
  13.3 6.7 %collective-permute-start.3 = (f32[96,128]{1,0:T(8,128)S(1)}, f32[96,128]{1,0:T(8,128)}, u32[]{:S(2)}, u32[]{:S(2)}) collective-permute-start(f32[96,128]{1,0:T(8,128)S(1)} %get-tuple-element.20.own_tail), channel_id=1, source_target_pairs={{1,2},{2,1},{0,4},{3,31},{5,6},{6,5},{4,0},{7,27},{9,10},{10,9},{8... | collective-permute-start | bytes 147464 | tf_op jit(solution)/shard_map/ppermute | solution.py:599
  20.1 1.3 %copy-start.12 = (bf16[4,1152,128]{2,1,0:T(8,128)(2,1)S(1)}, bf16[4,1152,128]{2,1,0:T(8,128)(2,1)}, u32[]{:S(2)}) copy-start(bf16[4,1152,128]{2,1,0:T(8,128)(2,1)} %copy-done.11) | copy-start | bytes 3538948

commit v2 on v1

--- a/solution.py
+++ b/solution.py
@@ -163,7 +163,7 @@
         own[g] = cells[g].astype(bf16)
 
 
-def join_kernel(sizes, place, sea, left, right, head, tail, even, odd):
+def join_kernel(sizes, sea, left, right, head, tail, even, odd):
     groups = sea.shape[0] // GROUP + 2
     lats = left.shape[1]
     blank = (None,) * 5
@@ -171,24 +171,24 @@
     high = edge_message(
         sizes, blank + (left.at[:, lats - LANES :], right.at[:, lats - LANES :]), groups, LANES - RIM, tail
     )
-    to_south = place[1] == 1
+    to_south = lax.axis_index("lat") % 2 == 1
     for c, (a, b) in enumerate(zip(low, high)):
         even[pl.ds(c * GROUP, GROUP)] = jnp.where(to_south, a, b)
         odd[pl.ds(c * GROUP, GROUP)] = jnp.where(to_south, b, a)
 
 
-def weights_kernel(w1, w2, w3, w4, biases, t1, t2, t3, t4):
+def weights_kernel(w1, w2, w3, w4, bias1, bias2, bias3, t1, t2, t3, t4):
     hidden = w2.shape[2]
     per = LANES // hidden
     lane = iota((hidden, LANES), 1)
-    fields = w1.shape[1] // GROUP
+    fields = w1.shape[2]
     rows = fields * GROUP
     out_lon = iota((rows, LANES), 1) // hidden
     in_lon = iota((rows, LANES), 0) % GROUP
     bias_row = iota((GROUP, LANES), 0)
 
-    def bias_rows(layer, tile):
-        part = 0.5 * biases[pl.ds(layer, 1), :]
+    def bias_rows(layer):
+        part = 0.5 * jnp.concatenate([(bias1, bias2, bias3)[layer][...]] * per, axis=1)
         b1 = part.astype(bf16).astype(f32)
         b2 = (part - b1).astype(bf16).astype(f32)
         b3 = part - b1 - b2
@@ -207,15 +207,23 @@
     pad = jnp.zeros((LANES - rows - 3 * GROUP, LANES), f32)
     empty = jnp.zeros((3 * GROUP, LANES), f32)
     for dj in range(3):
+        taps = []
+        for di in range(3):
+            cell = 0.5 * jnp.concatenate([w1[dj, di].astype(f32)] * per, axis=1)
+            taps.append(
+                jnp.concatenate(
+                    [jnp.broadcast_to(cell[c : c + 1], (GROUP, LANES)) for c in range(fields)], axis=0
+                )
+            )
         for half in range(2):
             for tile in range(2):
                 total = jnp.zeros((rows, LANES), f32)
                 for di in range(3):
                     hit = in_lon + GROUP * half == out_lon + per * tile + di + RIM
-                    total = jnp.where(hit, 0.5 * w1[dj * 3 + di].astype(f32), total)
+                    total = jnp.where(hit, taps[di], total)
                 extra = empty
                 if dj == 1 and half == 0:
-                    extra = jnp.concatenate([sea_rows(5, tile), bias_rows(0, tile)], axis=0)
+                    extra = jnp.concatenate([sea_rows(5, tile), bias_rows(0)], axis=0)
                 block = jnp.concatenate([total, extra, pad], axis=0)
                 t1[pl.ds((dj * 2 + half) * LANES, LANES), pl.ds(tile * LANES, LANES)] = block.astype(bf16)
 
@@ -242,7 +250,7 @@
                 [
                     jnp.zeros((2 * GROUP, LANES), f32),
                     sea_rows(6 + layer, tile),
-                    bias_rows(1 + layer, tile),
+                    bias_rows(1 + layer),
                     jnp.zeros((3 * GROUP, LANES), f32),
                 ],
                 axis=0,
@@ -271,14 +279,12 @@
 
 def main_kernel(
     sizes,
-    place,
     bias_last,
     own,
     u,
     v,
     h,
     sea,
-    coriolis,
     left,
     right,
     even_rim,
@@ -298,6 +304,8 @@
     force,
     turned,
     gaps,
+    results,
+    done,
 ):
     members, noises, levels = sizes
     fields = noises + 3 * levels
@@ -307,9 +315,10 @@
     blocks = (lats + GAP) // chunks
     rows = blocks * SUB
     gap_k = lats - (chunks - 1) * blocks
-    top = place[0] == 1
-    is_odd = place[1] == 1
-    bottom = place[2] == 1
+    lat_index, lat_count = lax.axis_index("lat"), lax.axis_size("lat")
+    top = lat_index == lat_count - 1
+    is_odd = lat_index % 2 == 1
+    bottom = lat_index == 0
     strip = odd_rim[...]
     south = jnp.where(is_odd, even_rim[...], jnp.where(bottom, 0.0, strip))
 
@@ -461,7 +470,9 @@
         force[pl.ds(r, step), :] = dot(jnp.concatenate(parts, axis=1), t4[...])
 
     ocean = sea[...].astype(f32)
-    turn = coriolis[...]
+    at_lat = iota((lons, lats), 1).astype(f32)
+    lat_rows = (lat_index * lats).astype(f32) + at_lat
+    turn = CORIOLIS * (2.0 * (lat_rows + 0.5) / (lats * lat_count) - 1.0)
     at_first = iota((lons, lats), 0) == 0
     at_last = iota((lons, lats), 0) == lons - 1
     at_south = iota((lons, lats), 1) == 0
@@ -514,10 +525,15 @@
             lap_v = av[1] + av[0] + av[3] + av[2] - 4.0 * cv
             dx = 0.5 * (pressure[1] - pressure[0])
             dy = 0.5 * (pressure[3] - pressure[2])
-            new_u[m, level] = ocean * (cu + TIME_STEP * (turn * cv - dx + push_u + VISCOSITY * lap_u))
-            new_v[m, level] = ocean * (cv + TIME_STEP * (-turn * cu - dy + push_v + VISCOSITY * lap_v))
+            results[0, m, level] = ocean * (cu + TIME_STEP * (turn * cv - dx + push_u + VISCOSITY * lap_u))
+            results[1, m, level] = ocean * (cv + TIME_STEP * (-turn * cu - dy + push_v + VISCOSITY * lap_v))
             flow = 0.5 * (ah[1] * au[1] - ah[0] * au[0]) + 0.5 * (ah[3] * av[3] - ah[2] * av[2])
-            new_h[m, level] = ch - TIME_STEP * flow
+            results[2, m, level] = ch - TIME_STEP * flow
+        for n, out in enumerate((new_u, new_v, new_h)):
+            pltpu.make_async_copy(results.at[n, m], out.at[m], done.at[n, m]).start()
+    for m in range(members):
+        for n, out in enumerate((new_u, new_v, new_h)):
+            pltpu.make_async_copy(results.at[n, m], out.at[m], done.at[n, m]).wait()
 
 
 def body(
@@ -547,7 +563,6 @@
     assert lats % LANES == 0 and SUB % members == 0 and (lats + GAP) % (SUB // members) == 0
     lon_count, lat_count = lax.axis_size("lon"), lax.axis_size("lat")
     assert lon_count % 2 == 0 and lat_count % 2 == 0
-    lat_index = lax.axis_index("lat")
     state = (noise, velocity_u, velocity_v, thickness, land_sea)
     whole = pl.BlockSpec(memory_space=pltpu.VMEM)
 
@@ -577,19 +592,20 @@
         in_specs=[whole] * 5,
         out_specs=[whole] * 3,
         scratch_shapes=[pltpu.VMEM((groups - 2, rows, LANES), f32)],
+        compiler_params=pltpu.CompilerParams(vmem_limit_bytes=8 * 2**20),
         cost_estimate=pl.CostEstimate(flops=10**7, bytes_accessed=10**7, transcendentals=0),
         name="own_cells",
     )(*state)
     last = lat_count - 1
-    place = jnp.stack([lat_index == last, lat_index % 2 == 1, lat_index == 0]).astype(jnp.int32)
     smem = pl.BlockSpec(memory_space=pltpu.SMEM)
     to_even, to_odd = pl.pallas_call(
         functools.partial(join_kernel, sizes),
         out_shape=[message] * 2,
-        in_specs=[smem] + [whole] * 5,
+        in_specs=[whole] * 5,
         out_specs=[whole] * 2,
+        compiler_params=pltpu.CompilerParams(vmem_limit_bytes=4 * 2**20),
         name="join_rims",
-    )(place, land_sea, left, right, own_head, own_tail)
+    )(land_sea, left, right, own_head, own_tail)
     even_rim = lax.ppermute(to_even, "lat", [(i, i ^ 1) for i in range(lat_count)])
     pairs = []
     for t in range(lon_count):
@@ -598,9 +614,6 @@
         pairs += [(at, (t ^ 1) * lat_count), (at + last, (lon_count - 1 - t) * lat_count + last)]
     odd_rim = lax.ppermute(to_odd, ("lon", "lat"), pairs)
 
-    taps = conv_first.transpose(3, 2, 1, 0)[:, :, :, None, None, :]
-    taps = jnp.broadcast_to(taps, (3, 3, fields, GROUP, LANES // hidden, hidden)).reshape(9, -1, LANES)
-    biases = jnp.tile(jnp.stack([bias_first, bias_second, bias_third]), (1, LANES // hidden))
     deep = -(-(lons + 2) * hidden // LANES) * LANES
     t1, t2, t3, t4 = pl.pallas_call(
         weights_kernel,
@@ -610,28 +623,29 @@
             pltpu.VMEM((8 * LANES, 2 * LANES), bf16),
             pltpu.VMEM((3 * deep, LANES), bf16),
         ],
-        in_specs=[whole] * 5,
+        in_specs=[whole] * 7,
         out_specs=[whole] * 4,
+        compiler_params=pltpu.CompilerParams(vmem_limit_bytes=8 * 2**20),
         cost_estimate=pl.CostEstimate(flops=10**7, bytes_accessed=3 * 10**6, transcendentals=0),
         name="banded_matrices",
     )(
-        taps,
+        conv_first.transpose(3, 2, 1, 0),
         conv_second.transpose(2, 3, 0, 1),
         conv_third.transpose(2, 3, 0, 1),
         conv_last.transpose(2, 3, 0, 1),
-        biases,
+        bias_first[None],
+        bias_second[None],
+        bias_third[None],
     )
 
-    lat_rows = (lat_index * lats + jnp.arange(lats)).astype(f32)
-    coriolis = CORIOLIS * (2.0 * (lat_rows + 0.5) / (lats * lat_count) - 1.0)
     padded = rows + 2 * SUB
     tiles = 2 * (groups - 1) + 1
     out = jax.ShapeDtypeStruct(velocity_u.shape, f32)
     return pl.pallas_call(
         functools.partial(main_kernel, sizes),
         out_shape=[out] * 3,
-        in_specs=[smem, smem] + [whole] * 15,
-        out_specs=[whole] * 3,
+        in_specs=[smem] + [whole] * 14,
+        out_specs=[pl.BlockSpec(memory_space=pltpu.HBM)] * 3,
         scratch_shapes=[
             pltpu.VMEM((2, rows, LANES), f32),
             pltpu.VMEM((groups, padded, LANES), bf16),
@@ -640,16 +654,16 @@
             pltpu.VMEM((rows, LANES), f32),
             pltpu.VMEM((4, LANES, LANES), f32),
             pltpu.VMEM((groups, 4 * RIM * SUB, LANES), f32),
+            pltpu.VMEM((3, *velocity_u.shape), f32),
+            pltpu.SemaphoreType.DMA((3, members)),
         ],
         compiler_params=pltpu.CompilerParams(vmem_limit_bytes=32 * 2**20),
         cost_estimate=pl.CostEstimate(flops=2 * 10**10, bytes_accessed=10**7, transcendentals=4 * 10**6),
         name="network_and_step",
     )(
-        place,
         bias_last,
         own,
         *state[1:],
-        coriolis[None],
         left,
         right,
         even_rim,

time: 38.3 us -> 31.6 us (0.83)
  the two profiles are of different devices: /device:TPU:12 before, /device:TPU:20 now
where the time goes in v2:
time: 31.6 us; the launch traced here: 31.3 us
  Pallas kernels  20.3 us (64%)
  waiting for transfers between devices  4.97 us (16%)
  starting transfers between devices  4.33 us (14%)
  local copies, waits for them, and re-layouts  0.82 us (3%)
  between operations  0.82 us (3%)
    pallas_call x1, Pallas kernels, body(): pl.pallas_call(functools.partial(main_kernel, sizes), out_shape=[out] * 3...  16.5 us
    ppermute x1, starting transfers between devices, body(): right = lax.ppermute(head, 'lon', [(b, a) for a, b in ring])  2.63 us
    ppermute x1, waiting for transfers between devices, body(): left = lax.ppermute(tail, 'lon', ring)  2.01 us
    ppermute x1, starting transfers between devices, body(): lax.ppermute(to_even, 'lat', [(i, i ^ 1) for i in range(lat_count)])  1.64 us
    ppermute x1, waiting for transfers between devices, body(): odd_rim = lax.ppermute(to_odd, ('lon', 'lat'), pairs)  1.58 us
    ppermute x1, waiting for transfers between devices, body(): lax.ppermute(to_even, 'lat', [(i, i ^ 1) for i in range(lat_count)])  1.39 us
    pallas_call x1, Pallas kernels, body(): pl.pallas_call(functools.partial(own_kernel, sizes), out_shape=[pltpu.VME...  1.32 us
    pallas_call x1, Pallas kernels, body(): pl.pallas_call(functools.partial(pack_lon_kernel, sizes), out_shape=[pltp...  1.26 us
  transfers between devices with their start and end apart: 4, of which 3 were waited for; matrix products, arithmetic and copies ran while one was open for 0% of the time, Pallas kernels for 8%

profile of v2, /device:TPU:20, one launch (start us, length us, event | category | flops | bytes accessed | tf_op | source)
XLA Modules:
  0.0 31.3 jit_solution(1477090294471315021)
XLA Ops:
  0.6 0.0 copy-start.3
  0.6 0.0 copy-start.2
  0.7 0.0 copy-start.1
  0.7 0.0 copy-start
  0.7 0.0 copy-start.11
  0.7 0.0 copy-start.10
  0.7 0.0 copy-start.9
  0.7 0.0 copy-start.5
  0.7 1.3 %pack_lon.1 = (f32[168,256]{1,0:T(8,128)S(1)}, f32[168,256]{1,0:T(8,128)S(1)}) custom-call(bf16[4,4,32,256]{3,2,1,0:T(8,128)(2,1)} %noise.3, f32[4,2,32,256]{3,2,1,0:T(8,128)} %u.5, f32[4,2,32,256]{3,2,1,0:T(8,128)} %v.5, f32[4,2,32,256]{3,2,1,0:T(8,128)} %h.5, s32[32,256]{1,0:T(8,128)} %sea.7), custom_call_target="tpu_custom_call" | custom-call | tf_op jit(solution)/shard_map/pack_lon/pallas_call | solution.py:570
  2.0 0.0 copy-start.12
  2.0 0.1 collective-permute-start
  2.1 2.6 %collective-permute-start.1 = (f32[168,256]{1,0:T(8,128)S(1)}, f32[168,256]{1,0:T(8,128)S(1)}, u32[]{:S(2)}, u32[]{:S(2)}) collective-permute-start(f32[168,256]{1,0:T(8,128)S(1)} %get-tuple-element.16), channel_id=1, source_target_pairs={{4,0},{8,4},{12,8},{16,12},{20,16},{24,20},{28,24},{0,28},{5,1},{9... | collective-permute-start | bytes 516104 | tf_op jit(solution)/shard_map/ppermute | solution.py:585
  4.7 0.0 copy-done.3
  4.7 0.0 copy-done.2
  4.7 0.0 copy-done.1
  4.7 0.0 copy-done
  4.7 0.0 copy-start.4
  4.7 0.7 %copy-done.4 = s32[32,256]{1,0:T(8,128)S(1)} copy-done((s32[32,256]{1,0:T(8,128)S(1)}, s32[32,256]{1,0:T(8,128)}, u32[]{:S(2)}) %copy-start.4) | copy-done | bytes 32792
  5.5 1.3 %own_cells.1 = (bf16[4,1152,128]{2,1,0:T(8,128)(2,1)S(1)}, f32[96,128]{1,0:T(8,128)S(1)}, f32[96,128]{1,0:T(8,128)S(1)}) custom-call(bf16[4,4,32,256]{3,2,1,0:T(8,128)(2,1)S(1)} %copy-done, f32[4,2,32,256]{3,2,1,0:T(8,128)S(1)} %copy-done.1, f32[4,2,32,256]{3,2,1,0:T(8,128)S(1)} %copy-done.2, f32[4,2,32,256]{3,2,1,0:T(8,128)S(1)} %copy-done.3, ...), custom_call_target="tpu_custom_call" | custom-call | flops 10000000 | bytes 10000000 | tf_op jit(solution)/shard_map/own_cells/pallas_call | solution.py:589
  6.8 2.0 %collective-permute-done.left = f32[168,256]{1,0:T(8,128)S(1)} collective-permute-done((f32[168,256]{1,0:T(8,128)S(1)}, f32[168,256]{1,0:T(8,128)S(1)}, u32[]{:S(2)}, u32[]{:S(2)}) %collective-permute-start) | collective-permute-done | bytes 172064 | tf_op jit(solution)/shard_map/ppermute | solution.py:584
  8.8 0.0 collective-permute-done.1.right
  8.8 0.2 join_rims.1
  9.1 1.6 %collective-permute-start.2 = (f32[96,128]{1,0:T(8,128)S(1)}, f32[96,128]{1,0:T(8,128)S(1)}, u32[]{:S(2)}, u32[]{:S(2)}) collective-permute-start(f32[96,128]{1,0:T(8,128)S(1)} %get-tuple-element.19), channel_id=1, source_target_pairs={{0,1},{1,0},{2,3},{3,2},{4,5},{5,4},{6,7},{7,6},{8,9},{9,8},{10,11... | collective-permute-start | bytes 147464 | tf_op jit(solution)/shard_map/ppermute | solution.py:609
  10.7 0.0 collective-permute-start.3
  10.7 0.0 copy-done.13
  10.7 0.0 copy-done.11
  10.7 0.0 copy-done.10
  10.8 0.0 copy-done.9
  10.8 1.0 %banded_matrices.1 = (bf16[768,256]{1,0:T(8,128)(2,1)S(1)}, bf16[1024,256]{1,0:T(8,128)(2,1)S(1)}, bf16[1024,256]{1,0:T(8,128)(2,1)S(1)}, bf16[3456,128]{1,0:T(8,128)(2,1)S(1)}) custom-call(bf16[3,3,10,32]{3,2,1,0:T(8,128)(2,1)S(1)} %bitcast.9, bf16[3,3,32,32]{3,2,1,0:T(8,128)(2,1)S(1)} %bitcast.10, bf16[3,3,32,32]{3,2,1,0:T(8,128)(2,1)S(1)} %bitcast.11, ...), custom_call_target="tpu_custom_call" | custom-call | flops 10000000 | bytes 3000000 | tf_op jit(solution)/shard_map/banded_matrices/pallas_call | solution.py:618
  11.8 1.4 %collective-permute-done.2.even_rim = f32[96,128]{1,0:T(8,128)S(1)} collective-permute-done((f32[96,128]{1,0:T(8,128)S(1)}, f32[96,128]{1,0:T(8,128)S(1)}, u32[]{:S(2)}, u32[]{:S(2)}) %collective-permute-start.2) | collective-permute-done | bytes 49184 | tf_op jit(solution)/shard_map/ppermute | solution.py:609
  13.2 1.6 %collective-permute-done.3.odd_rim = f32[96,128]{1,0:T(8,128)S(1)} collective-permute-done((f32[96,128]{1,0:T(8,128)S(1)}, f32[96,128]{1,0:T(8,128)S(1)}, u32[]{:S(2)}, u32[]{:S(2)}) %collective-permute-start.3) | collective-permute-done | bytes 49184 | tf_op jit(solution)/shard_map/ppermute | solution.py:615
  14.8 16.5 %network_and_step.1 = (f32[4,2,32,256]{3,2,1,0:T(8,128)}, f32[4,2,32,256]{3,2,1,0:T(8,128)}, f32[4,2,32,256]{3,2,1,0:T(8,128)}) custom-call(f32[4]{0:T(128)S(1)} %copy-done.12, bf16[4,1152,128]{2,1,0:T(8,128)(2,1)S(1)} %get-tuple-element.14.own, f32[4,2,32,256]{3,2,1,0:T(8,128)S(1)} %copy-done.1, f32[4,2,32,256]{3,2,1,0:T(8,128)S(1)} %copy-done.2, ...), custom_call_target="tpu_custom_call" | custom-call | flops 20000000000 | bytes 10000000 | tf_op jit(solution)/shard_map/network_and_step/pallas_call | solution.py:644
  (10 shorter events, 0.0 us)
Async XLA Ops:
  0.6 4.1 %copy-start.3 = (f32[4,2,32,256]{3,2,1,0:T(8,128)S(1)}, f32[4,2,32,256]{3,2,1,0:T(8,128)}, u32[]{:S(2)}) copy-start(f32[4,2,32,256]{3,2,1,0:T(8,128)} %h.5) | copy-start | bytes 786436
  0.6 4.1 %copy-start.2 = (f32[4,2,32,256]{3,2,1,0:T(8,128)S(1)}, f32[4,2,32,256]{3,2,1,0:T(8,128)}, u32[]{:S(2)}) copy-start(f32[4,2,32,256]{3,2,1,0:T(8,128)} %v.5) | copy-start | bytes 786436
  0.7 4.0 %copy-start.1 = (f32[4,2,32,256]{3,2,1,0:T(8,128)S(1)}, f32[4,2,32,256]{3,2,1,0:T(8,128)}, u32[]{:S(2)}) copy-start(f32[4,2,32,256]{3,2,1,0:T(8,128)} %u.5) | copy-start | bytes 786436
  0.7 4.0 %copy-start = (bf16[4,4,32,256]{3,2,1,0:T(8,128)(2,1)S(1)}, bf16[4,4,32,256]{3,2,1,0:T(8,128)(2,1)}, u32[]{:S(2)}) copy-start(bf16[4,4,32,256]{3,2,1,0:T(8,128)(2,1)} %noise.3) | copy-start | bytes 786436
  0.7 10.1 %copy-start.11 = (f32[32]{0:T(128)S(1)}, f32[32]{0:T(128)}, u32[]{:S(2)}) copy-start(f32[32]{0:T(128)} %param.23) | copy-start | bytes 388
  0.7 10.1 %copy-start.10 = (f32[32]{0:T(128)S(1)}, f32[32]{0:T(128)}, u32[]{:S(2)}) copy-start(f32[32]{0:T(128)} %param.21) | copy-start | bytes 388
  0.7 10.1 %copy-start.9 = (f32[32]{0:T(128)S(1)}, f32[32]{0:T(128)}, u32[]{:S(2)}) copy-start(f32[32]{0:T(128)} %param.19) | copy-start | bytes 388
  0.7 14.1 %copy-start.5 = (s32[32,256]{1,0:T(8,128)S(1)}, s32[32,256]{1,0:T(8,128)}, u32[]{:S(2)}) copy-start(s32[32,256]{1,0:T(8,128)} %sea.7) | copy-start | bytes 98308
  2.0 12.8 %copy-start.12 = (f32[4]{0:T(128)S(1)}, f32[4]{0:T(128)}, u32[]{:S(2)}) copy-start(f32[4]{0:T(128)} %bias_last.1) | copy-start | bytes 52
  2.0 6.8 %collective-permute-start = (f32[168,256]{1,0:T(8,128)S(1)}, f32[168,256]{1,0:T(8,128)S(1)}, u32[]{:S(2)}, u32[]{:S(2)}) collective-permute-start(f32[168,256]{1,0:T(8,128)S(1)} %get-tuple-element.15), channel_id=1, source_target_pairs={{0,4},{4,8},{8,12},{12,16},{16,20},{20,24},{24,28},{28,0},{1,5},{5... | collective-permute-start | bytes 516104 | tf_op jit(solution)/shard_map/ppermute | solution.py:584
  2.1 6.8 %collective-permute-start.1 = (f32[168,256]{1,0:T(8,128)S(1)}, f32[168,256]{1,0:T(8,128)S(1)}, u32[]{:S(2)}, u32[]{:S(2)}) collective-permute-start(f32[168,256]{1,0:T(8,128)S(1)} %get-tuple-element.16), channel_id=1, source_target_pairs={{4,0},{8,4},{12,8},{16,12},{20,16},{24,20},{28,24},{0,28},{5,1},{9... | collective-permute-start | bytes 516104 | tf_op jit(solution)/shard_map/ppermute | solution.py:585
  4.7 0.8 %copy-start.4 = (s32[32,256]{1,0:T(8,128)S(1)}, s32[32,256]{1,0:T(8,128)}, u32[]{:S(2)}) copy-start(s32[32,256]{1,0:T(8,128)} %sea.7) | copy-start | bytes 98308
  5.5 5.3 %copy-start.13 = (bf16[32,10,3,3]{0,3,2,1:T(4,128)(2,1)S(1)}, bf16[32,10,3,3]{0,3,2,1:T(4,128)(2,1)}, u32[]{:S(2)}) copy-start(bf16[32,10,3,3]{0,3,2,1:T(4,128)(2,1)} %param.18) | copy-start | bytes 17284
  5.5 5.3 %copy-start.6 = (bf16[32,32,3,3]{1,0,3,2:T(8,128)(2,1)S(1)}, bf16[32,32,3,3]{1,0,3,2:T(8,128)(2,1)}, u32[]{:S(2)}) copy-start(bf16[32,32,3,3]{1,0,3,2:T(8,128)(2,1)} %param.20) | copy-start | bytes 55300
  5.5 5.3 %copy-start.7 = (bf16[32,32,3,3]{1,0,3,2:T(8,128)(2,1)S(1)}, bf16[32,32,3,3]{1,0,3,2:T(8,128)(2,1)}, u32[]{:S(2)}) copy-start(bf16[32,32,3,3]{1,0,3,2:T(8,128)(2,1)} %param.22) | copy-start | bytes 55300
  5.5 5.3 %copy-start.8 = (bf16[4,32,3,3]{1,0,3,2:T(4,128)(2,1)S(1)}, bf16[4,32,3,3]{1,0,3,2:T(4,128)(2,1)}, u32[]{:S(2)}) copy-start(bf16[4,32,3,3]{1,0,3,2:T(4,128)(2,1)} %param.24) | copy-start | bytes 6916
  9.1 4.2 %collective-permute-start.2 = (f32[96,128]{1,0:T(8,128)S(1)}, f32[96,128]{1,0:T(8,128)S(1)}, u32[]{:S(2)}, u32[]{:S(2)}) collective-permute-start(f32[96,128]{1,0:T(8,128)S(1)} %get-tuple-element.19), channel_id=1, source_target_pairs={{0,1},{1,0},{2,3},{3,2},{4,5},{5,4},{6,7},{7,6},{8,9},{9,8},{10,11... | collective-permute-start | bytes 147464 | tf_op jit(solution)/shard_map/ppermute | solution.py:609
  10.7 4.1 %collective-permute-start.3 = (f32[96,128]{1,0:T(8,128)S(1)}, f32[96,128]{1,0:T(8,128)S(1)}, u32[]{:S(2)}, u32[]{:S(2)}) collective-permute-start(f32[96,128]{1,0:T(8,128)S(1)} %get-tuple-element.20.own_tail), channel_id=1, source_target_pairs={{1,2},{2,1},{0,4},{3,31},{5,6},{6,5},{4,0},{7,27},{9,10},{10,9},{8... | collective-permute-start | bytes 147464 | tf_op jit(solution)/shard_map/ppermute | solution.py:615

commit v3 on v2

--- a/solution.py
+++ b/solution.py
@@ -434,19 +434,19 @@
 
     spread = groups - 1
 
-    def layer_first(b, carry):
+    def layer_first(b):
         for n in range(rows // step):
             r = n * step
             parts = [first[b + e, pl.ds(r + SUB * d, step), :] for d in range(3) for e in range(2)]
             out = activate(dot(jnp.concatenate(parts, axis=1), t1[...]))
             odd[2 * b, pl.ds(SUB + r, step), :] = out[:, :LANES]
             odd[2 * b + 1, pl.ds(SUB + r, step), :] = out[:, LANES:]
-        return carry
-
-    lax.fori_loop(0, spread, layer_first, 0)
+
+    for b in range(spread):
+        layer_first(b)
     finish(odd, lons + 6)
 
-    def layer(x, y, t, b, carry):
+    def layer(x, y, t, b):
         for n in range(rows // step):
             r = n * step
             parts = [x[2 * b + e, pl.ds(r + SUB * d, step), :] for d in range(3) for e in range(2)]
@@ -456,11 +456,12 @@
             out = activate(dot(jnp.concatenate(parts, axis=1), t[...]))
             y[2 * b, pl.ds(SUB + r, step), :] = out[:, :LANES]
             y[2 * b + 1, pl.ds(SUB + r, step), :] = out[:, LANES:]
-        return carry
-
-    lax.fori_loop(0, spread, functools.partial(layer, odd, even, t2), 0)
+
+    for b in range(spread):
+        layer(odd, even, t2, b)
     finish(even, lons + 4)
-    lax.fori_loop(0, spread, functools.partial(layer, even, odd, t3), 0)
+    for b in range(spread):
+        layer(even, odd, t3, b)
     finish(odd, lons + 2)
 
     depth = t4.shape[0] // 3 // LANES

time: 31.6 us -> 30.8 us (0.975)
  Pallas kernels: 20.3 us -> 19.5 us
    pallas_call x1, Pallas kernels: 16.5 us -> 15.6 us  [body(): pl.pallas_call(functools.partial(main_kernel, sizes), out_shape=[out] * 3...]
where the time goes in v3:
time: 30.8 us; the launch traced here: 30.6 us
  Pallas kernels  19.5 us (63%)
  waiting for transfers between devices  4.97 us (16%)
  starting transfers between devices  4.33 us (14%)
  between operations  0.98 us (3%)
  local copies, waits for them, and re-layouts  0.82 us (3%)
    pallas_call x1, Pallas kernels, body(): pl.pallas_call(functools.partial(main_kernel, sizes), out_shape=[out] * 3...  15.6 us
    ppermute x1, starting transfers between devices, body(): right = lax.ppermute(head, 'lon', [(b, a) for a, b in ring])  2.63 us
    ppermute x1, waiting for transfers between devices, body(): left = lax.ppermute(tail, 'lon', ring)  2.01 us
    ppermute x1, starting transfers between devices, body(): lax.ppermute(to_even, 'lat', [(i, i ^ 1) for i in range(lat_count)])  1.64 us
    ppermute x1, waiting for transfers between devices, body(): odd_rim = lax.ppermute(to_odd, ('lon', 'lat'), pairs)  1.58 us
    ppermute x1, waiting for transfers between devices, body(): lax.ppermute(to_even, 'lat', [(i, i ^ 1) for i in range(lat_count)])  1.39 us
    pallas_call x1, Pallas kernels, body(): pl.pallas_call(functools.partial(own_kernel, sizes), out_shape=[pltpu.VME...  1.32 us
    pallas_call x1, Pallas kernels, body(): pl.pallas_call(functools.partial(pack_lon_kernel, sizes), out_shape=[pltp...  1.26 us
  transfers between devices with their start and end apart: 4, of which 3 were waited for; matrix products, arithmetic and copies ran while one was open for 0% of the time, Pallas kernels for 8%

profile of v3, /device:TPU:20, one launch (start us, length us, event | category | flops | bytes accessed | tf_op | source)
XLA Modules:
  0.0 30.6 jit_solution(8684857974289382692)
XLA Ops:
  0.6 0.0 copy-start.3
  0.6 0.0 copy-start.2
  0.7 0.0 copy-start.1
  0.7 0.0 copy-start
  0.7 0.0 copy-start.11
  0.7 0.0 copy-start.10
  0.7 0.0 copy-start.9
  0.7 0.0 copy-start.5
  0.7 1.3 %pack_lon.1 = (f32[168,256]{1,0:T(8,128)S(1)}, f32[168,256]{1,0:T(8,128)S(1)}) custom-call(bf16[4,4,32,256]{3,2,1,0:T(8,128)(2,1)} %noise.3, f32[4,2,32,256]{3,2,1,0:T(8,128)} %u.5, f32[4,2,32,256]{3,2,1,0:T(8,128)} %v.5, f32[4,2,32,256]{3,2,1,0:T(8,128)} %h.5, s32[32,256]{1,0:T(8,128)} %sea.7), custom_call_target="tpu_custom_call" | custom-call | tf_op jit(solution)/shard_map/pack_lon/pallas_call | solution.py:571
  2.0 0.0 copy-start.12
  2.0 0.1 collective-permute-start
  2.1 2.6 %collective-permute-start.1 = (f32[168,256]{1,0:T(8,128)S(1)}, f32[168,256]{1,0:T(8,128)S(1)}, u32[]{:S(2)}, u32[]{:S(2)}) collective-permute-start(f32[168,256]{1,0:T(8,128)S(1)} %get-tuple-element.16), channel_id=1, source_target_pairs={{4,0},{8,4},{12,8},{16,12},{20,16},{24,20},{28,24},{0,28},{5,1},{9... | collective-permute-start | bytes 516104 | tf_op jit(solution)/shard_map/ppermute | solution.py:586
  4.7 0.0 copy-done.3
  4.7 0.0 copy-done.2
  4.7 0.0 copy-done.1
  4.7 0.0 copy-done
  4.7 0.0 copy-start.4
  4.7 0.7 %copy-done.4 = s32[32,256]{1,0:T(8,128)S(1)} copy-done((s32[32,256]{1,0:T(8,128)S(1)}, s32[32,256]{1,0:T(8,128)}, u32[]{:S(2)}) %copy-start.4) | copy-done | bytes 32792
  5.5 1.3 %own_cells.1 = (bf16[4,1152,128]{2,1,0:T(8,128)(2,1)S(1)}, f32[96,128]{1,0:T(8,128)S(1)}, f32[96,128]{1,0:T(8,128)S(1)}) custom-call(bf16[4,4,32,256]{3,2,1,0:T(8,128)(2,1)S(1)} %copy-done, f32[4,2,32,256]{3,2,1,0:T(8,128)S(1)} %copy-done.1, f32[4,2,32,256]{3,2,1,0:T(8,128)S(1)} %copy-done.2, f32[4,2,32,256]{3,2,1,0:T(8,128)S(1)} %copy-done.3, ...), custom_call_target="tpu_custom_call" | custom-call | flops 10000000 | bytes 10000000 | tf_op jit(solution)/shard_map/own_cells/pallas_call | solution.py:590
  6.8 2.0 %collective-permute-done.left = f32[168,256]{1,0:T(8,128)S(1)} collective-permute-done((f32[168,256]{1,0:T(8,128)S(1)}, f32[168,256]{1,0:T(8,128)S(1)}, u32[]{:S(2)}, u32[]{:S(2)}) %collective-permute-start) | collective-permute-done | bytes 172064 | tf_op jit(solution)/shard_map/ppermute | solution.py:585
  8.8 0.0 collective-permute-done.1.right
  8.8 0.2 join_rims.1
  9.1 1.6 %collective-permute-start.2 = (f32[96,128]{1,0:T(8,128)S(1)}, f32[96,128]{1,0:T(8,128)S(1)}, u32[]{:S(2)}, u32[]{:S(2)}) collective-permute-start(f32[96,128]{1,0:T(8,128)S(1)} %get-tuple-element.19), channel_id=1, source_target_pairs={{0,1},{1,0},{2,3},{3,2},{4,5},{5,4},{6,7},{7,6},{8,9},{9,8},{10,11... | collective-permute-start | bytes 147464 | tf_op jit(solution)/shard_map/ppermute | solution.py:610
  10.7 0.0 collective-permute-start.3
  10.7 0.0 copy-done.13
  10.7 0.0 copy-done.11
  10.7 0.0 copy-done.10
  10.8 1.0 %banded_matrices.1 = (bf16[768,256]{1,0:T(8,128)(2,1)S(1)}, bf16[1024,256]{1,0:T(8,128)(2,1)S(1)}, bf16[1024,256]{1,0:T(8,128)(2,1)S(1)}, bf16[3456,128]{1,0:T(8,128)(2,1)S(1)}) custom-call(bf16[3,3,10,32]{3,2,1,0:T(8,128)(2,1)S(1)} %bitcast.9, bf16[3,3,32,32]{3,2,1,0:T(8,128)(2,1)S(1)} %bitcast.10, bf16[3,3,32,32]{3,2,1,0:T(8,128)(2,1)S(1)} %bitcast.11, ...), custom_call_target="tpu_custom_call" | custom-call | flops 10000000 | bytes 3000000 | tf_op jit(solution)/shard_map/banded_matrices/pallas_call | solution.py:619
  11.8 1.4 %collective-permute-done.2.even_rim = f32[96,128]{1,0:T(8,128)S(1)} collective-permute-done((f32[96,128]{1,0:T(8,128)S(1)}, f32[96,128]{1,0:T(8,128)S(1)}, u32[]{:S(2)}, u32[]{:S(2)}) %collective-permute-start.2) | collective-permute-done | bytes 49184 | tf_op jit(solution)/shard_map/ppermute | solution.py:610
  13.2 1.6 %collective-permute-done.3.odd_rim = f32[96,128]{1,0:T(8,128)S(1)} collective-permute-done((f32[96,128]{1,0:T(8,128)S(1)}, f32[96,128]{1,0:T(8,128)S(1)}, u32[]{:S(2)}, u32[]{:S(2)}) %collective-permute-start.3) | collective-permute-done | bytes 49184 | tf_op jit(solution)/shard_map/ppermute | solution.py:616
  14.8 0.0 copy-done.12
  14.8 15.6 %network_and_step.1 = (f32[4,2,32,256]{3,2,1,0:T(8,128)}, f32[4,2,32,256]{3,2,1,0:T(8,128)}, f32[4,2,32,256]{3,2,1,0:T(8,128)}) custom-call(f32[4]{0:T(128)S(1)} %copy-done.12, bf16[4,1152,128]{2,1,0:T(8,128)(2,1)S(1)} %get-tuple-element.14.own, f32[4,2,32,256]{3,2,1,0:T(8,128)S(1)} %copy-done.1, f32[4,2,32,256]{3,2,1,0:T(8,128)S(1)} %copy-done.2, ...), custom_call_target="tpu_custom_call" | custom-call | flops 20000000000 | bytes 10000000 | tf_op jit(solution)/shard_map/network_and_step/pallas_call | solution.py:645
  (10 shorter events, 0.0 us)
Async XLA Ops:
  0.6 4.1 %copy-start.3 = (f32[4,2,32,256]{3,2,1,0:T(8,128)S(1)}, f32[4,2,32,256]{3,2,1,0:T(8,128)}, u32[]{:S(2)}) copy-start(f32[4,2,32,256]{3,2,1,0:T(8,128)} %h.5) | copy-start | bytes 786436
  0.6 4.1 %copy-start.2 = (f32[4,2,32,256]{3,2,1,0:T(8,128)S(1)}, f32[4,2,32,256]{3,2,1,0:T(8,128)}, u32[]{:S(2)}) copy-start(f32[4,2,32,256]{3,2,1,0:T(8,128)} %v.5) | copy-start | bytes 786436
  0.7 4.0 %copy-start.1 = (f32[4,2,32,256]{3,2,1,0:T(8,128)S(1)}, f32[4,2,32,256]{3,2,1,0:T(8,128)}, u32[]{:S(2)}) copy-start(f32[4,2,32,256]{3,2,1,0:T(8,128)} %u.5) | copy-start | bytes 786436
  0.7 4.0 %copy-start = (bf16[4,4,32,256]{3,2,1,0:T(8,128)(2,1)S(1)}, bf16[4,4,32,256]{3,2,1,0:T(8,128)(2,1)}, u32[]{:S(2)}) copy-start(bf16[4,4,32,256]{3,2,1,0:T(8,128)(2,1)} %noise.3) | copy-start | bytes 786436
  0.7 10.1 %copy-start.11 = (f32[32]{0:T(128)S(1)}, f32[32]{0:T(128)}, u32[]{:S(2)}) copy-start(f32[32]{0:T(128)} %param.23) | copy-start | bytes 388
  0.7 10.1 %copy-start.10 = (f32[32]{0:T(128)S(1)}, f32[32]{0:T(128)}, u32[]{:S(2)}) copy-start(f32[32]{0:T(128)} %param.21) | copy-start | bytes 388
  0.7 10.1 %copy-start.9 = (f32[32]{0:T(128)S(1)}, f32[32]{0:T(128)}, u32[]{:S(2)}) copy-start(f32[32]{0:T(128)} %param.19) | copy-start | bytes 388
  0.7 14.1 %copy-start.5 = (s32[32,256]{1,0:T(8,128)S(1)}, s32[32,256]{1,0:T(8,128)}, u32[]{:S(2)}) copy-start(s32[32,256]{1,0:T(8,128)} %sea.7) | copy-start | bytes 98308
  2.0 12.8 %copy-start.12 = (f32[4]{0:T(128)S(1)}, f32[4]{0:T(128)}, u32[]{:S(2)}) copy-start(f32[4]{0:T(128)} %bias_last.1) | copy-start | bytes 52
  2.0 6.8 %collective-permute-start = (f32[168,256]{1,0:T(8,128)S(1)}, f32[168,256]{1,0:T(8,128)S(1)}, u32[]{:S(2)}, u32[]{:S(2)}) collective-permute-start(f32[168,256]{1,0:T(8,128)S(1)} %get-tuple-element.15), channel_id=1, source_target_pairs={{0,4},{4,8},{8,12},{12,16},{16,20},{20,24},{24,28},{28,0},{1,5},{5... | collective-permute-start | bytes 516104 | tf_op jit(solution)/shard_map/ppermute | solution.py:585
  2.1 6.8 %collective-permute-start.1 = (f32[168,256]{1,0:T(8,128)S(1)}, f32[168,256]{1,0:T(8,128)S(1)}, u32[]{:S(2)}, u32[]{:S(2)}) collective-permute-start(f32[168,256]{1,0:T(8,128)S(1)} %get-tuple-element.16), channel_id=1, source_target_pairs={{4,0},{8,4},{12,8},{16,12},{20,16},{24,20},{28,24},{0,28},{5,1},{9... | collective-permute-start | bytes 516104 | tf_op jit(solution)/shard_map/ppermute | solution.py:586
  4.7 0.8 %copy-start.4 = (s32[32,256]{1,0:T(8,128)S(1)}, s32[32,256]{1,0:T(8,128)}, u32[]{:S(2)}) copy-start(s32[32,256]{1,0:T(8,128)} %sea.7) | copy-start | bytes 98308
  5.5 5.3 %copy-start.13 = (bf16[32,10,3,3]{0,3,2,1:T(4,128)(2,1)S(1)}, bf16[32,10,3,3]{0,3,2,1:T(4,128)(2,1)}, u32[]{:S(2)}) copy-start(bf16[32,10,3,3]{0,3,2,1:T(4,128)(2,1)} %param.18) | copy-start | bytes 17284
  5.5 5.3 %copy-start.6 = (bf16[32,32,3,3]{1,0,3,2:T(8,128)(2,1)S(1)}, bf16[32,32,3,3]{1,0,3,2:T(8,128)(2,1)}, u32[]{:S(2)}) copy-start(bf16[32,32,3,3]{1,0,3,2:T(8,128)(2,1)} %param.20) | copy-start | bytes 55300
  5.5 5.3 %copy-start.7 = (bf16[32,32,3,3]{1,0,3,2:T(8,128)(2,1)S(1)}, bf16[32,32,3,3]{1,0,3,2:T(8,128)(2,1)}, u32[]{:S(2)}) copy-start(bf16[32,32,3,3]{1,0,3,2:T(8,128)(2,1)} %param.22) | copy-start | bytes 55300
  5.5 5.3 %copy-start.8 = (bf16[4,32,3,3]{1,0,3,2:T(4,128)(2,1)S(1)}, bf16[4,32,3,3]{1,0,3,2:T(4,128)(2,1)}, u32[]{:S(2)}) copy-start(bf16[4,32,3,3]{1,0,3,2:T(4,128)(2,1)} %param.24) | copy-start | bytes 6916
  9.1 4.2 %collective-permute-start.2 = (f32[96,128]{1,0:T(8,128)S(1)}, f32[96,128]{1,0:T(8,128)S(1)}, u32[]{:S(2)}, u32[]{:S(2)}) collective-permute-start(f32[96,128]{1,0:T(8,128)S(1)} %get-tuple-element.19), channel_id=1, source_target_pairs={{0,1},{1,0},{2,3},{3,2},{4,5},{5,4},{6,7},{7,6},{8,9},{9,8},{10,11... | collective-permute-start | bytes 147464 | tf_op jit(solution)/shard_map/ppermute | solution.py:610
  10.7 4.1 %collective-permute-start.3 = (f32[96,128]{1,0:T(8,128)S(1)}, f32[96,128]{1,0:T(8,128)S(1)}, u32[]{:S(2)}, u32[]{:S(2)}) collective-permute-start(f32[96,128]{1,0:T(8,128)S(1)} %get-tuple-element.20.own_tail), channel_id=1, source_target_pairs={{1,2},{2,1},{0,4},{3,31},{5,6},{6,5},{4,0},{7,27},{9,10},{10,9},{8... | collective-permute-start | bytes 147464 | tf_op jit(solution)/shard_map/ppermute | solution.py:616

commit v4 on v2

v4 whole, which is shorter than its diff:
```python
import functools

import jax
import jax.numpy as jnp
from jax import lax
from jax.experimental import pallas as pl
from jax.experimental.pallas import tpu as pltpu
from jax.sharding import PartitionSpec as P

REDUCED = 0.5
TIME_STEP = 0.2
VISCOSITY = 0.05
CORIOLIS = 0.4

RIM = 4
GAP = 16
NORTH, STRIP, GHOST, SOUTH = 0, 4, 8, 12
SUB = 16
LANES = 128
GROUP = 8
LAND = 2.0**100

f32 = jnp.float32
bf16 = jnp.bfloat16


def iota(shape, dim):
    return lax.broadcasted_iota(jnp.int32, shape, dim)


def dot(a, b):
    return jnp.dot(a, b, preferred_element_type=f32)


def rest(x):
    return x - x.astype(bf16).astype(f32)


def pack_lon_kernel(sizes, noise, u, v, h, sea, head, tail, noises_in, states, seas, wide, done):
    members, noises, levels = sizes
    fields = noises + 3 * levels
    lons, lats = sea.shape
    copies = [pltpu.make_async_copy(noise, noises_in, done.at[0])]
    for side in range(2):
        at = pl.ds(side * (lons - GROUP), GROUP)
        copies.append(pltpu.make_async_copy(sea.at[at], seas.at[side], done.at[1 + 4 * side]))
        for n, x in enumerate((u, v, h)):
            copies.append(
                pltpu.make_async_copy(x.at[:, :, at], states.at[side, n], done.at[2 + 4 * side + n])
            )
    for copy in copies:
        copy.start()
    for copy in copies:
        copy.wait()
    upper = iota((GROUP, lats), 0) < RIM

    def field(m, c, side):
        if c < noises:
            full = noises_in[m, c].astype(f32)
            return full[-GROUP:] if side else full[:GROUP]
        c -= noises
        return states[side, c // levels, m, c % levels]

    rests = members * fields * RIM + GROUP
    for m in range(members):
        for c in range(0, fields, 2):
            rows = pl.ds((m * fields + c) * RIM, GROUP)
            wide[0, rows] = jnp.where(upper, field(m, c, 0), pltpu.roll(field(m, c + 1, 0), RIM, 0))
            wide[1, rows] = jnp.where(upper, pltpu.roll(field(m, c, 1), RIM, 0), field(m, c + 1, 1))
        for c in range(noises, fields):
            row = pl.ds(rests + m * (fields - noises) + c - noises, 1)
            wide[0, row] = rest(field(m, c, 0)[:1])
            wide[1, row] = rest(field(m, c, 1)[GROUP - 1 :])
    rows = pl.ds(members * fields * RIM, GROUP)
    wide[0, rows] = jnp.where(upper, seas[0].astype(f32), 0.0)
    wide[1, rows] = jnp.where(upper, pltpu.roll(seas[1].astype(f32), RIM, 0), 0.0)
    head[...] = wide[0].astype(bf16)
    tail[...] = wide[1].astype(bf16)


def rim_tile(sizes, m, c, side, rim):
    members, noises, levels = sizes
    fields = noises + 3 * levels
    row = (m * fields + c) * RIM if c < fields else members * fields * RIM
    tile = rim[pl.ds(row // GROUP * GROUP, GROUP)]
    if (row // RIM) % 2 == side:
        return tile
    return pltpu.roll(tile, RIM, 0)


def window(tiles, following, mask, next_mask):
    pair = iota(mask.shape, 0) // 2
    zero = jnp.zeros_like(mask)
    more = []
    for start in range(0, len(tiles), 4):
        total = zero
        for n in range(min(4, len(tiles) - start)):
            moved = pltpu.roll(following[start + n], 2 * n, 0) if n else following[start]
            total = jnp.where(pair == n, moved, total)
        more.append(total)
    return jnp.concatenate(
        tiles + more + [mask - 1.0, next_mask - 1.0, jnp.ones_like(mask)], axis=0
    )


def store_lats(block, t, dst, tile, m, lats, chunks, buffer):
    blocks = (lats + GAP) // chunks
    buffer[...] = jnp.transpose(block)
    for q in range(chunks):
        lo = max(q * blocks, t * LANES)
        hi = min((q + 1) * blocks, (t + 1) * LANES, lats)
        if lo < hi:
            start = (lo - q * blocks) * SUB + m * chunks + q
            dst[tile, pl.ds(start, hi - lo, stride=SUB), :] = buffer[pl.ds(lo - t * LANES, hi - lo), :]


def own_kernel(sizes, noise, u, v, h, sea, own, head, tail, cells, turned):
    members, noises, levels = sizes
    fields = noises + 3 * levels
    lons, lats = sea.shape
    groups = lons // GROUP + 1
    chunks = SUB // members
    gap_k = lats - (chunks - 1) * ((lats + GAP) // chunks)
    lane = iota((GROUP, LANES), 1)
    for m in range(members):
        for g in range(groups):
            empty = pl.ds(gap_k * SUB + (m + 1) * chunks - 1, GAP, stride=SUB)
            cells[g, empty, :] = jnp.zeros((GAP, LANES), f32)

    def tiles_of(m, c, t):
        lanes = slice(t * LANES, (t + 1) * LANES)
        if c == fields:
            full = sea[:, lanes].astype(f32)
        elif c < noises:
            full = noise[m, c, :, lanes].astype(f32)
        else:
            full = (u, v, h)[(c - noises) // levels][m, (c - noises) % levels, :, lanes]
        full = pltpu.roll(full, lons - RIM, 0)
        tiles = [full[g * GROUP : (g + 1) * GROUP] for g in range(groups - 1)]
        return tiles[-1:] + tiles

    last = lats // LANES - 1
    lows = [jnp.zeros((GROUP, LANES), f32)] * (fields + 1)
    highs = [jnp.zeros((GROUP, LANES), f32)] * (fields + 1)
    blank = jnp.zeros((GROUP, LANES), f32)
    for t in range(last + 1):
        for m in range(members):
            tiles = [tiles_of(m, c, t) for c in range(fields + 1)]
            for g in range(groups):
                after = g + 1 if g + 1 < groups else None
                block = window(
                    [tiles[c][g] for c in range(fields)],
                    [blank if after is None else tiles[c][after] for c in range(fields)],
                    tiles[fields][g],
                    blank if after is None else tiles[fields][after],
                )
                store_lats(block, t, cells, g, m, lats, chunks, turned.at[(t * members + m) * groups + g])
            for c in range(fields + 1):
                for g in range(groups):
                    place = (g * members + m) * RIM
                    spot = (lane >= place) & (lane < place + RIM)
                    other = groups * members * RIM + g * members + m
                    if t == 0:
                        lows[c] = jnp.where(spot, pltpu.roll(tiles[c][g], place, 1), lows[c])
                        moved = pltpu.roll(rest(tiles[c][g]), other, 1)
                        lows[c] = jnp.where(lane == other, moved, lows[c])
                    if t == last:
                        first = LANES - RIM
                        moved = pltpu.roll(tiles[c][g], (place - first) % LANES, 1)
                        highs[c] = jnp.where(spot, moved, highs[c])
                        moved = pltpu.roll(rest(tiles[c][g]), (other + 1) % LANES, 1)
                        highs[c] = jnp.where(lane == other, moved, highs[c])
    for c in range(fields + 1):
        head[pl.ds(c * GROUP, GROUP)] = lows[c]
        tail[pl.ds(c * GROUP, GROUP)] = highs[c]
    for c in range(fields + 1, head.shape[0] // GROUP):
        head[pl.ds(c * GROUP, GROUP)] = blank
        tail[pl.ds(c * GROUP, GROUP)] = blank
    for g in range(groups):
        own[g] = cells[g].astype(bf16)


def join_kernel(sizes, lons, left, right, head, tail, even, odd, rims, wide):
    members, noises, levels = sizes
    fields = noises + 3 * levels
    groups = lons // GROUP + 1
    lats = left.shape[1]
    for side, rim in enumerate((left, right)):
        rims[side, 0] = rim[:, :LANES].astype(f32)
        rims[side, 1] = rim[:, lats - LANES :].astype(f32)
    lane = iota((GROUP, LANES), 1)
    upper = iota((GROUP, LANES), 0) < RIM
    to_south = lax.axis_index("lat") % 2 == 1
    for c in range(fields + 1):
        rows = pl.ds(c * GROUP, GROUP)
        ends = []
        for n, (part, first) in enumerate(((head, 0), (tail, LANES - RIM))):
            total = part[rows]
            for side in range(2):
                held = upper if side == 0 else ~upper
                for m in range(members):
                    place = ((groups - 1) * side * members + m) * RIM
                    tile = rim_tile(sizes, m, c, side, rims.at[side, n])
                    moved = pltpu.roll(tile, (place - first) % LANES, 1)
                    total = jnp.where(held & (lane >= place) & (lane < place + RIM), moved, total)
            ends.append(total)
        wide[0, rows] = jnp.where(to_south, ends[0], ends[1])
        wide[1, rows] = jnp.where(to_south, ends[1], ends[0])
    rows = pl.ds((fields + 1) * GROUP, wide.shape[1] - (fields + 1) * GROUP)
    wide[:, rows] = jnp.zeros((2, wide.shape[1] - (fields + 1) * GROUP, LANES), f32)
    even[...] = wide[0].astype(bf16)
    odd[...] = wide[1].astype(bf16)


def weights_kernel(w1, w2, w3, w4, bias1, bias2, bias3, t1, t2, t3, t4):
    hidden = w2.shape[2]
    per = LANES // hidden
    lane = iota((hidden, LANES), 1)
    fields = w1.shape[2]
    rows = fields * GROUP
    out_lon = iota((GROUP, LANES), 1) // hidden
    in_row = iota((GROUP, LANES), 0)
    bias_row = iota((GROUP, LANES), 0)

    def bias_rows(layer):
        part = 0.5 * jnp.concatenate([(bias1, bias2, bias3)[layer][...]] * per, axis=1)
        b1 = part.astype(bf16).astype(f32)
        b2 = (part - b1).astype(bf16).astype(f32)
        b3 = part - b1 - b2
        zero = jnp.zeros((GROUP, LANES), f32)
        return jnp.where(
            bias_row == 0,
            b1,
            jnp.where(bias_row == 1, b2, jnp.where(bias_row == 2, b3, zero)),
        )

    def sea_rows(shift, tile):
        lon = iota((2 * GROUP, LANES), 0)
        out = iota((2 * GROUP, LANES), 1) // hidden + per * tile
        return jnp.where(lon == out + shift, LAND, 0.0)

    for dj in range(3):
        taps = [0.5 * jnp.concatenate([w1[dj, di].astype(f32)] * per, axis=1) for di in range(3)]
        for tile in range(2):
            parts = []
            for c in range(fields):
                total = jnp.zeros((GROUP, LANES), f32)
                for di in range(3):
                    hit = in_row == out_lon + per * tile + di
                    total = jnp.where(hit, jnp.broadcast_to(taps[di][c : c + 1], (GROUP, LANES)), total)
                parts.append(total)
            for start in range(0, fields, 4):
                total = jnp.zeros((GROUP, LANES), f32)
                for n in range(min(4, fields - start)):
                    for di in range(3):
                        hit = in_row % 2 + GROUP == out_lon + per * tile + di
                        row = jnp.broadcast_to(taps[di][start + n : start + n + 1], (GROUP, LANES))
                        total = jnp.where(hit & (in_row // 2 == n), row, total)
                parts.append(total)
            if dj == 1:
                parts += [sea_rows(1, tile), bias_rows(0)]
            else:
                parts.append(jnp.zeros((3 * GROUP, LANES), f32))
            block = jnp.concatenate(parts, axis=0)
            t1[pl.ds(dj * LANES, LANES), pl.ds(tile * LANES, LANES)] = block.astype(bf16)

    for layer, (w, t) in enumerate(((w2, t2), (w3, t3))):
        for dj in range(3):
            taps = []
            for di in range(3):
                cell = 0.5 * w[di, dj].astype(f32)
                wide = jnp.concatenate([cell, jnp.zeros((hidden, LANES - hidden), f32)], axis=1)
                square = jnp.concatenate([wide] * per, axis=0)
                taps.append(jnp.transpose(square)[:hidden])
            for lon in range(GROUP + 2):
                for tile in range(2):
                    total = jnp.zeros((hidden, LANES), f32)
                    for di in range(3):
                        total = jnp.where(lane // hidden + per * tile == lon - di, taps[di], total)
                    if lon < GROUP:
                        row = dj * GROUP * hidden + lon * hidden
                    else:
                        row = 3 * GROUP * hidden + dj * 2 * hidden + (lon - GROUP) * hidden
                    t[pl.ds(row, hidden), pl.ds(tile * LANES, LANES)] = total.astype(bf16)
        for tile in range(2):
            block = jnp.concatenate(
                [
                    jnp.zeros((5 * GROUP, LANES), f32),
                    sea_rows(2 + layer, tile),
                    bias_rows(1 + layer),
                ],
                axis=0,
            )
            row = 3 * GROUP * hidden + 6 * hidden
            t[pl.ds(row, 2 * hidden), pl.ds(tile * LANES, LANES)] = block.astype(bf16)

    outs = w4.shape[2]
    half = LANES // 2
    lons = half // outs
    slot = iota((hidden, LANES), 1) // half
    out_lon = iota((hidden, LANES), 1) % lons
    taps = {}
    for dj in range(3):
        for di in range(3):
            cell = w4[di, dj].astype(f32)
            wide = jnp.concatenate([cell, jnp.zeros((outs, LANES - hidden), f32)], axis=1)
            square = jnp.concatenate(
                [jnp.broadcast_to(wide[c : c + 1], (lons, LANES)) for c in range(outs)] * 2, axis=0
            )
            taps[dj, di] = jnp.transpose(square)[:hidden]
    order = ((0, 1, 2, None), (1, 0, None, 2))
    for side in range(2):
        for lon in range(t4.shape[1] // hidden):
            for tile in range(2):
                total = jnp.zeros((hidden, LANES), f32)
                for place in range(2):
                    dj = order[side][2 * tile + place]
                    if dj is None:
                        continue
                    for di in range(3):
                        total = jnp.where((slot == place) & (out_lon == lon - di), taps[dj, di], total)
                t4[side, pl.ds(lon * hidden, hidden), pl.ds(tile * LANES, LANES)] = total.astype(bf16)


def main_kernel(
    sizes,
    bias_last,
    own,
    u,
    v,
    h,
    sea,
    left_in,
    right_in,
    even_rim,
    odd_rim,
    own_tail,
    t1,
    t2,
    t3,
    t4,
    new_u,
    new_v,
    new_h,
    left,
    right,
    cells,
    first,
    odd,
    even,
    force,
    gathered,
    buffers,
    turned,
    gaps,
    results,
    done,
):
    members, noises, levels = sizes
    fields = noises + 3 * levels
    lons, lats = sea.shape
    groups = lons // GROUP + 1
    chunks = SUB // members
    blocks = (lats + GAP) // chunks
    rows = blocks * SUB
    gap_k = lats - (chunks - 1) * blocks
    lat_index, lat_count = lax.axis_index("lat"), lax.axis_size("lat")
    top = lat_index == lat_count - 1
    is_odd = lat_index % 2 == 1
    bottom = lat_index == 0
    left[...] = left_in[...].astype(f32)
    right[...] = right_in[...].astype(f32)
    strip = odd_rim[...].astype(f32)
    paired = even_rim[...].astype(f32)
    south = jnp.where(is_odd, paired, jnp.where(bottom, 0.0, strip))

    wide = strip.shape[0]
    span = members * RIM
    lane = iota((wide, LANES), 1)
    rests = groups * span
    border = ((lane % RIM == 0) & (lane < rests)) | (lane >= rests)
    row_to = iota((wide, wide), 0)
    row_from = iota((wide, wide), 1)
    channel = row_to // GROUP
    mirrored = (channel == row_from // GROUP) & (row_from % GROUP == GROUP - 1 - row_to % GROUP)
    odd_parity = (channel >= noises) & (channel < noises + 2 * levels)
    flip_rows = jnp.where(mirrored, jnp.where(odd_parity, -1.0, 1.0), 0.0).astype(bf16)
    lane_from = iota((LANES, LANES), 0)
    lane_to = iota((LANES, LANES), 1)
    source = (groups - 1 - lane_to // span) * span + lane_to % span + RIM - 1
    moves = (lane_to % RIM == 0) & (lane_to < rests) & (lane_from == source)
    other = lane_to - rests
    source = rests + (groups - 1 - other // members) * members + other % members
    moves = moves | ((other >= 0) & (other < groups * members) & (lane_from == source))
    flip_lanes = jnp.where(moves, 1.0, 0.0).astype(bf16)
    pair = dot(flip_rows, jnp.concatenate([odd_rim[...], own_tail[...]], axis=1)).astype(bf16)
    folded = dot(pair[:, :LANES], flip_lanes)
    ghost = dot(pair[:, LANES:], flip_lanes)
    north = jnp.where(is_odd, strip, paired)
    north_rim = jnp.where(border & top, folded, north)

    for n, message in enumerate((north_rim, strip, ghost, south)):
        after = pltpu.roll(message, LANES - span, 1)
        cut = [message[c * GROUP : (c + 1) * GROUP] for c in range(fields + 1)]
        after = [after[c * GROUP : (c + 1) * GROUP] for c in range(fields + 1)]
        turned[n] = jnp.transpose(window(cut[:fields], after[:fields], cut[fields], after[fields]))
        for g in range(groups):
            for m in range(members):
                gap = (m - 1) % members if n == 3 else m
                start = n * RIM * SUB + gap * chunks + chunks - 1
                gaps[g, pl.ds(start, RIM, stride=SUB), :] = turned[n, pl.ds((g * members + m) * RIM, RIM), :]

    blank = jnp.zeros((GROUP, LANES), f32)
    for t in range(lats // LANES):
        lanes = slice(t * LANES, (t + 1) * LANES)
        for side, rim in enumerate((left, right)):
            for m in range(members):
                tiles = [rim_tile(sizes, m, c, side, rim.at[:, lanes]) for c in range(fields + 1)]
                block = window(tiles[:fields], [blank] * fields, tiles[fields], blank)
                buffer = buffers.at[(t * 2 + side) * members + m]
                store_lats(block, t, cells, side, m, lats, chunks, buffer)

    in_gap = iota((GAP * SUB, LANES), 0) % chunks == chunks - 1
    at_lane = iota((rows, LANES), 1)
    holds_lon = (at_lane < fields * GROUP) | (at_lane // GROUP == LANES // GROUP - 3)
    for g in range(groups):
        if g in (0, groups - 1):
            side = g // (groups - 1)
            from_rim = holds_lon & ((at_lane % GROUP < RIM) if side == 0 else (at_lane % GROUP >= RIM))
            first[g, pl.ds(SUB, rows), :] = jnp.where(from_rim, cells[side], own[g].astype(f32)).astype(bf16)
        else:
            first[g, pl.ds(SUB, rows), :] = own[g]
        spot = pl.ds((1 + gap_k) * SUB, GAP * SUB)
        kept = first[g, spot, :].astype(f32)
        first[g, spot, :] = jnp.where(in_gap, gaps[g], kept).astype(bf16)
        end = first[g, pl.ds(rows, SUB), :].astype(f32)
        first[g, pl.ds(0, SUB), :] = pltpu.roll(end, 1, 0).astype(bf16)
        begin = first[g, pl.ds(SUB, SUB), :].astype(f32)
        first[g, pl.ds(SUB + rows, SUB), :] = pltpu.roll(begin, SUB - 1, 0).astype(bf16)

    hidden = LANES // 4
    per = LANES // hidden
    tiles = odd.shape[0]
    cuts = 2
    step = rows // cuts
    lower = iota((step, LANES), 1) < 2 * hidden

    def activate(pre):
        return (pre * jnp.tanh(pre) + pre).astype(bf16)

    def finish(x, valid):
        used = (valid + per - 1) // per

        @pl.when(top)
        def _():
            strip_top = SUB * (1 + gap_k + STRIP + RIM - 1)
            own_top = SUB * gap_k
            strip_ghost = SUB * (1 + gap_k + GHOST)
            own_ghost = SUB * (1 + gap_k + NORTH)
            last_chunk = iota((SUB, LANES), 0) % chunks == chunks - 1
            spot = iota((SUB, LANES), 1) // hidden
            for src, dst in ((strip_top, own_ghost), (own_top, strip_ghost)):
                found = [x[t, pl.ds(src, SUB), :].astype(f32) for t in range(used)]
                for t in range(used):
                    total = x[t, pl.ds(dst, SUB), :].astype(f32)
                    for i in range(per):
                        lon = valid - 1 - (per * t + i)
                        if lon < 0:
                            continue
                        moved = pltpu.roll(found[lon // per], (hidden * (i - lon % per)) % LANES, 1)
                        total = jnp.where(last_chunk & (spot == i), moved, total)
                    x[t, pl.ds(dst, SUB), :] = total.astype(bf16)

        for t in range(used):
            end = x[t, pl.ds(rows, SUB), :].astype(f32)
            x[t, pl.ds(0, SUB), :] = pltpu.roll(end, 1, 0).astype(bf16)
            begin = x[t, pl.ds(SUB, SUB), :].astype(f32)
            x[t, pl.ds(SUB + rows, SUB), :] = pltpu.roll(begin, SUB - 1, 0).astype(bf16)

    for x in (odd, even):
        x[tiles - 1] = jnp.zeros(x.shape[1:], bf16)
    even[tiles - 2] = jnp.zeros(even.shape[1:], bf16)

    def put(y, b, r, out):
        for e in range(out.shape[1] // LANES):
            y[2 * b + e, pl.ds(SUB + r, step), :] = out[:, e * LANES : (e + 1) * LANES]

    for b in range(groups):
        for n in range(cuts):
            r = n * step
            parts = [first[b, pl.ds(r + SUB * d, step), :] for d in range(3)]
            put(odd, b, r, activate(dot(jnp.concatenate(parts, axis=1), t1[...])))
    finish(odd, lons + 6)

    width = GROUP * hidden

    def layer(x, y, t, left_over):
        for b in range(groups):
            for n in range(cuts):
                r = n * step

                def cells_of(tile, d):
                    return x[tile, pl.ds(r + SUB * d, step), :]

                def packed(tile):
                    more = [cells_of(tile, d) for d in range(3)]
                    return [
                        jnp.where(lower, more[0], pltpu.roll(more[1], 2 * hidden, 1)),
                        jnp.where(lower, more[2], first[b, pl.ds(r + SUB, step), :]),
                    ]

                if b < groups - 1:
                    parts = [cells_of(2 * b + e, d) for d in range(3) for e in range(2)] + packed(2 * b + 2)
                    matrix = t[...]
                elif left_over == per:
                    parts = [cells_of(2 * b, d) for d in range(3)] + packed(2 * b + 1)
                    lanes = pl.ds(0, LANES)
                    matrix = jnp.concatenate(
                        [t[pl.ds(d * width, LANES), lanes] for d in range(3)]
                        + [t[pl.ds(d * width + LANES, 2 * hidden), lanes] for d in range(3)]
                        + [t[pl.ds(3 * width + 6 * hidden, 2 * hidden), lanes]],
                        axis=0,
                    )
                else:
                    parts = [cells_of(2 * b, d) for d in range(3)] + [first[b, pl.ds(r + SUB, step), :]]
                    lanes = pl.ds(0, LANES)
                    matrix = jnp.concatenate(
                        [t[pl.ds(d * width, LANES), lanes] for d in range(3)]
                        + [jnp.zeros((2 * hidden, LANES), bf16)]
                        + [t[pl.ds(3 * width + 6 * hidden, 2 * hidden), lanes]],
                        axis=0,
                    )
                put(y, b, r, activate(dot(jnp.concatenate(parts, axis=1), matrix)))

    layer(odd, even, t2, per)
    finish(even, lons + 4)
    layer(even, odd, t3, per // 2)
    finish(odd, lons + 2)

    depth = t4.shape[1] // LANES
    long = (rows + 2 * SUB) // 2
    before = iota((long, LANES), 1) < LANES // 2
    for n in range(2):
        span_rows = pl.ds(n * long, long)
        sides = []
        for side in range(2):
            parts = [odd[side * (depth - 1) + t, span_rows, :] for t in range(depth)]
            sides.append(dot(jnp.concatenate(parts, axis=1), t4[side]))
        force[0, span_rows, :] = jnp.where(before, sides[0][:, :LANES], sides[1][:, :LANES])
        swapped = jnp.where(before, sides[1][:, :LANES], sides[0][:, :LANES])
        force[1, span_rows, :] = pltpu.roll(swapped, LANES // 2, 1)
        force[2, span_rows, :] = jnp.where(before, sides[0][:, LANES:], sides[1][:, LANES:])

    ocean = sea[...].astype(f32)
    at_lat = iota((lons, lats), 1).astype(f32)
    lat_rows = (lat_index * lats).astype(f32) + at_lat
    turn = CORIOLIS * (2.0 * (lat_rows + 0.5) / (lats * lat_count) - 1.0)
    at_first = iota((lons, lats), 0) == 0
    at_last = iota((lons, lats), 0) == lons - 1
    at_south = iota((lons, lats), 1) == 0
    at_north = iota((lons, lats), 1) == lats - 1
    lon_rests = members * fields * RIM + GROUP
    halves = lons // 2
    for m in range(members):
        for q in range(chunks):
            size = min(blocks, lats - q * blocks)
            total = force[0, pl.ds(m * chunks + q, size, stride=SUB), :]
            for d in range(1, 3):
                total = total + force[d, pl.ds(d * SUB + m * chunks + q, size, stride=SUB), :]
            gathered[m, pl.ds(q * blocks, size), :] = total
        turned_force = jnp.transpose(gathered[m])

        def push(c):
            parts = [
                turned_force[side * LANES // 2 + c * halves : side * LANES // 2 + (c + 1) * halves]
                for side in range(2)
            ]
            return (jnp.concatenate(parts, axis=0) + bias_last[c]) * ocean

        def rims(c):
            row = (m * fields + c) * RIM
            more = lon_rests + m * (fields - noises) + c - noises
            west = left[pl.ds(row + RIM - 1, 1)] + left[pl.ds(more, 1)]
            east = right[pl.ds(row, 1)] + right[pl.ds(more, 1)]
            low, high = [], []
            for g in range(groups):
                spot = (g * members + m) * RIM
                more = rests + g * members + m
                some = slice(c * GROUP, (c + 1) * GROUP)
                low.append(south[some, spot + RIM - 1 : spot + RIM] + south[some, more : more + 1])
                high.append(north_rim[some, spot : spot + 1] + north_rim[some, more : more + 1])
            low = jnp.broadcast_to(jnp.concatenate(low, axis=0), (lons + GROUP, LANES))
            high = jnp.broadcast_to(jnp.concatenate(high, axis=0), (lons + GROUP, LANES))
            low = pltpu.roll(low, lons + GROUP - RIM, 0)[:lons]
            high = pltpu.roll(high, lons + GROUP - RIM, 0)[:lons]
            repeat = lats // LANES
            return west, east, jnp.concatenate([low] * repeat, axis=1), jnp.concatenate([high] * repeat, axis=1)

        def around(x, rim):
            west, east, low, high = rim
            return (
                jnp.where(at_first, west, pltpu.roll(x, 1, 0)),
                jnp.where(at_last, east, pltpu.roll(x, lons - 1, 0)),
                jnp.where(at_south, low, pltpu.roll(x, 1, 1)),
                jnp.where(at_north, high, pltpu.roll(x, lats - 1, 1)),
            )

        sets = []
        for level in range(levels):
            sets.append(
                [
                    (x[m, level], around(x[m, level], rims(noises + n * levels + level)))
                    for n, x in enumerate((u, v, h))
                ]
            )
        for level in range(levels):
            (cu, au), (cv, av), (ch, ah) = sets[level]
            upper, lower_h = sets[0][2][1], sets[1][2][1]
            pressure = [upper[i] + lower_h[i] for i in range(4)]
            if level == 1:
                pressure = [pressure[i] + REDUCED * lower_h[i] for i in range(4)]
            lap_u = au[1] + au[0] + au[3] + au[2] - 4.0 * cu
            lap_v = av[1] + av[0] + av[3] + av[2] - 4.0 * cv
            dx = 0.5 * (pressure[1] - pressure[0])
            dy = 0.5 * (pressure[3] - pressure[2])
            gain_u = turn * cv - dx + push(level) + VISCOSITY * lap_u
            gain_v = -turn * cu - dy + push(levels + level) + VISCOSITY * lap_v
            results[0, m, level] = ocean * (cu + TIME_STEP * gain_u)
            results[1, m, level] = ocean * (cv + TIME_STEP * gain_v)
            flow = 0.5 * (ah[1] * au[1] - ah[0] * au[0]) + 0.5 * (ah[3] * av[3] - ah[2] * av[2])
            results[2, m, level] = ch - TIME_STEP * flow
        for n, out in enumerate((new_u, new_v, new_h)):
            pltpu.make_async_copy(results.at[n, m], out.at[m], done.at[n, m]).start()
    for m in range(members):
        for n, out in enumerate((new_u, new_v, new_h)):
            pltpu.make_async_copy(results.at[n, m], out.at[m], done.at[n, m]).wait()


def body(
    noise,
    velocity_u,
    velocity_v,
    thickness,
    land_sea,
    conv_first,
    bias_first,
    conv_second,
    bias_second,
    conv_third,
    bias_third,
    conv_last,
    bias_last,
):
    members, noises, lons, lats = noise.shape
    levels = velocity_u.shape[1]
    fields = noises + 3 * levels
    sizes = (members, noises, levels)
    hidden = conv_first.shape[0]
    outs = conv_last.shape[0]
    groups = lons // GROUP + 1
    rows = members * (lats + GAP)
    assert hidden * 4 == LANES and outs * lons == LANES and members * (RIM + 1) * groups <= LANES
    assert fields % 2 == 0 and 4 * -(-fields // 4) == 12 and GROUP * (fields + 6) == LANES and lons % 16 == 0
    assert lats % LANES == 0 and SUB % members == 0 and (lats + GAP) % (SUB // members) == 0
    lon_count, lat_count = lax.axis_size("lon"), lax.axis_size("lat")
    assert lon_count % 2 == 0 and lat_count % 2 == 0
    state = (noise, velocity_u, velocity_v, thickness, land_sea)
    whole = pl.BlockSpec(memory_space=pltpu.VMEM)

    tall = members * fields * RIM + GROUP + members * 3 * levels
    assert tall % SUB == 0
    head, tail = pl.pallas_call(
        functools.partial(pack_lon_kernel, sizes),
        out_shape=[pltpu.VMEM((tall, lats), bf16)] * 2,
        in_specs=[pl.BlockSpec(memory_space=pltpu.HBM)] * 5,
        out_specs=[whole] * 2,
        scratch_shapes=[
            pltpu.VMEM(noise.shape, noise.dtype),
            pltpu.VMEM((2, 3, members, levels, GROUP, lats), f32),
            pltpu.VMEM((2, GROUP, lats), land_sea.dtype),
            pltpu.VMEM((2, tall, lats), f32),
            pltpu.SemaphoreType.DMA((9,)),
        ],
        name="pack_lon",
    )(*state)
    ring = [(i, (i + 1) % lon_count) for i in range(lon_count)]
    left = lax.ppermute(tail, "lon", ring)
    right = lax.ppermute(head, "lon", [(b, a) for a, b in ring])

    wide = -(-(fields + 1) * GROUP // SUB) * SUB
    part = pltpu.VMEM((wide, LANES), f32)
    message = pltpu.VMEM((wide, LANES), bf16)
    own, own_head, own_tail = pl.pallas_call(
        functools.partial(own_kernel, sizes),
        out_shape=[pltpu.VMEM((groups, rows, LANES), bf16), part, part],
        in_specs=[whole] * 5,
        out_specs=[whole] * 3,
        scratch_shapes=[
            pltpu.VMEM((groups, rows, LANES), f32),
            pltpu.VMEM((members * groups * lats // LANES, LANES, LANES), f32),
        ],
        compiler_params=pltpu.CompilerParams(vmem_limit_bytes=8 * 2**20),
        cost_estimate=pl.CostEstimate(flops=10**7, bytes_accessed=10**7, transcendentals=0),
        name="own_cells",
    )(*state)
    last = lat_count - 1
    smem = pl.BlockSpec(memory_space=pltpu.SMEM)
    to_even, to_odd = pl.pallas_call(
        functools.partial(join_kernel, sizes, lons),
        out_shape=[message] * 2,
        in_specs=[whole] * 4,
        out_specs=[whole] * 2,
        scratch_shapes=[
            pltpu.VMEM((2, 2, tall, LANES), f32),
            pltpu.VMEM((2, wide, LANES), f32),
        ],
        compiler_params=pltpu.CompilerParams(vmem_limit_bytes=4 * 2**20),
        name="join_rims",
    )(left, right, own_head, own_tail)
    even_rim = lax.ppermute(to_even, "lat", [(i, i ^ 1) for i in range(lat_count)])
    pairs = []
    for t in range(lon_count):
        at = t * lat_count
        pairs += [(at + k, at + k - 1 + 2 * (k % 2)) for k in range(1, last)]
        pairs += [(at, (t ^ 1) * lat_count), (at + last, (lon_count - 1 - t) * lat_count + last)]
    odd_rim = lax.ppermute(to_odd, ("lon", "lat"), pairs)

    deep = -(-(lons // 2 + 2) * hidden // LANES) * LANES
    t1, t2, t3, t4 = pl.pallas_call(
        weights_kernel,
        out_shape=[
            pltpu.VMEM((3 * LANES, 2 * LANES), bf16),
            pltpu.VMEM((8 * LANES, 2 * LANES), bf16),
            pltpu.VMEM((8 * LANES, 2 * LANES), bf16),
            pltpu.VMEM((2, deep, 2 * LANES), bf16),
        ],
        in_specs=[whole] * 7,
        out_specs=[whole] * 4,
        compiler_params=pltpu.CompilerParams(vmem_limit_bytes=8 * 2**20),
        cost_estimate=pl.CostEstimate(flops=10**7, bytes_accessed=3 * 10**6, transcendentals=0),
        name="banded_matrices",
    )(
        conv_first.transpose(3, 2, 1, 0),
        conv_second.transpose(2, 3, 0, 1),
        conv_third.transpose(2, 3, 0, 1),
        conv_last.transpose(2, 3, 0, 1),
        bias_first[None],
        bias_second[None],
        bias_third[None],
    )

    padded = rows + 2 * SUB
    tiles = 2 * groups + 1
    out = jax.ShapeDtypeStruct(velocity_u.shape, f32)
    return pl.pallas_call(
        functools.partial(main_kernel, sizes),
        out_shape=[out] * 3,
        in_specs=[smem] + [whole] * 14,
        out_specs=[pl.BlockSpec(memory_space=pltpu.HBM)] * 3,
        scratch_shapes=[
            pltpu.VMEM((tall, lats), f32),
            pltpu.VMEM((tall, lats), f32),
            pltpu.VMEM((2, rows, LANES), f32),
            pltpu.VMEM((groups, padded, LANES), bf16),
            pltpu.VMEM((tiles, padded, LANES), bf16),
            pltpu.VMEM((tiles, padded, LANES), bf16),
            pltpu.VMEM((3, padded, LANES), f32),
            pltpu.VMEM((members, lats, LANES), f32),
            pltpu.VMEM((2 * members * lats // LANES, LANES, LANES), f32),
            pltpu.VMEM((4, LANES, LANES), f32),
            pltpu.VMEM((groups, GAP * SUB, LANES), f32),
            pltpu.VMEM((3, *velocity_u.shape), f32),
            pltpu.SemaphoreType.DMA((3, members)),
        ],
        compiler_params=pltpu.CompilerParams(vmem_limit_bytes=32 * 2**20),
        cost_estimate=pl.CostEstimate(flops=2 * 10**10, bytes_accessed=10**7, transcendentals=4 * 10**6),
        name="network_and_step",
    )(
        bias_last,
        own,
        *state[1:],
        left,
        right,
        even_rim,
        odd_rim,
        to_odd,
        t1,
        t2,
        t3,
        t4,
    )


def solution(mesh):
    tiles = P(None, None, "lon", "lat")
    return jax.shard_map(
        body,
        mesh=mesh,
        in_specs=(tiles,) * 4 + (P("lon", "lat"),) + (P(),) * 8,
        out_specs=(tiles,) * 3,
        check_vma=False,
    )
```

time: 31.6 us -> 32.2 us (1.019)
  local copies, waits for them, and re-layouts: 0.82 us -> 4.62 us
  waiting for transfers between devices: 4.97 us -> 2.8 us
  Pallas kernels: 20.3 us -> 19.1 us
    unnamed x29 -> x35, local copies, waits for them, and re-layouts: 0.82 us -> 4.62 us
    pallas_call x1, Pallas kernels: 16.5 us -> 14.3 us  [body(): pl.pallas_call(functools.partial(main_kernel, sizes), out_shape=[out] * 3...]
    ppermute x1, waiting for transfers between devices: 2.01 us -> 0.01 us  [body(): left = lax.ppermute(tail, 'lon', ring)]
    pallas_call x1, Pallas kernels: 1.32 us -> 2.26 us  [body(): pl.pallas_call(functools.partial(own_kernel, sizes), out_shape=[pltpu.VME...]
  transfers between devices with their start and end apart: 4 -> 4, of which waited for: 3 -> 2; matrix products, arithmetic and copies ran while one was open for 0% -> 0% of each run, Pallas kernels for 8% -> 10%
where the time goes in v4:
time: 32.2 us; the launch traced here: 31.9 us
  Pallas kernels  19.1 us (59%)
  local copies, waits for them, and re-layouts  4.62 us (14%)
  starting transfers between devices  4.33 us (13%)
  waiting for transfers between devices  2.8 us (9%)
  between operations  1.02 us (3%)
    pallas_call x1, Pallas kernels, body(): pl.pallas_call(functools.partial(main_kernel, sizes), out_shape=[out] * 3...  14.3 us
    unnamed x35, local copies, waits for them, and re-layouts  4.62 us
    ppermute x1, starting transfers between devices, body(): right = lax.ppermute(head, 'lon', [(b, a) for a, b in ring])  2.63 us
    pallas_call x1, Pallas kernels, body(): pl.pallas_call(functools.partial(own_kernel, sizes), out_shape=[pltpu.VME...  2.26 us
    ppermute x1, starting transfers between devices, body(): lax.ppermute(to_even, 'lat', [(i, i ^ 1) for i in range(lat_count)])  1.64 us
    ppermute x1, waiting for transfers between devices, body(): odd_rim = lax.ppermute(to_odd, ('lon', 'lat'), pairs)  1.58 us
    pallas_call x1, Pallas kernels, body(): pl.pallas_call(functools.partial(pack_lon_kernel, sizes), out_shape=[pltp...  1.41 us
    ppermute x1, waiting for transfers between devices, body(): lax.ppermute(to_even, 'lat', [(i, i ^ 1) for i in range(lat_count)])  1.22 us
  transfers between devices with their start and end apart: 4, of which 2 were waited for; matrix products, arithmetic and copies ran while one was open for 0% of the time, Pallas kernels for 10%

profile of v4, /device:TPU:20, one launch (start us, length us, event | category | flops | bytes accessed | tf_op | source)
XLA Modules:
  0.0 31.9 jit_solution(1939354455598528881)
XLA Ops:
  0.6 0.0 copy-start.8
  0.6 0.0 copy-start.6
  0.7 0.0 copy-start.4
  0.7 0.0 copy-start.2
  0.7 0.0 copy-start.16
  0.7 0.0 copy-start.11
  0.7 0.0 copy-start.14
  0.7 0.0 copy-start.10
  0.7 0.0 copy-start.13
  0.7 0.0 copy-start.9
  0.7 0.0 copy-start.12
  0.8 0.0 copy-start.15
  0.8 1.4 %pack_lon.1 = (bf16[192,256]{1,0:T(8,128)(2,1)S(1)}, bf16[192,256]{1,0:T(8,128)(2,1)S(1)}) custom-call(bf16[4,4,32,256]{3,2,1,0:T(8,128)(2,1)} %noise.3, f32[4,2,32,256]{3,2,1,0:T(8,128)} %u.5, f32[4,2,32,256]{3,2,1,0:T(8,128)} %v.5, f32[4,2,32,256]{3,2,1,0:T(8,128)} %h.5, s32[32,256]{1,0:T(8,128)} %sea.5), custom_call_target="tpu_custom_call" | custom-call | tf_op jit(solution)/shard_map/pack_lon/pallas_call | solution.py:672
  2.2 0.1 collective-permute-start
  2.2 2.6 %collective-permute-start.1 = (bf16[192,256]{1,0:T(8,128)(2,1)S(1)}, bf16[192,256]{1,0:T(8,128)(2,1)S(1)}, u32[]{:S(2)}, u32[]{:S(2)}) collective-permute-start(bf16[192,256]{1,0:T(8,128)(2,1)S(1)} %get-tuple-element.16), channel_id=1, source_target_pairs={{4,0},{8,4},{12,8},{16,12},{20,16},{24,20},{28,24},{0,28},{5,1},{9... | collective-permute-start | bytes 294920 | tf_op jit(solution)/shard_map/ppermute | solution.py:688
  4.9 0.9 %copy-done = bf16[4,4,32,256]{3,2,1,0:T(8,128)(2,1)S(1)} copy-done((bf16[4,4,32,256]{3,2,1,0:T(8,128)(2,1)S(1)}, bf16[4,4,32,256]{3,2,1,0:T(8,128)(2,1)}, u32[]{:S(2)}) %copy-start) | copy-done | bytes 262168
  5.8 0.9 %copy-done.1 = f32[4,2,32,256]{3,2,1,0:T(8,128)S(1)} copy-done((f32[4,2,32,256]{3,2,1,0:T(8,128)S(1)}, f32[4,2,32,256]{3,2,1,0:T(8,128)}, u32[]{:S(2)}) %copy-start.1) | copy-done | bytes 262168
  6.8 0.9 %copy-done.3 = f32[4,2,32,256]{3,2,1,0:T(8,128)S(1)} copy-done((f32[4,2,32,256]{3,2,1,0:T(8,128)S(1)}, f32[4,2,32,256]{3,2,1,0:T(8,128)}, u32[]{:S(2)}) %copy-start.3) | copy-done | bytes 262168
  7.7 0.9 %copy-done.5 = f32[4,2,32,256]{3,2,1,0:T(8,128)S(1)} copy-done((f32[4,2,32,256]{3,2,1,0:T(8,128)S(1)}, f32[4,2,32,256]{3,2,1,0:T(8,128)}, u32[]{:S(2)}) %copy-start.5) | copy-done | bytes 262168
  8.7 0.8 %copy-done.7 = s32[32,256]{1,0:T(8,128)S(1)} copy-done((s32[32,256]{1,0:T(8,128)S(1)}, s32[32,256]{1,0:T(8,128)}, u32[]{:S(2)}) %copy-start.7) | copy-done | bytes 32792
  9.4 2.3 %own_cells.1 = (bf16[5,1088,128]{2,1,0:T(8,128)(2,1)S(1)}, f32[96,128]{1,0:T(8,128)S(1)}, f32[96,128]{1,0:T(8,128)S(1)}) custom-call(bf16[4,4,32,256]{3,2,1,0:T(8,128)(2,1)S(1)} %copy-done, f32[4,2,32,256]{3,2,1,0:T(8,128)S(1)} %copy-done.1, f32[4,2,32,256]{3,2,1,0:T(8,128)S(1)} %copy-done.3, f32[4,2,32,256]{3,2,1,0:T(8,128)S(1)} %copy-done.5, ...), custom_call_target="tpu_custom_call" | custom-call | flops 10000000 | bytes 10000000 | tf_op jit(solution)/shard_map/own_cells/pallas_call | solution.py:693
  11.7 0.0 collective-permute-done.left.left_in
  11.7 0.0 collective-permute-done.1.right.right_in
  11.7 0.2 join_rims.1
  11.9 1.6 %collective-permute-start.2 = (bf16[96,128]{1,0:T(8,128)(2,1)S(1)}, bf16[96,128]{1,0:T(8,128)(2,1)S(1)}, u32[]{:S(2)}, u32[]{:S(2)}) collective-permute-start(bf16[96,128]{1,0:T(8,128)(2,1)S(1)} %get-tuple-element.19), channel_id=1, source_target_pairs={{0,1},{1,0},{2,3},{3,2},{4,5},{5,4},{6,7},{7,6},{8,9},{9,8},{10,11... | collective-permute-start | bytes 73736 | tf_op jit(solution)/shard_map/ppermute | solution.py:720
  13.5 0.0 collective-permute-start.3
  13.6 0.9 %banded_matrices.1 = (bf16[384,256]{1,0:T(8,128)(2,1)S(1)}, bf16[1024,256]{1,0:T(8,128)(2,1)S(1)}, bf16[1024,256]{1,0:T(8,128)(2,1)S(1)}, bf16[2,640,256]{2,1,0:T(8,128)(2,1)S(1)}) custom-call(bf16[3,3,10,32]{3,2,1,0:T(8,128)(2,1)S(1)} %bitcast.9, bf16[3,3,32,32]{3,2,1,0:T(8,128)(2,1)S(1)} %bitcast.10, bf16[3,3,32,32]{3,2,1,0:T(8,128)(2,1)S(1)} %bitcast.11, ...), custom_call_target="tpu_custom_call" | custom-call | flops 10000000 | bytes 3000000 | tf_op jit(solution)/shard_map/banded_matrices/pallas_call | solution.py:729
  14.6 1.2 %collective-permute-done.2.even_rim = bf16[96,128]{1,0:T(8,128)(2,1)S(1)} collective-permute-done((bf16[96,128]{1,0:T(8,128)(2,1)S(1)}, bf16[96,128]{1,0:T(8,128)(2,1)S(1)}, u32[]{:S(2)}, u32[]{:S(2)}) %collective-permute-start.2) | collective-permute-done | bytes 24608 | tf_op jit(solution)/shard_map/ppermute | solution.py:720
  15.8 1.6 %collective-permute-done.3.odd_rim = bf16[96,128]{1,0:T(8,128)(2,1)S(1)} collective-permute-done((bf16[96,128]{1,0:T(8,128)(2,1)S(1)}, bf16[96,128]{1,0:T(8,128)(2,1)S(1)}, u32[]{:S(2)}, u32[]{:S(2)}) %collective-permute-start.3) | collective-permute-done | bytes 24608 | tf_op jit(solution)/shard_map/ppermute | solution.py:726
  17.4 0.0 copy-done.2
  17.4 0.0 copy-done.15
  17.4 14.3 %network_and_step.1 = (f32[4,2,32,256]{3,2,1,0:T(8,128)}, f32[4,2,32,256]{3,2,1,0:T(8,128)}, f32[4,2,32,256]{3,2,1,0:T(8,128)}) custom-call(f32[4]{0:T(128)S(1)} %copy-done.15, bf16[5,1088,128]{2,1,0:T(8,128)(2,1)S(1)} %get-tuple-element.14.own, f32[4,2,32,256]{3,2,1,0:T(8,128)S(1)} %copy-done.2, f32[4,2,32,256]{3,2,1,0:T(8,128)S(1)} %copy-done.4, ...), custom_call_target="tpu_custom_call" | custom-call | flops 20000000000 | bytes 10000000 | tf_op jit(solution)/shard_map/network_and_step/pallas_call | solution.py:755
  (16 shorter events, 0.0 us)
Async XLA Ops:
  0.6 16.7 %copy-start.8 = (s32[32,256]{1,0:T(8,128)S(1)}, s32[32,256]{1,0:T(8,128)}, u32[]{:S(2)}) copy-start(s32[32,256]{1,0:T(8,128)} %sea.5) | copy-start | bytes 98308
  0.6 16.7 %copy-start.6 = (f32[4,2,32,256]{3,2,1,0:T(8,128)S(1)}, f32[4,2,32,256]{3,2,1,0:T(8,128)}, u32[]{:S(2)}) copy-start(f32[4,2,32,256]{3,2,1,0:T(8,128)} %h.5) | copy-start | bytes 786436
  0.7 16.7 %copy-start.4 = (f32[4,2,32,256]{3,2,1,0:T(8,128)S(1)}, f32[4,2,32,256]{3,2,1,0:T(8,128)}, u32[]{:S(2)}) copy-start(f32[4,2,32,256]{3,2,1,0:T(8,128)} %v.5) | copy-start | bytes 786436
  0.7 16.7 %copy-start.2 = (f32[4,2,32,256]{3,2,1,0:T(8,128)S(1)}, f32[4,2,32,256]{3,2,1,0:T(8,128)}, u32[]{:S(2)}) copy-start(f32[4,2,32,256]{3,2,1,0:T(8,128)} %u.5) | copy-start | bytes 786436
  0.7 12.8 %copy-start.16 = (bf16[32,10,3,3]{0,3,2,1:T(4,128)(2,1)S(1)}, bf16[32,10,3,3]{0,3,2,1:T(4,128)(2,1)}, u32[]{:S(2)}) copy-start(bf16[32,10,3,3]{0,3,2,1:T(4,128)(2,1)} %param.18) | copy-start | bytes 17284
  0.7 12.9 %copy-start.11 = (bf16[4,32,3,3]{1,0,3,2:T(4,128)(2,1)S(1)}, bf16[4,32,3,3]{1,0,3,2:T(4,128)(2,1)}, u32[]{:S(2)}) copy-start(bf16[4,32,3,3]{1,0,3,2:T(4,128)(2,1)} %param.24) | copy-start | bytes 6916
  0.7 12.9 %copy-start.14 = (f32[32]{0:T(128)S(1)}, f32[32]{0:T(128)}, u32[]{:S(2)}) copy-start(f32[32]{0:T(128)} %param.23) | copy-start | bytes 388
  0.7 12.9 %copy-start.10 = (bf16[32,32,3,3]{1,0,3,2:T(8,128)(2,1)S(1)}, bf16[32,32,3,3]{1,0,3,2:T(8,128)(2,1)}, u32[]{:S(2)}) copy-start(bf16[32,32,3,3]{1,0,3,2:T(8,128)(2,1)} %param.22) | copy-start | bytes 55300
  0.7 12.9 %copy-start.13 = (f32[32]{0:T(128)S(1)}, f32[32]{0:T(128)}, u32[]{:S(2)}) copy-start(f32[32]{0:T(128)} %param.21) | copy-start | bytes 388
  0.7 12.9 %copy-start.9 = (bf16[32,32,3,3]{1,0,3,2:T(8,128)(2,1)S(1)}, bf16[32,32,3,3]{1,0,3,2:T(8,128)(2,1)}, u32[]{:S(2)}) copy-start(bf16[32,32,3,3]{1,0,3,2:T(8,128)(2,1)} %param.20) | copy-start | bytes 55300
  0.7 12.9 %copy-start.12 = (f32[32]{0:T(128)S(1)}, f32[32]{0:T(128)}, u32[]{:S(2)}) copy-start(f32[32]{0:T(128)} %param.19) | copy-start | bytes 388
  0.8 16.6 %copy-start.15 = (f32[4]{0:T(128)S(1)}, f32[4]{0:T(128)}, u32[]{:S(2)}) copy-start(f32[4]{0:T(128)} %bias_last.1) | copy-start | bytes 52
  2.2 9.5 %collective-permute-start = (bf16[192,256]{1,0:T(8,128)(2,1)S(1)}, bf16[192,256]{1,0:T(8,128)(2,1)S(1)}, u32[]{:S(2)}, u32[]{:S(2)}) collective-permute-start(bf16[192,256]{1,0:T(8,128)(2,1)S(1)} %get-tuple-element.15), channel_id=1, source_target_pairs={{0,4},{4,8},{8,12},{12,16},{16,20},{20,24},{24,28},{28,0},{1,5},{5... | collective-permute-start | bytes 294920 | tf_op jit(solution)/shard_map/ppermute | solution.py:687
  2.2 9.5 %collective-permute-start.1 = (bf16[192,256]{1,0:T(8,128)(2,1)S(1)}, bf16[192,256]{1,0:T(8,128)(2,1)S(1)}, u32[]{:S(2)}, u32[]{:S(2)}) collective-permute-start(bf16[192,256]{1,0:T(8,128)(2,1)S(1)} %get-tuple-element.16), channel_id=1, source_target_pairs={{4,0},{8,4},{12,8},{16,12},{20,16},{24,20},{28,24},{0,28},{5,1},{9... | collective-permute-start | bytes 294920 | tf_op jit(solution)/shard_map/ppermute | solution.py:688
  4.9 0.9 %copy-start = (bf16[4,4,32,256]{3,2,1,0:T(8,128)(2,1)S(1)}, bf16[4,4,32,256]{3,2,1,0:T(8,128)(2,1)}, u32[]{:S(2)}) copy-start(bf16[4,4,32,256]{3,2,1,0:T(8,128)(2,1)} %noise.3) | copy-start | bytes 786436
  5.8 0.9 %copy-start.1 = (f32[4,2,32,256]{3,2,1,0:T(8,128)S(1)}, f32[4,2,32,256]{3,2,1,0:T(8,128)}, u32[]{:S(2)}) copy-start(f32[4,2,32,256]{3,2,1,0:T(8,128)} %u.5) | copy-start | bytes 786436
  6.8 0.9 %copy-start.3 = (f32[4,2,32,256]{3,2,1,0:T(8,128)S(1)}, f32[4,2,32,256]{3,2,1,0:T(8,128)}, u32[]{:S(2)}) copy-start(f32[4,2,32,256]{3,2,1,0:T(8,128)} %v.5) | copy-start | bytes 786436
  7.7 0.9 %copy-start.5 = (f32[4,2,32,256]{3,2,1,0:T(8,128)S(1)}, f32[4,2,32,256]{3,2,1,0:T(8,128)}, u32[]{:S(2)}) copy-start(f32[4,2,32,256]{3,2,1,0:T(8,128)} %h.5) | copy-start | bytes 786436
  8.7 0.8 %copy-start.7 = (s32[32,256]{1,0:T(8,128)S(1)}, s32[32,256]{1,0:T(8,128)}, u32[]{:S(2)}) copy-start(s32[32,256]{1,0:T(8,128)} %sea.5) | copy-start | bytes 98308
  11.9 3.9 %collective-permute-start.2 = (bf16[96,128]{1,0:T(8,128)(2,1)S(1)}, bf16[96,128]{1,0:T(8,128)(2,1)S(1)}, u32[]{:S(2)}, u32[]{:S(2)}) collective-permute-start(bf16[96,128]{1,0:T(8,128)(2,1)S(1)} %get-tuple-element.19), channel_id=1, source_target_pairs={{0,1},{1,0},{2,3},{3,2},{4,5},{5,4},{6,7},{7,6},{8,9},{9,8},{10,11... | collective-permute-start | bytes 73736 | tf_op jit(solution)/shard_map/ppermute | solution.py:720
  13.5 3.8 %collective-permute-start.3 = (bf16[96,128]{1,0:T(8,128)(2,1)S(1)}, bf16[96,128]{1,0:T(8,128)(2,1)S(1)}, u32[]{:S(2)}, u32[]{:S(2)}) collective-permute-start(bf16[96,128]{1,0:T(8,128)(2,1)S(1)} %get-tuple-element.20.own_tail), channel_id=1, source_target_pairs={{1,2},{2,1},{0,4},{3,31},{5,6},{6,5},{4,0},{7,27},{9,10},{10,9},{8... | collective-permute-start | bytes 73736 | tf_op jit(solution)/shard_map/ppermute | solution.py:726

commit v5 on v4

--- a/solution.py
+++ b/solution.py
@@ -114,70 +114,89 @@
             dst[tile, pl.ds(start, hi - lo, stride=SUB), :] = buffer[pl.ds(lo - t * LANES, hi - lo), :]
 
 
-def own_kernel(sizes, noise, u, v, h, sea, own, head, tail, cells, turned):
+def shifted_tiles(sizes, refs, m, c, t):
+    noise, u, v, h, sea = refs
+    members, noises, levels = sizes
+    fields = noises + 3 * levels
+    lons = sea.shape[0]
+    lanes = slice(t * LANES, (t + 1) * LANES)
+    if c == fields:
+        full = sea[:, lanes].astype(f32)
+    elif c < noises:
+        full = noise[m, c, :, lanes].astype(f32)
+    else:
+        full = (u, v, h)[(c - noises) // levels][m, (c - noises) % levels, :, lanes]
+    full = pltpu.roll(full, lons - RIM, 0)
+    tiles = [full[g * GROUP : (g + 1) * GROUP] for g in range(lons // GROUP)]
+    return tiles[-1:] + tiles
+
+
+def prepare_kernel(sizes, noise, u, v, h, sea, *refs):
+    weights, refs = refs[:7], refs[7:]
+    held, matrices, (head, tail, done) = refs[:5], refs[5:9], refs[9:]
+    members, noises, levels = sizes
+    fields = noises + 3 * levels
+    lons, lats = sea.shape
+    groups = lons // GROUP + 1
+    copies = [
+        pltpu.make_async_copy(x, y, done.at[n]) for n, (x, y) in enumerate(zip((noise, u, v, h, sea), held))
+    ]
+    for copy in copies:
+        copy.start()
+    weights_kernel(*weights, *matrices)
+    for copy in copies:
+        copy.wait()
+    lane = iota((GROUP, LANES), 1)
+    for out, t, first in ((head, 0, 0), (tail, lats // LANES - 1, LANES - RIM)):
+        for c in range(fields + 1):
+            total = jnp.zeros((GROUP, LANES), f32)
+            for m in range(members):
+                for g, tile in enumerate(shifted_tiles(sizes, held, m, c, t)):
+                    place = (g * members + m) * RIM
+                    moved = pltpu.roll(tile, (place - first) % LANES, 1)
+                    total = jnp.where((lane >= place) & (lane < place + RIM), moved, total)
+                    if noises <= c < fields:
+                        place = groups * members * RIM + g * members + m
+                        edge = 0 if out is head else LANES - 1
+                        moved = pltpu.roll(rest(tile), (place - edge) % LANES, 1)
+                        total = jnp.where(lane == place, moved, total)
+            out[pl.ds(c * GROUP, GROUP)] = total
+        for c in range(fields + 1, out.shape[0] // GROUP):
+            out[pl.ds(c * GROUP, GROUP)] = jnp.zeros((GROUP, LANES), f32)
+
+
+def cells_kernel(sizes, noise, u, v, h, sea, left, right, after, out, rims, cells, turned):
     members, noises, levels = sizes
     fields = noises + 3 * levels
     lons, lats = sea.shape
     groups = lons // GROUP + 1
     chunks = SUB // members
+    rows = cells.shape[1]
     gap_k = lats - (chunks - 1) * ((lats + GAP) // chunks)
-    lane = iota((GROUP, LANES), 1)
+    rims[0] = left[...].astype(f32)
+    rims[1] = right[...].astype(f32)
     for m in range(members):
         for g in range(groups):
             empty = pl.ds(gap_k * SUB + (m + 1) * chunks - 1, GAP, stride=SUB)
             cells[g, empty, :] = jnp.zeros((GAP, LANES), f32)
-
-    def tiles_of(m, c, t):
+    blank = jnp.zeros((GROUP, LANES), f32)
+    upper = iota((GROUP, LANES), 0) < RIM
+    for t in range(lats // LANES):
         lanes = slice(t * LANES, (t + 1) * LANES)
-        if c == fields:
-            full = sea[:, lanes].astype(f32)
-        elif c < noises:
-            full = noise[m, c, :, lanes].astype(f32)
-        else:
-            full = (u, v, h)[(c - noises) // levels][m, (c - noises) % levels, :, lanes]
-        full = pltpu.roll(full, lons - RIM, 0)
-        tiles = [full[g * GROUP : (g + 1) * GROUP] for g in range(groups - 1)]
-        return tiles[-1:] + tiles
-
-    last = lats // LANES - 1
-    lows = [jnp.zeros((GROUP, LANES), f32)] * (fields + 1)
-    highs = [jnp.zeros((GROUP, LANES), f32)] * (fields + 1)
-    blank = jnp.zeros((GROUP, LANES), f32)
-    for t in range(last + 1):
         for m in range(members):
-            tiles = [tiles_of(m, c, t) for c in range(fields + 1)]
+            tiles = []
+            for c in range(fields + 1):
+                groups_of = shifted_tiles(sizes, (noise, u, v, h, sea), m, c, t)
+                ends = [rim_tile(sizes, m, c, side, rims.at[side, :, lanes]) for side in range(2)]
+                groups_of[0] = jnp.where(upper, ends[0], groups_of[0])
+                groups_of[-1] = jnp.where(upper, groups_of[-1], ends[1])
+                tiles.append(groups_of)
             for g in range(groups):
-                after = g + 1 if g + 1 < groups else None
-                block = window(
-                    [tiles[c][g] for c in range(fields)],
-                    [blank if after is None else tiles[c][after] for c in range(fields)],
-                    tiles[fields][g],
-                    blank if after is None else tiles[fields][after],
-                )
+                following = [x[g + 1] if g + 1 < groups else blank for x in tiles]
+                block = window([x[g] for x in tiles[:fields]], following[:fields], tiles[fields][g], following[fields])
                 store_lats(block, t, cells, g, m, lats, chunks, turned.at[(t * members + m) * groups + g])
-            for c in range(fields + 1):
-                for g in range(groups):
-                    place = (g * members + m) * RIM
-                    spot = (lane >= place) & (lane < place + RIM)
-                    other = groups * members * RIM + g * members + m
-                    if t == 0:
-                        lows[c] = jnp.where(spot, pltpu.roll(tiles[c][g], place, 1), lows[c])
-                        moved = pltpu.roll(rest(tiles[c][g]), other, 1)
-                        lows[c] = jnp.where(lane == other, moved, lows[c])
-                    if t == last:
-                        first = LANES - RIM
-                        moved = pltpu.roll(tiles[c][g], (place - first) % LANES, 1)
-                        highs[c] = jnp.where(spot, moved, highs[c])
-                        moved = pltpu.roll(rest(tiles[c][g]), (other + 1) % LANES, 1)
-                        highs[c] = jnp.where(lane == other, moved, highs[c])
-    for c in range(fields + 1):
-        head[pl.ds(c * GROUP, GROUP)] = lows[c]
-        tail[pl.ds(c * GROUP, GROUP)] = highs[c]
-    for c in range(fields + 1, head.shape[0] // GROUP):
-        head[pl.ds(c * GROUP, GROUP)] = blank
-        tail[pl.ds(c * GROUP, GROUP)] = blank
     for g in range(groups):
-        own[g] = cells[g].astype(bf16)
+        out[g] = cells[g].astype(bf16)
 
 
 def join_kernel(sizes, lons, left, right, head, tail, even, odd, rims, wide):
@@ -344,13 +363,11 @@
     new_h,
     left,
     right,
-    cells,
     first,
     odd,
     even,
     force,
     gathered,
-    buffers,
     turned,
     gaps,
     results,
@@ -410,26 +427,9 @@
                 start = n * RIM * SUB + gap * chunks + chunks - 1
                 gaps[g, pl.ds(start, RIM, stride=SUB), :] = turned[n, pl.ds((g * members + m) * RIM, RIM), :]
 
-    blank = jnp.zeros((GROUP, LANES), f32)
-    for t in range(lats // LANES):
-        lanes = slice(t * LANES, (t + 1) * LANES)
-        for side, rim in enumerate((left, right)):
-            for m in range(members):
-                tiles = [rim_tile(sizes, m, c, side, rim.at[:, lanes]) for c in range(fields + 1)]
-                block = window(tiles[:fields], [blank] * fields, tiles[fields], blank)
-                buffer = buffers.at[(t * 2 + side) * members + m]
-                store_lats(block, t, cells, side, m, lats, chunks, buffer)
-
     in_gap = iota((GAP * SUB, LANES), 0) % chunks == chunks - 1
-    at_lane = iota((rows, LANES), 1)
-    holds_lon = (at_lane < fields * GROUP) | (at_lane // GROUP == LANES // GROUP - 3)
     for g in range(groups):
-        if g in (0, groups - 1):
-            side = g // (groups - 1)
-            from_rim = holds_lon & ((at_lane % GROUP < RIM) if side == 0 else (at_lane % GROUP >= RIM))
-            first[g, pl.ds(SUB, rows), :] = jnp.where(from_rim, cells[side], own[g].astype(f32)).astype(bf16)
-        else:
-            first[g, pl.ds(SUB, rows), :] = own[g]
+        first[g, pl.ds(SUB, rows), :] = own[g]
         spot = pl.ds((1 + gap_k) * SUB, GAP * SUB)
         kept = first[g, spot, :].astype(f32)
         first[g, spot, :] = jnp.where(in_gap, gaps[g], kept).astype(bf16)
@@ -441,7 +441,7 @@
     hidden = LANES // 4
     per = LANES // hidden
     tiles = odd.shape[0]
-    cuts = 2
+    cuts = 4
     step = rows // cuts
     lower = iota((step, LANES), 1) < 2 * hidden
 
@@ -690,19 +690,34 @@
     wide = -(-(fields + 1) * GROUP // SUB) * SUB
     part = pltpu.VMEM((wide, LANES), f32)
     message = pltpu.VMEM((wide, LANES), bf16)
-    own, own_head, own_tail = pl.pallas_call(
-        functools.partial(own_kernel, sizes),
-        out_shape=[pltpu.VMEM((groups, rows, LANES), bf16), part, part],
-        in_specs=[whole] * 5,
-        out_specs=[whole] * 3,
-        scratch_shapes=[
-            pltpu.VMEM((groups, rows, LANES), f32),
-            pltpu.VMEM((members * groups * lats // LANES, LANES, LANES), f32),
-        ],
+    deep = -(-(lons // 2 + 2) * hidden // LANES) * LANES
+    noise, velocity_u, velocity_v, thickness, land_sea, t1, t2, t3, t4, own_head, own_tail = pl.pallas_call(
+        functools.partial(prepare_kernel, sizes),
+        out_shape=[pltpu.VMEM(x.shape, x.dtype) for x in state]
+        + [
+            pltpu.VMEM((3 * LANES, 2 * LANES), bf16),
+            pltpu.VMEM((8 * LANES, 2 * LANES), bf16),
+            pltpu.VMEM((8 * LANES, 2 * LANES), bf16),
+            pltpu.VMEM((2, deep, 2 * LANES), bf16),
+        ]
+        + [part, part],
+        in_specs=[pl.BlockSpec(memory_space=pltpu.HBM)] * 5 + [whole] * 7,
+        out_specs=[whole] * 11,
+        scratch_shapes=[pltpu.SemaphoreType.DMA((5,))],
         compiler_params=pltpu.CompilerParams(vmem_limit_bytes=8 * 2**20),
         cost_estimate=pl.CostEstimate(flops=10**7, bytes_accessed=10**7, transcendentals=0),
-        name="own_cells",
-    )(*state)
+        name="prepare",
+    )(
+        *state,
+        conv_first.transpose(3, 2, 1, 0),
+        conv_second.transpose(2, 3, 0, 1),
+        conv_third.transpose(2, 3, 0, 1),
+        conv_last.transpose(2, 3, 0, 1),
+        bias_first[None],
+        bias_second[None],
+        bias_third[None],
+    )
+    state = (noise, velocity_u, velocity_v, thickness, land_sea)
     last = lat_count - 1
     smem = pl.BlockSpec(memory_space=pltpu.SMEM)
     to_even, to_odd = pl.pallas_call(
@@ -725,29 +740,20 @@
         pairs += [(at, (t ^ 1) * lat_count), (at + last, (lon_count - 1 - t) * lat_count + last)]
     odd_rim = lax.ppermute(to_odd, ("lon", "lat"), pairs)
 
-    deep = -(-(lons // 2 + 2) * hidden // LANES) * LANES
-    t1, t2, t3, t4 = pl.pallas_call(
-        weights_kernel,
-        out_shape=[
-            pltpu.VMEM((3 * LANES, 2 * LANES), bf16),
-            pltpu.VMEM((8 * LANES, 2 * LANES), bf16),
-            pltpu.VMEM((8 * LANES, 2 * LANES), bf16),
-            pltpu.VMEM((2, deep, 2 * LANES), bf16),
+    own = pl.pallas_call(
+        functools.partial(cells_kernel, sizes),
+        out_shape=pltpu.VMEM((groups, rows, LANES), bf16),
+        in_specs=[whole] * 8,
+        out_specs=whole,
+        scratch_shapes=[
+            pltpu.VMEM((2, tall, lats), f32),
+            pltpu.VMEM((groups, rows, LANES), f32),
+            pltpu.VMEM((members * groups * lats // LANES, LANES, LANES), f32),
         ],
-        in_specs=[whole] * 7,
-        out_specs=[whole] * 4,
-        compiler_params=pltpu.CompilerParams(vmem_limit_bytes=8 * 2**20),
-        cost_estimate=pl.CostEstimate(flops=10**7, bytes_accessed=3 * 10**6, transcendentals=0),
-        name="banded_matrices",
-    )(
-        conv_first.transpose(3, 2, 1, 0),
-        conv_second.transpose(2, 3, 0, 1),
-        conv_third.transpose(2, 3, 0, 1),
-        conv_last.transpose(2, 3, 0, 1),
-        bias_first[None],
-        bias_second[None],
-        bias_third[None],
-    )
+        compiler_params=pltpu.CompilerParams(vmem_limit_bytes=12 * 2**20),
+        cost_estimate=pl.CostEstimate(flops=10**7, bytes_accessed=10**7, transcendentals=0),
+        name="cells",
+    )(*state, left, right, to_even)
 
     padded = rows + 2 * SUB
     tiles = 2 * groups + 1
@@ -760,13 +766,11 @@
         scratch_shapes=[
             pltpu.VMEM((tall, lats), f32),
             pltpu.VMEM((tall, lats), f32),
-            pltpu.VMEM((2, rows, LANES), f32),
             pltpu.VMEM((groups, padded, LANES), bf16),
             pltpu.VMEM((tiles, padded, LANES), bf16),
             pltpu.VMEM((tiles, padded, LANES), bf16),
             pltpu.VMEM((3, padded, LANES), f32),
             pltpu.VMEM((members, lats, LANES), f32),
-            pltpu.VMEM((2 * members * lats // LANES, LANES, LANES), f32),
             pltpu.VMEM((4, LANES, LANES), f32),
             pltpu.VMEM((groups, GAP * SUB, LANES), f32),
             pltpu.VMEM((3, *velocity_u.shape), f32),

time: 32.2 us -> 36.7 us (1.14)
  local copies, waits for them, and re-layouts: 4.62 us -> 9.75 us
  waiting for transfers between devices: 2.8 us -> 2.21 us
    unnamed x35 -> x25, local copies, waits for them, and re-layouts: 4.62 us -> 9.75 us
    ppermute x1, waiting for transfers between devices: 1.22 us -> 0.63 us  [body(): lax.ppermute(to_even, 'lat', [(i, i ^ 1) for i in range(lat_count)])]
  transfers between devices with their start and end apart: 4 -> 4, of which waited for: 2 -> 2; matrix products, arithmetic and copies ran while one was open for 0% -> 2% of each run, Pallas kernels for 10% -> 9%
where the time goes in v5:
time: 36.7 us; the launch traced here: 36.1 us
  Pallas kernels  18.9 us (51%)
  local copies, waits for them, and re-layouts  9.75 us (27%)
  starting transfers between devices  4.33 us (12%)
  waiting for transfers between devices  2.21 us (6%)
  between operations  0.87 us (2%)
    pallas_call x1, Pallas kernels, body(): pl.pallas_call(functools.partial(main_kernel, sizes), out_shape=[out] * 3...  14.1 us
    unnamed x25, local copies, waits for them, and re-layouts  9.75 us
    ppermute x1, starting transfers between devices, body(): right = lax.ppermute(head, 'lon', [(b, a) for a, b in ring])  2.63 us
    pallas_call x1, Pallas kernels, body(): pl.pallas_call(functools.partial(prepare_kernel, sizes), out_shape=[pltpu...  1.79 us
    ppermute x1, starting transfers between devices, body(): lax.ppermute(to_even, 'lat', [(i, i ^ 1) for i in range(lat_count)])  1.64 us
    pallas_call x1, Pallas kernels, body(): pl.pallas_call(functools.partial(cells_kernel, sizes), out_shape=pltpu.VM...  1.61 us
    ppermute x1, waiting for transfers between devices, body(): odd_rim = lax.ppermute(to_odd, ('lon', 'lat'), pairs)  1.58 us
    pallas_call x1, Pallas kernels, body(): pl.pallas_call(functools.partial(pack_lon_kernel, sizes), out_shape=[pltp...  1.3 us
  transfers between devices with their start and end apart: 4, of which 2 were waited for; matrix products, arithmetic and copies ran while one was open for 2% of the time, Pallas kernels for 9%

profile of v5, /device:TPU:20, one launch (start us, length us, event | category | flops | bytes accessed | tf_op | source)
XLA Modules:
  0.0 36.1 jit_solution(17781148026387667506)
XLA Ops:
  0.6 1.3 %pack_lon.1 = (bf16[192,256]{1,0:T(8,128)(2,1)S(1)}, bf16[192,256]{1,0:T(8,128)(2,1)S(1)}) custom-call(bf16[4,4,32,256]{3,2,1,0:T(8,128)(2,1)} %noise.3, f32[4,2,32,256]{3,2,1,0:T(8,128)} %u.3, f32[4,2,32,256]{3,2,1,0:T(8,128)} %v.3, f32[4,2,32,256]{3,2,1,0:T(8,128)} %h.3, s32[32,256]{1,0:T(8,128)} %sea.3), custom_call_target="tpu_custom_call" | custom-call | tf_op jit(solution)/shard_map/pack_lon/pallas_call | solution.py:672
  1.9 0.1 collective-permute-start
  2.0 2.6 %collective-permute-start.1 = (bf16[192,256]{1,0:T(8,128)(2,1)S(1)}, bf16[192,256]{1,0:T(8,128)(2,1)S(1)}, u32[]{:S(2)}, u32[]{:S(2)}) collective-permute-start(bf16[192,256]{1,0:T(8,128)(2,1)S(1)} %get-tuple-element.24), channel_id=1, source_target_pairs={{4,0},{8,4},{12,8},{16,12},{20,16},{24,20},{28,24},{0,28},{5,1},{9... | collective-permute-start | bytes 294920 | tf_op jit(solution)/shard_map/ppermute | solution.py:688
  4.6 0.8 %copy.18 = bf16[32,10,3,3]{0,1,2,3:T(8,128)(2,1)S(1)} copy(bf16[32,10,3,3]{0,3,2,1:T(4,128)(2,1)} %param.18) | data formatting | bytes 11520 | tf_op args[5]
  5.4 0.0 copy-start
  5.4 0.9 %copy-done = bf16[4,4,32,256]{3,2,1,0:T(8,128)(2,1)S(1)} copy-done((bf16[4,4,32,256]{3,2,1,0:T(8,128)(2,1)S(1)}, bf16[4,4,32,256]{3,2,1,0:T(8,128)(2,1)}, u32[]{:S(2)}) %copy-start) | copy-done | bytes 262168
  6.3 0.0 copy-start.1
  6.3 0.9 %copy-done.1 = f32[4,2,32,256]{3,2,1,0:T(8,128)S(1)} copy-done((f32[4,2,32,256]{3,2,1,0:T(8,128)S(1)}, f32[4,2,32,256]{3,2,1,0:T(8,128)}, u32[]{:S(2)}) %copy-start.1) | copy-done | bytes 262168
  7.3 0.0 copy-start.2
  7.3 0.9 %copy-done.2 = f32[4,2,32,256]{3,2,1,0:T(8,128)S(1)} copy-done((f32[4,2,32,256]{3,2,1,0:T(8,128)S(1)}, f32[4,2,32,256]{3,2,1,0:T(8,128)}, u32[]{:S(2)}) %copy-start.2) | copy-done | bytes 262168
  8.2 0.0 copy-start.3
  8.2 0.9 %copy-done.3 = f32[4,2,32,256]{3,2,1,0:T(8,128)S(1)} copy-done((f32[4,2,32,256]{3,2,1,0:T(8,128)S(1)}, f32[4,2,32,256]{3,2,1,0:T(8,128)}, u32[]{:S(2)}) %copy-start.3) | copy-done | bytes 262168
  9.2 0.0 copy-start.4
  9.2 0.8 %copy-done.4 = s32[32,256]{1,0:T(8,128)S(1)} copy-done((s32[32,256]{1,0:T(8,128)S(1)}, s32[32,256]{1,0:T(8,128)}, u32[]{:S(2)}) %copy-start.4) | copy-done | bytes 32792
  10.0 0.9 %copy-done.5 = bf16[32,32,3,3]{1,0,3,2:T(8,128)(2,1)S(1)} copy-done((bf16[32,32,3,3]{1,0,3,2:T(8,128)(2,1)S(1)}, bf16[32,32,3,3]{1,0,3,2:T(8,128)(2,1)}, u32[]{:S(2)}) %copy-start.5) | copy-done | bytes 18456
  10.8 0.9 %copy-done.6 = bf16[32,32,3,3]{1,0,3,2:T(8,128)(2,1)S(1)} copy-done((bf16[32,32,3,3]{1,0,3,2:T(8,128)(2,1)S(1)}, bf16[32,32,3,3]{1,0,3,2:T(8,128)(2,1)}, u32[]{:S(2)}) %copy-start.6) | copy-done | bytes 18456
  11.7 0.7 %copy-done.7 = bf16[4,32,3,3]{1,0,3,2:T(4,128)(2,1)S(1)} copy-done((bf16[4,32,3,3]{1,0,3,2:T(4,128)(2,1)S(1)}, bf16[4,32,3,3]{1,0,3,2:T(4,128)(2,1)}, u32[]{:S(2)}) %copy-start.7) | copy-done | bytes 2328
  12.4 0.7 %copy-done.8 = f32[32]{0:T(128)S(1)} copy-done((f32[32]{0:T(128)S(1)}, f32[32]{0:T(128)}, u32[]{:S(2)}) %copy-start.8) | copy-done | bytes 152
  13.1 0.7 %copy-done.9 = f32[32]{0:T(128)S(1)} copy-done((f32[32]{0:T(128)S(1)}, f32[32]{0:T(128)}, u32[]{:S(2)}) %copy-start.9) | copy-done | bytes 152
  13.7 0.7 %copy-done.10 = f32[32]{0:T(128)S(1)} copy-done((f32[32]{0:T(128)S(1)}, f32[32]{0:T(128)}, u32[]{:S(2)}) %copy-start.10) | copy-done | bytes 152
  14.4 1.8 %prepare.1 = (bf16[4,4,32,256]{3,2,1,0:T(8,128)(2,1)S(1)}, f32[4,2,32,256]{3,2,1,0:T(8,128)S(1)}, f32[4,2,32,256]{3,2,1,0:T(8,128)S(1)}, f32[4,2,32,256]{3,2,1,0...) custom-call(bf16[4,4,32,256]{3,2,1,0:T(8,128)(2,1)S(1)} %copy-done, ...), custom_call_target="tpu_custom_call" | custom-call | flops 10000000 | bytes 10000000 | tf_op jit(solution)/shard_map/prepare/pallas_call | solution.py:694
  16.2 0.0 collective-permute-done.left.left_in
  16.2 0.0 collective-permute-done.1.right.right_in
  16.2 0.2 join_rims.1
  16.4 0.0 copy-start.11
  16.4 1.6 %collective-permute-start.2 = (bf16[96,128]{1,0:T(8,128)(2,1)S(1)}, bf16[96,128]{1,0:T(8,128)(2,1)S(1)}, u32[]{:S(2)}, u32[]{:S(2)}) collective-permute-start(bf16[96,128]{1,0:T(8,128)(2,1)S(1)} %get-tuple-element.27.after), channel_id=1, source_target_pairs={{0,1},{1,0},{2,3},{3,2},{4,5},{5,4},{6,7},{7,6},{8,9},{9,8},{10,11... | collective-permute-start | bytes 73736 | tf_op jit(solution)/shard_map/ppermute | solution.py:735
  18.0 0.0 collective-permute-start.3
  18.0 1.6 %cells.1.own = bf16[5,1088,128]{2,1,0:T(8,128)(2,1)S(1)} custom-call(bf16[4,4,32,256]{3,2,1,0:T(8,128)(2,1)S(1)} %get-tuple-element.18.noise, f32[4,2,32,256]{3,2,1,0:T(8,128)S(1)} %get-tuple-element.19.u, f32[4,2,32,256]{3,2,1,0:T(8,128)S(1)} %get-tuple-element.20.v, f32[4,2,32,256]{3,2,1,0:T(8,128)S(1)} %get-tuple-element.21.h, ...), custom_call_target="tpu_custom_call" | custom-call | flops 10000000 | bytes 10000000 | tf_op jit(solution)/shard_map/cells/pallas_call | solution.py:743
  19.6 0.6 %collective-permute-done.2.even_rim = bf16[96,128]{1,0:T(8,128)(2,1)S(1)} collective-permute-done((bf16[96,128]{1,0:T(8,128)(2,1)S(1)}, bf16[96,128]{1,0:T(8,128)(2,1)S(1)}, u32[]{:S(2)}, u32[]{:S(2)}) %collective-permute-start.2) | collective-permute-done | bytes 24608 | tf_op jit(solution)/shard_map/ppermute | solution.py:735
  20.3 1.6 %collective-permute-done.3.odd_rim = bf16[96,128]{1,0:T(8,128)(2,1)S(1)} collective-permute-done((bf16[96,128]{1,0:T(8,128)(2,1)S(1)}, bf16[96,128]{1,0:T(8,128)(2,1)S(1)}, u32[]{:S(2)}, u32[]{:S(2)}) %collective-permute-start.3) | collective-permute-done | bytes 24608 | tf_op jit(solution)/shard_map/ppermute | solution.py:741
  21.9 0.0 copy-done.11
  21.9 14.1 %network_and_step.1 = (f32[4,2,32,256]{3,2,1,0:T(8,128)}, f32[4,2,32,256]{3,2,1,0:T(8,128)}, f32[4,2,32,256]{3,2,1,0:T(8,128)}) custom-call(f32[4]{0:T(128)S(1)} %copy-done.11, bf16[5,1088,128]{2,1,0:T(8,128)(2,1)S(1)} %cells.1.own, f32[4,2,32,256]{3,2,1,0:T(8,128)S(1)} %get-tuple-element.19.u, f32[4,2,32,256]{3,2,1,0:T(8,128)S(1)} %get-tuple-element.20.v, ...), custom_call_target="tpu_custom_call" | custom-call | flops 20000000000 | bytes 10000000 | tf_op jit(solution)/shard_map/network_and_step/pallas_call | solution.py:761
  (6 shorter events, 0.0 us)
Async XLA Ops:
  1.9 14.3 %collective-permute-start = (bf16[192,256]{1,0:T(8,128)(2,1)S(1)}, bf16[192,256]{1,0:T(8,128)(2,1)S(1)}, u32[]{:S(2)}, u32[]{:S(2)}) collective-permute-start(bf16[192,256]{1,0:T(8,128)(2,1)S(1)} %get-tuple-element.23), channel_id=1, source_target_pairs={{0,4},{4,8},{8,12},{12,16},{16,20},{20,24},{24,28},{28,0},{1,5},{5... | collective-permute-start | bytes 294920 | tf_op jit(solution)/shard_map/ppermute | solution.py:687
  2.0 14.2 %collective-permute-start.1 = (bf16[192,256]{1,0:T(8,128)(2,1)S(1)}, bf16[192,256]{1,0:T(8,128)(2,1)S(1)}, u32[]{:S(2)}, u32[]{:S(2)}) collective-permute-start(bf16[192,256]{1,0:T(8,128)(2,1)S(1)} %get-tuple-element.24), channel_id=1, source_target_pairs={{4,0},{8,4},{12,8},{16,12},{20,16},{24,20},{28,24},{0,28},{5,1},{9... | collective-permute-start | bytes 294920 | tf_op jit(solution)/shard_map/ppermute | solution.py:688
  5.4 0.9 %copy-start = (bf16[4,4,32,256]{3,2,1,0:T(8,128)(2,1)S(1)}, bf16[4,4,32,256]{3,2,1,0:T(8,128)(2,1)}, u32[]{:S(2)}) copy-start(bf16[4,4,32,256]{3,2,1,0:T(8,128)(2,1)} %noise.3) | copy-start | bytes 786436
  6.3 0.9 %copy-start.1 = (f32[4,2,32,256]{3,2,1,0:T(8,128)S(1)}, f32[4,2,32,256]{3,2,1,0:T(8,128)}, u32[]{:S(2)}) copy-start(f32[4,2,32,256]{3,2,1,0:T(8,128)} %u.3) | copy-start | bytes 786436
  7.3 0.9 %copy-start.2 = (f32[4,2,32,256]{3,2,1,0:T(8,128)S(1)}, f32[4,2,32,256]{3,2,1,0:T(8,128)}, u32[]{:S(2)}) copy-start(f32[4,2,32,256]{3,2,1,0:T(8,128)} %v.3) | copy-start | bytes 786436
  8.2 0.9 %copy-start.3 = (f32[4,2,32,256]{3,2,1,0:T(8,128)S(1)}, f32[4,2,32,256]{3,2,1,0:T(8,128)}, u32[]{:S(2)}) copy-start(f32[4,2,32,256]{3,2,1,0:T(8,128)} %h.3) | copy-start | bytes 786436
  9.2 0.8 %copy-start.4 = (s32[32,256]{1,0:T(8,128)S(1)}, s32[32,256]{1,0:T(8,128)}, u32[]{:S(2)}) copy-start(s32[32,256]{1,0:T(8,128)} %sea.3) | copy-start | bytes 98308
  10.0 0.9 %copy-start.5 = (bf16[32,32,3,3]{1,0,3,2:T(8,128)(2,1)S(1)}, bf16[32,32,3,3]{1,0,3,2:T(8,128)(2,1)}, u32[]{:S(2)}) copy-start(bf16[32,32,3,3]{1,0,3,2:T(8,128)(2,1)} %param.20) | copy-start | bytes 55300
  10.8 0.9 %copy-start.6 = (bf16[32,32,3,3]{1,0,3,2:T(8,128)(2,1)S(1)}, bf16[32,32,3,3]{1,0,3,2:T(8,128)(2,1)}, u32[]{:S(2)}) copy-start(bf16[32,32,3,3]{1,0,3,2:T(8,128)(2,1)} %param.22) | copy-start | bytes 55300
  11.7 0.7 %copy-start.7 = (bf16[4,32,3,3]{1,0,3,2:T(4,128)(2,1)S(1)}, bf16[4,32,3,3]{1,0,3,2:T(4,128)(2,1)}, u32[]{:S(2)}) copy-start(bf16[4,32,3,3]{1,0,3,2:T(4,128)(2,1)} %param.24) | copy-start | bytes 6916
  12.4 0.7 %copy-start.8 = (f32[32]{0:T(128)S(1)}, f32[32]{0:T(128)}, u32[]{:S(2)}) copy-start(f32[32]{0:T(128)} %param.19) | copy-start | bytes 388
  13.1 0.7 %copy-start.9 = (f32[32]{0:T(128)S(1)}, f32[32]{0:T(128)}, u32[]{:S(2)}) copy-start(f32[32]{0:T(128)} %param.21) | copy-start | bytes 388
  13.7 0.7 %copy-start.10 = (f32[32]{0:T(128)S(1)}, f32[32]{0:T(128)}, u32[]{:S(2)}) copy-start(f32[32]{0:T(128)} %param.23) | copy-start | bytes 388
  16.4 5.5 %copy-start.11 = (f32[4]{0:T(128)S(1)}, f32[4]{0:T(128)}, u32[]{:S(2)}) copy-start(f32[4]{0:T(128)} %bias_last.1) | copy-start | bytes 52
  16.4 3.9 %collective-permute-start.2 = (bf16[96,128]{1,0:T(8,128)(2,1)S(1)}, bf16[96,128]{1,0:T(8,128)(2,1)S(1)}, u32[]{:S(2)}, u32[]{:S(2)}) collective-permute-start(bf16[96,128]{1,0:T(8,128)(2,1)S(1)} %get-tuple-element.27.after), channel_id=1, source_target_pairs={{0,1},{1,0},{2,3},{3,2},{4,5},{5,4},{6,7},{7,6},{8,9},{9,8},{10,11... | collective-permute-start | bytes 73736 | tf_op jit(solution)/shard_map/ppermute | solution.py:735
  18.0 3.8 %collective-permute-start.3 = (bf16[96,128]{1,0:T(8,128)(2,1)S(1)}, bf16[96,128]{1,0:T(8,128)(2,1)S(1)}, u32[]{:S(2)}, u32[]{:S(2)}) collective-permute-start(bf16[96,128]{1,0:T(8,128)(2,1)S(1)} %get-tuple-element.28.own_tail), channel_id=1, source_target_pairs={{1,2},{2,1},{0,4},{3,31},{5,6},{6,5},{4,0},{7,27},{9,10},{10,9},{8... | collective-permute-start | bytes 73736 | tf_op jit(solution)/shard_map/ppermute | solution.py:741

commit v6 on v5

--- a/solution.py
+++ b/solution.py
@@ -36,30 +36,25 @@
     return x - x.astype(bf16).astype(f32)
 
 
-def pack_lon_kernel(sizes, noise, u, v, h, sea, head, tail, noises_in, states, seas, wide, done):
+def pack_lon_kernel(sizes, count, *refs):
+    sources, held, (head, tail, wide, done) = refs[:count], refs[count : 2 * count], refs[2 * count :]
     members, noises, levels = sizes
     fields = noises + 3 * levels
+    noise, u, v, h, sea = held[:5]
     lons, lats = sea.shape
-    copies = [pltpu.make_async_copy(noise, noises_in, done.at[0])]
-    for side in range(2):
-        at = pl.ds(side * (lons - GROUP), GROUP)
-        copies.append(pltpu.make_async_copy(sea.at[at], seas.at[side], done.at[1 + 4 * side]))
-        for n, x in enumerate((u, v, h)):
-            copies.append(
-                pltpu.make_async_copy(x.at[:, :, at], states.at[side, n], done.at[2 + 4 * side + n])
-            )
+    copies = [pltpu.make_async_copy(x, y, done.at[n]) for n, (x, y) in enumerate(zip(sources, held))]
     for copy in copies:
         copy.start()
-    for copy in copies:
+    for copy in copies[:5]:
         copy.wait()
     upper = iota((GROUP, lats), 0) < RIM
 
     def field(m, c, side):
         if c < noises:
-            full = noises_in[m, c].astype(f32)
+            full = noise[m, c].astype(f32)
             return full[-GROUP:] if side else full[:GROUP]
         c -= noises
-        return states[side, c // levels, m, c % levels]
+        return (u, v, h)[c // levels][m, c % levels, pl.ds(side * (lons - GROUP), GROUP)]
 
     rests = members * fields * RIM + GROUP
     for m in range(members):
@@ -72,10 +67,13 @@
             wide[0, row] = rest(field(m, c, 0)[:1])
             wide[1, row] = rest(field(m, c, 1)[GROUP - 1 :])
     rows = pl.ds(members * fields * RIM, GROUP)
-    wide[0, rows] = jnp.where(upper, seas[0].astype(f32), 0.0)
-    wide[1, rows] = jnp.where(upper, pltpu.roll(seas[1].astype(f32), RIM, 0), 0.0)
+    ends = [sea[pl.ds(side * (lons - GROUP), GROUP)].astype(f32) for side in range(2)]
+    wide[0, rows] = jnp.where(upper, ends[0], 0.0)
+    wide[1, rows] = jnp.where(upper, pltpu.roll(ends[1], RIM, 0), 0.0)
     head[...] = wide[0].astype(bf16)
     tail[...] = wide[1].astype(bf16)
+    for copy in copies[5:]:
+        copy.wait()
 
 
 def rim_tile(sizes, m, c, side, rim):
@@ -132,20 +130,13 @@
 
 
 def prepare_kernel(sizes, noise, u, v, h, sea, *refs):
-    weights, refs = refs[:7], refs[7:]
-    held, matrices, (head, tail, done) = refs[:5], refs[5:9], refs[9:]
+    weights, matrices, (head, tail) = refs[:7], refs[7:11], refs[11:]
+    held = (noise, u, v, h, sea)
     members, noises, levels = sizes
     fields = noises + 3 * levels
     lons, lats = sea.shape
     groups = lons // GROUP + 1
-    copies = [
-        pltpu.make_async_copy(x, y, done.at[n]) for n, (x, y) in enumerate(zip((noise, u, v, h, sea), held))
-    ]
-    for copy in copies:
-        copy.start()
     weights_kernel(*weights, *matrices)
-    for copy in copies:
-        copy.wait()
     lane = iota((GROUP, LANES), 1)
     for out, t, first in ((head, 0, 0), (tail, lats // LANES - 1, LANES - RIM)):
         for c in range(fields + 1):
@@ -165,7 +156,7 @@
             out[pl.ds(c * GROUP, GROUP)] = jnp.zeros((GROUP, LANES), f32)
 
 
-def cells_kernel(sizes, noise, u, v, h, sea, left, right, after, out, rims, cells, turned):
+def cells_kernel(sizes, noise, u, v, h, sea, left, right, after, out, base, rims, cells, turned):
     members, noises, levels = sizes
     fields = noises + 3 * levels
     lons, lats = sea.shape
@@ -197,6 +188,58 @@
                 store_lats(block, t, cells, g, m, lats, chunks, turned.at[(t * members + m) * groups + g])
     for g in range(groups):
         out[g] = cells[g].astype(bf16)
+    step_kernel(sizes, u, v, h, sea, rims, base)
+
+
+def step_kernel(sizes, u, v, h, sea, rims, base):
+    members, noises, levels = sizes
+    fields = noises + 3 * levels
+    lons, lats = sea.shape
+    ocean = sea[...].astype(f32)
+    lat_count = lax.axis_size("lat")
+    lat_rows = (lax.axis_index("lat") * lats).astype(f32) + iota((lons, lats), 1).astype(f32)
+    turn = CORIOLIS * (2.0 * (lat_rows + 0.5) / (lats * lat_count) - 1.0)
+    at_first = iota((lons, lats), 0) == 0
+    at_last = iota((lons, lats), 0) == lons - 1
+    at_south = iota((lons, lats), 1) == 0
+    at_north = iota((lons, lats), 1) == lats - 1
+    lon_rests = members * fields * RIM + GROUP
+
+    def around(x, m, c):
+        row = (m * fields + c) * RIM
+        more = lon_rests + m * (fields - noises) + c - noises
+        west = rims[0, pl.ds(row + RIM - 1, 1)] + rims[0, pl.ds(more, 1)]
+        east = rims[1, pl.ds(row, 1)] + rims[1, pl.ds(more, 1)]
+        return (
+            jnp.where(at_first, west, pltpu.roll(x, 1, 0)),
+            jnp.where(at_last, east, pltpu.roll(x, lons - 1, 0)),
+            jnp.where(at_south, 0.0, pltpu.roll(x, 1, 1)),
+            jnp.where(at_north, 0.0, pltpu.roll(x, lats - 1, 1)),
+        )
+
+    for m in range(members):
+        sets = []
+        for level in range(levels):
+            sets.append(
+                [
+                    (x[m, level], around(x[m, level], m, noises + n * levels + level))
+                    for n, x in enumerate((u, v, h))
+                ]
+            )
+        for level in range(levels):
+            (cu, au), (cv, av), (ch, ah) = sets[level]
+            upper, lower = sets[0][2][1], sets[1][2][1]
+            pressure = [upper[i] + lower[i] for i in range(4)]
+            if level == 1:
+                pressure = [pressure[i] + REDUCED * lower[i] for i in range(4)]
+            lap_u = au[1] + au[0] + au[3] + au[2] - 4.0 * cu
+            lap_v = av[1] + av[0] + av[3] + av[2] - 4.0 * cv
+            dx = 0.5 * (pressure[1] - pressure[0])
+            dy = 0.5 * (pressure[3] - pressure[2])
+            base[0, m, level] = ocean * (cu + TIME_STEP * (turn * cv - dx + VISCOSITY * lap_u))
+            base[1, m, level] = ocean * (cv + TIME_STEP * (-turn * cu - dy + VISCOSITY * lap_v))
+            flow = 0.5 * (ah[1] * au[1] - ah[0] * au[0]) + 0.5 * (ah[3] * av[3] - ah[2] * av[2])
+            base[2, m, level] = ch - TIME_STEP * flow
 
 
 def join_kernel(sizes, lons, left, right, head, tail, even, odd, rims, wide):
@@ -235,8 +278,7 @@
     hidden = w2.shape[2]
     per = LANES // hidden
     lane = iota((hidden, LANES), 1)
-    fields = w1.shape[2]
-    rows = fields * GROUP
+    fields = w1.shape[0]
     out_lon = iota((GROUP, LANES), 1) // hidden
     in_row = iota((GROUP, LANES), 0)
     bias_row = iota((GROUP, LANES), 0)
@@ -259,22 +301,26 @@
         return jnp.where(lon == out + shift, LAND, 0.0)
 
     for dj in range(3):
-        taps = [0.5 * jnp.concatenate([w1[dj, di].astype(f32)] * per, axis=1) for di in range(3)]
+        taps = []
+        for di in range(3):
+            cells = [w1[c, di].astype(f32)[dj : dj + 1] for c in range(fields)]
+            taps.append(
+                [jnp.broadcast_to(0.5 * jnp.concatenate([x] * per, axis=1), (GROUP, LANES)) for x in cells]
+            )
         for tile in range(2):
             parts = []
             for c in range(fields):
                 total = jnp.zeros((GROUP, LANES), f32)
                 for di in range(3):
                     hit = in_row == out_lon + per * tile + di
-                    total = jnp.where(hit, jnp.broadcast_to(taps[di][c : c + 1], (GROUP, LANES)), total)
+                    total = jnp.where(hit, taps[di][c], total)
                 parts.append(total)
             for start in range(0, fields, 4):
                 total = jnp.zeros((GROUP, LANES), f32)
                 for n in range(min(4, fields - start)):
                     for di in range(3):
                         hit = in_row % 2 + GROUP == out_lon + per * tile + di
-                        row = jnp.broadcast_to(taps[di][start + n : start + n + 1], (GROUP, LANES))
-                        total = jnp.where(hit & (in_row // 2 == n), row, total)
+                        total = jnp.where(hit & (in_row // 2 == n), taps[di][start + n], total)
                 parts.append(total)
             if dj == 1:
                 parts += [sea_rows(1, tile), bias_rows(0)]
@@ -345,12 +391,8 @@
     sizes,
     bias_last,
     own,
-    u,
-    v,
-    h,
+    base,
     sea,
-    left_in,
-    right_in,
     even_rim,
     odd_rim,
     own_tail,
@@ -361,8 +403,6 @@
     new_u,
     new_v,
     new_h,
-    left,
-    right,
     first,
     odd,
     even,
@@ -385,8 +425,6 @@
     top = lat_index == lat_count - 1
     is_odd = lat_index % 2 == 1
     bottom = lat_index == 0
-    left[...] = left_in[...].astype(f32)
-    right[...] = right_in[...].astype(f32)
     strip = odd_rim[...].astype(f32)
     paired = even_rim[...].astype(f32)
     south = jnp.where(is_odd, paired, jnp.where(bottom, 0.0, strip))
@@ -441,7 +479,7 @@
     hidden = LANES // 4
     per = LANES // hidden
     tiles = odd.shape[0]
-    cuts = 4
+    cuts = 1
     step = rows // cuts
     lower = iota((step, LANES), 1) < 2 * hidden
 
@@ -552,15 +590,21 @@
         force[2, span_rows, :] = jnp.where(before, sides[0][:, LANES:], sides[1][:, LANES:])
 
     ocean = sea[...].astype(f32)
-    at_lat = iota((lons, lats), 1).astype(f32)
-    lat_rows = (lat_index * lats).astype(f32) + at_lat
-    turn = CORIOLIS * (2.0 * (lat_rows + 0.5) / (lats * lat_count) - 1.0)
-    at_first = iota((lons, lats), 0) == 0
-    at_last = iota((lons, lats), 0) == lons - 1
-    at_south = iota((lons, lats), 1) == 0
-    at_north = iota((lons, lats), 1) == lats - 1
-    lon_rests = members * fields * RIM + GROUP
+    narrow = iota((lons, LANES), 1)
+    at_south = narrow == 0
+    at_north = narrow == LANES - 1
     halves = lons // 2
+
+    def beyond(message, m, c, offset):
+        cells = []
+        some = slice(c * GROUP, (c + 1) * GROUP)
+        for g in range(groups):
+            spot = (g * members + m) * RIM + offset
+            more = rests + g * members + m
+            cells.append(message[some, spot : spot + 1] + message[some, more : more + 1])
+        whole = jnp.broadcast_to(jnp.concatenate(cells, axis=0), (lons + GROUP, LANES))
+        return pltpu.roll(whole, lons + GROUP - RIM, 0)[:lons]
+
     for m in range(members):
         for q in range(chunks):
             size = min(blocks, lats - q * blocks)
@@ -569,66 +613,37 @@
                 total = total + force[d, pl.ds(d * SUB + m * chunks + q, size, stride=SUB), :]
             gathered[m, pl.ds(q * blocks, size), :] = total
         turned_force = jnp.transpose(gathered[m])
-
-        def push(c):
-            parts = [
-                turned_force[side * LANES // 2 + c * halves : side * LANES // 2 + (c + 1) * halves]
-                for side in range(2)
-            ]
-            return (jnp.concatenate(parts, axis=0) + bias_last[c]) * ocean
-
-        def rims(c):
-            row = (m * fields + c) * RIM
-            more = lon_rests + m * (fields - noises) + c - noises
-            west = left[pl.ds(row + RIM - 1, 1)] + left[pl.ds(more, 1)]
-            east = right[pl.ds(row, 1)] + right[pl.ds(more, 1)]
-            low, high = [], []
-            for g in range(groups):
-                spot = (g * members + m) * RIM
-                more = rests + g * members + m
-                some = slice(c * GROUP, (c + 1) * GROUP)
-                low.append(south[some, spot + RIM - 1 : spot + RIM] + south[some, more : more + 1])
-                high.append(north_rim[some, spot : spot + 1] + north_rim[some, more : more + 1])
-            low = jnp.broadcast_to(jnp.concatenate(low, axis=0), (lons + GROUP, LANES))
-            high = jnp.broadcast_to(jnp.concatenate(high, axis=0), (lons + GROUP, LANES))
-            low = pltpu.roll(low, lons + GROUP - RIM, 0)[:lons]
-            high = pltpu.roll(high, lons + GROUP - RIM, 0)[:lons]
-            repeat = lats // LANES
-            return west, east, jnp.concatenate([low] * repeat, axis=1), jnp.concatenate([high] * repeat, axis=1)
-
-        def around(x, rim):
-            west, east, low, high = rim
-            return (
-                jnp.where(at_first, west, pltpu.roll(x, 1, 0)),
-                jnp.where(at_last, east, pltpu.roll(x, lons - 1, 0)),
-                jnp.where(at_south, low, pltpu.roll(x, 1, 1)),
-                jnp.where(at_north, high, pltpu.roll(x, lats - 1, 1)),
-            )
-
-        sets = []
+        rims = [
+            [beyond(message, m, c, offset) for c in range(noises, fields)]
+            for message, offset in ((south, RIM - 1), (north_rim, 0))
+        ]
         for level in range(levels):
-            sets.append(
-                [
-                    (x[m, level], around(x[m, level], rims(noises + n * levels + level)))
-                    for n, x in enumerate((u, v, h))
+            gains = []
+            for (sign, spot), rim in zip(((1.0, at_south), (-1.0, at_north)), rims):
+                ru, rv, rh = rim[level], rim[levels + level], rim[2 * levels + level]
+                pressure = rim[2 * levels] + rim[2 * levels + 1]
+                if level == 1:
+                    pressure = pressure + REDUCED * rh
+                gains.append(
+                    [
+                        jnp.where(spot, TIME_STEP * VISCOSITY * ru, 0.0),
+                        jnp.where(spot, TIME_STEP * (VISCOSITY * rv + sign * 0.5 * pressure), 0.0),
+                        jnp.where(spot, TIME_STEP * sign * 0.5 * (rh * rv), 0.0),
+                    ]
+                )
+            middle = [jnp.zeros((lons, lats - 2 * LANES), f32)] if lats > 2 * LANES else []
+            gains = [jnp.concatenate([gains[0][n]] + middle + [gains[1][n]], axis=1) for n in range(3)]
+
+            def push(c):
+                parts = [
+                    turned_force[side * LANES // 2 + c * halves : side * LANES // 2 + (c + 1) * halves]
+                    for side in range(2)
                 ]
-            )
-        for level in range(levels):
-            (cu, au), (cv, av), (ch, ah) = sets[level]
-            upper, lower_h = sets[0][2][1], sets[1][2][1]
-            pressure = [upper[i] + lower_h[i] for i in range(4)]
-            if level == 1:
-                pressure = [pressure[i] + REDUCED * lower_h[i] for i in range(4)]
-            lap_u = au[1] + au[0] + au[3] + au[2] - 4.0 * cu
-            lap_v = av[1] + av[0] + av[3] + av[2] - 4.0 * cv
-            dx = 0.5 * (pressure[1] - pressure[0])
-            dy = 0.5 * (pressure[3] - pressure[2])
-            gain_u = turn * cv - dx + push(level) + VISCOSITY * lap_u
-            gain_v = -turn * cu - dy + push(levels + level) + VISCOSITY * lap_v
-            results[0, m, level] = ocean * (cu + TIME_STEP * gain_u)
-            results[1, m, level] = ocean * (cv + TIME_STEP * gain_v)
-            flow = 0.5 * (ah[1] * au[1] - ah[0] * au[0]) + 0.5 * (ah[3] * av[3] - ah[2] * av[2])
-            results[2, m, level] = ch - TIME_STEP * flow
+                return TIME_STEP * (jnp.concatenate(parts, axis=0) + bias_last[c])
+
+            results[0, m, level] = base[0, m, level] + ocean * (gains[0] + push(level))
+            results[1, m, level] = base[1, m, level] + ocean * (gains[1] + push(levels + level))
+            results[2, m, level] = base[2, m, level] + gains[2]
         for n, out in enumerate((new_u, new_v, new_h)):
             pltpu.make_async_copy(results.at[n, m], out.at[m], done.at[n, m]).start()
     for m in range(members):
@@ -669,47 +684,8 @@
 
     tall = members * fields * RIM + GROUP + members * 3 * levels
     assert tall % SUB == 0
-    head, tail = pl.pallas_call(
-        functools.partial(pack_lon_kernel, sizes),
-        out_shape=[pltpu.VMEM((tall, lats), bf16)] * 2,
-        in_specs=[pl.BlockSpec(memory_space=pltpu.HBM)] * 5,
-        out_specs=[whole] * 2,
-        scratch_shapes=[
-            pltpu.VMEM(noise.shape, noise.dtype),
-            pltpu.VMEM((2, 3, members, levels, GROUP, lats), f32),
-            pltpu.VMEM((2, GROUP, lats), land_sea.dtype),
-            pltpu.VMEM((2, tall, lats), f32),
-            pltpu.SemaphoreType.DMA((9,)),
-        ],
-        name="pack_lon",
-    )(*state)
-    ring = [(i, (i + 1) % lon_count) for i in range(lon_count)]
-    left = lax.ppermute(tail, "lon", ring)
-    right = lax.ppermute(head, "lon", [(b, a) for a, b in ring])
-
-    wide = -(-(fields + 1) * GROUP // SUB) * SUB
-    part = pltpu.VMEM((wide, LANES), f32)
-    message = pltpu.VMEM((wide, LANES), bf16)
-    deep = -(-(lons // 2 + 2) * hidden // LANES) * LANES
-    noise, velocity_u, velocity_v, thickness, land_sea, t1, t2, t3, t4, own_head, own_tail = pl.pallas_call(
-        functools.partial(prepare_kernel, sizes),
-        out_shape=[pltpu.VMEM(x.shape, x.dtype) for x in state]
-        + [
-            pltpu.VMEM((3 * LANES, 2 * LANES), bf16),
-            pltpu.VMEM((8 * LANES, 2 * LANES), bf16),
-            pltpu.VMEM((8 * LANES, 2 * LANES), bf16),
-            pltpu.VMEM((2, deep, 2 * LANES), bf16),
-        ]
-        + [part, part],
-        in_specs=[pl.BlockSpec(memory_space=pltpu.HBM)] * 5 + [whole] * 7,
-        out_specs=[whole] * 11,
-        scratch_shapes=[pltpu.SemaphoreType.DMA((5,))],
-        compiler_params=pltpu.CompilerParams(vmem_limit_bytes=8 * 2**20),
-        cost_estimate=pl.CostEstimate(flops=10**7, bytes_accessed=10**7, transcendentals=0),
-        name="prepare",
-    )(
-        *state,
-        conv_first.transpose(3, 2, 1, 0),
+    args = state + (
+        conv_first.transpose(1, 2, 3, 0),
         conv_second.transpose(2, 3, 0, 1),
         conv_third.transpose(2, 3, 0, 1),
         conv_last.transpose(2, 3, 0, 1),
@@ -717,7 +693,41 @@
         bias_second[None],
         bias_third[None],
     )
-    state = (noise, velocity_u, velocity_v, thickness, land_sea)
+    count = len(args)
+    *held, head, tail = pl.pallas_call(
+        functools.partial(pack_lon_kernel, sizes, count),
+        out_shape=[pltpu.VMEM(x.shape, x.dtype) for x in args] + [pltpu.VMEM((tall, lats), bf16)] * 2,
+        in_specs=[pl.BlockSpec(memory_space=pltpu.HBM)] * count,
+        out_specs=[whole] * (count + 2),
+        scratch_shapes=[pltpu.VMEM((2, tall, lats), f32), pltpu.SemaphoreType.DMA((count,))],
+        compiler_params=pltpu.CompilerParams(vmem_limit_bytes=62 * 2**20),
+        name="pack_lon",
+    )(*args)
+    state = tuple(held[:5])
+    ring = [(i, (i + 1) % lon_count) for i in range(lon_count)]
+    left = lax.ppermute(tail, "lon", ring)
+    right = lax.ppermute(head, "lon", [(b, a) for a, b in ring])
+
+    wide = -(-(fields + 1) * GROUP // SUB) * SUB
+    part = pltpu.VMEM((wide, LANES), f32)
+    message = pltpu.VMEM((wide, LANES), bf16)
+    deep = -(-(lons // 2 + 2) * hidden // LANES) * LANES
+    t1, t2, t3, t4, own_head, own_tail = pl.pallas_call(
+        functools.partial(prepare_kernel, sizes),
+        out_shape=[
+            pltpu.VMEM((3 * LANES, 2 * LANES), bf16),
+            pltpu.VMEM((8 * LANES, 2 * LANES), bf16),
+            pltpu.VMEM((8 * LANES, 2 * LANES), bf16),
+            pltpu.VMEM((2, deep, 2 * LANES), bf16),
+            part,
+            part,
+        ],
+        in_specs=[whole] * count,
+        out_specs=[whole] * 6,
+        compiler_params=pltpu.CompilerParams(vmem_limit_bytes=8 * 2**20),
+        cost_estimate=pl.CostEstimate(flops=10**7, bytes_accessed=10**7, transcendentals=0),
+        name="prepare",
+    )(*held)
     last = lat_count - 1
     smem = pl.BlockSpec(memory_space=pltpu.SMEM)
     to_even, to_odd = pl.pallas_call(
@@ -740,11 +750,11 @@
         pairs += [(at, (t ^ 1) * lat_count), (at + last, (lon_count - 1 - t) * lat_count + last)]
     odd_rim = lax.ppermute(to_odd, ("lon", "lat"), pairs)
 
-    own = pl.pallas_call(
+    own, base = pl.pallas_call(
         functools.partial(cells_kernel, sizes),
-        out_shape=pltpu.VMEM((groups, rows, LANES), bf16),
+        out_shape=[pltpu.VMEM((groups, rows, LANES), bf16), pltpu.VMEM((3, *velocity_u.shape), f32)],
         in_specs=[whole] * 8,
-        out_specs=whole,
+        out_specs=[whole] * 2,
         scratch_shapes=[
             pltpu.VMEM((2, tall, lats), f32),
             pltpu.VMEM((groups, rows, LANES), f32),
@@ -761,11 +771,9 @@
     return pl.pallas_call(
         functools.partial(main_kernel, sizes),
         out_shape=[out] * 3,
-        in_specs=[smem] + [whole] * 14,
+        in_specs=[smem] + [whole] * 10,
         out_specs=[pl.BlockSpec(memory_space=pltpu.HBM)] * 3,
         scratch_shapes=[
-            pltpu.VMEM((tall, lats), f32),
-            pltpu.VMEM((tall, lats), f32),
             pltpu.VMEM((groups, padded, LANES), bf16),
             pltpu.VMEM((tiles, padded, LANES), bf16),
             pltpu.VMEM((tiles, padded, LANES), bf16),
@@ -782,9 +790,8 @@
     )(
         bias_last,
         own,
-        *state[1:],
-        left,
-        right,
+        base,
+        state[4],
         even_rim,
         odd_rim,
         to_odd,

time: 36.7 us -> 29.4 us (0.80)
  the two profiles are of different devices: /device:TPU:20 before, /device:TPU:11 now
where the time goes in v6:
time: 29.4 us; the launch traced here: 29.3 us
  Pallas kernels  20.8 us (71%)
  starting transfers between devices  4.48 us (15%)
  waiting for transfers between devices  3.29 us (11%)
  between operations  0.69 us (2%)
    pallas_call x1, Pallas kernels, body(): pl.pallas_call(functools.partial(main_kernel, sizes), out_shape=[out] * 3...  15.3 us
    ppermute x1, waiting for transfers between devices, body(): right = lax.ppermute(head, 'lon', [(b, a) for a, b in ring])  3.13 us
    ppermute x1, starting transfers between devices, body(): odd_rim = lax.ppermute(to_odd, ('lon', 'lat'), pairs)  2.42 us
    pallas_call x1, Pallas kernels, body(): pl.pallas_call(functools.partial(cells_kernel, sizes), out_shape=[pltpu.V...  2.26 us
    ppermute x1, starting transfers between devices, body(): left = lax.ppermute(tail, 'lon', ring)  1.82 us
    pallas_call x1, Pallas kernels, body(): pl.pallas_call(functools.partial(prepare_kernel, sizes), out_shape=[pltpu...  1.65 us
    pallas_call x1, Pallas kernels, body(): pl.pallas_call(functools.partial(pack_lon_kernel, sizes, count), out_shap...  1.43 us
  transfers between devices with their start and end apart: 4, of which 2 were waited for; matrix products, arithmetic and copies ran while one was open for 0% of the time, Pallas kernels for 13%

profile of v6, /device:TPU:11, one launch (start us, length us, event | category | flops | bytes accessed | tf_op | source)
XLA Modules:
  0.0 29.3 jit_solution(6446864324571713143)
XLA Ops:
  0.6 1.4 %pack_lon.1 = (bf16[4,4,32,256]{3,2,1,0:T(8,128)(2,1)S(1)}, f32[4,2,32,256]{3,2,1,0:T(8,128)S(1)}, f32[4,2,32,256]{3,2,1,0:T(8,128)S(1)}, f32[4,2,32,256]{3,2,1,...) custom-call(bf16[4,4,32,256]{3,2,1,0:T(8,128)(2,1)} %refs_0_.1, ...), custom_call_target="tpu_custom_call" | custom-call | tf_op jit(solution)/shard_map/pack_lon/pallas_call | solution.py:697
  2.1 1.8 %collective-permute-start = (bf16[192,256]{1,0:T(8,128)(2,1)S(1)}, bf16[192,256]{1,0:T(8,128)(2,1)S(1)}, u32[]{:S(2)}, u32[]{:S(2)}) collective-permute-start(bf16[192,256]{1,0:T(8,128)(2,1)S(1)} %get-tuple-element.32), channel_id=1, source_target_pairs={{0,4},{4,8},{8,12},{12,16},{16,20},{20,24},{24,28},{28,0},{1,5},{5... | collective-permute-start | bytes 294920 | tf_op jit(solution)/shard_map/ppermute | solution.py:708
  3.9 0.0 collective-permute-start.1
  3.9 0.0 copy-start
  3.9 1.6 %prepare.1 = (bf16[384,256]{1,0:T(8,128)(2,1)S(1)}, bf16[1024,256]{1,0:T(8,128)(2,1)S(1)}, bf16[1024,256]{1,0:T(8,128)(2,1)S(1)}, bf16[2,640,256]{2,1,0:T(8,128)...) custom-call(bf16[4,4,32,256]{3,2,1,0:T(8,128)(2,1)S(1)} %get-tuple-element.27.noise, ...), custom_call_target="tpu_custom_call" | custom-call | flops 10000000 | bytes 10000000 | tf_op jit(solution)/shard_map/prepare/pallas_call | solution.py:715
  5.6 0.2 collective-permute-done.left
  5.7 3.1 %collective-permute-done.1.right = bf16[192,256]{1,0:T(8,128)(2,1)S(1)} collective-permute-done((bf16[192,256]{1,0:T(8,128)(2,1)S(1)}, bf16[192,256]{1,0:T(8,128)(2,1)S(1)}, u32[]{:S(2)}, u32[]{:S(2)}) %collective-permute-start.1) | collective-permute-done | bytes 98336 | tf_op jit(solution)/shard_map/ppermute | solution.py:709
  8.8 0.2 join_rims.1
  9.0 0.2 collective-permute-start.2
  9.2 2.4 %collective-permute-start.3 = (bf16[96,128]{1,0:T(8,128)(2,1)S(1)}, bf16[96,128]{1,0:T(8,128)(2,1)S(1)}, u32[]{:S(2)}, u32[]{:S(2)}) collective-permute-start(bf16[96,128]{1,0:T(8,128)(2,1)S(1)} %get-tuple-element.46.own_tail), channel_id=1, source_target_pairs={{1,2},{2,1},{0,4},{3,31},{5,6},{6,5},{4,0},{7,27},{9,10},{10,9},{8... | collective-permute-start | bytes 73736 | tf_op jit(solution)/shard_map/ppermute | solution.py:751
  11.7 2.3 %cells.1 = (bf16[5,1088,128]{2,1,0:T(8,128)(2,1)S(1)}, f32[3,4,2,32,256]{4,3,2,1,0:T(8,128)S(1)}) custom-call(bf16[4,4,32,256]{3,2,1,0:T(8,128)(2,1)S(1)} %get-tuple-element.27.noise, f32[4,2,32,256]{3,2,1,0:T(8,128)S(1)} %get-tuple-element.28.u, f32[4,2,32,256]{3,2,1,0:T(8,128)S(1)} %get-tuple-element.29.v, f32[4,2,32,256]{3,2,1,0:T(8,128)S(1)} %get-tuple-element.30.h, ...), custom_call_target="tpu_custom_call" | custom-call | flops 10000000 | bytes 10000000 | tf_op jit(solution)/shard_map/cells/pallas_call | solution.py:753
  13.9 0.0 collective-permute-done.2.even_rim
  13.9 0.0 collective-permute-done.3.odd_rim
  14.0 0.0 copy-done
  14.0 15.3 %network_and_step.1 = (f32[4,2,32,256]{3,2,1,0:T(8,128)}, f32[4,2,32,256]{3,2,1,0:T(8,128)}, f32[4,2,32,256]{3,2,1,0:T(8,128)}) custom-call(f32[4]{0:T(128)S(1)} %copy-done, bf16[5,1088,128]{2,1,0:T(8,128)(2,1)S(1)} %get-tuple-element.44.own, f32[3,4,2,32,256]{4,3,2,1,0:T(8,128)S(1)} %get-tuple-element.45.base, s32[32,256]{1,0:T(8,128)S(1)} %get-tuple-element.31.sea, ...), custom_call_target="tpu_custom_call" | custom-call | flops 20000000000 | bytes 10000000 | tf_op jit(solution)/shard_map/network_and_step/pallas_call | solution.py:771
Async XLA Ops:
  2.1 3.6 %collective-permute-start = (bf16[192,256]{1,0:T(8,128)(2,1)S(1)}, bf16[192,256]{1,0:T(8,128)(2,1)S(1)}, u32[]{:S(2)}, u32[]{:S(2)}) collective-permute-start(bf16[192,256]{1,0:T(8,128)(2,1)S(1)} %get-tuple-element.32), channel_id=1, source_target_pairs={{0,4},{4,8},{8,12},{12,16},{16,20},{20,24},{24,28},{28,0},{1,5},{5... | collective-permute-start | bytes 294920 | tf_op jit(solution)/shard_map/ppermute | solution.py:708
  3.9 4.9 %collective-permute-start.1 = (bf16[192,256]{1,0:T(8,128)(2,1)S(1)}, bf16[192,256]{1,0:T(8,128)(2,1)S(1)}, u32[]{:S(2)}, u32[]{:S(2)}) collective-permute-start(bf16[192,256]{1,0:T(8,128)(2,1)S(1)} %get-tuple-element.33), channel_id=1, source_target_pairs={{4,0},{8,4},{12,8},{16,12},{20,16},{24,20},{28,24},{0,28},{5,1},{9... | collective-permute-start | bytes 294920 | tf_op jit(solution)/shard_map/ppermute | solution.py:709
  3.9 10.1 %copy-start = (f32[4]{0:T(128)S(1)}, f32[4]{0:T(128)}, u32[]{:S(2)}) copy-start(f32[4]{0:T(128)} %bias_last.1) | copy-start | bytes 52
  9.0 4.9 %collective-permute-start.2 = (bf16[96,128]{1,0:T(8,128)(2,1)S(1)}, bf16[96,128]{1,0:T(8,128)(2,1)S(1)}, u32[]{:S(2)}, u32[]{:S(2)}) collective-permute-start(bf16[96,128]{1,0:T(8,128)(2,1)S(1)} %get-tuple-element.43.after), channel_id=1, source_target_pairs={{0,1},{1,0},{2,3},{3,2},{4,5},{5,4},{6,7},{7,6},{8,9},{9,8},{10,11... | collective-permute-start | bytes 73736 | tf_op jit(solution)/shard_map/ppermute | solution.py:745
  9.2 4.7 %collective-permute-start.3 = (bf16[96,128]{1,0:T(8,128)(2,1)S(1)}, bf16[96,128]{1,0:T(8,128)(2,1)S(1)}, u32[]{:S(2)}, u32[]{:S(2)}) collective-permute-start(bf16[96,128]{1,0:T(8,128)(2,1)S(1)} %get-tuple-element.46.own_tail), channel_id=1, source_target_pairs={{1,2},{2,1},{0,4},{3,31},{5,6},{6,5},{4,0},{7,27},{9,10},{10,9},{8... | collective-permute-start | bytes 73736 | tf_op jit(solution)/shard_map/ppermute | solution.py:751

commit v7 on v6

--- a/solution.py
+++ b/solution.py
@@ -479,9 +479,8 @@
     hidden = LANES // 4
     per = LANES // hidden
     tiles = odd.shape[0]
-    cuts = 1
-    step = rows // cuts
-    lower = iota((step, LANES), 1) < 2 * hidden
+    piece = 8 * SUB
+    pieces = [(r, min(piece, rows - r)) for r in range(0, rows, piece)]
 
     def activate(pre):
         return (pre * jnp.tanh(pre) + pre).astype(bf16)
@@ -520,12 +519,12 @@
     even[tiles - 2] = jnp.zeros(even.shape[1:], bf16)
 
     def put(y, b, r, out):
+        step = out.shape[0]
         for e in range(out.shape[1] // LANES):
             y[2 * b + e, pl.ds(SUB + r, step), :] = out[:, e * LANES : (e + 1) * LANES]
 
     for b in range(groups):
-        for n in range(cuts):
-            r = n * step
+        for r, step in pieces:
             parts = [first[b, pl.ds(r + SUB * d, step), :] for d in range(3)]
             put(odd, b, r, activate(dot(jnp.concatenate(parts, axis=1), t1[...])))
     finish(odd, lons + 6)
@@ -534,8 +533,8 @@
 
     def layer(x, y, t, left_over):
         for b in range(groups):
-            for n in range(cuts):
-                r = n * step
+            for r, step in pieces:
+                lower = iota((step, LANES), 1) < 2 * hidden
 
                 def cells_of(tile, d):
                     return x[tile, pl.ds(r + SUB * d, step), :]
@@ -576,10 +575,11 @@
     finish(odd, lons + 2)
 
     depth = t4.shape[1] // LANES
-    long = (rows + 2 * SUB) // 2
-    before = iota((long, LANES), 1) < LANES // 2
-    for n in range(2):
-        span_rows = pl.ds(n * long, long)
+    padded = rows + 2 * SUB
+    for r in range(0, padded, piece):
+        long = min(piece, padded - r)
+        before = iota((long, LANES), 1) < LANES // 2
+        span_rows = pl.ds(r, long)
         sides = []
         for side in range(2):
             parts = [odd[side * (depth - 1) + t, span_rows, :] for t in range(depth)]

time: 29.4 us -> 29.3 us (level)
  no operation moved by 1% of the time
where the time goes in v7:
time: 29.3 us; the launch traced here: 29.2 us
  Pallas kernels  20.6 us (70%)
  starting transfers between devices  4.48 us (15%)
  waiting for transfers between devices  3.29 us (11%)
  between operations  0.85 us (3%)
    pallas_call x1, Pallas kernels, body(): pl.pallas_call(functools.partial(main_kernel, sizes), out_shape=[out] * 3...  15.1 us
    ppermute x1, waiting for transfers between devices, body(): right = lax.ppermute(head, 'lon', [(b, a) for a, b in ring])  3.13 us
    ppermute x1, starting transfers between devices, body(): odd_rim = lax.ppermute(to_odd, ('lon', 'lat'), pairs)  2.42 us
    pallas_call x1, Pallas kernels, body(): pl.pallas_call(functools.partial(cells_kernel, sizes), out_shape=[pltpu.V...  2.26 us
    ppermute x1, starting transfers between devices, body(): left = lax.ppermute(tail, 'lon', ring)  1.82 us
    pallas_call x1, Pallas kernels, body(): pl.pallas_call(functools.partial(prepare_kernel, sizes), out_shape=[pltpu...  1.65 us
    pallas_call x1, Pallas kernels, body(): pl.pallas_call(functools.partial(pack_lon_kernel, sizes, count), out_shap...  1.43 us
  transfers between devices with their start and end apart: 4, of which 2 were waited for; matrix products, arithmetic and copies ran while one was open for 0% of the time, Pallas kernels for 13%

profile of v7, /device:TPU:11, one launch (start us, length us, event | category | flops | bytes accessed | tf_op | source)
XLA Modules:
  0.0 29.2 jit_solution(14748440651739204802)
XLA Ops:
  0.6 1.4 %pack_lon.1 = (bf16[4,4,32,256]{3,2,1,0:T(8,128)(2,1)S(1)}, f32[4,2,32,256]{3,2,1,0:T(8,128)S(1)}, f32[4,2,32,256]{3,2,1,0:T(8,128)S(1)}, f32[4,2,32,256]{3,2,1,...) custom-call(bf16[4,4,32,256]{3,2,1,0:T(8,128)(2,1)} %refs_0_.1, ...), custom_call_target="tpu_custom_call" | custom-call | tf_op jit(solution)/shard_map/pack_lon/pallas_call | solution.py:697
  2.1 1.8 %collective-permute-start = (bf16[192,256]{1,0:T(8,128)(2,1)S(1)}, bf16[192,256]{1,0:T(8,128)(2,1)S(1)}, u32[]{:S(2)}, u32[]{:S(2)}) collective-permute-start(bf16[192,256]{1,0:T(8,128)(2,1)S(1)} %get-tuple-element.32), channel_id=1, source_target_pairs={{0,4},{4,8},{8,12},{12,16},{16,20},{20,24},{24,28},{28,0},{1,5},{5... | collective-permute-start | bytes 294920 | tf_op jit(solution)/shard_map/ppermute | solution.py:708
  3.9 0.0 collective-permute-start.1
  3.9 0.0 copy-start
  3.9 1.6 %prepare.1 = (bf16[384,256]{1,0:T(8,128)(2,1)S(1)}, bf16[1024,256]{1,0:T(8,128)(2,1)S(1)}, bf16[1024,256]{1,0:T(8,128)(2,1)S(1)}, bf16[2,640,256]{2,1,0:T(8,128)...) custom-call(bf16[4,4,32,256]{3,2,1,0:T(8,128)(2,1)S(1)} %get-tuple-element.27.noise, ...), custom_call_target="tpu_custom_call" | custom-call | flops 10000000 | bytes 10000000 | tf_op jit(solution)/shard_map/prepare/pallas_call | solution.py:715
  5.6 0.2 collective-permute-done.left
  5.7 3.1 %collective-permute-done.1.right = bf16[192,256]{1,0:T(8,128)(2,1)S(1)} collective-permute-done((bf16[192,256]{1,0:T(8,128)(2,1)S(1)}, bf16[192,256]{1,0:T(8,128)(2,1)S(1)}, u32[]{:S(2)}, u32[]{:S(2)}) %collective-permute-start.1) | collective-permute-done | bytes 98336 | tf_op jit(solution)/shard_map/ppermute | solution.py:709
  8.8 0.2 join_rims.1
  9.0 0.2 collective-permute-start.2
  9.2 2.4 %collective-permute-start.3 = (bf16[96,128]{1,0:T(8,128)(2,1)S(1)}, bf16[96,128]{1,0:T(8,128)(2,1)S(1)}, u32[]{:S(2)}, u32[]{:S(2)}) collective-permute-start(bf16[96,128]{1,0:T(8,128)(2,1)S(1)} %get-tuple-element.46.own_tail), channel_id=1, source_target_pairs={{1,2},{2,1},{0,4},{3,31},{5,6},{6,5},{4,0},{7,27},{9,10},{10,9},{8... | collective-permute-start | bytes 73736 | tf_op jit(solution)/shard_map/ppermute | solution.py:751
  11.7 2.3 %cells.1 = (bf16[5,1088,128]{2,1,0:T(8,128)(2,1)S(1)}, f32[3,4,2,32,256]{4,3,2,1,0:T(8,128)S(1)}) custom-call(bf16[4,4,32,256]{3,2,1,0:T(8,128)(2,1)S(1)} %get-tuple-element.27.noise, f32[4,2,32,256]{3,2,1,0:T(8,128)S(1)} %get-tuple-element.28.u, f32[4,2,32,256]{3,2,1,0:T(8,128)S(1)} %get-tuple-element.29.v, f32[4,2,32,256]{3,2,1,0:T(8,128)S(1)} %get-tuple-element.30.h, ...), custom_call_target="tpu_custom_call" | custom-call | flops 10000000 | bytes 10000000 | tf_op jit(solution)/shard_map/cells/pallas_call | solution.py:753
  13.9 0.0 collective-permute-done.2.even_rim
  13.9 0.0 collective-permute-done.3.odd_rim
  14.0 0.0 copy-done
  14.0 15.1 %network_and_step.1 = (f32[4,2,32,256]{3,2,1,0:T(8,128)}, f32[4,2,32,256]{3,2,1,0:T(8,128)}, f32[4,2,32,256]{3,2,1,0:T(8,128)}) custom-call(f32[4]{0:T(128)S(1)} %copy-done, bf16[5,1088,128]{2,1,0:T(8,128)(2,1)S(1)} %get-tuple-element.44.own, f32[3,4,2,32,256]{4,3,2,1,0:T(8,128)S(1)} %get-tuple-element.45.base, s32[32,256]{1,0:T(8,128)S(1)} %get-tuple-element.31.sea, ...), custom_call_target="tpu_custom_call" | custom-call | flops 20000000000 | bytes 10000000 | tf_op jit(solution)/shard_map/network_and_step/pallas_call | solution.py:771
Async XLA Ops:
  2.1 3.6 %collective-permute-start = (bf16[192,256]{1,0:T(8,128)(2,1)S(1)}, bf16[192,256]{1,0:T(8,128)(2,1)S(1)}, u32[]{:S(2)}, u32[]{:S(2)}) collective-permute-start(bf16[192,256]{1,0:T(8,128)(2,1)S(1)} %get-tuple-element.32), channel_id=1, source_target_pairs={{0,4},{4,8},{8,12},{12,16},{16,20},{20,24},{24,28},{28,0},{1,5},{5... | collective-permute-start | bytes 294920 | tf_op jit(solution)/shard_map/ppermute | solution.py:708
  3.9 4.9 %collective-permute-start.1 = (bf16[192,256]{1,0:T(8,128)(2,1)S(1)}, bf16[192,256]{1,0:T(8,128)(2,1)S(1)}, u32[]{:S(2)}, u32[]{:S(2)}) collective-permute-start(bf16[192,256]{1,0:T(8,128)(2,1)S(1)} %get-tuple-element.33), channel_id=1, source_target_pairs={{4,0},{8,4},{12,8},{16,12},{20,16},{24,20},{28,24},{0,28},{5,1},{9... | collective-permute-start | bytes 294920 | tf_op jit(solution)/shard_map/ppermute | solution.py:709
  3.9 10.1 %copy-start = (f32[4]{0:T(128)S(1)}, f32[4]{0:T(128)}, u32[]{:S(2)}) copy-start(f32[4]{0:T(128)} %bias_last.1) | copy-start | bytes 52
  9.0 4.9 %collective-permute-start.2 = (bf16[96,128]{1,0:T(8,128)(2,1)S(1)}, bf16[96,128]{1,0:T(8,128)(2,1)S(1)}, u32[]{:S(2)}, u32[]{:S(2)}) collective-permute-start(bf16[96,128]{1,0:T(8,128)(2,1)S(1)} %get-tuple-element.43.after), channel_id=1, source_target_pairs={{0,1},{1,0},{2,3},{3,2},{4,5},{5,4},{6,7},{7,6},{8,9},{9,8},{10,11... | collective-permute-start | bytes 73736 | tf_op jit(solution)/shard_map/ppermute | solution.py:745
  9.2 4.7 %collective-permute-start.3 = (bf16[96,128]{1,0:T(8,128)(2,1)S(1)}, bf16[96,128]{1,0:T(8,128)(2,1)S(1)}, u32[]{:S(2)}, u32[]{:S(2)}) collective-permute-start(bf16[96,128]{1,0:T(8,128)(2,1)S(1)} %get-tuple-element.46.own_tail), channel_id=1, source_target_pairs={{1,2},{2,1},{0,4},{3,31},{5,6},{6,5},{4,0},{7,27},{9,10},{10,9},{8... | collective-permute-start | bytes 73736 | tf_op jit(solution)/shard_map/ppermute | solution.py:751

commit v8 on v7

--- a/solution.py
+++ b/solution.py
@@ -37,7 +37,7 @@
 
 
 def pack_lon_kernel(sizes, count, *refs):
-    sources, held, (head, tail, wide, done) = refs[:count], refs[count : 2 * count], refs[2 * count :]
+    sources, held, (even, odd, wide, done) = refs[:count], refs[count : 2 * count], refs[2 * count :]
     members, noises, levels = sizes
     fields = noises + 3 * levels
     noise, u, v, h, sea = held[:5]
@@ -70,10 +70,17 @@
     ends = [sea[pl.ds(side * (lons - GROUP), GROUP)].astype(f32) for side in range(2)]
     wide[0, rows] = jnp.where(upper, ends[0], 0.0)
     wide[1, rows] = jnp.where(upper, pltpu.roll(ends[1], RIM, 0), 0.0)
-    head[...] = wide[0].astype(bf16)
-    tail[...] = wide[1].astype(bf16)
+    is_odd = lax.axis_index("lon") % 2 == 1
+    even[...] = jnp.where(is_odd, wide[0], wide[1]).astype(bf16)
+    odd[...] = jnp.where(is_odd, wide[1], wide[0]).astype(bf16)
     for copy in copies[5:]:
         copy.wait()
+
+
+def lon_rims(even, odd, lanes=slice(None)):
+    is_odd = lax.axis_index("lon") % 2 == 1
+    a, b = even[:, lanes].astype(f32), odd[:, lanes].astype(f32)
+    return jnp.where(is_odd, a, b), jnp.where(is_odd, b, a)
 
 
 def rim_tile(sizes, m, c, side, rim):
@@ -130,7 +137,7 @@
 
 
 def prepare_kernel(sizes, noise, u, v, h, sea, *refs):
-    weights, matrices, (head, tail) = refs[:7], refs[7:11], refs[11:]
+    weights, matrices, (head, tail, middle, pre, cells, turned) = refs[:7], refs[7:11], refs[11:]
     held = (noise, u, v, h, sea)
     members, noises, levels = sizes
     fields = noises + 3 * levels
@@ -154,9 +161,53 @@
             out[pl.ds(c * GROUP, GROUP)] = total
         for c in range(fields + 1, out.shape[0] // GROUP):
             out[pl.ds(c * GROUP, GROUP)] = jnp.zeros((GROUP, LANES), f32)
-
-
-def cells_kernel(sizes, noise, u, v, h, sea, left, right, after, out, base, rims, cells, turned):
+    chunks = SUB // members
+    rows = cells.shape[1]
+    gap_k = lats - (chunks - 1) * ((lats + GAP) // chunks)
+    inner = groups - 2
+    for m in range(members):
+        for g in range(inner):
+            empty = pl.ds(gap_k * SUB + (m + 1) * chunks - 1, GAP, stride=SUB)
+            cells[g, empty, :] = jnp.zeros((GAP, LANES), f32)
+    for t in range(lats // LANES):
+        for m in range(members):
+            tiles = [shifted_tiles(sizes, held, m, c, t) for c in range(fields + 1)]
+            for g in range(1, inner + 1):
+                following = [x[g + 1] for x in tiles]
+                block = window([x[g] for x in tiles[:fields]], following[:fields], tiles[fields][g], following[fields])
+                buffer = turned.at[(t * members + m) * inner + g - 1]
+                store_lats(block, t, cells, g - 1, m, lats, chunks, buffer)
+    for g in range(inner):
+        middle[g, pl.ds(SUB, rows), :] = cells[g].astype(bf16)
+        wrap(middle.at[g], rows)
+    for g in range(inner):
+        for r, step in row_pieces(rows):
+            parts = [middle[g, pl.ds(r + SUB * d, step), :] for d in range(3)]
+            put(pre, g + 1, r, activate(dot(jnp.concatenate(parts, axis=1), matrices[0][...])))
+
+
+def row_pieces(rows):
+    half = rows // 2 // SUB * SUB
+    return [(0, half), (half, rows - half)]
+
+
+def activate(pre):
+    return (pre * jnp.tanh(pre) + pre).astype(bf16)
+
+
+def put(y, b, r, out):
+    for e in range(out.shape[1] // LANES):
+        y[2 * b + e, pl.ds(SUB + r, out.shape[0]), :] = out[:, e * LANES : (e + 1) * LANES]
+
+
+def wrap(x, rows):
+    end = x[pl.ds(rows, SUB), :].astype(f32)
+    x[pl.ds(0, SUB), :] = pltpu.roll(end, 1, 0).astype(bf16)
+    begin = x[pl.ds(SUB, SUB), :].astype(f32)
+    x[pl.ds(SUB + rows, SUB), :] = pltpu.roll(begin, SUB - 1, 0).astype(bf16)
+
+
+def cells_kernel(sizes, noise, u, v, h, sea, lon_even, lon_odd, after, out, base, rims, cells, turned):
     members, noises, levels = sizes
     fields = noises + 3 * levels
     lons, lats = sea.shape
@@ -164,12 +215,11 @@
     chunks = SUB // members
     rows = cells.shape[1]
     gap_k = lats - (chunks - 1) * ((lats + GAP) // chunks)
-    rims[0] = left[...].astype(f32)
-    rims[1] = right[...].astype(f32)
+    rims[0], rims[1] = lon_rims(lon_even, lon_odd)
     for m in range(members):
-        for g in range(groups):
+        for side in range(2):
             empty = pl.ds(gap_k * SUB + (m + 1) * chunks - 1, GAP, stride=SUB)
-            cells[g, empty, :] = jnp.zeros((GAP, LANES), f32)
+            cells[side, empty, :] = jnp.zeros((GAP, LANES), f32)
     blank = jnp.zeros((GROUP, LANES), f32)
     upper = iota((GROUP, LANES), 0) < RIM
     for t in range(lats // LANES):
@@ -182,12 +232,12 @@
                 groups_of[0] = jnp.where(upper, ends[0], groups_of[0])
                 groups_of[-1] = jnp.where(upper, groups_of[-1], ends[1])
                 tiles.append(groups_of)
-            for g in range(groups):
+            for side, g in enumerate((0, groups - 1)):
                 following = [x[g + 1] if g + 1 < groups else blank for x in tiles]
                 block = window([x[g] for x in tiles[:fields]], following[:fields], tiles[fields][g], following[fields])
-                store_lats(block, t, cells, g, m, lats, chunks, turned.at[(t * members + m) * groups + g])
-    for g in range(groups):
-        out[g] = cells[g].astype(bf16)
+                store_lats(block, t, cells, side, m, lats, chunks, turned.at[(t * members + m) * 2 + side])
+    for side in range(2):
+        out[side, pl.ds(SUB, rows), :] = cells[side].astype(bf16)
     step_kernel(sizes, u, v, h, sea, rims, base)
 
 
@@ -242,14 +292,13 @@
             base[2, m, level] = ch - TIME_STEP * flow
 
 
-def join_kernel(sizes, lons, left, right, head, tail, even, odd, rims, wide):
+def join_kernel(sizes, lons, lon_even, lon_odd, head, tail, even, odd, rims, wide):
     members, noises, levels = sizes
     fields = noises + 3 * levels
     groups = lons // GROUP + 1
-    lats = left.shape[1]
-    for side, rim in enumerate((left, right)):
-        rims[side, 0] = rim[:, :LANES].astype(f32)
-        rims[side, 1] = rim[:, lats - LANES :].astype(f32)
+    lats = lon_even.shape[1]
+    for n, lanes in enumerate((slice(0, LANES), slice(lats - LANES, lats))):
+        rims[0, n], rims[1, n] = lon_rims(lon_even, lon_odd, lanes)
     lane = iota((GROUP, LANES), 1)
     upper = iota((GROUP, LANES), 0) < RIM
     to_south = lax.axis_index("lat") % 2 == 1
@@ -390,7 +439,9 @@
 def main_kernel(
     sizes,
     bias_last,
-    own,
+    middle_in,
+    ends_in,
+    pre_in,
     base,
     sea,
     even_rim,
@@ -403,7 +454,8 @@
     new_u,
     new_v,
     new_h,
-    first,
+    middle,
+    ends,
     odd,
     even,
     force,
@@ -465,25 +517,18 @@
                 start = n * RIM * SUB + gap * chunks + chunks - 1
                 gaps[g, pl.ds(start, RIM, stride=SUB), :] = turned[n, pl.ds((g * members + m) * RIM, RIM), :]
 
+    first = [ends.at[0]] + [middle.at[g] for g in range(groups - 2)] + [ends.at[1]]
     in_gap = iota((GAP * SUB, LANES), 0) % chunks == chunks - 1
     for g in range(groups):
-        first[g, pl.ds(SUB, rows), :] = own[g]
         spot = pl.ds((1 + gap_k) * SUB, GAP * SUB)
-        kept = first[g, spot, :].astype(f32)
-        first[g, spot, :] = jnp.where(in_gap, gaps[g], kept).astype(bf16)
-        end = first[g, pl.ds(rows, SUB), :].astype(f32)
-        first[g, pl.ds(0, SUB), :] = pltpu.roll(end, 1, 0).astype(bf16)
-        begin = first[g, pl.ds(SUB, SUB), :].astype(f32)
-        first[g, pl.ds(SUB + rows, SUB), :] = pltpu.roll(begin, SUB - 1, 0).astype(bf16)
+        kept = first[g][spot, :].astype(f32)
+        first[g][spot, :] = jnp.where(in_gap, gaps[g], kept).astype(bf16)
+        wrap(first[g], rows)
 
     hidden = LANES // 4
     per = LANES // hidden
     tiles = odd.shape[0]
-    piece = 8 * SUB
-    pieces = [(r, min(piece, rows - r)) for r in range(0, rows, piece)]
-
-    def activate(pre):
-        return (pre * jnp.tanh(pre) + pre).astype(bf16)
+    pieces = row_pieces(rows)
 
     def finish(x, valid):
         used = (valid + per - 1) // per
@@ -509,24 +554,25 @@
                     x[t, pl.ds(dst, SUB), :] = total.astype(bf16)
 
         for t in range(used):
-            end = x[t, pl.ds(rows, SUB), :].astype(f32)
-            x[t, pl.ds(0, SUB), :] = pltpu.roll(end, 1, 0).astype(bf16)
-            begin = x[t, pl.ds(SUB, SUB), :].astype(f32)
-            x[t, pl.ds(SUB + rows, SUB), :] = pltpu.roll(begin, SUB - 1, 0).astype(bf16)
+            wrap(x.at[t], rows)
 
     for x in (odd, even):
         x[tiles - 1] = jnp.zeros(x.shape[1:], bf16)
     even[tiles - 2] = jnp.zeros(even.shape[1:], bf16)
 
-    def put(y, b, r, out):
-        step = out.shape[0]
-        for e in range(out.shape[1] // LANES):
-            y[2 * b + e, pl.ds(SUB + r, step), :] = out[:, e * LANES : (e + 1) * LANES]
-
-    for b in range(groups):
+    for b in (0, groups - 1):
         for r, step in pieces:
-            parts = [first[b, pl.ds(r + SUB * d, step), :] for d in range(3)]
+            parts = [first[b][pl.ds(r + SUB * d, step), :] for d in range(3)]
             put(odd, b, r, activate(dot(jnp.concatenate(parts, axis=1), t1[...])))
+    near = (gap_k - 1) * SUB
+    for b in range(1, groups - 1):
+        parts = []
+        for d in range(3):
+            some = [first[b][pl.ds(near + SUB * d, rows - near), :], first[b][pl.ds(SUB * d, SUB), :]]
+            parts.append(jnp.concatenate(some, axis=0))
+        out = activate(dot(jnp.concatenate(parts, axis=1), t1[...]))
+        put(odd, b, near, out[: rows - near])
+        put(odd, b, 0, out[rows - near :])
     finish(odd, lons + 6)
 
     width = GROUP * hidden
@@ -543,7 +589,7 @@
                     more = [cells_of(tile, d) for d in range(3)]
                     return [
                         jnp.where(lower, more[0], pltpu.roll(more[1], 2 * hidden, 1)),
-                        jnp.where(lower, more[2], first[b, pl.ds(r + SUB, step), :]),
+                        jnp.where(lower, more[2], first[b][pl.ds(r + SUB, step), :]),
                     ]
 
                 if b < groups - 1:
@@ -559,7 +605,7 @@
                         axis=0,
                     )
                 else:
-                    parts = [cells_of(2 * b, d) for d in range(3)] + [first[b, pl.ds(r + SUB, step), :]]
+                    parts = [cells_of(2 * b, d) for d in range(3)] + [first[b][pl.ds(r + SUB, step), :]]
                     lanes = pl.ds(0, LANES)
                     matrix = jnp.concatenate(
                         [t[pl.ds(d * width, LANES), lanes] for d in range(3)]
@@ -576,8 +622,7 @@
 
     depth = t4.shape[1] // LANES
     padded = rows + 2 * SUB
-    for r in range(0, padded, piece):
-        long = min(piece, padded - r)
+    for r, long in row_pieces(padded):
         before = iota((long, LANES), 1) < LANES // 2
         span_rows = pl.ds(r, long)
         sides = []
@@ -694,7 +739,7 @@
         bias_third[None],
     )
     count = len(args)
-    *held, head, tail = pl.pallas_call(
+    *held, to_even, to_odd = pl.pallas_call(
         functools.partial(pack_lon_kernel, sizes, count),
         out_shape=[pltpu.VMEM(x.shape, x.dtype) for x in args] + [pltpu.VMEM((tall, lats), bf16)] * 2,
         in_specs=[pl.BlockSpec(memory_space=pltpu.HBM)] * count,
@@ -704,15 +749,16 @@
         name="pack_lon",
     )(*args)
     state = tuple(held[:5])
-    ring = [(i, (i + 1) % lon_count) for i in range(lon_count)]
-    left = lax.ppermute(tail, "lon", ring)
-    right = lax.ppermute(head, "lon", [(b, a) for a, b in ring])
+    lon_even = lax.ppermute(to_even, "lon", [(i, i ^ 1) for i in range(lon_count)])
+    lon_odd = lax.ppermute(to_odd, "lon", [(i, (i - 1 + 2 * (i % 2)) % lon_count) for i in range(lon_count)])
 
     wide = -(-(fields + 1) * GROUP // SUB) * SUB
     part = pltpu.VMEM((wide, LANES), f32)
     message = pltpu.VMEM((wide, LANES), bf16)
     deep = -(-(lons // 2 + 2) * hidden // LANES) * LANES
-    t1, t2, t3, t4, own_head, own_tail = pl.pallas_call(
+    padded = rows + 2 * SUB
+    tiles = 2 * groups + 1
+    t1, t2, t3, t4, own_head, own_tail, middle, pre = pl.pallas_call(
         functools.partial(prepare_kernel, sizes),
         out_shape=[
             pltpu.VMEM((3 * LANES, 2 * LANES), bf16),
@@ -721,10 +767,16 @@
             pltpu.VMEM((2, deep, 2 * LANES), bf16),
             part,
             part,
+            pltpu.VMEM((groups - 2, padded, LANES), bf16),
+            pltpu.VMEM((tiles, padded, LANES), bf16),
         ],
         in_specs=[whole] * count,
-        out_specs=[whole] * 6,
-        compiler_params=pltpu.CompilerParams(vmem_limit_bytes=8 * 2**20),
+        out_specs=[whole] * 8,
+        scratch_shapes=[
+            pltpu.VMEM((groups - 2, rows, LANES), f32),
+            pltpu.VMEM((members * (groups - 2) * lats // LANES, LANES, LANES), f32),
+        ],
+        compiler_params=pltpu.CompilerParams(vmem_limit_bytes=12 * 2**20),
         cost_estimate=pl.CostEstimate(flops=10**7, bytes_accessed=10**7, transcendentals=0),
         name="prepare",
     )(*held)
@@ -741,7 +793,7 @@
         ],
         compiler_params=pltpu.CompilerParams(vmem_limit_bytes=4 * 2**20),
         name="join_rims",
-    )(left, right, own_head, own_tail)
+    )(lon_even, lon_odd, own_head, own_tail)
     even_rim = lax.ppermute(to_even, "lat", [(i, i ^ 1) for i in range(lat_count)])
     pairs = []
     for t in range(lon_count):
@@ -750,32 +802,29 @@
         pairs += [(at, (t ^ 1) * lat_count), (at + last, (lon_count - 1 - t) * lat_count + last)]
     odd_rim = lax.ppermute(to_odd, ("lon", "lat"), pairs)
 
-    own, base = pl.pallas_call(
+    ends, base = pl.pallas_call(
         functools.partial(cells_kernel, sizes),
-        out_shape=[pltpu.VMEM((groups, rows, LANES), bf16), pltpu.VMEM((3, *velocity_u.shape), f32)],
+        out_shape=[pltpu.VMEM((2, padded, LANES), bf16), pltpu.VMEM((3, *velocity_u.shape), f32)],
         in_specs=[whole] * 8,
         out_specs=[whole] * 2,
         scratch_shapes=[
             pltpu.VMEM((2, tall, lats), f32),
-            pltpu.VMEM((groups, rows, LANES), f32),
-            pltpu.VMEM((members * groups * lats // LANES, LANES, LANES), f32),
+            pltpu.VMEM((2, rows, LANES), f32),
+            pltpu.VMEM((2 * members * lats // LANES, LANES, LANES), f32),
         ],
         compiler_params=pltpu.CompilerParams(vmem_limit_bytes=12 * 2**20),
         cost_estimate=pl.CostEstimate(flops=10**7, bytes_accessed=10**7, transcendentals=0),
         name="cells",
-    )(*state, left, right, to_even)
-
-    padded = rows + 2 * SUB
-    tiles = 2 * groups + 1
+    )(*state, lon_even, lon_odd, to_even)
+
     out = jax.ShapeDtypeStruct(velocity_u.shape, f32)
     return pl.pallas_call(
         functools.partial(main_kernel, sizes),
-        out_shape=[out] * 3,
-        in_specs=[smem] + [whole] * 10,
-        out_specs=[pl.BlockSpec(memory_space=pltpu.HBM)] * 3,
+        out_shape=[out] * 3 + [pltpu.VMEM(x.shape, x.dtype) for x in (middle, ends, pre)],
+        in_specs=[smem] + [whole] * 12,
+        out_specs=[pl.BlockSpec(memory_space=pltpu.HBM)] * 3 + [whole] * 3,
+        input_output_aliases={1: 3, 2: 4, 3: 5},
         scratch_shapes=[
-            pltpu.VMEM((groups, padded, LANES), bf16),
-            pltpu.VMEM((tiles, padded, LANES), bf16),
             pltpu.VMEM((tiles, padded, LANES), bf16),
             pltpu.VMEM((3, padded, LANES), f32),
             pltpu.VMEM((members, lats, LANES), f32),
@@ -789,7 +838,9 @@
         name="network_and_step",
     )(
         bias_last,
-        own,
+        middle,
+        ends,
+        pre,
         base,
         state[4],
         even_rim,
@@ -799,7 +850,7 @@
         t2,
         t3,
         t4,
-    )
+    )[:3]
 
 
 def solution(mesh):

time: 29.3 us -> 27.3 us (0.932)
  the two profiles are of different devices: /device:TPU:11 before, /device:TPU:20 now
where the time goes in v8:
time: 27.3 us; the launch traced here: 27.2 us
  Pallas kernels  19.6 us (72%)
  waiting for transfers between devices  3.69 us (14%)
  starting transfers between devices  3.25 us (12%)
  between operations  0.69 us (3%)
    pallas_call x1, Pallas kernels, body(): pl.pallas_call(functools.partial(main_kernel, sizes), out_shape=[out] * 3...  13.7 us
    pallas_call x1, Pallas kernels, body(): pl.pallas_call(functools.partial(prepare_kernel, sizes), out_shape=[pltpu...  2.89 us
    ppermute x1, starting transfers between devices, body(): lax.ppermute(to_even, 'lat', [(i, i ^ 1) for i in range(lat_count)])  1.64 us
    ppermute x1, waiting for transfers between devices, body(): odd_rim = lax.ppermute(to_odd, ('lon', 'lat'), pairs)  1.58 us
    ppermute x1, starting transfers between devices, body(): lax.ppermute(to_odd, 'lon', [(i, (i - 1 + 2 * (i % 2)) % lon_count) for i...  1.54 us
    pallas_call x1, Pallas kernels, body(): pl.pallas_call(functools.partial(pack_lon_kernel, sizes, count), out_shap...  1.46 us
    pallas_call x1, Pallas kernels, body(): pl.pallas_call(functools.partial(cells_kernel, sizes), out_shape=[pltpu.V...  1.39 us
    ppermute x1, waiting for transfers between devices, body(): lax.ppermute(to_odd, 'lon', [(i, (i - 1 + 2 * (i % 2)) % lon_count) for i...  1.27 us
  transfers between devices with their start and end apart: 4, of which 3 were waited for; matrix products, arithmetic and copies ran while one was open for 0% of the time, Pallas kernels for 16%

profile of v8, /device:TPU:20, one launch (start us, length us, event | category | flops | bytes accessed | tf_op | source)
XLA Modules:
  0.0 27.2 jit_solution(15164365711515853164)
XLA Ops:
  0.6 0.0 copy-start
  0.6 1.5 %pack_lon.1 = (bf16[4,4,32,256]{3,2,1,0:T(8,128)(2,1)S(1)}, f32[4,2,32,256]{3,2,1,0:T(8,128)S(1)}, f32[4,2,32,256]{3,2,1,0:T(8,128)S(1)}, f32[4,2,32,256]{3,2,1,...) custom-call(bf16[4,4,32,256]{3,2,1,0:T(8,128)(2,1)} %refs_0_.1, ...), custom_call_target="tpu_custom_call" | custom-call | tf_op jit(solution)/shard_map/pack_lon/pallas_call | solution.py:742
  2.1 0.1 collective-permute-start
  2.2 1.5 %collective-permute-start.1 = (bf16[192,256]{1,0:T(8,128)(2,1)S(1)}, bf16[192,256]{1,0:T(8,128)(2,1)S(1)}, u32[]{:S(2)}, u32[]{:S(2)}) collective-permute-start(bf16[192,256]{1,0:T(8,128)(2,1)S(1)} %get-tuple-element.46), channel_id=1, source_target_pairs={{0,28},{4,8},{8,4},{12,16},{16,12},{20,24},{24,20},{28,0},{1,29},{... | collective-permute-start | bytes 294920 | tf_op jit(solution)/shard_map/ppermute | solution.py:753
  3.7 2.9 %prepare.1 = (bf16[384,256]{1,0:T(8,128)(2,1)S(1)}, bf16[1024,256]{1,0:T(8,128)(2,1)S(1)}, bf16[1024,256]{1,0:T(8,128)(2,1)S(1)}, bf16[2,640,256]{2,1,0:T(8,128)...) custom-call(bf16[4,4,32,256]{3,2,1,0:T(8,128)(2,1)S(1)} %get-tuple-e, ...), custom_call_target="tpu_custom_call" | custom-call | flops 10000000 | bytes 10000000 | tf_op jit(solution)/shard_map/prepare/pallas_call | solution.py:761
  6.6 0.0 collective-permute-done.lon_even
  6.6 1.3 %collective-permute-done.1.lon_odd = bf16[192,256]{1,0:T(8,128)(2,1)S(1)} collective-permute-done((bf16[192,256]{1,0:T(8,128)(2,1)S(1)}, bf16[192,256]{1,0:T(8,128)(2,1)S(1)}, u32[]{:S(2)}, u32[]{:S(2)}) %collective-permute-start.1) | collective-permute-done | bytes 98336 | tf_op jit(solution)/shard_map/ppermute | solution.py:753
  7.9 0.2 join_rims.1
  8.1 1.6 %collective-permute-start.2 = (bf16[96,128]{1,0:T(8,128)(2,1)S(1)}, bf16[96,128]{1,0:T(8,128)(2,1)S(1)}, u32[]{:S(2)}, u32[]{:S(2)}) collective-permute-start(bf16[96,128]{1,0:T(8,128)(2,1)S(1)} %get-tuple-element.49.after), channel_id=1, source_target_pairs={{0,1},{1,0},{2,3},{3,2},{4,5},{5,4},{6,7},{7,6},{8,9},{9,8},{10,11... | collective-permute-start | bytes 73736 | tf_op jit(solution)/shard_map/ppermute | solution.py:797
  9.7 0.0 collective-permute-start.3
  9.7 1.4 %cells.1 = (bf16[2,1120,128]{2,1,0:T(8,128)(2,1)S(1)}, f32[3,4,2,32,256]{4,3,2,1,0:T(8,128)S(1)}) custom-call(bf16[4,4,32,256]{3,2,1,0:T(8,128)(2,1)S(1)} %get-tuple-element.32.noise, f32[4,2,32,256]{3,2,1,0:T(8,128)S(1)} %get-tuple-element.33.u, f32[4,2,32,256]{3,2,1,0:T(8,128)S(1)} %get-tuple-element.34.v, f32[4,2,32,256]{3,2,1,0:T(8,128)S(1)} %get-tuple-element.35.h, ...), custom_call_target="tpu_custom_call" | custom-call | flops 10000000 | bytes 10000000 | tf_op jit(solution)/shard_map/cells/pallas_call | solution.py:805
  11.1 0.8 %collective-permute-done.2.even_rim = bf16[96,128]{1,0:T(8,128)(2,1)S(1)} collective-permute-done((bf16[96,128]{1,0:T(8,128)(2,1)S(1)}, bf16[96,128]{1,0:T(8,128)(2,1)S(1)}, u32[]{:S(2)}, u32[]{:S(2)}) %collective-permute-start.2) | collective-permute-done | bytes 24608 | tf_op jit(solution)/shard_map/ppermute | solution.py:797
  12.0 1.6 %collective-permute-done.3.odd_rim = bf16[96,128]{1,0:T(8,128)(2,1)S(1)} collective-permute-done((bf16[96,128]{1,0:T(8,128)(2,1)S(1)}, bf16[96,128]{1,0:T(8,128)(2,1)S(1)}, u32[]{:S(2)}, u32[]{:S(2)}) %collective-permute-start.3) | collective-permute-done | bytes 24608 | tf_op jit(solution)/shard_map/ppermute | solution.py:803
  13.5 0.0 copy-done
  13.5 13.7 %network_and_step.1 = (f32[4,2,32,256]{3,2,1,0:T(8,128)}, f32[4,2,32,256]{3,2,1,0:T(8,128)}, f32[4,2,32,256]{3,2,1,0:T(8,128)}, bf16[3,1120,128]{2,1,0:T(8,128)(...) custom-call(f32[4]{0:T(128)S(1)} %copy-done, ...), custom_call_target="tpu_custom_call", output_to_operand_aliasing={{3}: (1, {}), {4}: (2, {}), {5}: (3, {})} | custom-call | flops 20000000000 | bytes 10000000 | tf_op jit(solution)/shard_map/network_and_step/pallas_call | solution.py:821
Async XLA Ops:
  0.6 12.9 %copy-start = (f32[4]{0:T(128)S(1)}, f32[4]{0:T(128)}, u32[]{:S(2)}) copy-start(f32[4]{0:T(128)} %bias_last.1) | copy-start | bytes 52
  2.1 4.5 %collective-permute-start = (bf16[192,256]{1,0:T(8,128)(2,1)S(1)}, bf16[192,256]{1,0:T(8,128)(2,1)S(1)}, u32[]{:S(2)}, u32[]{:S(2)}) collective-permute-start(bf16[192,256]{1,0:T(8,128)(2,1)S(1)} %get-tuple-element.45), channel_id=1, source_target_pairs={{0,4},{4,0},{8,12},{12,8},{16,20},{20,16},{24,28},{28,24},{1,5},{5... | collective-permute-start | bytes 294920 | tf_op jit(solution)/shard_map/ppermute | solution.py:752
  2.2 5.7 %collective-permute-start.1 = (bf16[192,256]{1,0:T(8,128)(2,1)S(1)}, bf16[192,256]{1,0:T(8,128)(2,1)S(1)}, u32[]{:S(2)}, u32[]{:S(2)}) collective-permute-start(bf16[192,256]{1,0:T(8,128)(2,1)S(1)} %get-tuple-element.46), channel_id=1, source_target_pairs={{0,28},{4,8},{8,4},{12,16},{16,12},{20,24},{24,20},{28,0},{1,29},{... | collective-permute-start | bytes 294920 | tf_op jit(solution)/shard_map/ppermute | solution.py:753
  8.1 3.9 %collective-permute-start.2 = (bf16[96,128]{1,0:T(8,128)(2,1)S(1)}, bf16[96,128]{1,0:T(8,128)(2,1)S(1)}, u32[]{:S(2)}, u32[]{:S(2)}) collective-permute-start(bf16[96,128]{1,0:T(8,128)(2,1)S(1)} %get-tuple-element.49.after), channel_id=1, source_target_pairs={{0,1},{1,0},{2,3},{3,2},{4,5},{5,4},{6,7},{7,6},{8,9},{9,8},{10,11... | collective-permute-start | bytes 73736 | tf_op jit(solution)/shard_map/ppermute | solution.py:797
  9.7 3.8 %collective-permute-start.3 = (bf16[96,128]{1,0:T(8,128)(2,1)S(1)}, bf16[96,128]{1,0:T(8,128)(2,1)S(1)}, u32[]{:S(2)}, u32[]{:S(2)}) collective-permute-start(bf16[96,128]{1,0:T(8,128)(2,1)S(1)} %get-tuple-element.53.own_tail), channel_id=1, source_target_pairs={{1,2},{2,1},{0,4},{3,31},{5,6},{6,5},{4,0},{7,27},{9,10},{10,9},{8... | collective-permute-start | bytes 73736 | tf_op jit(solution)/shard_map/ppermute | solution.py:803

commit v9 on v8

--- a/solution.py
+++ b/solution.py
@@ -86,9 +86,12 @@
 def rim_tile(sizes, m, c, side, rim):
     members, noises, levels = sizes
     fields = noises + 3 * levels
-    row = (m * fields + c) * RIM if c < fields else members * fields * RIM
-    tile = rim[pl.ds(row // GROUP * GROUP, GROUP)]
-    if (row // RIM) % 2 == side:
+    if c < fields:
+        start = m * (fields * RIM) + c * RIM // GROUP * GROUP
+    else:
+        start = members * fields * RIM
+    tile = rim[pl.ds(pl.multiple_of(start, GROUP), GROUP)]
+    if (c if c < fields else 0) % 2 == side:
         return tile
     return pltpu.roll(tile, RIM, 0)
 
@@ -145,22 +148,26 @@
     groups = lons // GROUP + 1
     weights_kernel(*weights, *matrices)
     lane = iota((GROUP, LANES), 1)
+    zero = jnp.zeros((GROUP, LANES), f32)
     for out, t, first in ((head, 0, 0), (tail, lats // LANES - 1, LANES - RIM)):
-        for c in range(fields + 1):
-            total = jnp.zeros((GROUP, LANES), f32)
-            for m in range(members):
+        edge = 0 if first == 0 else LANES - 1
+
+        def add_member(m, totals):
+            totals = list(totals)
+            for c in range(fields + 1):
                 for g, tile in enumerate(shifted_tiles(sizes, held, m, c, t)):
                     place = (g * members + m) * RIM
-                    moved = pltpu.roll(tile, (place - first) % LANES, 1)
-                    total = jnp.where((lane >= place) & (lane < place + RIM), moved, total)
+                    moved = pltpu.roll(tile, lax.rem(place + LANES - first, LANES), 1)
+                    totals[c] = jnp.where((lane >= place) & (lane < place + RIM), moved, totals[c])
                     if noises <= c < fields:
                         place = groups * members * RIM + g * members + m
-                        edge = 0 if out is head else LANES - 1
-                        moved = pltpu.roll(rest(tile), (place - edge) % LANES, 1)
-                        total = jnp.where(lane == place, moved, total)
-            out[pl.ds(c * GROUP, GROUP)] = total
-        for c in range(fields + 1, out.shape[0] // GROUP):
-            out[pl.ds(c * GROUP, GROUP)] = jnp.zeros((GROUP, LANES), f32)
+                        moved = pltpu.roll(rest(tile), lax.rem(place + LANES - edge, LANES), 1)
+                        totals[c] = jnp.where(lane == place, moved, totals[c])
+            return tuple(totals)
+
+        totals = lax.fori_loop(0, members, add_member, (zero,) * (fields + 1))
+        for c in range(out.shape[0] // GROUP):
+            out[pl.ds(c * GROUP, GROUP)] = totals[c] if c < len(totals) else zero
     chunks = SUB // members
     rows = cells.shape[1]
     gap_k = lats - (chunks - 1) * ((lats + GAP) // chunks)
@@ -170,20 +177,27 @@
             empty = pl.ds(gap_k * SUB + (m + 1) * chunks - 1, GAP, stride=SUB)
             cells[g, empty, :] = jnp.zeros((GAP, LANES), f32)
     for t in range(lats // LANES):
-        for m in range(members):
+
+        def lay_out(m, carry):
             tiles = [shifted_tiles(sizes, held, m, c, t) for c in range(fields + 1)]
             for g in range(1, inner + 1):
                 following = [x[g + 1] for x in tiles]
                 block = window([x[g] for x in tiles[:fields]], following[:fields], tiles[fields][g], following[fields])
-                buffer = turned.at[(t * members + m) * inner + g - 1]
-                store_lats(block, t, cells, g - 1, m, lats, chunks, buffer)
+                store_lats(block, t, cells, g - 1, m, lats, chunks, turned.at[g - 1])
+            return carry
+
+        lax.fori_loop(0, members, lay_out, 0)
     for g in range(inner):
-        middle[g, pl.ds(SUB, rows), :] = cells[g].astype(bf16)
-        wrap(middle.at[g], rows)
-    for g in range(inner):
+        middle[g + 1, pl.ds(SUB, rows), :] = cells[g].astype(bf16)
+        wrap(middle.at[g + 1], rows)
+
+    def first_layer(g, carry):
         for r, step in row_pieces(rows):
             parts = [middle[g, pl.ds(r + SUB * d, step), :] for d in range(3)]
-            put(pre, g + 1, r, activate(dot(jnp.concatenate(parts, axis=1), matrices[0][...])))
+            put(pre, g, r, activate(dot(jnp.concatenate(parts, axis=1), matrices[0][...])))
+        return carry
+
+    lax.fori_loop(1, inner + 1, first_layer, 0)
 
 
 def row_pieces(rows):
@@ -207,7 +221,7 @@
     x[pl.ds(SUB + rows, SUB), :] = pltpu.roll(begin, SUB - 1, 0).astype(bf16)
 
 
-def cells_kernel(sizes, noise, u, v, h, sea, lon_even, lon_odd, after, out, base, rims, cells, turned):
+def cells_kernel(sizes, noise, u, v, h, sea, lon_even, lon_odd, after, given, out, base, rims, cells, turned):
     members, noises, levels = sizes
     fields = noises + 3 * levels
     lons, lats = sea.shape
@@ -224,7 +238,8 @@
     upper = iota((GROUP, LANES), 0) < RIM
     for t in range(lats // LANES):
         lanes = slice(t * LANES, (t + 1) * LANES)
-        for m in range(members):
+
+        def lay_out(m, carry):
             tiles = []
             for c in range(fields + 1):
                 groups_of = shifted_tiles(sizes, (noise, u, v, h, sea), m, c, t)
@@ -235,9 +250,12 @@
             for side, g in enumerate((0, groups - 1)):
                 following = [x[g + 1] if g + 1 < groups else blank for x in tiles]
                 block = window([x[g] for x in tiles[:fields]], following[:fields], tiles[fields][g], following[fields])
-                store_lats(block, t, cells, side, m, lats, chunks, turned.at[(t * members + m) * 2 + side])
-    for side in range(2):
-        out[side, pl.ds(SUB, rows), :] = cells[side].astype(bf16)
+                store_lats(block, t, cells, side, m, lats, chunks, turned.at[side])
+            return carry
+
+        lax.fori_loop(0, members, lay_out, 0)
+    for side, g in enumerate((0, groups - 1)):
+        out[g, pl.ds(SUB, rows), :] = cells[side].astype(bf16)
     step_kernel(sizes, u, v, h, sea, rims, base)
 
 
@@ -267,7 +285,7 @@
             jnp.where(at_north, 0.0, pltpu.roll(x, lats - 1, 1)),
         )
 
-    for m in range(members):
+    def member(m, carry):
         sets = []
         for level in range(levels):
             sets.append(
@@ -290,6 +308,9 @@
             base[1, m, level] = ocean * (cv + TIME_STEP * (-turn * cu - dy + VISCOSITY * lap_v))
             flow = 0.5 * (ah[1] * au[1] - ah[0] * au[0]) + 0.5 * (ah[3] * av[3] - ah[2] * av[2])
             base[2, m, level] = ch - TIME_STEP * flow
+        return carry
+
+    lax.fori_loop(0, members, member, 0)
 
 
 def join_kernel(sizes, lons, lon_even, lon_odd, head, tail, even, odd, rims, wide):
@@ -439,8 +460,7 @@
 def main_kernel(
     sizes,
     bias_last,
-    middle_in,
-    ends_in,
+    first_in,
     pre_in,
     base,
     sea,
@@ -454,14 +474,14 @@
     new_u,
     new_v,
     new_h,
-    middle,
-    ends,
+    first,
     odd,
     even,
     force,
     gathered,
     turned,
     gaps,
+    messages,
     results,
     done,
 ):
@@ -507,23 +527,33 @@
     north_rim = jnp.where(border & top, folded, north)
 
     for n, message in enumerate((north_rim, strip, ghost, south)):
+        messages[n] = message
+
+    def lay_out(n, carry):
+        message = messages[n]
         after = pltpu.roll(message, LANES - span, 1)
         cut = [message[c * GROUP : (c + 1) * GROUP] for c in range(fields + 1)]
         after = [after[c * GROUP : (c + 1) * GROUP] for c in range(fields + 1)]
-        turned[n] = jnp.transpose(window(cut[:fields], after[:fields], cut[fields], after[fields]))
+        turned[...] = jnp.transpose(window(cut[:fields], after[:fields], cut[fields], after[fields]))
         for g in range(groups):
             for m in range(members):
-                gap = (m - 1) % members if n == 3 else m
-                start = n * RIM * SUB + gap * chunks + chunks - 1
-                gaps[g, pl.ds(start, RIM, stride=SUB), :] = turned[n, pl.ds((g * members + m) * RIM, RIM), :]
-
-    first = [ends.at[0]] + [middle.at[g] for g in range(groups - 2)] + [ends.at[1]]
+                gap = jnp.where(n == 3, (m - 1) % members, m)
+                start = n * (RIM * SUB) + gap * chunks + chunks - 1
+                gaps[g, pl.ds(start, RIM, stride=SUB), :] = turned[pl.ds((g * members + m) * RIM, RIM), :]
+        return carry
+
+    lax.fori_loop(0, 4, lay_out, 0)
+
     in_gap = iota((GAP * SUB, LANES), 0) % chunks == chunks - 1
-    for g in range(groups):
+
+    def fill_gap(g, carry):
         spot = pl.ds((1 + gap_k) * SUB, GAP * SUB)
-        kept = first[g][spot, :].astype(f32)
-        first[g][spot, :] = jnp.where(in_gap, gaps[g], kept).astype(bf16)
-        wrap(first[g], rows)
+        kept = first[g, spot, :].astype(f32)
+        first[g, spot, :] = jnp.where(in_gap, gaps[g], kept).astype(bf16)
+        wrap(first.at[g], rows)
+        return carry
+
+    lax.fori_loop(0, groups, fill_gap, 0)
 
     hidden = LANES // 4
     per = LANES // hidden
@@ -541,44 +571,60 @@
             own_ghost = SUB * (1 + gap_k + NORTH)
             last_chunk = iota((SUB, LANES), 0) % chunks == chunks - 1
             spot = iota((SUB, LANES), 1) // hidden
-            for src, dst in ((strip_top, own_ghost), (own_top, strip_ghost)):
-                found = [x[t, pl.ds(src, SUB), :].astype(f32) for t in range(used)]
-                for t in range(used):
+            edge = (valid - 1) % per
+
+            def turn_tile(t, carry):
+                high = (valid - 1) // per - t
+                low = jnp.maximum(high - 1, 0)
+                for src, dst in ((strip_top, own_ghost), (own_top, strip_ghost)):
+                    found = [x[n, pl.ds(src, SUB), :].astype(f32) for n in (high, low)]
                     total = x[t, pl.ds(dst, SUB), :].astype(f32)
                     for i in range(per):
-                        lon = valid - 1 - (per * t + i)
-                        if lon < 0:
-                            continue
-                        moved = pltpu.roll(found[lon // per], (hidden * (i - lon % per)) % LANES, 1)
+                        lon = edge - i
+                        moved = pltpu.roll(found[0 if lon >= 0 else 1], (hidden * (i - lon % per)) % LANES, 1)
                         total = jnp.where(last_chunk & (spot == i), moved, total)
                     x[t, pl.ds(dst, SUB), :] = total.astype(bf16)
-
-        for t in range(used):
+                return carry
+
+            lax.fori_loop(0, used, turn_tile, 0)
+
+        def wrap_tile(t, carry):
             wrap(x.at[t], rows)
+            return carry
+
+        lax.fori_loop(0, used, wrap_tile, 0)
 
     for x in (odd, even):
         x[tiles - 1] = jnp.zeros(x.shape[1:], bf16)
     even[tiles - 2] = jnp.zeros(even.shape[1:], bf16)
 
-    for b in (0, groups - 1):
+    def first_ends(side, carry):
+        b = side * (groups - 1)
         for r, step in pieces:
-            parts = [first[b][pl.ds(r + SUB * d, step), :] for d in range(3)]
+            parts = [first[b, pl.ds(r + SUB * d, step), :] for d in range(3)]
             put(odd, b, r, activate(dot(jnp.concatenate(parts, axis=1), t1[...])))
+        return carry
+
+    lax.fori_loop(0, 2, first_ends, 0)
     near = (gap_k - 1) * SUB
-    for b in range(1, groups - 1):
+
+    def first_middle(b, carry):
         parts = []
         for d in range(3):
-            some = [first[b][pl.ds(near + SUB * d, rows - near), :], first[b][pl.ds(SUB * d, SUB), :]]
+            some = [first[b, pl.ds(near + SUB * d, rows - near), :], first[b, pl.ds(SUB * d, SUB), :]]
             parts.append(jnp.concatenate(some, axis=0))
         out = activate(dot(jnp.concatenate(parts, axis=1), t1[...]))
         put(odd, b, near, out[: rows - near])
         put(odd, b, 0, out[rows - near :])
+        return carry
+
+    lax.fori_loop(1, groups - 1, first_middle, 0)
     finish(odd, lons + 6)
 
     width = GROUP * hidden
 
     def layer(x, y, t, left_over):
-        for b in range(groups):
+        def block(b, last=False):
             for r, step in pieces:
                 lower = iota((step, LANES), 1) < 2 * hidden
 
@@ -589,10 +635,10 @@
                     more = [cells_of(tile, d) for d in range(3)]
                     return [
                         jnp.where(lower, more[0], pltpu.roll(more[1], 2 * hidden, 1)),
-                        jnp.where(lower, more[2], first[b][pl.ds(r + SUB, step), :]),
+                        jnp.where(lower, more[2], first[b, pl.ds(r + SUB, step), :]),
                     ]
 
-                if b < groups - 1:
+                if not last:
                     parts = [cells_of(2 * b + e, d) for d in range(3) for e in range(2)] + packed(2 * b + 2)
                     matrix = t[...]
                 elif left_over == per:
@@ -605,7 +651,7 @@
                         axis=0,
                     )
                 else:
-                    parts = [cells_of(2 * b, d) for d in range(3)] + [first[b][pl.ds(r + SUB, step), :]]
+                    parts = [cells_of(2 * b, d) for d in range(3)] + [first[b, pl.ds(r + SUB, step), :]]
                     lanes = pl.ds(0, LANES)
                     matrix = jnp.concatenate(
                         [t[pl.ds(d * width, LANES), lanes] for d in range(3)]
@@ -615,6 +661,13 @@
                     )
                 put(y, b, r, activate(dot(jnp.concatenate(parts, axis=1), matrix)))
 
+        def turn(b, carry):
+            block(b)
+            return carry
+
+        lax.fori_loop(0, groups - 1, turn, 0)
+        block(groups - 1, last=True)
+
     layer(odd, even, t2, per)
     finish(even, lons + 4)
     layer(even, odd, t3, per // 2)
@@ -622,9 +675,11 @@
 
     depth = t4.shape[1] // LANES
     padded = rows + 2 * SUB
-    for r, long in row_pieces(padded):
-        before = iota((long, LANES), 1) < LANES // 2
-        span_rows = pl.ds(r, long)
+    long = padded // 2
+    before = iota((long, LANES), 1) < LANES // 2
+
+    def last_layer(n, carry):
+        span_rows = pl.ds(pl.multiple_of(n * long, SUB), long)
         sides = []
         for side in range(2):
             parts = [odd[side * (depth - 1) + t, span_rows, :] for t in range(depth)]
@@ -633,6 +688,9 @@
         swapped = jnp.where(before, sides[1][:, :LANES], sides[0][:, :LANES])
         force[1, span_rows, :] = pltpu.roll(swapped, LANES // 2, 1)
         force[2, span_rows, :] = jnp.where(before, sides[0][:, LANES:], sides[1][:, LANES:])
+        return carry
+
+    lax.fori_loop(0, 2, last_layer, 0)
 
     ocean = sea[...].astype(f32)
     narrow = iota((lons, LANES), 1)
@@ -640,28 +698,30 @@
     at_north = narrow == LANES - 1
     halves = lons // 2
 
-    def beyond(message, m, c, offset):
-        cells = []
-        some = slice(c * GROUP, (c + 1) * GROUP)
+    def beyond(n, m, offset, to):
+        some = pl.ds(noises * GROUP, (fields - noises) * GROUP)
+        columns = []
         for g in range(groups):
             spot = (g * members + m) * RIM + offset
             more = rests + g * members + m
-            cells.append(message[some, spot : spot + 1] + message[some, more : more + 1])
-        whole = jnp.broadcast_to(jnp.concatenate(cells, axis=0), (lons + GROUP, LANES))
-        return pltpu.roll(whole, lons + GROUP - RIM, 0)[:lons]
-
-    for m in range(members):
+            tall = messages[n, some, :]
+            column = pltpu.roll(tall, lax.rem(LANES + to - spot, LANES), 1)
+            columns.append(column + pltpu.roll(tall, lax.rem(LANES + to - more, LANES), 1))
+        cells = []
+        for c in range(fields - noises):
+            whole = jnp.concatenate([x[c * GROUP : (c + 1) * GROUP] for x in columns], axis=0)
+            cells.append(pltpu.roll(whole, lons + GROUP - RIM, 0)[:lons])
+        return cells
+
+    def member(m, carry):
         for q in range(chunks):
             size = min(blocks, lats - q * blocks)
             total = force[0, pl.ds(m * chunks + q, size, stride=SUB), :]
             for d in range(1, 3):
                 total = total + force[d, pl.ds(d * SUB + m * chunks + q, size, stride=SUB), :]
-            gathered[m, pl.ds(q * blocks, size), :] = total
-        turned_force = jnp.transpose(gathered[m])
-        rims = [
-            [beyond(message, m, c, offset) for c in range(noises, fields)]
-            for message, offset in ((south, RIM - 1), (north_rim, 0))
-        ]
+            gathered[pl.ds(q * blocks, size), :] = total
+        turned_force = jnp.transpose(gathered[...])
+        rims = [beyond(3, m, RIM - 1, 0), beyond(0, m, 0, LANES - 1)]
         for level in range(levels):
             gains = []
             for (sign, spot), rim in zip(((1.0, at_south), (-1.0, at_north)), rims):
@@ -691,6 +751,9 @@
             results[2, m, level] = base[2, m, level] + gains[2]
         for n, out in enumerate((new_u, new_v, new_h)):
             pltpu.make_async_copy(results.at[n, m], out.at[m], done.at[n, m]).start()
+        return carry
+
+    lax.fori_loop(0, members, member, 0)
     for m in range(members):
         for n, out in enumerate((new_u, new_v, new_h)):
             pltpu.make_async_copy(results.at[n, m], out.at[m], done.at[n, m]).wait()
@@ -758,7 +821,7 @@
     deep = -(-(lons // 2 + 2) * hidden // LANES) * LANES
     padded = rows + 2 * SUB
     tiles = 2 * groups + 1
-    t1, t2, t3, t4, own_head, own_tail, middle, pre = pl.pallas_call(
+    t1, t2, t3, t4, own_head, own_tail, windows, pre = pl.pallas_call(
         functools.partial(prepare_kernel, sizes),
         out_shape=[
             pltpu.VMEM((3 * LANES, 2 * LANES), bf16),
@@ -767,14 +830,14 @@
             pltpu.VMEM((2, deep, 2 * LANES), bf16),
             part,
             part,
-            pltpu.VMEM((groups - 2, padded, LANES), bf16),
+            pltpu.VMEM((groups, padded, LANES), bf16),
             pltpu.VMEM((tiles, padded, LANES), bf16),
         ],
         in_specs=[whole] * count,
         out_specs=[whole] * 8,
         scratch_shapes=[
             pltpu.VMEM((groups - 2, rows, LANES), f32),
-            pltpu.VMEM((members * (groups - 2) * lats // LANES, LANES, LANES), f32),
+            pltpu.VMEM((groups - 2, LANES, LANES), f32),
         ],
         compiler_params=pltpu.CompilerParams(vmem_limit_bytes=12 * 2**20),
         cost_estimate=pl.CostEstimate(flops=10**7, bytes_accessed=10**7, transcendentals=0),
@@ -802,34 +865,36 @@
         pairs += [(at, (t ^ 1) * lat_count), (at + last, (lon_count - 1 - t) * lat_count + last)]
     odd_rim = lax.ppermute(to_odd, ("lon", "lat"), pairs)
 
-    ends, base = pl.pallas_call(
+    windows, base = pl.pallas_call(
         functools.partial(cells_kernel, sizes),
-        out_shape=[pltpu.VMEM((2, padded, LANES), bf16), pltpu.VMEM((3, *velocity_u.shape), f32)],
-        in_specs=[whole] * 8,
+        out_shape=[pltpu.VMEM(windows.shape, bf16), pltpu.VMEM((3, *velocity_u.shape), f32)],
+        in_specs=[whole] * 9,
         out_specs=[whole] * 2,
+        input_output_aliases={8: 0},
         scratch_shapes=[
             pltpu.VMEM((2, tall, lats), f32),
             pltpu.VMEM((2, rows, LANES), f32),
-            pltpu.VMEM((2 * members * lats // LANES, LANES, LANES), f32),
+            pltpu.VMEM((2, LANES, LANES), f32),
         ],
         compiler_params=pltpu.CompilerParams(vmem_limit_bytes=12 * 2**20),
         cost_estimate=pl.CostEstimate(flops=10**7, bytes_accessed=10**7, transcendentals=0),
         name="cells",
-    )(*state, lon_even, lon_odd, to_even)
+    )(*state, lon_even, lon_odd, to_even, windows)
 
     out = jax.ShapeDtypeStruct(velocity_u.shape, f32)
     return pl.pallas_call(
         functools.partial(main_kernel, sizes),
-        out_shape=[out] * 3 + [pltpu.VMEM(x.shape, x.dtype) for x in (middle, ends, pre)],
-        in_specs=[smem] + [whole] * 12,
-        out_specs=[pl.BlockSpec(memory_space=pltpu.HBM)] * 3 + [whole] * 3,
-        input_output_aliases={1: 3, 2: 4, 3: 5},
+        out_shape=[out] * 3 + [pltpu.VMEM(x.shape, x.dtype) for x in (windows, pre)],
+        in_specs=[smem] + [whole] * 11,
+        out_specs=[pl.BlockSpec(memory_space=pltpu.HBM)] * 3 + [whole] * 2,
+        input_output_aliases={1: 3, 2: 4},
         scratch_shapes=[
             pltpu.VMEM((tiles, padded, LANES), bf16),
             pltpu.VMEM((3, padded, LANES), f32),
-            pltpu.VMEM((members, lats, LANES), f32),
-            pltpu.VMEM((4, LANES, LANES), f32),
+            pltpu.VMEM((lats, LANES), f32),
+            pltpu.VMEM((LANES, LANES), f32),
             pltpu.VMEM((groups, GAP * SUB, LANES), f32),
+            pltpu.VMEM((4, wide, LANES), f32),
             pltpu.VMEM((3, *velocity_u.shape), f32),
             pltpu.SemaphoreType.DMA((3, members)),
         ],
@@ -838,8 +903,7 @@
         name="network_and_step",
     )(
         bias_last,
-        middle,
-        ends,
+        windows,
         pre,
         base,
         state[4],

time: 27.3 us -> 33.6 us (1.23)
  the two profiles are of different devices: /device:TPU:20 before, /device:TPU:24 now
where the time goes in v9:
time: 33.6 us; the launch traced here: 33.5 us
  Pallas kernels  27.6 us (82%)
  starting transfers between devices  3.14 us (9%)
  waiting for transfers between devices  2.03 us (6%)
  between operations  0.7 us (2%)
    pallas_call x1, Pallas kernels, body(): pl.pallas_call(functools.partial(main_kernel, sizes), out_shape=[out] * 3...  18.5 us
    pallas_call x1, Pallas kernels, body(): pl.pallas_call(functools.partial(prepare_kernel, sizes), out_shape=[pltpu...  5.39 us
    ppermute x1, starting transfers between devices, body(): lax.ppermute(to_odd, 'lon', [(i, (i - 1 + 2 * (i % 2)) % lon_count) for i...  2.55 us
    pallas_call x1, Pallas kernels, body(): pl.pallas_call(functools.partial(cells_kernel, sizes), out_shape=[pltpu.V...  2.12 us
    pallas_call x1, Pallas kernels, body(): pl.pallas_call(functools.partial(pack_lon_kernel, sizes, count), out_shap...  1.46 us
    ppermute x1, waiting for transfers between devices, body(): lax.ppermute(to_even, 'lat', [(i, i ^ 1) for i in range(lat_count)])  1.25 us
    ppermute x1, waiting for transfers between devices, body(): odd_rim = lax.ppermute(to_odd, ('lon', 'lat'), pairs)  0.77 us
  transfers between devices with their start and end apart: 4, of which 2 were waited for; matrix products, arithmetic and copies ran while one was open for 0% of the time, Pallas kernels for 22%

profile of v9, /device:TPU:24, one launch (start us, length us, event | category | flops | bytes accessed | tf_op | source)
XLA Modules:
  0.0 33.5 jit_solution(1870913921842591278)
XLA Ops:
  0.6 1.5 %pack_lon.1 = (bf16[4,4,32,256]{3,2,1,0:T(8,128)(2,1)S(1)}, f32[4,2,32,256]{3,2,1,0:T(8,128)S(1)}, f32[4,2,32,256]{3,2,1,0:T(8,128)S(1)}, f32[4,2,32,256]{3,2,1,...) custom-call(bf16[4,4,32,256]{3,2,1,0:T(8,128)(2,1)} %refs_0_.1, ...), custom_call_target="tpu_custom_call" | custom-call | tf_op jit(solution)/shard_map/pack_lon/pallas_call | solution.py:805
  2.1 0.1 collective-permute-start
  2.2 2.5 %collective-permute-start.1 = (bf16[192,256]{1,0:T(8,128)(2,1)S(1)}, bf16[192,256]{1,0:T(8,128)(2,1)S(1)}, u32[]{:S(2)}, u32[]{:S(2)}) collective-permute-start(bf16[192,256]{1,0:T(8,128)(2,1)S(1)} %get-tuple-element.38), channel_id=1, source_target_pairs={{0,28},{4,8},{8,4},{12,16},{16,12},{20,24},{24,20},{28,0},{1,29},{... | collective-permute-start | bytes 294920 | tf_op jit(solution)/shard_map/ppermute | solution.py:816
  4.7 5.4 %prepare.1 = (bf16[384,256]{1,0:T(8,128)(2,1)S(1)}, bf16[1024,256]{1,0:T(8,128)(2,1)S(1)}, bf16[1024,256]{1,0:T(8,128)(2,1)S(1)}, bf16[2,640,256]{2,1,0:T(8,128)...) custom-call(bf16[4,4,32,256]{3,2,1,0:T(8,128)(2,1)S(1)} %get-tuple-e, ...), custom_call_target="tpu_custom_call" | custom-call | flops 10000000 | bytes 10000000 | tf_op jit(solution)/shard_map/prepare/pallas_call | solution.py:824
  10.1 0.0 collective-permute-done.lon_even
  10.1 0.0 collective-permute-done.1.lon_odd
  10.1 0.2 join_rims.1
  10.3 0.0 copy-start
  10.3 0.5 %collective-permute-start.2 = (bf16[96,128]{1,0:T(8,128)(2,1)S(1)}, bf16[96,128]{1,0:T(8,128)(2,1)S(1)}, u32[]{:S(2)}, u32[]{:S(2)}) collective-permute-start(bf16[96,128]{1,0:T(8,128)(2,1)S(1)} %get-tuple-element.48.after), channel_id=1, source_target_pairs={{0,1},{1,0},{2,3},{3,2},{4,5},{5,4},{6,7},{7,6},{8,9},{9,8},{10,11... | collective-permute-start | bytes 73736 | tf_op jit(solution)/shard_map/ppermute | solution.py:860
  10.9 0.0 collective-permute-start.3
  10.9 2.1 %cells.1 = (bf16[5,1120,128]{2,1,0:T(8,128)(2,1)S(1)}, f32[3,4,2,32,256]{4,3,2,1,0:T(8,128)S(1)}) custom-call(bf16[4,4,32,256]{3,2,1,0:T(8,128)(2,1)S(1)} %get-tuple-element.32.noise, f32[4,2,32,256]{3,2,1,0:T(8,128)S(1)} %get-tuple-element.33.u, f32[4,2,32,256]{3,2,1,0:T(8,128)S(1)} %get-tuple-element.34.v, ...), custom_call_target="tpu_custom_call", output_to_operand_aliasing={{0}: (8, {})} | custom-call | flops 10000000 | bytes 10000000 | tf_op jit(solution)/shard_map/cells/pallas_call | solution.py:868
  13.0 1.2 %collective-permute-done.2.even_rim = bf16[96,128]{1,0:T(8,128)(2,1)S(1)} collective-permute-done((bf16[96,128]{1,0:T(8,128)(2,1)S(1)}, bf16[96,128]{1,0:T(8,128)(2,1)S(1)}, u32[]{:S(2)}, u32[]{:S(2)}) %collective-permute-start.2) | collective-permute-done | bytes 24608 | tf_op jit(solution)/shard_map/ppermute | solution.py:860
  14.2 0.8 %collective-permute-done.3.odd_rim = bf16[96,128]{1,0:T(8,128)(2,1)S(1)} collective-permute-done((bf16[96,128]{1,0:T(8,128)(2,1)S(1)}, bf16[96,128]{1,0:T(8,128)(2,1)S(1)}, u32[]{:S(2)}, u32[]{:S(2)}) %collective-permute-start.3) | collective-permute-done | bytes 24608 | tf_op jit(solution)/shard_map/ppermute | solution.py:866
  15.0 0.0 copy-done
  15.0 18.5 %network_and_step.1 = (f32[4,2,32,256]{3,2,1,0:T(8,128)}, f32[4,2,32,256]{3,2,1,0:T(8,128)}, f32[4,2,32,256]{3,2,1,0:T(8,128)}, bf16[5,1120,128]{2,1,0:T(8,128)(2,1)S(1)}, bf16[11,1120,128]{2,1,0:T(8,128)(2,1)S(1)}) custom-call(f32[4]{0:T(128)S(1)} %copy-done, ...), custom_call_target="tpu_custom_call", output_to_operand_aliasing={{3}: (1, {}), {4}: (2, {})} | custom-call | flops 20000000000 | bytes 10000000 | tf_op jit(solution)/shard_map/network_and_step/pallas_call | solution.py:885
Async XLA Ops:
  2.1 8.0 %collective-permute-start = (bf16[192,256]{1,0:T(8,128)(2,1)S(1)}, bf16[192,256]{1,0:T(8,128)(2,1)S(1)}, u32[]{:S(2)}, u32[]{:S(2)}) collective-permute-start(bf16[192,256]{1,0:T(8,128)(2,1)S(1)} %get-tuple-element.37), channel_id=1, source_target_pairs={{0,4},{4,0},{8,12},{12,8},{16,20},{20,16},{24,28},{28,24},{1,5},{5... | collective-permute-start | bytes 294920 | tf_op jit(solution)/shard_map/ppermute | solution.py:815
  2.2 8.0 %collective-permute-start.1 = (bf16[192,256]{1,0:T(8,128)(2,1)S(1)}, bf16[192,256]{1,0:T(8,128)(2,1)S(1)}, u32[]{:S(2)}, u32[]{:S(2)}) collective-permute-start(bf16[192,256]{1,0:T(8,128)(2,1)S(1)} %get-tuple-element.38), channel_id=1, source_target_pairs={{0,28},{4,8},{8,4},{12,16},{16,12},{20,24},{24,20},{28,0},{1,29},{... | collective-permute-start | bytes 294920 | tf_op jit(solution)/shard_map/ppermute | solution.py:816
  10.3 4.7 %copy-start = (f32[4]{0:T(128)S(1)}, f32[4]{0:T(128)}, u32[]{:S(2)}) copy-start(f32[4]{0:T(128)} %bias_last.1) | copy-start | bytes 52
  10.3 3.9 %collective-permute-start.2 = (bf16[96,128]{1,0:T(8,128)(2,1)S(1)}, bf16[96,128]{1,0:T(8,128)(2,1)S(1)}, u32[]{:S(2)}, u32[]{:S(2)}) collective-permute-start(bf16[96,128]{1,0:T(8,128)(2,1)S(1)} %get-tuple-element.48.after), channel_id=1, source_target_pairs={{0,1},{1,0},{2,3},{3,2},{4,5},{5,4},{6,7},{7,6},{8,9},{9,8},{10,11... | collective-permute-start | bytes 73736 | tf_op jit(solution)/shard_map/ppermute | solution.py:860
  10.9 4.2 %collective-permute-start.3 = (bf16[96,128]{1,0:T(8,128)(2,1)S(1)}, bf16[96,128]{1,0:T(8,128)(2,1)S(1)}, u32[]{:S(2)}, u32[]{:S(2)}) collective-permute-start(bf16[96,128]{1,0:T(8,128)(2,1)S(1)} %get-tuple-element.53.own_tail), channel_id=1, source_target_pairs={{1,2},{2,1},{0,4},{3,31},{5,6},{6,5},{4,0},{7,27},{9,10},{10,9},{8... | collective-permute-start | bytes 73736 | tf_op jit(solution)/shard_map/ppermute | solution.py:866

commit v10 on v8

--- a/solution.py
+++ b/solution.py
@@ -575,9 +575,51 @@
         put(odd, b, 0, out[rows - near :])
     finish(odd, lons + 6)
 
+    ocean = sea[...].astype(f32)
+    narrow = iota((lons, LANES), 1)
+    at_south = narrow == 0
+    at_north = narrow == LANES - 1
+
+    def beyond(message, m, offset, to):
+        tall = message[noises * GROUP : fields * GROUP]
+        columns = []
+        for g in range(groups):
+            spot = (g * members + m) * RIM + offset
+            more = rests + g * members + m
+            column = pltpu.roll(tall, (to - spot) % LANES, 1)
+            columns.append(column + pltpu.roll(tall, (to - more) % LANES, 1))
+        cells = []
+        for c in range(fields - noises):
+            whole = jnp.concatenate([x[c * GROUP : (c + 1) * GROUP] for x in columns], axis=0)
+            cells.append(pltpu.roll(whole, lons + GROUP - RIM, 0)[:lons])
+        return cells
+
+    def step_rims(m):
+        rims = [beyond(south, m, RIM - 1, 0), beyond(north_rim, m, 0, LANES - 1)]
+        for level in range(levels):
+            gains = []
+            for (sign, spot), rim in zip(((1.0, at_south), (-1.0, at_north)), rims):
+                ru, rv, rh = rim[level], rim[levels + level], rim[2 * levels + level]
+                pressure = rim[2 * levels] + rim[2 * levels + 1]
+                if level == 1:
+                    pressure = pressure + REDUCED * rh
+                gains.append(
+                    [
+                        jnp.where(spot, TIME_STEP * VISCOSITY * ru, 0.0),
+                        jnp.where(spot, TIME_STEP * (VISCOSITY * rv + sign * 0.5 * pressure), 0.0),
+                        jnp.where(spot, TIME_STEP * sign * 0.5 * (rh * rv), 0.0),
+                    ]
+                )
+            middle = [jnp.zeros((lons, lats - 2 * LANES), f32)] if lats > 2 * LANES else []
+            gains = [jnp.concatenate([gains[0][n]] + middle + [gains[1][n]], axis=1) for n in range(3)]
+            results[0, m, level] = base[0, m, level] + ocean * gains[0]
+            results[1, m, level] = base[1, m, level] + ocean * gains[1]
+            results[2, m, level] = base[2, m, level] + gains[2]
+        pltpu.make_async_copy(results.at[2, m], new_h.at[m], done.at[2, m]).start()
+
     width = GROUP * hidden
 
-    def layer(x, y, t, left_over):
+    def layer(x, y, t, left_over, beside):
         for b in range(groups):
             for r, step in pieces:
                 lower = iota((step, LANES), 1) < 2 * hidden
@@ -614,10 +656,15 @@
                         axis=0,
                     )
                 put(y, b, r, activate(dot(jnp.concatenate(parts, axis=1), matrix)))
-
-    layer(odd, even, t2, per)
+            for m in beside.get(b, ()):
+                step_rims(m)
+
+    beside = {}
+    for m in range(members):
+        beside.setdefault(min(m, groups - 1), []).append(m)
+    layer(odd, even, t2, per, beside)
     finish(even, lons + 4)
-    layer(even, odd, t3, per // 2)
+    layer(even, odd, t3, per // 2, {})
     finish(odd, lons + 2)
 
     depth = t4.shape[1] // LANES
@@ -634,22 +681,7 @@
         force[1, span_rows, :] = pltpu.roll(swapped, LANES // 2, 1)
         force[2, span_rows, :] = jnp.where(before, sides[0][:, LANES:], sides[1][:, LANES:])
 
-    ocean = sea[...].astype(f32)
-    narrow = iota((lons, LANES), 1)
-    at_south = narrow == 0
-    at_north = narrow == LANES - 1
     halves = lons // 2
-
-    def beyond(message, m, c, offset):
-        cells = []
-        some = slice(c * GROUP, (c + 1) * GROUP)
-        for g in range(groups):
-            spot = (g * members + m) * RIM + offset
-            more = rests + g * members + m
-            cells.append(message[some, spot : spot + 1] + message[some, more : more + 1])
-        whole = jnp.broadcast_to(jnp.concatenate(cells, axis=0), (lons + GROUP, LANES))
-        return pltpu.roll(whole, lons + GROUP - RIM, 0)[:lons]
-
     for m in range(members):
         for q in range(chunks):
             size = min(blocks, lats - q * blocks)
@@ -658,38 +690,15 @@
                 total = total + force[d, pl.ds(d * SUB + m * chunks + q, size, stride=SUB), :]
             gathered[m, pl.ds(q * blocks, size), :] = total
         turned_force = jnp.transpose(gathered[m])
-        rims = [
-            [beyond(message, m, c, offset) for c in range(noises, fields)]
-            for message, offset in ((south, RIM - 1), (north_rim, 0))
-        ]
-        for level in range(levels):
-            gains = []
-            for (sign, spot), rim in zip(((1.0, at_south), (-1.0, at_north)), rims):
-                ru, rv, rh = rim[level], rim[levels + level], rim[2 * levels + level]
-                pressure = rim[2 * levels] + rim[2 * levels + 1]
-                if level == 1:
-                    pressure = pressure + REDUCED * rh
-                gains.append(
-                    [
-                        jnp.where(spot, TIME_STEP * VISCOSITY * ru, 0.0),
-                        jnp.where(spot, TIME_STEP * (VISCOSITY * rv + sign * 0.5 * pressure), 0.0),
-                        jnp.where(spot, TIME_STEP * sign * 0.5 * (rh * rv), 0.0),
-                    ]
-                )
-            middle = [jnp.zeros((lons, lats - 2 * LANES), f32)] if lats > 2 * LANES else []
-            gains = [jnp.concatenate([gains[0][n]] + middle + [gains[1][n]], axis=1) for n in range(3)]
-
-            def push(c):
+        for n, out in enumerate((new_u, new_v)):
+            for level in range(levels):
+                c = n * levels + level
                 parts = [
                     turned_force[side * LANES // 2 + c * halves : side * LANES // 2 + (c + 1) * halves]
                     for side in range(2)
                 ]
-                return TIME_STEP * (jnp.concatenate(parts, axis=0) + bias_last[c])
-
-            results[0, m, level] = base[0, m, level] + ocean * (gains[0] + push(level))
-            results[1, m, level] = base[1, m, level] + ocean * (gains[1] + push(levels + level))
-            results[2, m, level] = base[2, m, level] + gains[2]
-        for n, out in enumerate((new_u, new_v, new_h)):
+                push = TIME_STEP * (jnp.concatenate(parts, axis=0) + bias_last[c])
+                results[n, m, level] = results[n, m, level] + ocean * push
             pltpu.make_async_copy(results.at[n, m], out.at[m], done.at[n, m]).start()
     for m in range(members):
         for n, out in enumerate((new_u, new_v, new_h)):

time: 27.3 us -> 23.7 us (0.87)
  Pallas kernels: 19.6 us -> 15.9 us
    pallas_call x1, Pallas kernels: 13.7 us -> 10 us  [body(): pl.pallas_call(functools.partial(main_kernel, sizes), out_shape=[out] * 3...]
  transfers between devices with their start and end apart: 4 -> 4, of which waited for: 3 -> 3; matrix products, arithmetic and copies ran while one was open for 0% -> 0% of each run, Pallas kernels for 16% -> 18%
where the time goes in v10:
time: 23.7 us; the launch traced here: 23.6 us
  Pallas kernels  15.9 us (67%)
  waiting for transfers between devices  3.69 us (16%)
  starting transfers between devices  3.25 us (14%)
  between operations  0.69 us (3%)
    pallas_call x1, Pallas kernels, body(): pl.pallas_call(functools.partial(main_kernel, sizes), out_shape=[out] * 3...  10 us
    pallas_call x1, Pallas kernels, body(): pl.pallas_call(functools.partial(prepare_kernel, sizes), out_shape=[pltpu...  2.89 us
    ppermute x1, starting transfers between devices, body(): lax.ppermute(to_even, 'lat', [(i, i ^ 1) for i in range(lat_count)])  1.64 us
    ppermute x1, waiting for transfers between devices, body(): odd_rim = lax.ppermute(to_odd, ('lon', 'lat'), pairs)  1.58 us
    ppermute x1, starting transfers between devices, body(): lax.ppermute(to_odd, 'lon', [(i, (i - 1 + 2 * (i % 2)) % lon_count) for i...  1.54 us
    pallas_call x1, Pallas kernels, body(): pl.pallas_call(functools.partial(pack_lon_kernel, sizes, count), out_shap...  1.46 us
    pallas_call x1, Pallas kernels, body(): pl.pallas_call(functools.partial(cells_kernel, sizes), out_shape=[pltpu.V...  1.39 us
    ppermute x1, waiting for transfers between devices, body(): lax.ppermute(to_odd, 'lon', [(i, (i - 1 + 2 * (i % 2)) % lon_count) for i...  1.27 us
  transfers between devices with their start and end apart: 4, of which 3 were waited for; matrix products, arithmetic and copies ran while one was open for 0% of the time, Pallas kernels for 18%

profile of v10, /device:TPU:20, one launch (start us, length us, event | category | flops | bytes accessed | tf_op | source)
XLA Modules:
  0.0 23.6 jit_solution(15465937369515101970)
XLA Ops:
  0.6 0.0 copy-start
  0.6 1.5 %pack_lon.1 = (bf16[4,4,32,256]{3,2,1,0:T(8,128)(2,1)S(1)}, f32[4,2,32,256]{3,2,1,0:T(8,128)S(1)}, f32[4,2,32,256]{3,2,1,0:T(8,128)S(1)}, f32[4,2,32,256]{3,2,1,...) custom-call(bf16[4,4,32,256]{3,2,1,0:T(8,128)(2,1)} %refs_0_.1, ...), custom_call_target="tpu_custom_call" | custom-call | tf_op jit(solution)/shard_map/pack_lon/pallas_call | solution.py:751
  2.1 0.1 collective-permute-start
  2.2 1.5 %collective-permute-start.1 = (bf16[192,256]{1,0:T(8,128)(2,1)S(1)}, bf16[192,256]{1,0:T(8,128)(2,1)S(1)}, u32[]{:S(2)}, u32[]{:S(2)}) collective-permute-start(bf16[192,256]{1,0:T(8,128)(2,1)S(1)} %get-tuple-element.46), channel_id=1, source_target_pairs={{0,28},{4,8},{8,4},{12,16},{16,12},{20,24},{24,20},{28,0},{1,29},{... | collective-permute-start | bytes 294920 | tf_op jit(solution)/shard_map/ppermute | solution.py:762
  3.7 2.9 %prepare.1 = (bf16[384,256]{1,0:T(8,128)(2,1)S(1)}, bf16[1024,256]{1,0:T(8,128)(2,1)S(1)}, bf16[1024,256]{1,0:T(8,128)(2,1)S(1)}, bf16[2,640,256]{2,1,0:T(8,128)...) custom-call(bf16[4,4,32,256]{3,2,1,0:T(8,128)(2,1)S(1)} %get-tuple-e, ...), custom_call_target="tpu_custom_call" | custom-call | flops 10000000 | bytes 10000000 | tf_op jit(solution)/shard_map/prepare/pallas_call | solution.py:770
  6.6 0.0 collective-permute-done.lon_even
  6.6 1.3 %collective-permute-done.1.lon_odd = bf16[192,256]{1,0:T(8,128)(2,1)S(1)} collective-permute-done((bf16[192,256]{1,0:T(8,128)(2,1)S(1)}, bf16[192,256]{1,0:T(8,128)(2,1)S(1)}, u32[]{:S(2)}, u32[]{:S(2)}) %collective-permute-start.1) | collective-permute-done | bytes 98336 | tf_op jit(solution)/shard_map/ppermute | solution.py:762
  7.9 0.2 join_rims.1
  8.1 1.6 %collective-permute-start.2 = (bf16[96,128]{1,0:T(8,128)(2,1)S(1)}, bf16[96,128]{1,0:T(8,128)(2,1)S(1)}, u32[]{:S(2)}, u32[]{:S(2)}) collective-permute-start(bf16[96,128]{1,0:T(8,128)(2,1)S(1)} %get-tuple-element.49.after), channel_id=1, source_target_pairs={{0,1},{1,0},{2,3},{3,2},{4,5},{5,4},{6,7},{7,6},{8,9},{9,8},{10,11... | collective-permute-start | bytes 73736 | tf_op jit(solution)/shard_map/ppermute | solution.py:806
  9.7 0.0 collective-permute-start.3
  9.7 1.4 %cells.1 = (bf16[2,1120,128]{2,1,0:T(8,128)(2,1)S(1)}, f32[3,4,2,32,256]{4,3,2,1,0:T(8,128)S(1)}) custom-call(bf16[4,4,32,256]{3,2,1,0:T(8,128)(2,1)S(1)} %get-tuple-element.32.noise, f32[4,2,32,256]{3,2,1,0:T(8,128)S(1)} %get-tuple-element.33.u, f32[4,2,32,256]{3,2,1,0:T(8,128)S(1)} %get-tuple-element.34.v, f32[4,2,32,256]{3,2,1,0:T(8,128)S(1)} %get-tuple-element.35.h, ...), custom_call_target="tpu_custom_call" | custom-call | flops 10000000 | bytes 10000000 | tf_op jit(solution)/shard_map/cells/pallas_call | solution.py:814
  11.1 0.8 %collective-permute-done.2.even_rim = bf16[96,128]{1,0:T(8,128)(2,1)S(1)} collective-permute-done((bf16[96,128]{1,0:T(8,128)(2,1)S(1)}, bf16[96,128]{1,0:T(8,128)(2,1)S(1)}, u32[]{:S(2)}, u32[]{:S(2)}) %collective-permute-start.2) | collective-permute-done | bytes 24608 | tf_op jit(solution)/shard_map/ppermute | solution.py:806
  12.0 1.6 %collective-permute-done.3.odd_rim = bf16[96,128]{1,0:T(8,128)(2,1)S(1)} collective-permute-done((bf16[96,128]{1,0:T(8,128)(2,1)S(1)}, bf16[96,128]{1,0:T(8,128)(2,1)S(1)}, u32[]{:S(2)}, u32[]{:S(2)}) %collective-permute-start.3) | collective-permute-done | bytes 24608 | tf_op jit(solution)/shard_map/ppermute | solution.py:812
  13.5 0.0 copy-done
  13.5 10.0 %network_and_step.1 = (f32[4,2,32,256]{3,2,1,0:T(8,128)}, f32[4,2,32,256]{3,2,1,0:T(8,128)}, f32[4,2,32,256]{3,2,1,0:T(8,128)}, bf16[3,1120,128]{2,1,0:T(8,128)(...) custom-call(f32[4]{0:T(128)S(1)} %copy-done, ...), custom_call_target="tpu_custom_call", output_to_operand_aliasing={{3}: (1, {}), {4}: (2, {}), {5}: (3, {})} | custom-call | flops 20000000000 | bytes 10000000 | tf_op jit(solution)/shard_map/network_and_step/pallas_call | solution.py:830
Async XLA Ops:
  0.6 12.9 %copy-start = (f32[4]{0:T(128)S(1)}, f32[4]{0:T(128)}, u32[]{:S(2)}) copy-start(f32[4]{0:T(128)} %bias_last.1) | copy-start | bytes 52
  2.1 4.5 %collective-permute-start = (bf16[192,256]{1,0:T(8,128)(2,1)S(1)}, bf16[192,256]{1,0:T(8,128)(2,1)S(1)}, u32[]{:S(2)}, u32[]{:S(2)}) collective-permute-start(bf16[192,256]{1,0:T(8,128)(2,1)S(1)} %get-tuple-element.45), channel_id=1, source_target_pairs={{0,4},{4,0},{8,12},{12,8},{16,20},{20,16},{24,28},{28,24},{1,5},{5... | collective-permute-start | bytes 294920 | tf_op jit(solution)/shard_map/ppermute | solution.py:761
  2.2 5.7 %collective-permute-start.1 = (bf16[192,256]{1,0:T(8,128)(2,1)S(1)}, bf16[192,256]{1,0:T(8,128)(2,1)S(1)}, u32[]{:S(2)}, u32[]{:S(2)}) collective-permute-start(bf16[192,256]{1,0:T(8,128)(2,1)S(1)} %get-tuple-element.46), channel_id=1, source_target_pairs={{0,28},{4,8},{8,4},{12,16},{16,12},{20,24},{24,20},{28,0},{1,29},{... | collective-permute-start | bytes 294920 | tf_op jit(solution)/shard_map/ppermute | solution.py:762
  8.1 3.9 %collective-permute-start.2 = (bf16[96,128]{1,0:T(8,128)(2,1)S(1)}, bf16[96,128]{1,0:T(8,128)(2,1)S(1)}, u32[]{:S(2)}, u32[]{:S(2)}) collective-permute-start(bf16[96,128]{1,0:T(8,128)(2,1)S(1)} %get-tuple-element.49.after), channel_id=1, source_target_pairs={{0,1},{1,0},{2,3},{3,2},{4,5},{5,4},{6,7},{7,6},{8,9},{9,8},{10,11... | collective-permute-start | bytes 73736 | tf_op jit(solution)/shard_map/ppermute | solution.py:806
  9.7 3.8 %collective-permute-start.3 = (bf16[96,128]{1,0:T(8,128)(2,1)S(1)}, bf16[96,128]{1,0:T(8,128)(2,1)S(1)}, u32[]{:S(2)}, u32[]{:S(2)}) collective-permute-start(bf16[96,128]{1,0:T(8,128)(2,1)S(1)} %get-tuple-element.53.own_tail), channel_id=1, source_target_pairs={{1,2},{2,1},{0,4},{3,31},{5,6},{6,5},{4,0},{7,27},{9,10},{10,9},{8... | collective-permute-start | bytes 73736 | tf_op jit(solution)/shard_map/ppermute | solution.py:812

commit v11 on v10

--- a/solution.py
+++ b/solution.py
@@ -207,7 +207,7 @@
     x[pl.ds(SUB + rows, SUB), :] = pltpu.roll(begin, SUB - 1, 0).astype(bf16)
 
 
-def cells_kernel(sizes, noise, u, v, h, sea, lon_even, lon_odd, after, out, base, rims, cells, turned):
+def cells_kernel(sizes, noise, u, v, h, sea, lon_odd, lon_even, after, out, base, rims, cells, turned):
     members, noises, levels = sizes
     fields = noises + 3 * levels
     lons, lats = sea.shape
@@ -292,7 +292,7 @@
             base[2, m, level] = ch - TIME_STEP * flow
 
 
-def join_kernel(sizes, lons, lon_even, lon_odd, head, tail, even, odd, rims, wide):
+def join_kernel(sizes, lons, lon_odd, lon_even, head, tail, even, odd, rims, wide):
     members, noises, levels = sizes
     fields = noises + 3 * levels
     groups = lons // GROUP + 1
@@ -444,8 +444,8 @@
     pre_in,
     base,
     sea,
+    odd_rim,
     even_rim,
-    odd_rim,
     own_tail,
     t1,
     t2,
@@ -460,8 +460,6 @@
     even,
     force,
     gathered,
-    turned,
-    gaps,
     results,
     done,
 ):
@@ -506,23 +504,32 @@
     north = jnp.where(is_odd, strip, paired)
     north_rim = jnp.where(border & top, folded, north)
 
+    spread_row = iota((groups * RIM * SUB, LANES), 0)
+    spread_lane = iota((groups * RIM * SUB, LANES), 1)
+    line = spread_row // (RIM * SUB) * span + spread_row // SUB % RIM
+    of_member = spread_row % SUB // chunks
+    next_member = jnp.where(of_member == members - 1, 0, of_member + 1)
+    spreads = [
+        jnp.where(spread_lane == line + member * RIM, 1.0, 0.0).astype(bf16) for member in (of_member, next_member)
+    ]
+    gaps = []
     for n, message in enumerate((north_rim, strip, ghost, south)):
         after = pltpu.roll(message, LANES - span, 1)
         cut = [message[c * GROUP : (c + 1) * GROUP] for c in range(fields + 1)]
         after = [after[c * GROUP : (c + 1) * GROUP] for c in range(fields + 1)]
-        turned[n] = jnp.transpose(window(cut[:fields], after[:fields], cut[fields], after[fields]))
-        for g in range(groups):
-            for m in range(members):
-                gap = (m - 1) % members if n == 3 else m
-                start = n * RIM * SUB + gap * chunks + chunks - 1
-                gaps[g, pl.ds(start, RIM, stride=SUB), :] = turned[n, pl.ds((g * members + m) * RIM, RIM), :]
+        block = window(cut[:fields], after[:fields], cut[fields], after[fields]).astype(bf16)
+        gaps.append(
+            lax.dot_general(spreads[n // 3], block, (((1,), (1,)), ((), ())), preferred_element_type=f32)
+        )
 
     first = [ends.at[0]] + [middle.at[g] for g in range(groups - 2)] + [ends.at[1]]
-    in_gap = iota((GAP * SUB, LANES), 0) % chunks == chunks - 1
+    in_gap = iota((RIM * SUB, LANES), 0) % chunks == chunks - 1
     for g in range(groups):
-        spot = pl.ds((1 + gap_k) * SUB, GAP * SUB)
-        kept = first[g][spot, :].astype(f32)
-        first[g][spot, :] = jnp.where(in_gap, gaps[g], kept).astype(bf16)
+        for n in range(4):
+            spot = pl.ds((1 + gap_k + n * RIM) * SUB, RIM * SUB)
+            kept = first[g][spot, :].astype(f32)
+            filled = gaps[n][g * RIM * SUB : (g + 1) * RIM * SUB]
+            first[g][spot, :] = jnp.where(in_gap, filled, kept).astype(bf16)
         wrap(first[g], rows)
 
     hidden = LANES // 4
@@ -758,8 +765,8 @@
         name="pack_lon",
     )(*args)
     state = tuple(held[:5])
+    lon_odd = lax.ppermute(to_odd, "lon", [(i, (i - 1 + 2 * (i % 2)) % lon_count) for i in range(lon_count)])
     lon_even = lax.ppermute(to_even, "lon", [(i, i ^ 1) for i in range(lon_count)])
-    lon_odd = lax.ppermute(to_odd, "lon", [(i, (i - 1 + 2 * (i % 2)) % lon_count) for i in range(lon_count)])
 
     wide = -(-(fields + 1) * GROUP // SUB) * SUB
     part = pltpu.VMEM((wide, LANES), f32)
@@ -802,14 +809,14 @@
         ],
         compiler_params=pltpu.CompilerParams(vmem_limit_bytes=4 * 2**20),
         name="join_rims",
-    )(lon_even, lon_odd, own_head, own_tail)
-    even_rim = lax.ppermute(to_even, "lat", [(i, i ^ 1) for i in range(lat_count)])
+    )(lon_odd, lon_even, own_head, own_tail)
     pairs = []
     for t in range(lon_count):
         at = t * lat_count
         pairs += [(at + k, at + k - 1 + 2 * (k % 2)) for k in range(1, last)]
         pairs += [(at, (t ^ 1) * lat_count), (at + last, (lon_count - 1 - t) * lat_count + last)]
     odd_rim = lax.ppermute(to_odd, ("lon", "lat"), pairs)
+    even_rim = lax.ppermute(to_even, "lat", [(i, i ^ 1) for i in range(lat_count)])
 
     ends, base = pl.pallas_call(
         functools.partial(cells_kernel, sizes),
@@ -824,7 +831,7 @@
         compiler_params=pltpu.CompilerParams(vmem_limit_bytes=12 * 2**20),
         cost_estimate=pl.CostEstimate(flops=10**7, bytes_accessed=10**7, transcendentals=0),
         name="cells",
-    )(*state, lon_even, lon_odd, to_even)
+    )(*state, lon_odd, lon_even, to_even)
 
     out = jax.ShapeDtypeStruct(velocity_u.shape, f32)
     return pl.pallas_call(
@@ -837,8 +844,6 @@
             pltpu.VMEM((tiles, padded, LANES), bf16),
             pltpu.VMEM((3, padded, LANES), f32),
             pltpu.VMEM((members, lats, LANES), f32),
-            pltpu.VMEM((4, LANES, LANES), f32),
-            pltpu.VMEM((groups, GAP * SUB, LANES), f32),
             pltpu.VMEM((3, *velocity_u.shape), f32),
             pltpu.SemaphoreType.DMA((3, members)),
         ],
@@ -852,8 +857,8 @@
         pre,
         base,
         state[4],
+        odd_rim,
         even_rim,
-        odd_rim,
         to_odd,
         t1,
         t2,

time: 23.7 us -> 24.1 us (1.017)
  the two profiles are of different devices: /device:TPU:20 before, /device:TPU:16 now
where the time goes in v11:
time: 24.1 us; the launch traced here: 23.9 us
  Pallas kernels  16.1 us (67%)
  starting transfers between devices  3.6 us (15%)
  waiting for transfers between devices  3.53 us (15%)
  between operations  0.68 us (3%)
    pallas_call x1, Pallas kernels, body(): pl.pallas_call(functools.partial(main_kernel, sizes), out_shape=[out] * 3...  10.2 us
    pallas_call x1, Pallas kernels, body(): pl.pallas_call(functools.partial(prepare_kernel, sizes), out_shape=[pltpu...  2.89 us
    ppermute x1, starting transfers between devices, body(): lax.ppermute(to_odd, 'lon', [(i, (i - 1 + 2 * (i % 2)) % lon_count) for i...  1.95 us
    ppermute x1, starting transfers between devices, body(): lax.ppermute(to_even, 'lat', [(i, i ^ 1) for i in range(lat_count)])  1.64 us
    ppermute x1, waiting for transfers between devices, body(): odd_rim = lax.ppermute(to_odd, ('lon', 'lat'), pairs)  1.58 us
    pallas_call x1, Pallas kernels, body(): pl.pallas_call(functools.partial(pack_lon_kernel, sizes, count), out_shap...  1.46 us
    pallas_call x1, Pallas kernels, body(): pl.pallas_call(functools.partial(cells_kernel, sizes), out_shape=[pltpu.V...  1.39 us
    ppermute x1, waiting for transfers between devices, body(): lax.ppermute(to_odd, 'lon', [(i, (i - 1 + 2 * (i % 2)) % lon_count) for i...  1.1 us
  transfers between devices with their start and end apart: 4, of which 3 were waited for; matrix products, arithmetic and copies ran while one was open for 0% of the time, Pallas kernels for 18%

profile of v11, /device:TPU:16, one launch (start us, length us, event | category | flops | bytes accessed | tf_op | source)
XLA Modules:
  0.0 23.9 jit_solution(17200895632822738391)
XLA Ops:
  0.6 0.0 copy-start
  0.6 1.5 %pack_lon.1 = (bf16[4,4,32,256]{3,2,1,0:T(8,128)(2,1)S(1)}, f32[4,2,32,256]{3,2,1,0:T(8,128)S(1)}, f32[4,2,32,256]{3,2,1,0:T(8,128)S(1)}, f32[4,2,32,256]{3,2,1,...) custom-call(bf16[4,4,32,256]{3,2,1,0:T(8,128)(2,1)} %refs_0_.1, ...), custom_call_target="tpu_custom_call" | custom-call | tf_op jit(solution)/shard_map/pack_lon/pallas_call | solution.py:758
  2.1 2.0 %collective-permute-start = (bf16[192,256]{1,0:T(8,128)(2,1)S(1)}, bf16[192,256]{1,0:T(8,128)(2,1)S(1)}, u32[]{:S(2)}, u32[]{:S(2)}) collective-permute-start(bf16[192,256]{1,0:T(8,128)(2,1)S(1)} %get-tuple-element.45), channel_id=1, source_target_pairs={{0,28},{4,8},{8,4},{12,16},{16,12},{20,24},{24,20},{28,0},{1,29},{... | collective-permute-start | bytes 294920 | tf_op jit(solution)/shard_map/ppermute | solution.py:768
  4.1 0.0 collective-permute-start.1
  4.1 2.9 %prepare.1 = (bf16[384,256]{1,0:T(8,128)(2,1)S(1)}, bf16[1024,256]{1,0:T(8,128)(2,1)S(1)}, bf16[1024,256]{1,0:T(8,128)(2,1)S(1)}, bf16[2,640,256]{2,1,0:T(8,128)...) custom-call(bf16[4,4,32,256]{3,2,1,0:T(8,128)(2,1)S(1)} %get-tuple-e, ...), custom_call_target="tpu_custom_call" | custom-call | flops 10000000 | bytes 10000000 | tf_op jit(solution)/shard_map/prepare/pallas_call | solution.py:777
  7.0 1.1 %collective-permute-done.lon_odd = bf16[192,256]{1,0:T(8,128)(2,1)S(1)} collective-permute-done((bf16[192,256]{1,0:T(8,128)(2,1)S(1)}, bf16[192,256]{1,0:T(8,128)(2,1)S(1)}, u32[]{:S(2)}, u32[]{:S(2)}) %collective-permute-start) | collective-permute-done | bytes 98336 | tf_op jit(solution)/shard_map/ppermute | solution.py:768
  8.1 0.0 collective-permute-done.1.lon_even
  8.1 0.2 join_rims.1
  8.2 1.6 %collective-permute-start.3 = (bf16[96,128]{1,0:T(8,128)(2,1)S(1)}, bf16[96,128]{1,0:T(8,128)(2,1)S(1)}, u32[]{:S(2)}, u32[]{:S(2)}) collective-permute-start(bf16[96,128]{1,0:T(8,128)(2,1)S(1)} %get-tuple-element.49.after), channel_id=1, source_target_pairs={{0,1},{1,0},{2,3},{3,2},{4,5},{5,4},{6,7},{7,6},{8,9},{9,8},{10,11... | collective-permute-start | bytes 73736 | tf_op jit(solution)/shard_map/ppermute | solution.py:819
  9.9 0.0 collective-permute-start.2
  9.9 1.4 %cells.1 = (bf16[2,1120,128]{2,1,0:T(8,128)(2,1)S(1)}, f32[3,4,2,32,256]{4,3,2,1,0:T(8,128)S(1)}) custom-call(bf16[4,4,32,256]{3,2,1,0:T(8,128)(2,1)S(1)} %get-tuple-element.32.noise, f32[4,2,32,256]{3,2,1,0:T(8,128)S(1)} %get-tuple-element.33.u, f32[4,2,32,256]{3,2,1,0:T(8,128)S(1)} %get-tuple-element.34.v, f32[4,2,32,256]{3,2,1,0:T(8,128)S(1)} %get-tuple-element.35.h, ...), custom_call_target="tpu_custom_call" | custom-call | flops 10000000 | bytes 10000000 | tf_op jit(solution)/shard_map/cells/pallas_call | solution.py:821
  11.3 0.8 %collective-permute-done.3.even_rim = bf16[96,128]{1,0:T(8,128)(2,1)S(1)} collective-permute-done((bf16[96,128]{1,0:T(8,128)(2,1)S(1)}, bf16[96,128]{1,0:T(8,128)(2,1)S(1)}, u32[]{:S(2)}, u32[]{:S(2)}) %collective-permute-start.3) | collective-permute-done | bytes 24608 | tf_op jit(solution)/shard_map/ppermute | solution.py:819
  12.1 1.6 %collective-permute-done.2.odd_rim = bf16[96,128]{1,0:T(8,128)(2,1)S(1)} collective-permute-done((bf16[96,128]{1,0:T(8,128)(2,1)S(1)}, bf16[96,128]{1,0:T(8,128)(2,1)S(1)}, u32[]{:S(2)}, u32[]{:S(2)}) %collective-permute-start.2) | collective-permute-done | bytes 24608 | tf_op jit(solution)/shard_map/ppermute | solution.py:818
  13.7 0.0 copy-done
  13.7 10.2 %network_and_step.1 = (f32[4,2,32,256]{3,2,1,0:T(8,128)}, f32[4,2,32,256]{3,2,1,0:T(8,128)}, f32[4,2,32,256]{3,2,1,0:T(8,128)}, bf16[3,1120,128]{2,1,0:T(8,128)(...) custom-call(f32[4]{0:T(128)S(1)} %copy-done, ...), custom_call_target="tpu_custom_call", output_to_operand_aliasing={{3}: (1, {}), {4}: (2, {}), {5}: (3, {})} | custom-call | flops 20000000000 | bytes 10000000 | tf_op jit(solution)/shard_map/network_and_step/pallas_call | solution.py:837
Async XLA Ops:
  0.6 13.1 %copy-start = (f32[4]{0:T(128)S(1)}, f32[4]{0:T(128)}, u32[]{:S(2)}) copy-start(f32[4]{0:T(128)} %bias_last.1) | copy-start | bytes 52
  2.1 6.0 %collective-permute-start = (bf16[192,256]{1,0:T(8,128)(2,1)S(1)}, bf16[192,256]{1,0:T(8,128)(2,1)S(1)}, u32[]{:S(2)}, u32[]{:S(2)}) collective-permute-start(bf16[192,256]{1,0:T(8,128)(2,1)S(1)} %get-tuple-element.45), channel_id=1, source_target_pairs={{0,28},{4,8},{8,4},{12,16},{16,12},{20,24},{24,20},{28,0},{1,29},{... | collective-permute-start | bytes 294920 | tf_op jit(solution)/shard_map/ppermute | solution.py:768
  4.1 4.0 %collective-permute-start.1 = (bf16[192,256]{1,0:T(8,128)(2,1)S(1)}, bf16[192,256]{1,0:T(8,128)(2,1)S(1)}, u32[]{:S(2)}, u32[]{:S(2)}) collective-permute-start(bf16[192,256]{1,0:T(8,128)(2,1)S(1)} %get-tuple-element.46), channel_id=1, source_target_pairs={{0,4},{4,0},{8,12},{12,8},{16,20},{20,16},{24,28},{28,24},{1,5},{5... | collective-permute-start | bytes 294920 | tf_op jit(solution)/shard_map/ppermute | solution.py:769
  8.2 3.9 %collective-permute-start.3 = (bf16[96,128]{1,0:T(8,128)(2,1)S(1)}, bf16[96,128]{1,0:T(8,128)(2,1)S(1)}, u32[]{:S(2)}, u32[]{:S(2)}) collective-permute-start(bf16[96,128]{1,0:T(8,128)(2,1)S(1)} %get-tuple-element.49.after), channel_id=1, source_target_pairs={{0,1},{1,0},{2,3},{3,2},{4,5},{5,4},{6,7},{7,6},{8,9},{9,8},{10,11... | collective-permute-start | bytes 73736 | tf_op jit(solution)/shard_map/ppermute | solution.py:819
  9.9 3.8 %collective-permute-start.2 = (bf16[96,128]{1,0:T(8,128)(2,1)S(1)}, bf16[96,128]{1,0:T(8,128)(2,1)S(1)}, u32[]{:S(2)}, u32[]{:S(2)}) collective-permute-start(bf16[96,128]{1,0:T(8,128)(2,1)S(1)} %get-tuple-element.53.own_tail), channel_id=1, source_target_pairs={{1,2},{2,1},{0,4},{3,31},{5,6},{6,5},{4,0},{7,27},{9,10},{10,9},{8... | collective-permute-start | bytes 73736 | tf_op jit(solution)/shard_map/ppermute | solution.py:818

commit v12 on v10

--- a/solution.py
+++ b/solution.py
@@ -137,13 +137,13 @@
 
 
 def prepare_kernel(sizes, noise, u, v, h, sea, *refs):
-    weights, matrices, (head, tail, middle, pre, cells, turned) = refs[:7], refs[7:11], refs[11:]
+    w1, bias1, t1, head, tail, middle, pre, cells, turned = refs
     held = (noise, u, v, h, sea)
     members, noises, levels = sizes
     fields = noises + 3 * levels
     lons, lats = sea.shape
     groups = lons // GROUP + 1
-    weights_kernel(*weights, *matrices)
+    first_weights(w1, bias1, t1)
     lane = iota((GROUP, LANES), 1)
     for out, t, first in ((head, 0, 0), (tail, lats // LANES - 1, LANES - RIM)):
         for c in range(fields + 1):
@@ -183,7 +183,7 @@
     for g in range(inner):
         for r, step in row_pieces(rows):
             parts = [middle[g, pl.ds(r + SUB * d, step), :] for d in range(3)]
-            put(pre, g + 1, r, activate(dot(jnp.concatenate(parts, axis=1), matrices[0][...])))
+            put(pre, g + 1, r, activate(dot(jnp.concatenate(parts, axis=1), t1[...])))
 
 
 def row_pieces(rows):
@@ -207,7 +207,8 @@
     x[pl.ds(SUB + rows, SUB), :] = pltpu.roll(begin, SUB - 1, 0).astype(bf16)
 
 
-def cells_kernel(sizes, noise, u, v, h, sea, lon_even, lon_odd, after, out, base, rims, cells, turned):
+def cells_kernel(sizes, noise, u, v, h, sea, lon_even, lon_odd, after, *refs):
+    weights, (t1, _, out, base, pre, *matrices, rims, cells, turned) = refs[:5], refs[5:]
     members, noises, levels = sizes
     fields = noises + 3 * levels
     lons, lats = sea.shape
@@ -238,6 +239,12 @@
                 store_lats(block, t, cells, side, m, lats, chunks, turned.at[(t * members + m) * 2 + side])
     for side in range(2):
         out[side, pl.ds(SUB, rows), :] = cells[side].astype(bf16)
+        wrap(out.at[side], rows)
+    for side in range(2):
+        for r, step in row_pieces(rows):
+            parts = [out[side, pl.ds(r + SUB * d, step), :] for d in range(3)]
+            put(pre, side * (groups - 1), r, activate(dot(jnp.concatenate(parts, axis=1), t1[...])))
+    other_weights(*weights, *matrices)
     step_kernel(sizes, u, v, h, sea, rims, base)
 
 
@@ -323,17 +330,12 @@
     odd[...] = wide[1].astype(bf16)
 
 
-def weights_kernel(w1, w2, w3, w4, bias1, bias2, bias3, t1, t2, t3, t4):
-    hidden = w2.shape[2]
+def extra_rows(hidden):
     per = LANES // hidden
-    lane = iota((hidden, LANES), 1)
-    fields = w1.shape[0]
-    out_lon = iota((GROUP, LANES), 1) // hidden
-    in_row = iota((GROUP, LANES), 0)
     bias_row = iota((GROUP, LANES), 0)
 
-    def bias_rows(layer):
-        part = 0.5 * jnp.concatenate([(bias1, bias2, bias3)[layer][...]] * per, axis=1)
+    def bias_rows(bias):
+        part = 0.5 * jnp.concatenate([bias[...]] * per, axis=1)
         b1 = part.astype(bf16).astype(f32)
         b2 = (part - b1).astype(bf16).astype(f32)
         b3 = part - b1 - b2
@@ -349,6 +351,16 @@
         out = iota((2 * GROUP, LANES), 1) // hidden + per * tile
         return jnp.where(lon == out + shift, LAND, 0.0)
 
+    return sea_rows, bias_rows
+
+
+def first_weights(w1, bias1, t1):
+    hidden = w1.shape[3]
+    per = LANES // hidden
+    sea_rows, bias_rows = extra_rows(hidden)
+    fields = w1.shape[0]
+    out_lon = iota((GROUP, LANES), 1) // hidden
+    in_row = iota((GROUP, LANES), 0)
     for dj in range(3):
         taps = []
         for di in range(3):
@@ -372,13 +384,19 @@
                         total = jnp.where(hit & (in_row // 2 == n), taps[di][start + n], total)
                 parts.append(total)
             if dj == 1:
-                parts += [sea_rows(1, tile), bias_rows(0)]
+                parts += [sea_rows(1, tile), bias_rows(bias1)]
             else:
                 parts.append(jnp.zeros((3 * GROUP, LANES), f32))
             block = jnp.concatenate(parts, axis=0)
             t1[pl.ds(dj * LANES, LANES), pl.ds(tile * LANES, LANES)] = block.astype(bf16)
 
-    for layer, (w, t) in enumerate(((w2, t2), (w3, t3))):
+
+def other_weights(w2, w3, w4, bias2, bias3, t2, t3, t4):
+    hidden = w2.shape[2]
+    per = LANES // hidden
+    lane = iota((hidden, LANES), 1)
+    sea_rows, bias_rows = extra_rows(hidden)
+    for layer, (w, bias, t) in enumerate(((w2, bias2, t2), (w3, bias3, t3))):
         for dj in range(3):
             taps = []
             for di in range(3):
@@ -401,7 +419,7 @@
                 [
                     jnp.zeros((5 * GROUP, LANES), f32),
                     sea_rows(2 + layer, tile),
-                    bias_rows(1 + layer),
+                    bias_rows(bias),
                 ],
                 axis=0,
             )
@@ -560,12 +578,8 @@
         x[tiles - 1] = jnp.zeros(x.shape[1:], bf16)
     even[tiles - 2] = jnp.zeros(even.shape[1:], bf16)
 
-    for b in (0, groups - 1):
-        for r, step in pieces:
-            parts = [first[b][pl.ds(r + SUB * d, step), :] for d in range(3)]
-            put(odd, b, r, activate(dot(jnp.concatenate(parts, axis=1), t1[...])))
     near = (gap_k - 1) * SUB
-    for b in range(1, groups - 1):
+    for b in range(groups):
         parts = []
         for d in range(3):
             some = [first[b][pl.ds(near + SUB * d, rows - near), :], first[b][pl.ds(SUB * d, SUB), :]]
@@ -682,13 +696,13 @@
         force[2, span_rows, :] = jnp.where(before, sides[0][:, LANES:], sides[1][:, LANES:])
 
     halves = lons // 2
+    for r, step in pieces:
+        total = force[0, pl.ds(r, step), :] + force[1, pl.ds(r + SUB, step), :]
+        force[0, pl.ds(r, step), :] = total + force[2, pl.ds(r + 2 * SUB, step), :]
     for m in range(members):
         for q in range(chunks):
             size = min(blocks, lats - q * blocks)
-            total = force[0, pl.ds(m * chunks + q, size, stride=SUB), :]
-            for d in range(1, 3):
-                total = total + force[d, pl.ds(d * SUB + m * chunks + q, size, stride=SUB), :]
-            gathered[m, pl.ds(q * blocks, size), :] = total
+            gathered[m, pl.ds(q * blocks, size), :] = force[0, pl.ds(m * chunks + q, size, stride=SUB), :]
         turned_force = jnp.transpose(gathered[m])
         for n, out in enumerate((new_u, new_v)):
             for level in range(levels):
@@ -767,20 +781,17 @@
     deep = -(-(lons // 2 + 2) * hidden // LANES) * LANES
     padded = rows + 2 * SUB
     tiles = 2 * groups + 1
-    t1, t2, t3, t4, own_head, own_tail, middle, pre = pl.pallas_call(
+    t1, own_head, own_tail, middle, pre = pl.pallas_call(
         functools.partial(prepare_kernel, sizes),
         out_shape=[
             pltpu.VMEM((3 * LANES, 2 * LANES), bf16),
-            pltpu.VMEM((8 * LANES, 2 * LANES), bf16),
-            pltpu.VMEM((8 * LANES, 2 * LANES), bf16),
-            pltpu.VMEM((2, deep, 2 * LANES), bf16),
             part,
             part,
             pltpu.VMEM((groups - 2, padded, LANES), bf16),
             pltpu.VMEM((tiles, padded, LANES), bf16),
         ],
-        in_specs=[whole] * count,
-        out_specs=[whole] * 8,
+        in_specs=[whole] * 7,
+        out_specs=[whole] * 5,
         scratch_shapes=[
             pltpu.VMEM((groups - 2, rows, LANES), f32),
             pltpu.VMEM((members * (groups - 2) * lats // LANES, LANES, LANES), f32),
@@ -788,7 +799,7 @@
         compiler_params=pltpu.CompilerParams(vmem_limit_bytes=12 * 2**20),
         cost_estimate=pl.CostEstimate(flops=10**7, bytes_accessed=10**7, transcendentals=0),
         name="prepare",
-    )(*held)
+    )(*held[:6], held[9])
     last = lat_count - 1
     smem = pl.BlockSpec(memory_space=pltpu.SMEM)
     to_even, to_odd = pl.pallas_call(
@@ -811,11 +822,19 @@
         pairs += [(at, (t ^ 1) * lat_count), (at + last, (lon_count - 1 - t) * lat_count + last)]
     odd_rim = lax.ppermute(to_odd, ("lon", "lat"), pairs)
 
-    ends, base = pl.pallas_call(
+    ends, base, pre, t2, t3, t4 = pl.pallas_call(
         functools.partial(cells_kernel, sizes),
-        out_shape=[pltpu.VMEM((2, padded, LANES), bf16), pltpu.VMEM((3, *velocity_u.shape), f32)],
-        in_specs=[whole] * 8,
-        out_specs=[whole] * 2,
+        out_shape=[
+            pltpu.VMEM((2, padded, LANES), bf16),
+            pltpu.VMEM((3, *velocity_u.shape), f32),
+            pltpu.VMEM(pre.shape, bf16),
+            pltpu.VMEM((8 * LANES, 2 * LANES), bf16),
+            pltpu.VMEM((8 * LANES, 2 * LANES), bf16),
+            pltpu.VMEM((2, deep, 2 * LANES), bf16),
+        ],
+        in_specs=[whole] * 15,
+        out_specs=[whole] * 6,
+        input_output_aliases={14: 2},
         scratch_shapes=[
             pltpu.VMEM((2, tall, lats), f32),
             pltpu.VMEM((2, rows, LANES), f32),
@@ -824,7 +843,7 @@
         compiler_params=pltpu.CompilerParams(vmem_limit_bytes=12 * 2**20),
         cost_estimate=pl.CostEstimate(flops=10**7, bytes_accessed=10**7, transcendentals=0),
         name="cells",
-    )(*state, lon_even, lon_odd, to_even)
+    )(*state, lon_even, lon_odd, to_even, *held[6:9], *held[10:12], t1, pre)
 
     out = jax.ShapeDtypeStruct(velocity_u.shape, f32)
     return pl.pallas_call(

time: 23.7 us -> 23.7 us (level)
  the two profiles are of different devices: /device:TPU:20 before, /device:TPU:12 now
where the time goes in v12:
time: 23.7 us; the launch traced here: 23.5 us
  Pallas kernels  16 us (68%)
  starting transfers between devices  4.82 us (20%)
  waiting for transfers between devices  2.01 us (8%)
  between operations  0.72 us (3%)
    pallas_call x1, Pallas kernels, body(): pl.pallas_call(functools.partial(main_kernel, sizes), out_shape=[out] * 3...  9.55 us
    ppermute x1, starting transfers between devices, body(): odd_rim = lax.ppermute(to_odd, ('lon', 'lat'), pairs)  3.14 us
    pallas_call x1, Pallas kernels, body(): pl.pallas_call(functools.partial(cells_kernel, sizes), out_shape=[pltpu.V...  2.62 us
    pallas_call x1, Pallas kernels, body(): pl.pallas_call(functools.partial(prepare_kernel, sizes), out_shape=[pltpu...  2.16 us
    ppermute x1, waiting for transfers between devices, body(): lax.ppermute(to_odd, 'lon', [(i, (i - 1 + 2 * (i % 2)) % lon_count) for i...  2 us
    ppermute x1, starting transfers between devices, body(): lax.ppermute(to_odd, 'lon', [(i, (i - 1 + 2 * (i % 2)) % lon_count) for i...  1.54 us
    pallas_call x1, Pallas kernels, body(): pl.pallas_call(functools.partial(pack_lon_kernel, sizes, count), out_shap...  1.46 us
  transfers between devices with their start and end apart: 4, of which 1 were waited for; matrix products, arithmetic and copies ran while one was open for 0% of the time, Pallas kernels for 20%

profile of v12, /device:TPU:12, one launch (start us, length us, event | category | flops | bytes accessed | tf_op | source)
XLA Modules:
  0.0 23.5 jit_solution(2931164527820601179)
XLA Ops:
  0.6 1.5 %pack_lon.1 = (bf16[4,4,32,256]{3,2,1,0:T(8,128)(2,1)S(1)}, f32[4,2,32,256]{3,2,1,0:T(8,128)S(1)}, f32[4,2,32,256]{3,2,1,0:T(8,128)S(1)}, f32[4,2,32,256]{3,2,1,...) custom-call(bf16[4,4,32,256]{3,2,1,0:T(8,128)(2,1)} %refs_0_.1, ...), custom_call_target="tpu_custom_call" | custom-call | tf_op jit(solution)/shard_map/pack_lon/pallas_call | solution.py:765
  2.1 0.0 copy-start
  2.1 0.1 collective-permute-start
  2.2 1.5 %collective-permute-start.1 = (bf16[192,256]{1,0:T(8,128)(2,1)S(1)}, bf16[192,256]{1,0:T(8,128)(2,1)S(1)}, u32[]{:S(2)}, u32[]{:S(2)}) collective-permute-start(bf16[192,256]{1,0:T(8,128)(2,1)S(1)} %get-tuple-element.42), channel_id=1, source_target_pairs={{0,28},{4,8},{8,4},{12,16},{16,12},{20,24},{24,20},{28,0},{1,29},{... | collective-permute-start | bytes 294920 | tf_op jit(solution)/shard_map/ppermute | solution.py:776
  3.7 2.2 %prepare.1 = (bf16[384,256]{1,0:T(8,128)(2,1)S(1)}, f32[96,128]{1,0:T(8,128)S(1)}, f32[96,128]{1,0:T(8,128)S(1)}, bf16[3,1120,128]{2,1,0:T(8,128)(2,1)S(1)}, bf16[11,1120,128]{2,1,0:T(8,128)(2,1)S(1)}) custom-call(bf16[4,4,32,256]{3,2,1,0:T(8,128)(2,1)S(1)} %get-tuple-element.33.noise, f32[4,2,32,256]{3,2,1,0:T(8,128)S(1)} %get-tuple-element.34.u, ...), custom_call_target="tpu_custom_call" | custom-call | flops 10000000 | bytes 10000000 | tf_op jit(solution)/shard_map/prepare/pallas_call | solution.py:784
  5.9 0.0 collective-permute-done.lon_even
  5.9 2.0 %collective-permute-done.1.lon_odd = bf16[192,256]{1,0:T(8,128)(2,1)S(1)} collective-permute-done((bf16[192,256]{1,0:T(8,128)(2,1)S(1)}, bf16[192,256]{1,0:T(8,128)(2,1)S(1)}, u32[]{:S(2)}, u32[]{:S(2)}) %collective-permute-start.1) | collective-permute-done | bytes 98336 | tf_op jit(solution)/shard_map/ppermute | solution.py:776
  7.9 0.2 join_rims.1
  8.1 0.1 collective-permute-start.2
  8.2 3.1 %collective-permute-start.3 = (bf16[96,128]{1,0:T(8,128)(2,1)S(1)}, bf16[96,128]{1,0:T(8,128)(2,1)S(1)}, u32[]{:S(2)}, u32[]{:S(2)}) collective-permute-start(bf16[96,128]{1,0:T(8,128)(2,1)S(1)} %get-tuple-element.56.own_tail), channel_id=1, source_target_pairs={{1,2},{2,1},{0,4},{3,31},{5,6},{6,5},{4,0},{7,27},{9,10},{10,9},{8... | collective-permute-start | bytes 73736 | tf_op jit(solution)/shard_map/ppermute | solution.py:823
  11.3 2.6 %cells.1 = (bf16[2,1120,128]{2,1,0:T(8,128)(2,1)S(1)}, f32[3,4,2,32,256]{4,3,2,1,0:T(8,128)S(1)}, bf16[11,1120,128]{2,1,0:T(8,128)(2,1)S(1)}, bf16[1024,256]{1,0...) custom-call(bf16[4,4,32,256]{3,2,1,0:T(8,128)(2,1)S(1)} %get-tuple-e, ...), custom_call_target="tpu_custom_call", output_to_operand_aliasing={{2}: (14, {})} | custom-call | flops 10000000 | bytes 10000000 | tf_op jit(solution)/shard_map/cells/pallas_call | solution.py:825
  13.9 0.0 collective-permute-done.2.even_rim
  13.9 0.0 collective-permute-done.3.odd_rim
  13.9 0.0 copy-done
  14.0 9.6 %network_and_step.1 = (f32[4,2,32,256]{3,2,1,0:T(8,128)}, f32[4,2,32,256]{3,2,1,0:T(8,128)}, f32[4,2,32,256]{3,2,1,0:T(8,128)}, bf16[3,1120,128]{2,1,0:T(8,128)(...) custom-call(f32[4]{0:T(128)S(1)} %copy-done, ...), custom_call_target="tpu_custom_call", output_to_operand_aliasing={{3}: (1, {}), {4}: (2, {}), {5}: (3, {})} | custom-call | flops 20000000000 | bytes 10000000 | tf_op jit(solution)/shard_map/network_and_step/pallas_call | solution.py:849
Async XLA Ops:
  2.1 11.8 %copy-start = (f32[4]{0:T(128)S(1)}, f32[4]{0:T(128)}, u32[]{:S(2)}) copy-start(f32[4]{0:T(128)} %bias_last.1) | copy-start | bytes 52
  2.1 3.8 %collective-permute-start = (bf16[192,256]{1,0:T(8,128)(2,1)S(1)}, bf16[192,256]{1,0:T(8,128)(2,1)S(1)}, u32[]{:S(2)}, u32[]{:S(2)}) collective-permute-start(bf16[192,256]{1,0:T(8,128)(2,1)S(1)} %get-tuple-element.41), channel_id=1, source_target_pairs={{0,4},{4,0},{8,12},{12,8},{16,20},{20,16},{24,28},{28,24},{1,5},{5... | collective-permute-start | bytes 294920 | tf_op jit(solution)/shard_map/ppermute | solution.py:775
  2.2 5.7 %collective-permute-start.1 = (bf16[192,256]{1,0:T(8,128)(2,1)S(1)}, bf16[192,256]{1,0:T(8,128)(2,1)S(1)}, u32[]{:S(2)}, u32[]{:S(2)}) collective-permute-start(bf16[192,256]{1,0:T(8,128)(2,1)S(1)} %get-tuple-element.42), channel_id=1, source_target_pairs={{0,28},{4,8},{8,4},{12,16},{16,12},{20,24},{24,20},{28,0},{1,29},{... | collective-permute-start | bytes 294920 | tf_op jit(solution)/shard_map/ppermute | solution.py:776
  8.1 5.8 %collective-permute-start.2 = (bf16[96,128]{1,0:T(8,128)(2,1)S(1)}, bf16[96,128]{1,0:T(8,128)(2,1)S(1)}, u32[]{:S(2)}, u32[]{:S(2)}) collective-permute-start(bf16[96,128]{1,0:T(8,128)(2,1)S(1)} %get-tuple-element.45.after), channel_id=1, source_target_pairs={{0,1},{1,0},{2,3},{3,2},{4,5},{5,4},{6,7},{7,6},{8,9},{9,8},{10,11... | collective-permute-start | bytes 73736 | tf_op jit(solution)/shard_map/ppermute | solution.py:817
  8.2 5.8 %collective-permute-start.3 = (bf16[96,128]{1,0:T(8,128)(2,1)S(1)}, bf16[96,128]{1,0:T(8,128)(2,1)S(1)}, u32[]{:S(2)}, u32[]{:S(2)}) collective-permute-start(bf16[96,128]{1,0:T(8,128)(2,1)S(1)} %get-tuple-element.56.own_tail), channel_id=1, source_target_pairs={{1,2},{2,1},{0,4},{3,31},{5,6},{6,5},{4,0},{7,27},{9,10},{10,9},{8... | collective-permute-start | bytes 73736 | tf_op jit(solution)/shard_map/ppermute | solution.py:823

commit v13 on v12

--- a/solution.py
+++ b/solution.py
@@ -137,13 +137,14 @@
 
 
 def prepare_kernel(sizes, noise, u, v, h, sea, *refs):
-    w1, bias1, t1, head, tail, middle, pre, cells, turned = refs
+    w1, w2, w3, bias1, bias2, bias3, t1, t2, t3, head, tail, middle, pre, cells, turned = refs
     held = (noise, u, v, h, sea)
     members, noises, levels = sizes
     fields = noises + 3 * levels
     lons, lats = sea.shape
     groups = lons // GROUP + 1
     first_weights(w1, bias1, t1)
+    hidden_weights(w2, w3, bias2, bias3, t2, t3)
     lane = iota((GROUP, LANES), 1)
     for out, t, first in ((head, 0, 0), (tail, lats // LANES - 1, LANES - RIM)):
         for c in range(fields + 1):
@@ -186,9 +187,9 @@
             put(pre, g + 1, r, activate(dot(jnp.concatenate(parts, axis=1), t1[...])))
 
 
-def row_pieces(rows):
-    half = rows // 2 // SUB * SUB
-    return [(0, half), (half, rows - half)]
+def row_pieces(rows, count=2):
+    cuts = [rows // SUB * n // count * SUB for n in range(count + 1)]
+    return [(a, b - a) for a, b in zip(cuts, cuts[1:])]
 
 
 def activate(pre):
@@ -208,7 +209,7 @@
 
 
 def cells_kernel(sizes, noise, u, v, h, sea, lon_even, lon_odd, after, *refs):
-    weights, (t1, _, out, base, pre, *matrices, rims, cells, turned) = refs[:5], refs[5:]
+    w4, t1, _, out, base, pre, t4, rims, cells, turned = refs
     members, noises, levels = sizes
     fields = noises + 3 * levels
     lons, lats = sea.shape
@@ -244,7 +245,7 @@
         for r, step in row_pieces(rows):
             parts = [out[side, pl.ds(r + SUB * d, step), :] for d in range(3)]
             put(pre, side * (groups - 1), r, activate(dot(jnp.concatenate(parts, axis=1), t1[...])))
-    other_weights(*weights, *matrices)
+    last_weights(w4, t4)
     step_kernel(sizes, u, v, h, sea, rims, base)
 
 
@@ -391,7 +392,7 @@
             t1[pl.ds(dj * LANES, LANES), pl.ds(tile * LANES, LANES)] = block.astype(bf16)
 
 
-def other_weights(w2, w3, w4, bias2, bias3, t2, t3, t4):
+def hidden_weights(w2, w3, bias2, bias3, t2, t3):
     hidden = w2.shape[2]
     per = LANES // hidden
     lane = iota((hidden, LANES), 1)
@@ -426,6 +427,9 @@
             row = 3 * GROUP * hidden + 6 * hidden
             t[pl.ds(row, 2 * hidden), pl.ds(tile * LANES, LANES)] = block.astype(bf16)
 
+
+def last_weights(w4, t4):
+    hidden = w4.shape[3]
     outs = w4.shape[2]
     half = LANES // 2
     lons = half // outs
@@ -546,7 +550,7 @@
     hidden = LANES // 4
     per = LANES // hidden
     tiles = odd.shape[0]
-    pieces = row_pieces(rows)
+    pieces = row_pieces(rows, 4)
 
     def finish(x, valid):
         used = (valid + per - 1) // per
@@ -683,7 +687,7 @@
 
     depth = t4.shape[1] // LANES
     padded = rows + 2 * SUB
-    for r, long in row_pieces(padded):
+    for r, long in row_pieces(padded, 4):
         before = iota((long, LANES), 1) < LANES // 2
         span_rows = pl.ds(r, long)
         sides = []
@@ -781,17 +785,19 @@
     deep = -(-(lons // 2 + 2) * hidden // LANES) * LANES
     padded = rows + 2 * SUB
     tiles = 2 * groups + 1
-    t1, own_head, own_tail, middle, pre = pl.pallas_call(
+    t1, t2, t3, own_head, own_tail, middle, pre = pl.pallas_call(
         functools.partial(prepare_kernel, sizes),
         out_shape=[
             pltpu.VMEM((3 * LANES, 2 * LANES), bf16),
+            pltpu.VMEM((8 * LANES, 2 * LANES), bf16),
+            pltpu.VMEM((8 * LANES, 2 * LANES), bf16),
             part,
             part,
             pltpu.VMEM((groups - 2, padded, LANES), bf16),
             pltpu.VMEM((tiles, padded, LANES), bf16),
         ],
-        in_specs=[whole] * 7,
-        out_specs=[whole] * 5,
+        in_specs=[whole] * 11,
+        out_specs=[whole] * 7,
         scratch_shapes=[
             pltpu.VMEM((groups - 2, rows, LANES), f32),
             pltpu.VMEM((members * (groups - 2) * lats // LANES, LANES, LANES), f32),
@@ -799,7 +805,7 @@
         compiler_params=pltpu.CompilerParams(vmem_limit_bytes=12 * 2**20),
         cost_estimate=pl.CostEstimate(flops=10**7, bytes_accessed=10**7, transcendentals=0),
         name="prepare",
-    )(*held[:6], held[9])
+    )(*held[:8], *held[9:])
     last = lat_count - 1
     smem = pl.BlockSpec(memory_space=pltpu.SMEM)
     to_even, to_odd = pl.pallas_call(
@@ -822,19 +828,17 @@
         pairs += [(at, (t ^ 1) * lat_count), (at + last, (lon_count - 1 - t) * lat_count + last)]
     odd_rim = lax.ppermute(to_odd, ("lon", "lat"), pairs)
 
-    ends, base, pre, t2, t3, t4 = pl.pallas_call(
+    ends, base, pre, t4 = pl.pallas_call(
         functools.partial(cells_kernel, sizes),
         out_shape=[
             pltpu.VMEM((2, padded, LANES), bf16),
             pltpu.VMEM((3, *velocity_u.shape), f32),
             pltpu.VMEM(pre.shape, bf16),
-            pltpu.VMEM((8 * LANES, 2 * LANES), bf16),
-            pltpu.VMEM((8 * LANES, 2 * LANES), bf16),
             pltpu.VMEM((2, deep, 2 * LANES), bf16),
         ],
-        in_specs=[whole] * 15,
-        out_specs=[whole] * 6,
-        input_output_aliases={14: 2},
+        in_specs=[whole] * 11,
+        out_specs=[whole] * 4,
+        input_output_aliases={10: 2},
         scratch_shapes=[
             pltpu.VMEM((2, tall, lats), f32),
             pltpu.VMEM((2, rows, LANES), f32),
@@ -843,7 +847,7 @@
         compiler_params=pltpu.CompilerParams(vmem_limit_bytes=12 * 2**20),
         cost_estimate=pl.CostEstimate(flops=10**7, bytes_accessed=10**7, transcendentals=0),
         name="cells",
-    )(*state, lon_even, lon_odd, to_even, *held[6:9], *held[10:12], t1, pre)
+    )(*state, lon_even, lon_odd, to_even, held[8], t1, pre)
 
     out = jax.ShapeDtypeStruct(velocity_u.shape, f32)
     return pl.pallas_call(

time: 23.7 us -> 23.3 us (0.983)
  the two profiles are of different devices: /device:TPU:12 before, /device:TPU:20 now
where the time goes in v13:
time: 23.3 us; the launch traced here: 23.1 us
  Pallas kernels  15.9 us (68%)
  waiting for transfers between devices  3.28 us (14%)
  starting transfers between devices  3.25 us (14%)
  between operations  0.69 us (3%)
    pallas_call x1, Pallas kernels, body(): pl.pallas_call(functools.partial(main_kernel, sizes), out_shape=[out] * 3...  9.57 us
    pallas_call x1, Pallas kernels, body(): pl.pallas_call(functools.partial(prepare_kernel, sizes), out_shape=[pltpu...  2.59 us
    pallas_call x1, Pallas kernels, body(): pl.pallas_call(functools.partial(cells_kernel, sizes), out_shape=[pltpu.V...  2.11 us
    ppermute x1, starting transfers between devices, body(): lax.ppermute(to_even, 'lat', [(i, i ^ 1) for i in range(lat_count)])  1.64 us
    ppermute x1, waiting for transfers between devices, body(): odd_rim = lax.ppermute(to_odd, ('lon', 'lat'), pairs)  1.58 us
    ppermute x1, waiting for transfers between devices, body(): lax.ppermute(to_odd, 'lon', [(i, (i - 1 + 2 * (i % 2)) % lon_count) for i...  1.57 us
    ppermute x1, starting transfers between devices, body(): lax.ppermute(to_odd, 'lon', [(i, (i - 1 + 2 * (i % 2)) % lon_count) for i...  1.54 us
    pallas_call x1, Pallas kernels, body(): pl.pallas_call(functools.partial(pack_lon_kernel, sizes, count), out_shap...  1.46 us
  transfers between devices with their start and end apart: 4, of which 3 were waited for; matrix products, arithmetic and copies ran while one was open for 0% of the time, Pallas kernels for 20%

profile of v13, /device:TPU:20, one launch (start us, length us, event | category | flops | bytes accessed | tf_op | source)
XLA Modules:
  0.0 23.1 jit_solution(14599982080366883602)
XLA Ops:
  0.6 1.5 %pack_lon.1 = (bf16[4,4,32,256]{3,2,1,0:T(8,128)(2,1)S(1)}, f32[4,2,32,256]{3,2,1,0:T(8,128)S(1)}, f32[4,2,32,256]{3,2,1,0:T(8,128)S(1)}, f32[4,2,32,256]{3,2,1,...) custom-call(bf16[4,4,32,256]{3,2,1,0:T(8,128)(2,1)} %refs_0_.1, ...), custom_call_target="tpu_custom_call" | custom-call | tf_op jit(solution)/shard_map/pack_lon/pallas_call | solution.py:769
  2.1 0.0 copy-start
  2.1 0.1 collective-permute-start
  2.2 1.5 %collective-permute-start.1 = (bf16[192,256]{1,0:T(8,128)(2,1)S(1)}, bf16[192,256]{1,0:T(8,128)(2,1)S(1)}, u32[]{:S(2)}, u32[]{:S(2)}) collective-permute-start(bf16[192,256]{1,0:T(8,128)(2,1)S(1)} %get-tuple-element.46), channel_id=1, source_target_pairs={{0,28},{4,8},{8,4},{12,16},{16,12},{20,24},{24,20},{28,0},{1,29},{... | collective-permute-start | bytes 294920 | tf_op jit(solution)/shard_map/ppermute | solution.py:780
  3.7 2.6 %prepare.1 = (bf16[384,256]{1,0:T(8,128)(2,1)S(1)}, bf16[1024,256]{1,0:T(8,128)(2,1)S(1)}, bf16[1024,256]{1,0:T(8,128)(2,1)S(1)}, f32[96,128]{1,0:T(8,128)S(1)},...) custom-call(bf16[4,4,32,256]{3,2,1,0:T(8,128)(2,1)S(1)} %get-tuple-element.33.noise, ...), custom_call_target="tpu_custom_call" | custom-call | flops 10000000 | bytes 10000000 | tf_op jit(solution)/shard_map/prepare/pallas_call | solution.py:788
  6.3 0.0 collective-permute-done.lon_even
  6.3 1.6 %collective-permute-done.1.lon_odd = bf16[192,256]{1,0:T(8,128)(2,1)S(1)} collective-permute-done((bf16[192,256]{1,0:T(8,128)(2,1)S(1)}, bf16[192,256]{1,0:T(8,128)(2,1)S(1)}, u32[]{:S(2)}, u32[]{:S(2)}) %collective-permute-start.1) | collective-permute-done | bytes 98336 | tf_op jit(solution)/shard_map/ppermute | solution.py:780
  7.9 0.2 join_rims.1
  8.1 1.6 %collective-permute-start.2 = (bf16[96,128]{1,0:T(8,128)(2,1)S(1)}, bf16[96,128]{1,0:T(8,128)(2,1)S(1)}, u32[]{:S(2)}, u32[]{:S(2)}) collective-permute-start(bf16[96,128]{1,0:T(8,128)(2,1)S(1)} %get-tuple-element.49.after), channel_id=1, source_target_pairs={{0,1},{1,0},{2,3},{3,2},{4,5},{5,4},{6,7},{7,6},{8,9},{9,8},{10,11... | collective-permute-start | bytes 73736 | tf_op jit(solution)/shard_map/ppermute | solution.py:823
  9.7 0.0 collective-permute-start.3
  9.7 2.1 %cells.1 = (bf16[2,1120,128]{2,1,0:T(8,128)(2,1)S(1)}, f32[3,4,2,32,256]{4,3,2,1,0:T(8,128)S(1)}, bf16[11,1120,128]{2,1,0:T(8,128)(2,1)S(1)}, bf16[2,640,256]{2,1,0:T(8,128)(2,1)S(1)}) custom-call(bf16[4,4,32,256]{3,2,1,0:T(8,128)(2,1)S(1)} %get-tuple-element.33.noise, f32[4,2,32,256]{3,2,1,0:T(8,128)S(1)} %get-tuple-element.34.u, ...), custom_call_target="tpu_custom_call", output_to_operand_aliasing={{2}: (10, {})} | custom-call | flops 10000000 | bytes 10000000 | tf_op jit(solution)/shard_map/cells/pallas_call | solution.py:831
  11.8 0.1 collective-permute-done.2.even_rim
  12.0 1.6 %collective-permute-done.3.odd_rim = bf16[96,128]{1,0:T(8,128)(2,1)S(1)} collective-permute-done((bf16[96,128]{1,0:T(8,128)(2,1)S(1)}, bf16[96,128]{1,0:T(8,128)(2,1)S(1)}, u32[]{:S(2)}, u32[]{:S(2)}) %collective-permute-start.3) | collective-permute-done | bytes 24608 | tf_op jit(solution)/shard_map/ppermute | solution.py:829
  13.5 0.0 copy-done
  13.6 9.6 %network_and_step.1 = (f32[4,2,32,256]{3,2,1,0:T(8,128)}, f32[4,2,32,256]{3,2,1,0:T(8,128)}, f32[4,2,32,256]{3,2,1,0:T(8,128)}, bf16[3,1120,128]{2,1,0:T(8,128)(...) custom-call(f32[4]{0:T(128)S(1)} %copy-done, ...), custom_call_target="tpu_custom_call", output_to_operand_aliasing={{3}: (1, {}), {4}: (2, {}), {5}: (3, {})} | custom-call | flops 20000000000 | bytes 10000000 | tf_op jit(solution)/shard_map/network_and_step/pallas_call | solution.py:853
Async XLA Ops:
  2.1 11.5 %copy-start = (f32[4]{0:T(128)S(1)}, f32[4]{0:T(128)}, u32[]{:S(2)}) copy-start(f32[4]{0:T(128)} %bias_last.1) | copy-start | bytes 52
  2.1 4.2 %collective-permute-start = (bf16[192,256]{1,0:T(8,128)(2,1)S(1)}, bf16[192,256]{1,0:T(8,128)(2,1)S(1)}, u32[]{:S(2)}, u32[]{:S(2)}) collective-permute-start(bf16[192,256]{1,0:T(8,128)(2,1)S(1)} %get-tuple-element.45), channel_id=1, source_target_pairs={{0,4},{4,0},{8,12},{12,8},{16,20},{20,16},{24,28},{28,24},{1,5},{5... | collective-permute-start | bytes 294920 | tf_op jit(solution)/shard_map/ppermute | solution.py:779
  2.2 5.7 %collective-permute-start.1 = (bf16[192,256]{1,0:T(8,128)(2,1)S(1)}, bf16[192,256]{1,0:T(8,128)(2,1)S(1)}, u32[]{:S(2)}, u32[]{:S(2)}) collective-permute-start(bf16[192,256]{1,0:T(8,128)(2,1)S(1)} %get-tuple-element.46), channel_id=1, source_target_pairs={{0,28},{4,8},{8,4},{12,16},{16,12},{20,24},{24,20},{28,0},{1,29},{... | collective-permute-start | bytes 294920 | tf_op jit(solution)/shard_map/ppermute | solution.py:780
  8.1 3.9 %collective-permute-start.2 = (bf16[96,128]{1,0:T(8,128)(2,1)S(1)}, bf16[96,128]{1,0:T(8,128)(2,1)S(1)}, u32[]{:S(2)}, u32[]{:S(2)}) collective-permute-start(bf16[96,128]{1,0:T(8,128)(2,1)S(1)} %get-tuple-element.49.after), channel_id=1, source_target_pairs={{0,1},{1,0},{2,3},{3,2},{4,5},{5,4},{6,7},{7,6},{8,9},{9,8},{10,11... | collective-permute-start | bytes 73736 | tf_op jit(solution)/shard_map/ppermute | solution.py:823
  9.7 3.8 %collective-permute-start.3 = (bf16[96,128]{1,0:T(8,128)(2,1)S(1)}, bf16[96,128]{1,0:T(8,128)(2,1)S(1)}, u32[]{:S(2)}, u32[]{:S(2)}) collective-permute-start(bf16[96,128]{1,0:T(8,128)(2,1)S(1)} %get-tuple-element.56.own_tail), channel_id=1, source_target_pairs={{1,2},{2,1},{0,4},{3,31},{5,6},{6,5},{4,0},{7,27},{9,10},{10,9},{8... | collective-permute-start | bytes 73736 | tf_op jit(solution)/shard_map/ppermute | solution.py:829

commit v14 on v13

--- a/solution.py
+++ b/solution.py
@@ -799,8 +799,8 @@
         in_specs=[whole] * 11,
         out_specs=[whole] * 7,
         scratch_shapes=[
-            pltpu.VMEM((groups - 2, rows, LANES), f32),
-            pltpu.VMEM((members * (groups - 2) * lats // LANES, LANES, LANES), f32),
+            pltpu.VMEM((groups - 1, rows, LANES), f32),
+            pltpu.VMEM((members * (groups - 2) * lats // LANES + 1, LANES, LANES), f32),
         ],
         compiler_params=pltpu.CompilerParams(vmem_limit_bytes=12 * 2**20),
         cost_estimate=pl.CostEstimate(flops=10**7, bytes_accessed=10**7, transcendentals=0),
@@ -841,8 +841,8 @@
         input_output_aliases={10: 2},
         scratch_shapes=[
             pltpu.VMEM((2, tall, lats), f32),
-            pltpu.VMEM((2, rows, LANES), f32),
-            pltpu.VMEM((2 * members * lats // LANES, LANES, LANES), f32),
+            pltpu.VMEM((3, rows, LANES), f32),
+            pltpu.VMEM((2 * members * lats // LANES + 1, LANES, LANES), f32),
         ],
         compiler_params=pltpu.CompilerParams(vmem_limit_bytes=12 * 2**20),
         cost_estimate=pl.CostEstimate(flops=10**7, bytes_accessed=10**7, transcendentals=0),
@@ -859,9 +859,9 @@
         scratch_shapes=[
             pltpu.VMEM((tiles, padded, LANES), bf16),
             pltpu.VMEM((3, padded, LANES), f32),
-            pltpu.VMEM((members, lats, LANES), f32),
-            pltpu.VMEM((4, LANES, LANES), f32),
-            pltpu.VMEM((groups, GAP * SUB, LANES), f32),
+            pltpu.VMEM((members + 1, lats, LANES), f32),
+            pltpu.VMEM((5, LANES, LANES), f32),
+            pltpu.VMEM((groups + 1, GAP * SUB, LANES), f32),
             pltpu.VMEM((3, *velocity_u.shape), f32),
             pltpu.SemaphoreType.DMA((3, members)),
         ],

time: 23.3 us -> 23.3 us (level)
  no operation moved by 1% of the time
where the time goes in v14:
time: 23.3 us; the launch traced here: 23.1 us
  Pallas kernels  15.9 us (68%)
  waiting for transfers between devices  3.28 us (14%)
  starting transfers between devices  3.25 us (14%)
  between operations  0.69 us (3%)
    pallas_call x1, Pallas kernels, body(): pl.pallas_call(functools.partial(main_kernel, sizes), out_shape=[out] * 3...  9.57 us
    pallas_call x1, Pallas kernels, body(): pl.pallas_call(functools.partial(prepare_kernel, sizes), out_shape=[pltpu...  2.59 us
    pallas_call x1, Pallas kernels, body(): pl.pallas_call(functools.partial(cells_kernel, sizes), out_shape=[pltpu.V...  2.11 us
    ppermute x1, starting transfers between devices, body(): lax.ppermute(to_even, 'lat', [(i, i ^ 1) for i in range(lat_count)])  1.64 us
    ppermute x1, waiting for transfers between devices, body(): odd_rim = lax.ppermute(to_odd, ('lon', 'lat'), pairs)  1.58 us
    ppermute x1, waiting for transfers between devices, body(): lax.ppermute(to_odd, 'lon', [(i, (i - 1 + 2 * (i % 2)) % lon_count) for i...  1.57 us
    ppermute x1, starting transfers between devices, body(): lax.ppermute(to_odd, 'lon', [(i, (i - 1 + 2 * (i % 2)) % lon_count) for i...  1.54 us
    pallas_call x1, Pallas kernels, body(): pl.pallas_call(functools.partial(pack_lon_kernel, sizes, count), out_shap...  1.46 us
  transfers between devices with their start and end apart: 4, of which 3 were waited for; matrix products, arithmetic and copies ran while one was open for 0% of the time, Pallas kernels for 20%

profile of v14, /device:TPU:20, one launch (start us, length us, event | category | flops | bytes accessed | tf_op | source)
XLA Modules:
  0.0 23.1 jit_solution(8986905346401811335)
XLA Ops:
  0.6 1.5 %pack_lon.1 = (bf16[4,4,32,256]{3,2,1,0:T(8,128)(2,1)S(1)}, f32[4,2,32,256]{3,2,1,0:T(8,128)S(1)}, f32[4,2,32,256]{3,2,1,0:T(8,128)S(1)}, f32[4,2,32,256]{3,2,1,...) custom-call(bf16[4,4,32,256]{3,2,1,0:T(8,128)(2,1)} %refs_0_.1, ...), custom_call_target="tpu_custom_call" | custom-call | tf_op jit(solution)/shard_map/pack_lon/pallas_call | solution.py:769
  2.1 0.0 copy-start
  2.1 0.1 collective-permute-start
  2.2 1.5 %collective-permute-start.1 = (bf16[192,256]{1,0:T(8,128)(2,1)S(1)}, bf16[192,256]{1,0:T(8,128)(2,1)S(1)}, u32[]{:S(2)}, u32[]{:S(2)}) collective-permute-start(bf16[192,256]{1,0:T(8,128)(2,1)S(1)} %get-tuple-element.46), channel_id=1, source_target_pairs={{0,28},{4,8},{8,4},{12,16},{16,12},{20,24},{24,20},{28,0},{1,29},{... | collective-permute-start | bytes 294920 | tf_op jit(solution)/shard_map/ppermute | solution.py:780
  3.7 2.6 %prepare.1 = (bf16[384,256]{1,0:T(8,128)(2,1)S(1)}, bf16[1024,256]{1,0:T(8,128)(2,1)S(1)}, bf16[1024,256]{1,0:T(8,128)(2,1)S(1)}, f32[96,128]{1,0:T(8,128)S(1)},...) custom-call(bf16[4,4,32,256]{3,2,1,0:T(8,128)(2,1)S(1)} %get-tuple-element.33.noise, ...), custom_call_target="tpu_custom_call" | custom-call | flops 10000000 | bytes 10000000 | tf_op jit(solution)/shard_map/prepare/pallas_call | solution.py:788
  6.3 0.0 collective-permute-done.lon_even
  6.3 1.6 %collective-permute-done.1.lon_odd = bf16[192,256]{1,0:T(8,128)(2,1)S(1)} collective-permute-done((bf16[192,256]{1,0:T(8,128)(2,1)S(1)}, bf16[192,256]{1,0:T(8,128)(2,1)S(1)}, u32[]{:S(2)}, u32[]{:S(2)}) %collective-permute-start.1) | collective-permute-done | bytes 98336 | tf_op jit(solution)/shard_map/ppermute | solution.py:780
  7.9 0.2 join_rims.1
  8.1 1.6 %collective-permute-start.2 = (bf16[96,128]{1,0:T(8,128)(2,1)S(1)}, bf16[96,128]{1,0:T(8,128)(2,1)S(1)}, u32[]{:S(2)}, u32[]{:S(2)}) collective-permute-start(bf16[96,128]{1,0:T(8,128)(2,1)S(1)} %get-tuple-element.49.after), channel_id=1, source_target_pairs={{0,1},{1,0},{2,3},{3,2},{4,5},{5,4},{6,7},{7,6},{8,9},{9,8},{10,11... | collective-permute-start | bytes 73736 | tf_op jit(solution)/shard_map/ppermute | solution.py:823
  9.7 0.0 collective-permute-start.3
  9.7 2.1 %cells.1 = (bf16[2,1120,128]{2,1,0:T(8,128)(2,1)S(1)}, f32[3,4,2,32,256]{4,3,2,1,0:T(8,128)S(1)}, bf16[11,1120,128]{2,1,0:T(8,128)(2,1)S(1)}, bf16[2,640,256]{2,1,0:T(8,128)(2,1)S(1)}) custom-call(bf16[4,4,32,256]{3,2,1,0:T(8,128)(2,1)S(1)} %get-tuple-element.33.noise, f32[4,2,32,256]{3,2,1,0:T(8,128)S(1)} %get-tuple-element.34.u, ...), custom_call_target="tpu_custom_call", output_to_operand_aliasing={{2}: (10, {})} | custom-call | flops 10000000 | bytes 10000000 | tf_op jit(solution)/shard_map/cells/pallas_call | solution.py:831
  11.8 0.1 collective-permute-done.2.even_rim
  12.0 1.6 %collective-permute-done.3.odd_rim = bf16[96,128]{1,0:T(8,128)(2,1)S(1)} collective-permute-done((bf16[96,128]{1,0:T(8,128)(2,1)S(1)}, bf16[96,128]{1,0:T(8,128)(2,1)S(1)}, u32[]{:S(2)}, u32[]{:S(2)}) %collective-permute-start.3) | collective-permute-done | bytes 24608 | tf_op jit(solution)/shard_map/ppermute | solution.py:829
  13.5 0.0 copy-done
  13.6 9.6 %network_and_step.1 = (f32[4,2,32,256]{3,2,1,0:T(8,128)}, f32[4,2,32,256]{3,2,1,0:T(8,128)}, f32[4,2,32,256]{3,2,1,0:T(8,128)}, bf16[3,1120,128]{2,1,0:T(8,128)(...) custom-call(f32[4]{0:T(128)S(1)} %copy-done, ...), custom_call_target="tpu_custom_call", output_to_operand_aliasing={{3}: (1, {}), {4}: (2, {}), {5}: (3, {})} | custom-call | flops 20000000000 | bytes 10000000 | tf_op jit(solution)/shard_map/network_and_step/pallas_call | solution.py:853
Async XLA Ops:
  2.1 11.5 %copy-start = (f32[4]{0:T(128)S(1)}, f32[4]{0:T(128)}, u32[]{:S(2)}) copy-start(f32[4]{0:T(128)} %bias_last.1) | copy-start | bytes 52
  2.1 4.2 %collective-permute-start = (bf16[192,256]{1,0:T(8,128)(2,1)S(1)}, bf16[192,256]{1,0:T(8,128)(2,1)S(1)}, u32[]{:S(2)}, u32[]{:S(2)}) collective-permute-start(bf16[192,256]{1,0:T(8,128)(2,1)S(1)} %get-tuple-element.45), channel_id=1, source_target_pairs={{0,4},{4,0},{8,12},{12,8},{16,20},{20,16},{24,28},{28,24},{1,5},{5... | collective-permute-start | bytes 294920 | tf_op jit(solution)/shard_map/ppermute | solution.py:779
  2.2 5.7 %collective-permute-start.1 = (bf16[192,256]{1,0:T(8,128)(2,1)S(1)}, bf16[192,256]{1,0:T(8,128)(2,1)S(1)}, u32[]{:S(2)}, u32[]{:S(2)}) collective-permute-start(bf16[192,256]{1,0:T(8,128)(2,1)S(1)} %get-tuple-element.46), channel_id=1, source_target_pairs={{0,28},{4,8},{8,4},{12,16},{16,12},{20,24},{24,20},{28,0},{1,29},{... | collective-permute-start | bytes 294920 | tf_op jit(solution)/shard_map/ppermute | solution.py:780
  8.1 3.9 %collective-permute-start.2 = (bf16[96,128]{1,0:T(8,128)(2,1)S(1)}, bf16[96,128]{1,0:T(8,128)(2,1)S(1)}, u32[]{:S(2)}, u32[]{:S(2)}) collective-permute-start(bf16[96,128]{1,0:T(8,128)(2,1)S(1)} %get-tuple-element.49.after), channel_id=1, source_target_pairs={{0,1},{1,0},{2,3},{3,2},{4,5},{5,4},{6,7},{7,6},{8,9},{9,8},{10,11... | collective-permute-start | bytes 73736 | tf_op jit(solution)/shard_map/ppermute | solution.py:823
  9.7 3.8 %collective-permute-start.3 = (bf16[96,128]{1,0:T(8,128)(2,1)S(1)}, bf16[96,128]{1,0:T(8,128)(2,1)S(1)}, u32[]{:S(2)}, u32[]{:S(2)}) collective-permute-start(bf16[96,128]{1,0:T(8,128)(2,1)S(1)} %get-tuple-element.56.own_tail), channel_id=1, source_target_pairs={{1,2},{2,1},{0,4},{3,31},{5,6},{6,5},{4,0},{7,27},{9,10},{10,9},{8... | collective-permute-start | bytes 73736 | tf_op jit(solution)/shard_map/ppermute | solution.py:829
